TPU v7x, 32 devices: a whole 2x2x4 slice. The times are simulated.
32 devices in a mesh: rep: 2 (over core), ep: 4 (over z), dp: 4 (over y, x).
Axes of the slice: x: 2, y: 2, z: 4, core: 2. Of those that a mesh axis runs over, the one named last changes fastest.
Arguments:
- tokens: bfloat16 [1024, 2048], P(('rep', 'ep', 'dp')), may hold values from -6 to 6
- upstream: bfloat16 [1024, 2048], P(('rep', 'ep', 'dp')), may hold values from -6 to 6
- expert_ids: int32 [1024, 2], P(('rep', 'ep', 'dp')), may hold values from 0 to 3, all different within a row; in each aligned block of 32 rows (0 to 31, 32 to 63, ...) at most 20 rows name the same one
- route_weight: bfloat16 [1024, 2], P(('rep', 'ep', 'dp')), may hold values from 0.099609375 to 1
- gate_weight: bfloat16 [4, 384, 2048], P('ep', 'dp'), may hold values from -0.125 to 0.125
- up_weight: bfloat16 [4, 384, 2048], P('ep', 'dp'), may hold values from -0.125 to 0.125
- down_weight: bfloat16 [4, 384, 2048], P('ep', 'dp'), may hold values from -0.3125 to 0.3125
Outputs:
- d_tokens: bfloat16 [1024, 2048], P(('rep', 'ep', 'dp'))
- d_probs: bfloat16 [1024, 2], P(('rep', 'ep', 'dp'))
- grad_down: float32 [4, 384, 2048], P('ep', 'dp')
Inputs may be any that keep to these rules, and one draw needn't show every extreme that they name: `expert_ids`: each row names 2 different experts; among the rows of one device no expert is named by more than 20 rows, and in every draw some expert is named by exactly 20 rows of some device.
All inputs are finite; a program needn't handle non-finite values.
Results may differ from a plain program's by a relative error of at most 0.012.
Values may be sent and summed in bfloat16 or wider, within the bound.
No kernel may reach another device: no remote copies, remote signals or barrier semaphores. Data moves between devices by JAX's collectives and lax.ppermute only.
A program may use at most 64 MiB of HBM per device.

v0:
```python
import jax
import jax.numpy as jnp
from jax import lax
from jax.sharding import PartitionSpec as P


def contract_last(left, right):
    return lax.dot_general(
        left, right, (((1,), (1,)), ((), ())), preferred_element_type=jnp.float32
    )


def local(tokens, upstream, expert_ids, route_weight, gate_weight, up_weight, down_weight):
    tok_dev, model_width = tokens.shape
    top_count = expert_ids.shape[1]
    experts = lax.axis_size("ep")
    capacity = 2 * ((5 * tok_dev * top_count + 8 * experts - 1) // (8 * experts))
    route_count = tok_dev * top_count
    flat_ids = expert_ids.reshape(route_count)
    onehot = (flat_ids[:, None] == jnp.arange(experts, dtype=jnp.int32)[None, :]).astype(jnp.int32)
    before = jnp.cumsum(onehot, axis=0) - onehot
    rank_in = jnp.sum(before * onehot, axis=1)
    slot_index = flat_ids * capacity + rank_in
    slot_count = experts * capacity
    owner = (
        jnp.full((slot_count,), route_count, jnp.int32)
        .at[slot_index]
        .set(jnp.arange(route_count, dtype=jnp.int32))
    )
    is_valid = owner < route_count
    owner_safe = jnp.minimum(owner, route_count - 1)
    token_row = owner_safe // top_count
    x_send = jnp.where(is_valid[:, None], tokens[token_row], jnp.zeros((), tokens.dtype)).reshape(
        experts, capacity, model_width
    )
    dy_send = jnp.where(
        is_valid[:, None], upstream[token_row], jnp.zeros((), upstream.dtype)
    ).reshape(experts, capacity, model_width)
    weight_send = jnp.where(
        is_valid, route_weight.reshape(route_count)[owner_safe], jnp.zeros((), route_weight.dtype)
    ).reshape(experts, capacity)
    arrived = (
        lax.all_to_all(x_send, "ep", split_axis=0, concat_axis=0, tiled=True),
        lax.all_to_all(dy_send, "ep", split_axis=0, concat_axis=0, tiled=True),
        lax.all_to_all(weight_send, "ep", split_axis=0, concat_axis=0, tiled=True),
    )
    x_rows = arrived[0].reshape(slot_count, model_width)
    dy_rows = arrived[1].reshape(slot_count, model_width)
    weight_rows = arrived[2].reshape(slot_count)
    d_out = (weight_rows.astype(jnp.float32)[:, None] * dy_rows.astype(jnp.float32)).astype(
        jnp.bfloat16
    )
    gate_piece = lax.all_gather(gate_weight, "dp", axis=1, tiled=True)[0]
    up_piece = lax.all_gather(up_weight, "dp", axis=1, tiled=True)[0]
    down_piece = lax.all_gather(down_weight, "dp", axis=1, tiled=True)[0]
    gate_pre = contract_last(x_rows, gate_piece)
    up_pre = contract_last(x_rows, up_piece)
    sig_gate = jax.nn.sigmoid(gate_pre)
    silu_gate = gate_pre * sig_gate
    act_rows = (silu_gate * up_pre).astype(jnp.bfloat16)
    out_sum = jnp.dot(act_rows, down_piece, preferred_element_type=jnp.float32)
    d_act = contract_last(d_out, down_piece)
    d_gate = (d_act * up_pre * sig_gate * (1.0 + gate_pre * (1.0 - sig_gate))).astype(jnp.bfloat16)
    d_up = (d_act * silu_gate).astype(jnp.bfloat16)
    dx_sum = jnp.dot(d_gate, gate_piece, preferred_element_type=jnp.float32)
    dx_sum = dx_sum + jnp.dot(d_up, up_piece, preferred_element_type=jnp.float32)
    grad_piece = lax.dot_general(
        act_rows, d_out, (((0,), (0,)), ((), ())), preferred_element_type=jnp.float32
    )
    grad_full = grad_piece
    out_sum, dx_sum, grad_full = (out_sum, dx_sum, grad_full)
    dprob_rows = (
        jnp.sum(dy_rows.astype(jnp.float32) * out_sum, axis=-1)
        .astype(jnp.bfloat16)
        .reshape(experts, capacity)
    )
    dx_rows = dx_sum.astype(jnp.bfloat16).reshape(experts, capacity, model_width)
    returned = (
        lax.all_to_all(dx_rows, "ep", split_axis=0, concat_axis=0, tiled=True),
        lax.all_to_all(dprob_rows, "ep", split_axis=0, concat_axis=0, tiled=True),
    )
    dx_slots = returned[0].reshape(slot_count, model_width)
    dprob_slots = returned[1].reshape(slot_count)
    route_dx = dx_slots[slot_index].astype(jnp.float32).reshape(tok_dev, top_count, model_width)
    d_tokens = jnp.sum(route_dx, axis=1).astype(jnp.bfloat16)
    d_probs = dprob_slots[slot_index].reshape(tok_dev, top_count)
    grad_shard = lax.psum_scatter(
        grad_full.astype(jnp.bfloat16), "dp", scatter_dimension=0, tiled=True
    )
    grad_total = lax.psum(grad_shard, "rep").astype(jnp.float32)
    return (d_tokens, d_probs, grad_total[None])


def solution(mesh):
    placed = (
        P(("rep", "ep", "dp"), None),
        P(("rep", "ep", "dp"), None),
        P(("rep", "ep", "dp"), None),
        P(("rep", "ep", "dp"), None),
        P("ep", "dp", None),
        P("ep", "dp", None),
        P("ep", "dp", None),
    )
    return jax.shard_map(
        local,
        mesh=mesh,
        in_specs=placed,
        out_specs=(P(("rep", "ep", "dp"), None), P(("rep", "ep", "dp"), None), P("ep", "dp", None)),
        check_vma=False,
    )
```

profile of v0, /device:TPU:0, one launch (start us, length us, event | category | flops | bytes accessed | tf_op | source)
XLA Modules:
  0.0 172.2 jit_solution(17504008220606196376)
XLA Ops:
  7.2 0.7 all-gather.8.cloned.1.call-update
  8.0 0.7 all-gather.6.cloned.1.call-update
  8.7 0.8 copy.25
  9.4 0.7 broadcast_multiply_fusion
  10.2 0.1 mul.58
  10.3 0.1 eq.15
  10.4 0.8 copy.26
  11.2 0.1 reshape.111
  11.4 0.1 reduce_window_sum.11
  11.5 0.2 select_reduce_fusion
  11.7 0.8 scatter_custom_fusion
  12.5 1.2 gather_fusion
  13.7 0.7 all_to_all.25
  14.4 6.3 %all-to-all-start = ((bf16[4,1,20]{2,1,0:T(2,128)(2,1)}), bf16[4,1,20]{2,1,0:T(2,128)(2,1)S(1)}, u32[]{:S(2)}, u32[]{:S(2)}) async-start(bf16[4,1,20]{2,1,0:T(2,128)(2,1)} %all_to_all.25), calls=%async_computation | async-start | bytes 4096 | tf_op jit(solution)/shard_map/all_to_all | solution.py:45
  20.7 0.7 all-gather.4.cloned.1.call-update
  21.5 0.8 gather_fusion.1
  22.4 0.8 gather_fusion.2
  23.3 0.9 broadcast_select_fusion.1
  24.2 2.0 %all-to-all-done = bf16[4,1,20]{2,1,0:T(2,128)(2,1)S(1)} async-done(((bf16[4,1,20]{2,1,0:T(2,128)(2,1)}), bf16[4,1,20]{2,1,0:T(2,128)(2,1)S(1)}, u32[]{:S(2)}, u32[]{:S(2)}) %all-to-all-start) | async-done | bytes 192 | tf_op jit(solution)/shard_map/all_to_all | solution.py:45
  26.2 14.0 %all_to_all.31 = bf16[4,20,2048]{2,1,0:T(8,128)(2,1)S(1)} all-to-all(bf16[4,20,2048]{2,1,0:T(8,128)(2,1)S(1)} %get-tuple-element.16), channel_id=1, replica_groups=mesh['rep'=2,'ep'=4,'dp'=4] {'ep'}, dimensions={0} | all-to-all | bytes 655360 | tf_op jit(solution)/shard_map/all_to_all | solution.py:43
  40.2 3.5 %all-to-all-start.1 = ((bf16[4,20,2048]{2,1,0:T(8,128)(2,1)}), bf16[4,20,2048]{2,1,0:T(8,128)(2,1)S(1)}, u32[]{:S(2)}, u32[]{:S(2)}) async-start(bf16[4,20,2048]{2,1,0:T(8,128)(2,1)} %get-tuple-element.15), calls=%async_computation.1 | async-start | bytes 786432 | tf_op jit(solution)/shard_map/all_to_all | solution.py:44
  43.9 10.3 %all-to-all-done.1 = bf16[4,20,2048]{2,1,0:T(8,128)(2,1)S(1)} async-done(((bf16[4,20,2048]{2,1,0:T(8,128)(2,1)}), bf16[4,20,2048]{2,1,0:T(8,128)(2,1)S(1)}, u32[]{:S(2)}, u32[]{:S(2)}) %all-to-all-start.1) | async-done | bytes 327712 | tf_op jit(solution)/shard_map/all_to_all | solution.py:44
  54.2 2.0 %fusion.3 = f32[80,384]{1,0:T(8,128)S(1)} fusion(bf16[80,2048]{1,0:T(8,128)(2,1)S(1)} %reshape.112, bf16[1,384,2048]{2,1,0:T(8,128)(2,1)} %all-gather.8.cloned.1.call-done), kind=kOutput, calls=%fused_computation.12 | convolution fusion | flops 125829120 | bytes 2023424 | tf_op jit(solution)/shard_map/dot_general | solution.py:8
  56.2 20.2 %all-gather.6.cloned.1.call-done = bf16[1,384,2048]{2,1,0:T(8,128)(2,1)} async-done(((bf16[1,96,2048]{2,1,0:T(8,128)(2,1)}), bf16[1,384,2048]{2,1,0:T(8,128)(2,1)}) %all-gather.6.cloned.1.call-update) | async-done | bytes 1572880 | tf_op jit(solution)/shard_map/all_gather | solution.py:54
  76.4 2.0 %multiply_convert_fusion.3 = (bf16[80,384]{1,0:T(8,128)(2,1)S(1)}, f32[80,384]{1,0:T(8,128)S(1)}) fusion(f32[80,384]{1,0:T(8,128)S(1)} %fusion.3, bf16[80,2048]{1,0:T(8,128)(2,1)S(1)} %reshape.112, bf16[1,384,2048]{2,1,0:T(8,128)(2,1)} %all-gather.6.cloned.1.call-done), kind=kOutput, calls=%fused_computation.26 | convolution fusion | flops 126013440 | bytes 2207744 | tf_op jit(solution)/shard_map/dot_general | solution.py:8
  78.4 1.8 %convolution_convert_fusion = bf16[384,2048]{1,0:T(8,128)(2,1)} fusion(bf16[80,384]{1,0:T(8,128)(2,1)S(1)} %get-tuple-element.19, f32[80,2048]{1,0:T(8,128)S(1)} %reshape.118, f32[80]{0:T(128)S(1)} %reshape.119), kind=kOutput, calls=%fused_computation.6 | convolution fusion | flops 126943232 | bytes 2289984 | tf_op jit(solution)/shard_map/dot_general | solution.py:67
  80.2 0.1 multiply_convert_fusion
  80.4 0.8 convert_element_type.75
  81.2 28.1 %all-gather.4.cloned.1.call-done = bf16[1,384,2048]{2,1,0:T(8,128)(2,1)} async-done(((bf16[1,96,2048]{2,1,0:T(8,128)(2,1)}), bf16[1,384,2048]{2,1,0:T(8,128)(2,1)}) %all-gather.4.cloned.1.call-update) | async-done | bytes 1572880 | tf_op jit(solution)/shard_map/all_gather | solution.py:55
  109.3 2.1 %fusion.11 = bf16[80]{0:T(256)(128)(2,1)S(1)} fusion(f32[80,2048]{1,0:T(8,128)S(1)} %reshape.118, bf16[80,384]{1,0:T(8,128)(2,1)S(1)} %get-tuple-element.19, bf16[1,384,2048]{2,1,0:T(8,128)(2,1)} %all-gather.4.cloned.1.call-done), kind=kOutput, calls=%fused_computation.20 | convolution fusion | flops 126156720 | bytes 2289824 | tf_op jit(solution)/shard_map/dot_general | solution.py:61
  111.3 0.7 convert_element_type.91
  112.0 4.6 %all-to-all-start.4 = ((bf16[4,1,20]{2,1,0:T(2,128)(2,1)}), bf16[4,1,20]{2,1,0:T(2,128)(2,1)S(1)}, u32[]{:S(2)}, u32[]{:S(2)}) async-start(bf16[4,1,20]{2,1,0:T(2,128)(2,1)} %convert_element_type.91), calls=%async_computation.4 | async-start | bytes 4096 | tf_op jit(solution)/shard_map/all_to_all | solution.py:80
  116.6 1.6 fusion.9
  118.2 0.4 fusion.1
  118.6 1.0 copy-done.4
  119.7 0.4 fusion
  120.1 0.8 reshape.113
  120.9 1.2 all-to-all-done.4
  122.1 3.9 %all-to-all-start.3 = ((bf16[4,20,2048]{2,1,0:T(8,128)(2,1)}), bf16[4,20,2048]{2,1,0:T(8,128)(2,1)S(1)}, u32[]{:S(2)}, u32[]{:S(2)}) async-start(bf16[4,20,2048]{2,1,0:T(8,128)(2,1)} %reshape.113), calls=%async_computation.3 | async-start | bytes 786432 | tf_op jit(solution)/shard_map/all_to_all | solution.py:79
  126.0 17.1 %reduce-scatter.2.cloned.1.call-done = bf16[96,2048]{1,0:T(8,128)(2,1)} async-done(((bf16[384,2048]{1,0:T(8,128)(2,1)}), bf16[96,2048]{1,0:T(8,128)(2,1)}) %reduce-scatter.2.cloned.1.call-update) | async-done | bytes 393232 | tf_op jit(solution)/shard_map/reduce_scatter | solution.py:87
  143.2 0.8 gather_fusion.4
  144.0 0.1 reshape.116
  144.1 0.6 copy.29
  144.8 0.7 gather_fusion.3
  145.6 0.2 gather.27
  145.8 1.3 reduce_sum.34
  147.1 16.7 %all-reduce.2.cloned.1.call-done = bf16[1,96,2048]{2,1,0:T(8,128)(2,1)} async-done(((bf16[1,96,2048]{2,1,0:T(8,128)(2,1)}), bf16[1,96,2048]{2,1,0:T(8,128)(2,1)}) %all-reduce.2.cloned.1.call-update) | async-done | bytes 393232 | tf_op jit(solution)/shard_map/psum | solution.py:90
  163.8 1.9 %broadcast_in_dim.49 = f32[1,96,2048]{2,1,0:T(8,128)} convert(bf16[1,96,2048]{2,1,0:T(8,128)(2,1)} %all-reduce.2.cloned.1.call-done) | non-fusion elementwise | flops 196608 | bytes 1179648 | tf_op jit(solution)/shard_map/broadcast_in_dim | solution.py:91
  (38 shorter events, 1.1 us)
Async XLA Ops:
  7.2 14.3 %copy-start = (bf16[32,2048]{1,0:T(8,128)(2,1)S(1)}, bf16[32,2048]{1,0:T(8,128)(2,1)}, u32[]{:S(2)}) copy-start(bf16[32,2048]{1,0:T(8,128)(2,1)} %param.8) | copy-start | bytes 393220
  7.2 47.0 %all-gather.8.cloned.1.call-start = ((), (), s32[]{:S(2)}) async-start(), calls=%async_computation.8 | async-start | bytes 1966080 | tf_op jit(solution)/shard_map/all_gather | solution.py:53
  7.9 68.5 %all-gather.6.cloned.1.call-start = ((), (), s32[]{:S(2)}) async-start(), calls=%async_computation.7 | async-start | bytes 1966080 | tf_op jit(solution)/shard_map/all_gather | solution.py:54
  14.4 11.8 %all-to-all-start = ((bf16[4,1,20]{2,1,0:T(2,128)(2,1)}), bf16[4,1,20]{2,1,0:T(2,128)(2,1)S(1)}, u32[]{:S(2)}, u32[]{:S(2)}) async-start(bf16[4,1,20]{2,1,0:T(2,128)(2,1)} %all_to_all.25), calls=%async_computation | async-start | bytes 4096 | tf_op jit(solution)/shard_map/all_to_all | solution.py:45
  20.7 88.6 %all-gather.4.cloned.1.call-start = ((), (), s32[]{:S(2)}) async-start(), calls=%async_computation.6 | async-start | bytes 1966080 | tf_op jit(solution)/shard_map/all_gather | solution.py:55
  21.4 1.0 copy-start.1
  40.2 14.0 %all-to-all-start.1 = ((bf16[4,20,2048]{2,1,0:T(8,128)(2,1)}), bf16[4,20,2048]{2,1,0:T(8,128)(2,1)S(1)}, u32[]{:S(2)}, u32[]{:S(2)}) async-start(bf16[4,20,2048]{2,1,0:T(8,128)(2,1)} %get-tuple-element.15), calls=%async_computation.1 | async-start | bytes 786432 | tf_op jit(solution)/shard_map/all_to_all | solution.py:44
  43.6 99.4 %reduce-scatter.2.cloned.1.call-start = ((), (), s32[]{:S(2)}) async-start(), calls=%async_computation.9 | async-start | bytes 1966080 | tf_op jit(solution)/shard_map/reduce_scatter | solution.py:87
  109.3 7.3 %copy-start.3 = (bf16[1,384,2048]{2,1,0:T(8,128)(2,1)S(1)}, bf16[1,384,2048]{2,1,0:T(8,128)(2,1)}, u32[]{:S(2)}) copy-start(bf16[1,384,2048]{2,1,0:T(8,128)(2,1)} %all-gather.4.cloned.1.call-done) | copy-start | bytes 4718596
  111.3 6.9 %copy-start.2 = (bf16[1,384,2048]{2,1,0:T(8,128)(2,1)S(1)}, bf16[1,384,2048]{2,1,0:T(8,128)(2,1)}, u32[]{:S(2)}) copy-start(bf16[1,384,2048]{2,1,0:T(8,128)(2,1)} %all-gather.8.cloned.1.call-done) | copy-start | bytes 4718596
  112.0 10.1 %all-to-all-start.4 = ((bf16[4,1,20]{2,1,0:T(2,128)(2,1)}), bf16[4,1,20]{2,1,0:T(2,128)(2,1)S(1)}, u32[]{:S(2)}, u32[]{:S(2)}) async-start(bf16[4,1,20]{2,1,0:T(2,128)(2,1)} %convert_element_type.91), calls=%async_computation.4 | async-start | bytes 4096 | tf_op jit(solution)/shard_map/all_to_all | solution.py:80
  118.2 1.5 copy-start.4
  122.1 22.7 %all-to-all-start.3 = ((bf16[4,20,2048]{2,1,0:T(8,128)(2,1)}), bf16[4,20,2048]{2,1,0:T(8,128)(2,1)S(1)}, u32[]{:S(2)}, u32[]{:S(2)}) async-start(bf16[4,20,2048]{2,1,0:T(8,128)(2,1)} %reshape.113), calls=%async_computation.3 | async-start | bytes 786432 | tf_op jit(solution)/shard_map/all_to_all | solution.py:79
  126.0 37.8 %all-reduce.2.cloned.1.call-start = ((), (), s32[]{:S(2)}) async-start(), calls=%async_computation.10 | async-start | bytes 786432 | tf_op jit(solution)/shard_map/psum | solution.py:90
Sparse Core Ops, SparseCore 0:
  9.9 33.6 all-gather.7
  45.4 30.9 all-gather.5
  78.3 30.9 all-gather.3
  112.1 30.9 reduce-scatter.1
  145.3 18.4 all-reduce.1
where the time goes:
time: 173 us; the launch traced here: 172 us
  waiting for transfers between devices  97.6 us (56%)
  starting transfers between devices  18.4 us (11%)
  blocking collectives  14 us (8%)
  between operations  14 us (8%)
  local copies, waits for them, and re-layouts  12.6 us (7%)
  matrix products  10.3 us (6%)
  other arithmetic  5.4 us (3%)
    all_gather x1, waiting for transfers between devices, local(): down_piece = lax.all_gather(down_weight, 'dp', axis=1, tiled=True)[0]  28.1 us
    all_gather x1, waiting for transfers between devices, local(): up_piece = lax.all_gather(up_weight, 'dp', axis=1, tiled=True)[0]  20.2 us
    reduce_scatter x1, waiting for transfers between devices, local(): lax.psum_scatter(grad_full.astype(jnp.bfloat16), 'dp', scatter_dimension=...  17.1 us
    psum x1, waiting for transfers between devices, local(): grad_total = lax.psum(grad_shard, 'rep').astype(jnp.float32)  16.7 us
    all_to_all x1, blocking collectives, local(): lax.all_to_all(x_send, 'ep', split_axis=0, concat_axis=0, tiled=True)  14 us
    all_to_all x1, waiting for transfers between devices, local(): lax.all_to_all(dy_send, 'ep', split_axis=0, concat_axis=0, tiled=True)  10.3 us
    all_to_all x1, starting transfers between devices, local(): lax.all_to_all(weight_send, 'ep', split_axis=0, concat_axis=0, tiled=True)  6.32 us
    dot_general x3, matrix products, contract_last(): lax.dot_general(left, right, (((1,), (1,)), ((), ())), preferred_element_...  5.59 us
  transfers between devices with their start and end apart: 9, of which 7 were waited for; matrix products, arithmetic and copies ran while one was open for 14% of the time, Pallas kernels for 0%

commit v1 on v0

v1 whole, which is shorter than its diff:
```python
import jax
import jax.numpy as jnp
from jax import lax
from jax.sharding import PartitionSpec as P


def contract_last(left, right):
    return lax.dot_general(
        left, right, (((1,), (1,)), ((), ())), preferred_element_type=jnp.float32
    )


def contract_first(left, right):
    return lax.dot_general(
        left, right, (((0,), (0,)), ((), ())), preferred_element_type=jnp.float32
    )


def swap(value, axis, mask):
    return lax.ppermute(value, axis, [(i, i ^ mask) for i in range(lax.axis_size(axis))])


def local(tokens, upstream, expert_ids, route_weight, gate_weight, up_weight, down_weight):
    tok_dev, width = tokens.shape
    top = expert_ids.shape[1]
    experts, shards, reps = lax.axis_size("ep"), lax.axis_size("dp"), lax.axis_size("rep")
    cap = 2 * ((5 * tok_dev * top + 8 * experts - 1) // (8 * experts))
    rep, me = lax.axis_index("rep"), lax.axis_index("ep")
    hidden = gate_weight.shape[1] // reps

    mine = jnp.concatenate(
        [lax.dynamic_slice_in_dim(w[0], rep * hidden, hidden, 0) for w in (gate_weight, up_weight, down_weight)]
    )
    blocks = [mine] + [swap(mine, "dp", m) for m in range(1, shards)]

    onehot = (expert_ids[:, :, None] == jnp.arange(experts)[None, None, :]).astype(jnp.float32)
    named = jnp.sum(onehot, axis=1)
    before = jnp.dot(
        (jnp.arange(tok_dev)[:, None] > jnp.arange(tok_dev)[None, :]).astype(jnp.float32), named
    )
    rank = jnp.sum(before[:, None, :] * onehot, axis=2).astype(jnp.int32)
    d_out = (route_weight.astype(jnp.float32)[:, :, None] * upstream.astype(jnp.float32)[:, None, :]).astype(
        jnp.bfloat16
    )
    place = (expert_ids ^ me) * cap + rank
    select = (place[None, :, :] == jnp.arange(experts * cap)[:, None, None]).astype(jnp.bfloat16)
    x_send = jnp.dot(jnp.sum(select, axis=2), tokens, preferred_element_type=jnp.float32)
    dy_send = jnp.dot(
        select.transpose(0, 2, 1).reshape(experts * cap, top * tok_dev),
        d_out.transpose(1, 0, 2).reshape(top * tok_dev, width),
        preferred_element_type=jnp.float32,
    )
    send = jnp.concatenate(
        [x_send.reshape(experts, cap, width), dy_send.reshape(experts, cap, width)], axis=1
    ).astype(jnp.bfloat16)
    if experts <= 8:
        chunks = [send[0]] + [swap(send[m], "ep", m) for m in range(1, experts)]
    else:
        moved = lax.all_to_all(send[jnp.arange(experts) ^ me], "ep", split_axis=0, concat_axis=0, tiled=True)
        moved = moved[jnp.arange(experts) ^ me]
        chunks = [moved]
    other = [swap(c, "rep", 1) for c in chunks]
    rows = jnp.concatenate([c.reshape(-1, 2 * cap, width) for c in chunks + other])
    x_rows = rows[:, :cap].reshape(-1, width)
    d_out_rows = rows[:, cap:].reshape(-1, width)

    gate = jnp.concatenate([b[:hidden] for b in blocks])
    up = jnp.concatenate([b[hidden : 2 * hidden] for b in blocks])
    down = jnp.concatenate([b[2 * hidden :] for b in blocks])
    gate_pre = contract_last(x_rows, gate)
    up_pre = contract_last(x_rows, up)
    d_act = contract_last(d_out_rows, down)
    sig = jax.nn.sigmoid(gate_pre)
    silu = gate_pre * sig
    act = silu * up_pre
    d_gate = (d_act * up_pre * sig * (1.0 + gate_pre * (1.0 - sig))).astype(jnp.bfloat16)
    d_up = (d_act * silu).astype(jnp.bfloat16)
    act16 = act.astype(jnp.bfloat16)
    prob = jnp.sum(act * d_act, axis=1)
    dx = jnp.dot(d_gate, gate, preferred_element_type=jnp.float32)
    dx = dx + jnp.dot(d_up, up, preferred_element_type=jnp.float32)
    grad = contract_first(act16, d_out_rows).astype(jnp.bfloat16).reshape(shards, hidden, width)

    slots = experts * cap
    packed = jnp.concatenate(
        [
            dx.reshape(2 * experts, cap, width),
            jnp.pad(prob.reshape(2 * experts, 1, cap), ((0, 0), (0, 3), (0, width - cap))),
        ],
        axis=1,
    ).reshape(2, experts, cap + 4, width)
    home = packed[0] + swap(packed[1].astype(jnp.bfloat16), "rep", 1).astype(jnp.float32)
    home = home.astype(jnp.bfloat16)
    if experts <= 8:
        back = jnp.stack([home[0]] + [swap(home[m], "ep", m) for m in range(1, experts)])
    else:
        back = lax.all_to_all(home[jnp.arange(experts) ^ me], "ep", split_axis=0, concat_axis=0, tiled=True)
        back = back[jnp.arange(experts) ^ me]
    d_tokens = contract_first(jnp.sum(select, axis=2), back[:, :cap].reshape(slots, width)).astype(jnp.bfloat16)
    prob_back = back[:, cap, :cap].reshape(slots).astype(jnp.float32)
    d_probs = jnp.sum(select.astype(jnp.float32) * prob_back[:, None, None], axis=0)
    d_probs = (d_probs / route_weight.astype(jnp.float32)).astype(jnp.bfloat16)

    total = grad[0].astype(jnp.float32)
    for m in range(1, shards):
        total = total + swap(grad[m], "dp", m).astype(jnp.float32)
    total = total.astype(jnp.bfloat16)
    theirs = swap(total, "rep", 1)
    first = rep == 0
    grad_total = jnp.concatenate([jnp.where(first, total, theirs), jnp.where(first, theirs, total)])
    return (d_tokens, d_probs, grad_total.astype(jnp.float32)[None])


def solution(mesh):
    rows = P(("rep", "ep", "dp"), None)
    weights = P("ep", "dp", None)
    return jax.shard_map(
        local,
        mesh=mesh,
        in_specs=(rows,) * 4 + (weights,) * 3,
        out_specs=(rows, rows, weights),
        check_vma=False,
    )
```

time: 173 us -> 77.2 us (0.45)
  waiting for transfers between devices: 97.6 us -> 34.6 us
  blocking collectives: 14 us -> 0 us
  between operations: 14 us -> 1.08 us
  local copies, waits for them, and re-layouts: 12.6 us -> 7.84 us
  matrix products: 10.3 us -> 7.67 us
    all_gather x3 -> x0, waiting for transfers between devices: 48.3 us -> none  [the longest x1 28.1 us: local(): down_piece = lax.all_gather(down_weight, 'dp', axis=1, tiled=True)[0]]
    ppermute x0 -> x18, waiting for transfers between devices: none -> 34.6 us  [swap(): lax.ppermute(value, axis, [(i, i ^ mask) for i in range(lax.axis_size(axi...]
    ppermute x0 -> x18, starting transfers between devices: none -> 18.7 us  [swap(): lax.ppermute(value, axis, [(i, i ^ mask) for i in range(lax.axis_size(axi...]
    all_to_all x4 -> x0, starting transfers between devices: 18.3 us -> none  [the longest x1 6.32 us: local(): lax.all_to_all(weight_send, 'ep', split_axis=0, concat_axis=0, tiled=True)]
    reduce_scatter x1 -> x0, waiting for transfers between devices: 17.1 us -> none  [local(): lax.psum_scatter(grad_full.astype(jnp.bfloat16), 'dp', scatter_dimension=...]
    psum x1 -> x0, waiting for transfers between devices: 16.7 us -> none  [local(): grad_total = lax.psum(grad_shard, 'rep').astype(jnp.float32)]
    all_to_all x1 -> x0, blocking collectives: 14 us -> none  [local(): lax.all_to_all(x_send, 'ep', split_axis=0, concat_axis=0, tiled=True)]
    all_to_all x4 -> x0, waiting for transfers between devices: 13.4 us -> none  [the longest x1 10.3 us: local(): lax.all_to_all(dy_send, 'ep', split_axis=0, concat_axis=0, tiled=True)]
  transfers between devices with their start and end apart: 9 -> 18, of which waited for: 7 -> 11; matrix products, arithmetic and copies ran while one was open for 14% -> 7% of each run, Pallas kernels for 0% -> 0%
where the time goes in v1:
time: 77.2 us; the launch traced here: 76.8 us
  waiting for transfers between devices  34.6 us (45%)
  starting transfers between devices  18.7 us (24%)
  local copies, waits for them, and re-layouts  7.84 us (10%)
  matrix products  7.67 us (10%)
  other arithmetic  6.96 us (9%)
  between operations  1.08 us (1%)
    ppermute x18, waiting for transfers between devices, swap(): lax.ppermute(value, axis, [(i, i ^ mask) for i in range(lax.axis_size(axi...  34.6 us
    ppermute x18, starting transfers between devices, swap(): lax.ppermute(value, axis, [(i, i ^ mask) for i in range(lax.axis_size(axi...  18.7 us
    slice x3, local copies, waits for them, and re-layouts, local(): gate = jnp.concatenate([b[:hidden] for b in blocks])  3.5 us
    dot_general x3, matrix products, contract_last(): lax.dot_general(left, right, (((1,), (1,)), ((), ())), preferred_element_...  1.9 us
    unnamed x36, local copies, waits for them, and re-layouts  1.79 us
  transfers between devices with their start and end apart: 18, of which 11 were waited for; matrix products, arithmetic and copies ran while one was open for 7% of the time, Pallas kernels for 0%

profile of v1, /device:TPU:0, one launch (start us, length us, event | category | flops | bytes accessed | tf_op | source)
XLA Modules:
  0.0 76.8 jit_solution(14484215750385866334)
XLA Ops:
  0.7 0.7 convert_reduce_fusion
  1.5 0.7 select_reduce_fusion
  2.2 0.7 convert_add_fusion
  3.0 0.9 %convert_element_type.98 = f32[32,2048]{1,0:T(8,128)S(1)} convert(bf16[32,2048]{1,0:T(8,128)(2,1)} %param.8) | non-fusion elementwise | flops 65536 | bytes 393216 | tf_op jit(solution)/shard_map/convert_element_type | solution.py:42
  3.9 0.7 convert_bitcast_fusion
  5.0 1.3 %convolution_convert_fusion.2 = bf16[4,20,2048]{2,1,0:T(8,128)(2,1)S(1)} fusion(bf16[32,2048]{1,0:T(8,128)(2,1)} %param.7, bf16[4,20,32]{1,0,2:T(4,128)(2,1)S(1)} %dot_general.33), kind=kOutput, calls=%fused_computation.3 | convolution fusion | flops 10649600 | bytes 463872 | tf_op jit(solution)/shard_map/dot_general | solution.py:47
  6.2 0.3 convolution_convert_fusion.1
  6.7 3.1 %collective-permute-start = (bf16[40,2048]{1,0:T(8,128)(2,1)S(1)}, bf16[40,2048]{1,0:T(8,128)(2,1)S(1)}, u32[]{:S(2)}, u32[]{:S(2)}) collective-permute-start(bf16[40,2048]{1,0:T(8,128)(2,1)S(1)} %get-tuple-element.10), channel_id=1, source_target_pairs={{0,4},{4,0},{8,12},{12,8},{1,5},{5,1},{9,13},{13,9},{2,6},{6,2},{1... | collective-permute-start | bytes 491528 | tf_op jit(solution)/shard_map/ppermute | solution.py:20
  9.9 0.6 copy-done.1
  10.5 0.9 %pad_maximum_fusion.2 = bf16[144,2048]{1,0:T(8,128)(2,1)} fusion(bf16[48,2048]{1,0:T(8,128)(2,1)S(1)} %dynamic-slice_bitcast_fusion.2, bf16[48,2048]{1,0:T(8,128)(2,1)S(1)} %get-tuple-element.30, bf16[48,2048]{1,0:T(8,128)(2,1)S(1)} %get-tuple-element.31), kind=kLoop, calls=%fused_computation.26 | loop fusion | flops 1769472 | bytes 1179648 | tf_op jit(solution)/shard_map/concatenate | solution.py:31
  11.4 2.5 %collective-permute-start.9 = (bf16[144,2048]{1,0:T(8,128)(2,1)}, bf16[144,2048]{1,0:T(8,128)(2,1)}, u32[]{:S(2)}, u32[]{:S(2)}) collective-permute-start(bf16[144,2048]{1,0:T(8,128)(2,1)} %pad_maximum_fusion.2), channel_id=1, source_target_pairs={{0,3},{1,2},{2,1},{3,0},{4,7},{5,6},{6,5},{7,4},{8,11},{9,10},{10,... | collective-permute-start | bytes 1769480 | tf_op jit(solution)/shard_map/ppermute | solution.py:20
  13.8 0.5 collective-permute-start.8
  14.3 0.5 collective-permute-start.7
  14.9 2.6 %collective-permute-start.1 = (bf16[40,2048]{1,0:T(8,128)(2,1)S(1)}, bf16[40,2048]{1,0:T(8,128)(2,1)S(1)}, u32[]{:S(2)}, u32[]{:S(2)}) collective-permute-start(bf16[40,2048]{1,0:T(8,128)(2,1)S(1)} %get-tuple-element.12), channel_id=1, source_target_pairs={{0,8},{4,12},{8,0},{12,4},{1,9},{5,13},{9,1},{13,5},{2,10},{6,14},... | collective-permute-start | bytes 491528 | tf_op jit(solution)/shard_map/ppermute | solution.py:20
  17.5 0.3 collective-permute-start.2
  17.8 9.9 %collective-permute-done.1 = bf16[40,2048]{1,0:T(8,128)(2,1)S(1)} collective-permute-done((bf16[40,2048]{1,0:T(8,128)(2,1)S(1)}, bf16[40,2048]{1,0:T(8,128)(2,1)S(1)}, u32[]{:S(2)}, u32[]{:S(2)}) %collective-permute-start.1) | collective-permute-done | bytes 163872 | tf_op jit(solution)/shard_map/ppermute | solution.py:20
  27.7 0.6 collective-permute-start.4
  28.3 0.8 %collective-permute-done.3 = bf16[40,2048]{1,0:T(8,128)(2,1)S(1)} collective-permute-done((bf16[40,2048]{1,0:T(8,128)(2,1)S(1)}, bf16[40,2048]{1,0:T(8,128)(2,1)S(1)}, u32[]{:S(2)}, u32[]{:S(2)}) %collective-permute-start.3) | collective-permute-done | bytes 163872 | tf_op jit(solution)/shard_map/ppermute | solution.py:20
  29.3 0.4 collective-permute-start.6
  29.7 0.8 %collective-permute-done.5 = bf16[40,2048]{1,0:T(8,128)(2,1)S(1)} collective-permute-done((bf16[40,2048]{1,0:T(8,128)(2,1)S(1)}, bf16[40,2048]{1,0:T(8,128)(2,1)S(1)}, u32[]{:S(2)}, u32[]{:S(2)}) %collective-permute-start.5) | collective-permute-done | bytes 163872 | tf_op jit(solution)/shard_map/ppermute | solution.py:20
  30.5 0.2 collective-permute-done.6
  30.7 0.2 fusion.43
  31.2 1.2 %fusion.47 = (bf16[48,2048]{1,0:T(8,128)(2,1)S(1)}, bf16[48,2048]{1,0:T(8,128)(2,1)S(1)}, bf16[48,2048]{1,0:T(8,128)(2,1)S(1)}) fusion(bf16[144,2048]{1,0:T(8,128)(2,1)} %collective-permute-done.9), kind=kLoop, calls=%fused_computation.99 | loop fusion | bytes 1179648 | tf_op jit(solution)/shard_map/slice | solution.py:67
  32.4 7.6 %collective-permute-done.8 = bf16[144,2048]{1,0:T(8,128)(2,1)} collective-permute-done((bf16[144,2048]{1,0:T(8,128)(2,1)}, bf16[144,2048]{1,0:T(8,128)(2,1)}, u32[]{:S(2)}, u32[]{:S(2)}) %collective-permute-start.8) | collective-permute-done | bytes 589856 | tf_op jit(solution)/shard_map/ppermute | solution.py:20
  40.0 1.2 %fusion.46 = (bf16[48,2048]{1,0:T(8,128)(2,1)S(1)}, bf16[48,2048]{1,0:T(8,128)(2,1)S(1)}, bf16[48,2048]{1,0:T(8,128)(2,1)S(1)}) fusion(bf16[144,2048]{1,0:T(8,128)(2,1)} %collective-permute-done.8), kind=kLoop, calls=%fused_computation.98 | loop fusion | bytes 1179648 | tf_op jit(solution)/shard_map/slice | solution.py:67
  41.2 1.2 %fusion.45 = (bf16[48,2048]{1,0:T(8,128)(2,1)S(1)}, bf16[48,2048]{1,0:T(8,128)(2,1)S(1)}, bf16[48,2048]{1,0:T(8,128)(2,1)S(1)}) fusion(bf16[144,2048]{1,0:T(8,128)(2,1)} %collective-permute-done.7), kind=kLoop, calls=%fused_computation.97 | loop fusion | bytes 1179648 | tf_op jit(solution)/shard_map/slice | solution.py:67
  42.4 0.4 fusion.20
  42.8 0.5 copy-done.4
  43.3 0.4 fusion.18
  43.7 0.4 convolution_convert_fusion
  44.1 0.6 copy-done.2
  44.7 1.1 %multiply_reduce_fusion = (f32[160]{0:T(256)S(1)}, f32[160,192]{1,0:T(8,128)}) fusion(f32[160,192]{1,0:T(8,128)S(1)} %fusion.20, f32[160,192]{1,0:T(8,128)S(1)} %fusion.18, bf16[160,2048]{1,0:T(8,128)(2,1)S(1)} %reshape.141, bf16[48,2048]{1,0:T(8,128)(2,1)S(1)} %get-tuple-element.21, bf16[48,2048]{1,0:T(8,128)(2,1)S(1)} %get-tuple-element.18, ...), kind=kOutput, calls=%fused_computation.52 | convolution fusion | flops 129189728 | bytes 1811072 | tf_op jit(solution)/shard_map/dot_general | solution.py:8
  45.9 1.4 %fusion.19 = f32[160,2048]{1,0:T(8,128)S(1)} fusion(bf16[48,2048]{1,0:T(8,128)(2,1)S(1)} %get-tuple-element.20, bf16[48,2048]{1,0:T(8,128)(2,1)S(1)} %get-tuple-element.17, bf16[48,2048]{1,0:T(8,128)(2,1)S(1)} %get-tuple-element.14, bf16[48,2048]{1,0:T(8,128)(2,1)S(1)} %copy-done.6, f32[160,192]{1,0:T(8,128)} %get-tuple-element.29, f32[160,192]{1,0:T(8,128)} %copy-done.9), kind=kOutput, calls=%fused_computation.58 | convolution fusion | flops 129159168 | bytes 2342912 | tf_op jit(solution)/shard_map/dot_general | solution.py:81
  47.3 1.4 %convolution_add_fusion = f32[160,2048]{1,0:T(8,128)} fusion(f32[160,2048]{1,0:T(8,128)S(1)} %fusion.19, bf16[48,2048]{1,0:T(8,128)(2,1)S(1)} %get-tuple-element.19, bf16[48,2048]{1,0:T(8,128)(2,1)S(1)} %get-tuple-element.16, bf16[48,2048]{1,0:T(8,128)(2,1)S(1)} %get-tuple-element.13, bf16[48,2048]{1,0:T(8,128)(2,1)S(1)} %copy-done.4, ...), kind=kOutput, calls=%fused_computation | convolution fusion | flops 129609728 | bytes 3776512 | tf_op jit(solution)/shard_map/dot_general | solution.py:80
  48.8 1.4 %reshape.143 = f32[8,20,2048]{2,1,0:T(8,128)S(1)} reshape(f32[160,2048]{1,0:T(8,128)} %convolution_add_fusion) | data formatting | bytes 2621440 | tf_op jit(solution)/shard_map/reshape | solution.py:87
  50.2 1.8 %collective-permute-start.16 = (bf16[48,2048]{1,0:T(8,128)(2,1)S(1)}, bf16[48,2048]{1,0:T(8,128)(2,1)S(1)}, u32[]{:S(2)}, u32[]{:S(2)}) collective-permute-start(bf16[48,2048]{1,0:T(8,128)(2,1)S(1)} %get-tuple-element.6), channel_id=1, source_target_pairs={{0,3},{1,2},{2,1},{3,0},{4,7},{5,6},{6,5},{7,4},{8,11},{9,10},{10,... | collective-permute-start | bytes 589832 | tf_op jit(solution)/shard_map/ppermute | solution.py:20
  52.0 1.2 %collective-permute-start.15 = (bf16[48,2048]{1,0:T(8,128)(2,1)S(1)}, bf16[48,2048]{1,0:T(8,128)(2,1)S(1)}, u32[]{:S(2)}, u32[]{:S(2)}) collective-permute-start(bf16[48,2048]{1,0:T(8,128)(2,1)S(1)} %get-tuple-element.7), channel_id=1, source_target_pairs={{0,2},{1,3},{2,0},{3,1},{4,6},{5,7},{6,4},{7,5},{8,10},{9,11},{10,... | collective-permute-start | bytes 589832 | tf_op jit(solution)/shard_map/ppermute | solution.py:20
  53.2 0.5 collective-permute-start.14
  54.0 4.9 %collective-permute-done.16 = bf16[48,2048]{1,0:T(8,128)(2,1)S(1)} collective-permute-done((bf16[48,2048]{1,0:T(8,128)(2,1)S(1)}, bf16[48,2048]{1,0:T(8,128)(2,1)S(1)}, u32[]{:S(2)}, u32[]{:S(2)}) %collective-permute-start.16) | collective-permute-done | bytes 196640 | tf_op jit(solution)/shard_map/ppermute | solution.py:20
  59.0 3.2 %collective-permute-done.15 = bf16[48,2048]{1,0:T(8,128)(2,1)S(1)} collective-permute-done((bf16[48,2048]{1,0:T(8,128)(2,1)S(1)}, bf16[48,2048]{1,0:T(8,128)(2,1)S(1)}, u32[]{:S(2)}, u32[]{:S(2)}) %collective-permute-start.15) | collective-permute-done | bytes 196640 | tf_op jit(solution)/shard_map/ppermute | solution.py:20
  62.6 2.5 %collective-permute-start.13 = (bf16[24,2048]{1,0:T(8,128)(2,1)S(1)}, bf16[24,2048]{1,0:T(8,128)(2,1)S(1)}, u32[]{:S(2)}, u32[]{:S(2)}) collective-permute-start(bf16[24,2048]{1,0:T(8,128)(2,1)S(1)} %get-tuple-element.25), channel_id=1, source_target_pairs={{0,12},{4,8},{8,4},{12,0},{1,13},{5,9},{9,5},{13,1},{2,14},{6,10},... | collective-permute-start | bytes 294920 | tf_op jit(solution)/shard_map/ppermute | solution.py:20
  65.2 0.2 collective-permute-start.12
  65.4 1.7 %collective-permute-start.11 = (bf16[24,2048]{1,0:T(8,128)(2,1)S(1)}, bf16[24,2048]{1,0:T(8,128)(2,1)S(1)}, u32[]{:S(2)}, u32[]{:S(2)}) collective-permute-start(bf16[24,2048]{1,0:T(8,128)(2,1)S(1)} %get-tuple-element.27), channel_id=1, source_target_pairs={{0,4},{4,0},{8,12},{12,8},{1,5},{5,1},{9,13},{13,9},{2,6},{6,2},{1... | collective-permute-start | bytes 294920 | tf_op jit(solution)/shard_map/ppermute | solution.py:20
  67.1 0.9 %maximum_convert_fusion = f32[1,96,2048]{2,1,0:T(8,128)} fusion(bf16[1,48,2048]{2,1,0:T(8,128)(2,1)S(1)} %get-tuple-element.23, bf16[1,48,2048]{2,1,0:T(8,128)(2,1)S(1)} %get-tuple-element.22), kind=kLoop, calls=%fused_computation.30 | loop fusion | flops 786432 | bytes 1179648 | tf_op jit(solution)/shard_map/convert_element_type | solution.py:111
  68.1 2.1 %collective-permute-done.13 = bf16[24,2048]{1,0:T(8,128)(2,1)S(1)} collective-permute-done((bf16[24,2048]{1,0:T(8,128)(2,1)S(1)}, bf16[24,2048]{1,0:T(8,128)(2,1)S(1)}, u32[]{:S(2)}, u32[]{:S(2)}) %collective-permute-start.13) | collective-permute-done | bytes 98336 | tf_op jit(solution)/shard_map/ppermute | solution.py:20
  70.2 4.9 %collective-permute-done.12 = bf16[24,2048]{1,0:T(8,128)(2,1)S(1)} collective-permute-done((bf16[24,2048]{1,0:T(8,128)(2,1)S(1)}, bf16[24,2048]{1,0:T(8,128)(2,1)S(1)}, u32[]{:S(2)}, u32[]{:S(2)}) %collective-permute-start.12) | collective-permute-done | bytes 98336 | tf_op jit(solution)/shard_map/ppermute | solution.py:20
  75.2 0.8 %convolution_convert_fusion.3 = bf16[32,2048]{1,0:T(8,128)(2,1)} fusion(bf16[80,32]{0,1:T(8,128)(2,1)S(1)} %fusion.30, bf16[80,2048]{1,0:T(8,128)(2,1)S(1)} %reshape.145), kind=kOutput, calls=%fused_computation.4 | convolution fusion | flops 10551296 | bytes 463872 | tf_op jit(solution)/shard_map/dot_general | solution.py:14
  76.3 0.5 fusion.33
  (72 shorter events, 2.6 us)
Async XLA Ops:
  0.6 9.1 %copy-start = (bf16[1,96,2048]{2,1,0:T(8,128)(2,1)S(1)}, bf16[1,96,2048]{2,1,0:T(8,128)(2,1)}, u32[]{:S(2)}) copy-start(bf16[1,96,2048]{2,1,0:T(8,128)(2,1)} %param.13) | copy-start | bytes 1179652
  4.9 4.9 %copy-start.11 = (bf16[1,96,2048]{2,1,0:T(8,128)(2,1)S(1)}, bf16[1,96,2048]{2,1,0:T(8,128)(2,1)}, u32[]{:S(2)}) copy-start(bf16[1,96,2048]{2,1,0:T(8,128)(2,1)} %param.12) | copy-start | bytes 1179652
  5.0 4.9 %copy-start.12 = (bf16[1,96,2048]{2,1,0:T(8,128)(2,1)S(1)}, bf16[1,96,2048]{2,1,0:T(8,128)(2,1)}, u32[]{:S(2)}) copy-start(bf16[1,96,2048]{2,1,0:T(8,128)(2,1)} %param.11) | copy-start | bytes 1179652
  6.7 10.8 %collective-permute-start = (bf16[40,2048]{1,0:T(8,128)(2,1)S(1)}, bf16[40,2048]{1,0:T(8,128)(2,1)S(1)}, u32[]{:S(2)}, u32[]{:S(2)}) collective-permute-start(bf16[40,2048]{1,0:T(8,128)(2,1)S(1)} %get-tuple-element.10), channel_id=1, source_target_pairs={{0,4},{4,0},{8,12},{12,8},{1,5},{5,1},{9,13},{13,9},{2,6},{6,2},{1... | collective-permute-start | bytes 491528 | tf_op jit(solution)/shard_map/ppermute | solution.py:20
  9.8 0.7 copy-start.1
  9.9 1.5 %copy-start.3 = (bf16[48,2048]{1,0:T(8,128)(2,1)}, bf16[48,2048]{1,0:T(8,128)(2,1)S(1)}, u32[]{:S(2)}) copy-start(bf16[48,2048]{1,0:T(8,128)(2,1)S(1)} %get-tuple-element.31) | copy-start | bytes 589828
  9.9 4.0 %copy-start.5 = (bf16[48,2048]{1,0:T(8,128)(2,1)}, bf16[48,2048]{1,0:T(8,128)(2,1)S(1)}, u32[]{:S(2)}) copy-start(bf16[48,2048]{1,0:T(8,128)(2,1)S(1)} %get-tuple-element.30) | copy-start | bytes 589828
  11.4 19.9 %collective-permute-start.9 = (bf16[144,2048]{1,0:T(8,128)(2,1)}, bf16[144,2048]{1,0:T(8,128)(2,1)}, u32[]{:S(2)}, u32[]{:S(2)}) collective-permute-start(bf16[144,2048]{1,0:T(8,128)(2,1)} %pad_maximum_fusion.2), channel_id=1, source_target_pairs={{0,3},{1,2},{2,1},{3,0},{4,7},{5,6},{6,5},{7,4},{8,11},{9,10},{10,... | collective-permute-start | bytes 1769480 | tf_op jit(solution)/shard_map/ppermute | solution.py:20
  13.8 26.2 %collective-permute-start.8 = (bf16[144,2048]{1,0:T(8,128)(2,1)}, bf16[144,2048]{1,0:T(8,128)(2,1)}, u32[]{:S(2)}, u32[]{:S(2)}) collective-permute-start(bf16[144,2048]{1,0:T(8,128)(2,1)} %pad_maximum_fusion.2), channel_id=1, source_target_pairs={{0,2},{1,3},{2,0},{3,1},{4,6},{5,7},{6,4},{7,5},{8,10},{9,11},{10,... | collective-permute-start | bytes 1769480 | tf_op jit(solution)/shard_map/ppermute | solution.py:20
  14.3 26.8 %collective-permute-start.7 = (bf16[144,2048]{1,0:T(8,128)(2,1)}, bf16[144,2048]{1,0:T(8,128)(2,1)}, u32[]{:S(2)}, u32[]{:S(2)}) collective-permute-start(bf16[144,2048]{1,0:T(8,128)(2,1)} %pad_maximum_fusion.2), channel_id=1, source_target_pairs={{0,1},{1,0},{2,3},{3,2},{4,5},{5,4},{6,7},{7,6},{8,9},{9,8},{10,11... | collective-permute-start | bytes 1769480 | tf_op jit(solution)/shard_map/ppermute | solution.py:20
  14.9 12.8 %collective-permute-start.1 = (bf16[40,2048]{1,0:T(8,128)(2,1)S(1)}, bf16[40,2048]{1,0:T(8,128)(2,1)S(1)}, u32[]{:S(2)}, u32[]{:S(2)}) collective-permute-start(bf16[40,2048]{1,0:T(8,128)(2,1)S(1)} %get-tuple-element.12), channel_id=1, source_target_pairs={{0,8},{4,12},{8,0},{12,4},{1,9},{5,13},{9,1},{13,5},{2,10},{6,14},... | collective-permute-start | bytes 491528 | tf_op jit(solution)/shard_map/ppermute | solution.py:20
  17.5 10.2 %collective-permute-start.2 = (bf16[40,2048]{1,0:T(8,128)(2,1)S(1)}, bf16[40,2048]{1,0:T(8,128)(2,1)S(1)}, u32[]{:S(2)}, u32[]{:S(2)}) collective-permute-start(bf16[40,2048]{1,0:T(8,128)(2,1)S(1)} %get-tuple-element.11), channel_id=1, source_target_pairs={{0,12},{4,8},{8,4},{12,0},{1,13},{5,9},{9,5},{13,1},{2,14},{6,10},... | collective-permute-start | bytes 491528 | tf_op jit(solution)/shard_map/ppermute | solution.py:20
  27.7 1.4 %collective-permute-start.3 = (bf16[40,2048]{1,0:T(8,128)(2,1)S(1)}, bf16[40,2048]{1,0:T(8,128)(2,1)S(1)}, u32[]{:S(2)}, u32[]{:S(2)}) collective-permute-start(bf16[40,2048]{1,0:T(8,128)(2,1)S(1)} %get-tuple-element.8), channel_id=1, source_target_pairs={{0,16},{16,0},{1,17},{17,1},{2,18},{18,2},{3,19},{19,3},{4,20},{20... | collective-permute-start | bytes 491528 | tf_op jit(solution)/shard_map/ppermute | solution.py:20
  27.7 1.6 %collective-permute-start.4 = (bf16[40,2048]{1,0:T(8,128)(2,1)S(1)}, bf16[40,2048]{1,0:T(8,128)(2,1)S(1)}, u32[]{:S(2)}, u32[]{:S(2)}) collective-permute-start(bf16[40,2048]{1,0:T(8,128)(2,1)S(1)} %collective-permute-done), channel_id=1, source_target_pairs={{0,16},{16,0},{1,17},{17,1},{2,18},{18,2},{3,19},{19,3},{4,20},{20... | collective-permute-start | bytes 491528 | tf_op jit(solution)/shard_map/ppermute | solution.py:20
  29.1 1.4 %collective-permute-start.5 = (bf16[40,2048]{1,0:T(8,128)(2,1)S(1)}, bf16[40,2048]{1,0:T(8,128)(2,1)S(1)}, u32[]{:S(2)}, u32[]{:S(2)}) collective-permute-start(bf16[40,2048]{1,0:T(8,128)(2,1)S(1)} %collective-permute-done.1), channel_id=1, source_target_pairs={{0,16},{16,0},{1,17},{17,1},{2,18},{18,2},{3,19},{19,3},{4,20},{20... | collective-permute-start | bytes 491528 | tf_op jit(solution)/shard_map/ppermute | solution.py:20
  29.3 1.4 %collective-permute-start.6 = (bf16[40,2048]{1,0:T(8,128)(2,1)S(1)}, bf16[40,2048]{1,0:T(8,128)(2,1)S(1)}, u32[]{:S(2)}, u32[]{:S(2)}) collective-permute-start(bf16[40,2048]{1,0:T(8,128)(2,1)S(1)} %collective-permute-done.2), channel_id=1, source_target_pairs={{0,16},{16,0},{1,17},{17,1},{2,18},{18,2},{3,19},{19,3},{4,20},{20... | collective-permute-start | bytes 491528 | tf_op jit(solution)/shard_map/ppermute | solution.py:20
  31.2 11.1 %copy-start.6 = (bf16[48,2048]{1,0:T(8,128)(2,1)S(1)}, bf16[48,2048]{1,0:T(8,128)(2,1)}, u32[]{:S(2)}) copy-start(bf16[48,2048]{1,0:T(8,128)(2,1)} %copy-done.5) | copy-start | bytes 589828
  42.4 0.9 %copy-start.4 = (bf16[48,2048]{1,0:T(8,128)(2,1)S(1)}, bf16[48,2048]{1,0:T(8,128)(2,1)}, u32[]{:S(2)}) copy-start(bf16[48,2048]{1,0:T(8,128)(2,1)} %copy-done.3) | copy-start | bytes 589828
  42.8 1.3 %copy-start.7 = (f32[160,192]{1,0:T(8,128)}, f32[160,192]{1,0:T(8,128)S(1)}, u32[]{:S(2)}) copy-start(f32[160,192]{1,0:T(8,128)S(1)} %fusion.20) | copy-start | bytes 368644
  43.7 2.1 %copy-start.9 = (f32[160,192]{1,0:T(8,128)}, f32[160,192]{1,0:T(8,128)S(1)}, u32[]{:S(2)}) copy-start(f32[160,192]{1,0:T(8,128)S(1)} %fusion.18) | copy-start | bytes 368644
  43.7 1.0 %copy-start.2 = (bf16[48,2048]{1,0:T(8,128)(2,1)S(1)}, bf16[48,2048]{1,0:T(8,128)(2,1)}, u32[]{:S(2)}) copy-start(bf16[48,2048]{1,0:T(8,128)(2,1)} %copy-done.1) | copy-start | bytes 589828
  45.9 1.4 %copy-start.8 = (f32[160,192]{1,0:T(8,128)S(1)}, f32[160,192]{1,0:T(8,128)}, u32[]{:S(2)}) copy-start(f32[160,192]{1,0:T(8,128)} %copy-done.7) | copy-start | bytes 368644
  45.9 1.4 %copy-start.10 = (f32[160,192]{1,0:T(8,128)S(1)}, f32[160,192]{1,0:T(8,128)}, u32[]{:S(2)}) copy-start(f32[160,192]{1,0:T(8,128)} %copy-done.9) | copy-start | bytes 368644
  45.9 1.4 %copy-start.14 = (f32[160,192]{1,0:T(8,128)S(1)}, f32[160,192]{1,0:T(8,128)}, u32[]{:S(2)}) copy-start(f32[160,192]{1,0:T(8,128)} %get-tuple-element.29) | copy-start | bytes 368644
  50.2 8.8 %collective-permute-start.16 = (bf16[48,2048]{1,0:T(8,128)(2,1)S(1)}, bf16[48,2048]{1,0:T(8,128)(2,1)S(1)}, u32[]{:S(2)}, u32[]{:S(2)}) collective-permute-start(bf16[48,2048]{1,0:T(8,128)(2,1)S(1)} %get-tuple-element.6), channel_id=1, source_target_pairs={{0,3},{1,2},{2,1},{3,0},{4,7},{5,6},{6,5},{7,4},{8,11},{9,10},{10,... | collective-permute-start | bytes 589832 | tf_op jit(solution)/shard_map/ppermute | solution.py:20
  52.0 10.2 %collective-permute-start.15 = (bf16[48,2048]{1,0:T(8,128)(2,1)S(1)}, bf16[48,2048]{1,0:T(8,128)(2,1)S(1)}, u32[]{:S(2)}, u32[]{:S(2)}) collective-permute-start(bf16[48,2048]{1,0:T(8,128)(2,1)S(1)} %get-tuple-element.7), channel_id=1, source_target_pairs={{0,2},{1,3},{2,0},{3,1},{4,6},{5,7},{6,4},{7,5},{8,10},{9,11},{10,... | collective-permute-start | bytes 589832 | tf_op jit(solution)/shard_map/ppermute | solution.py:20
  53.2 9.1 %collective-permute-start.14 = (bf16[48,2048]{1,0:T(8,128)(2,1)S(1)}, bf16[48,2048]{1,0:T(8,128)(2,1)S(1)}, u32[]{:S(2)}, u32[]{:S(2)}) collective-permute-start(bf16[48,2048]{1,0:T(8,128)(2,1)S(1)} %get-tuple-element.5), channel_id=1, source_target_pairs={{0,1},{1,0},{2,3},{3,2},{4,5},{5,4},{6,7},{7,6},{8,9},{9,8},{10,11... | collective-permute-start | bytes 589832 | tf_op jit(solution)/shard_map/ppermute | solution.py:20
  54.0 8.5 %collective-permute-start.10 = (bf16[4,24,2048]{2,1,0:T(8,128)(2,1)S(1)}, bf16[4,24,2048]{2,1,0:T(8,128)(2,1)S(1)}, u32[]{:S(2)}, u32[]{:S(2)}) collective-permute-start(bf16[4,24,2048]{2,1,0:T(8,128)(2,1)S(1)} %slice.181), channel_id=1, source_target_pairs={{0,16},{16,0},{1,17},{17,1},{2,18},{18,2},{3,19},{19,3},{4,20},{20... | collective-permute-start | bytes 1179656 | tf_op jit(solution)/shard_map/ppermute | solution.py:20
  62.4 4.7 %collective-permute-start.17 = (bf16[48,2048]{1,0:T(8,128)(2,1)S(1)}, bf16[48,2048]{1,0:T(8,128)(2,1)S(1)}, u32[]{:S(2)}, u32[]{:S(2)}) collective-permute-start(bf16[48,2048]{1,0:T(8,128)(2,1)S(1)} %add_convert_fusion), channel_id=1, source_target_pairs={{0,16},{16,0},{1,17},{17,1},{2,18},{18,2},{3,19},{19,3},{4,20},{20... | collective-permute-start | bytes 589832 | tf_op jit(solution)/shard_map/ppermute | solution.py:20
  62.6 7.6 %collective-permute-start.13 = (bf16[24,2048]{1,0:T(8,128)(2,1)S(1)}, bf16[24,2048]{1,0:T(8,128)(2,1)S(1)}, u32[]{:S(2)}, u32[]{:S(2)}) collective-permute-start(bf16[24,2048]{1,0:T(8,128)(2,1)S(1)} %get-tuple-element.25), channel_id=1, source_target_pairs={{0,12},{4,8},{8,4},{12,0},{1,13},{5,9},{9,5},{13,1},{2,14},{6,10},... | collective-permute-start | bytes 294920 | tf_op jit(solution)/shard_map/ppermute | solution.py:20
  65.2 9.9 %collective-permute-start.12 = (bf16[24,2048]{1,0:T(8,128)(2,1)S(1)}, bf16[24,2048]{1,0:T(8,128)(2,1)S(1)}, u32[]{:S(2)}, u32[]{:S(2)}) collective-permute-start(bf16[24,2048]{1,0:T(8,128)(2,1)S(1)} %get-tuple-element.26), channel_id=1, source_target_pairs={{0,8},{4,12},{8,0},{12,4},{1,9},{5,13},{9,1},{13,5},{2,10},{6,14},... | collective-permute-start | bytes 294920 | tf_op jit(solution)/shard_map/ppermute | solution.py:20
  65.4 9.7 %collective-permute-start.11 = (bf16[24,2048]{1,0:T(8,128)(2,1)S(1)}, bf16[24,2048]{1,0:T(8,128)(2,1)S(1)}, u32[]{:S(2)}, u32[]{:S(2)}) collective-permute-start(bf16[24,2048]{1,0:T(8,128)(2,1)S(1)} %get-tuple-element.27), channel_id=1, source_target_pairs={{0,4},{4,0},{8,12},{12,8},{1,5},{5,1},{9,13},{13,9},{2,6},{6,2},{1... | collective-permute-start | bytes 294920 | tf_op jit(solution)/shard_map/ppermute | solution.py:20
  67.1 9.2 %copy-start.13 = (bf16[32,2]{0,1:T(2,128)(2,1)S(1)}, bf16[32,2]{0,1:T(2,128)(2,1)}, u32[]{:S(2)}) copy-start(bf16[32,2]{0,1:T(2,128)(2,1)} %param.10) | copy-start | bytes 388

commit v2 on v1

v2 whole, which is shorter than its diff:
```python
import functools

import jax
import jax.numpy as jnp
from jax import lax
from jax.experimental import pallas as pl
from jax.experimental.pallas import tpu as pltpu
from jax.sharding import PartitionSpec as P

LANES = 128
VMEM_BYTES = 48 * 1024 * 1024
f32, bf16 = jnp.float32, jnp.bfloat16


def dot(left, right, contract):
    return lax.dot_general(left, right, ((contract[0:1], contract[1:2]), ((), ())), preferred_element_type=f32)


def swap(value, axis, mask):
    return lax.ppermute(value, axis, [(i, i ^ mask) for i in range(lax.axis_size(axis))])


def kernel_call(body, inputs, outputs, flops=0, **kwargs):
    whole = pl.BlockSpec(memory_space=pltpu.VMEM)
    moved = sum(a.size * a.dtype.itemsize for a in inputs + outputs)
    return pl.pallas_call(
        body,
        out_shape=outputs,
        in_specs=kwargs.pop("in_specs", [whole] * len(inputs)),
        out_specs=[whole] * len(outputs),
        cost_estimate=pl.CostEstimate(flops=flops, bytes_accessed=moved, transcendentals=0),
        compiler_params=pltpu.CompilerParams(vmem_limit_bytes=VMEM_BYTES),
        **kwargs,
    )(*inputs)


def iota(shape, dim):
    return lax.broadcasted_iota(jnp.int32, shape, dim)


def dispatch_kernel(experts, cap, chunk_count, *refs):
    tokens, upstream, ids, route_weight, gate, up, down = refs[:7]
    chunks = refs[7 : 7 + chunk_count]
    slot_out, first, second, sems = refs[7 + chunk_count :]
    hidden, half = first.shape[0] // 3, first.shape[1]
    rep = lax.axis_index("rep")
    copies = []
    for i, weight in enumerate((gate, up, down)):
        for j, piece in enumerate((first, second)):
            copies.append(
                pltpu.make_async_copy(
                    weight.at[0, pl.ds(pl.multiple_of(rep * hidden, hidden), hidden), pl.ds(j * half, half)],
                    piece.at[pl.ds(i * hidden, hidden)],
                    sems.at[2 * i + j],
                )
            )
            copies[-1].start()

    tok_dev, top = ids.shape
    rows = experts * cap // chunk_count
    me = lax.axis_index("ep")
    wide = -(-experts // LANES) * LANES
    expert_of_lane = iota((tok_dev, wide), 1)
    named = [(expert_of_lane == ids[:, k : k + 1]).astype(f32) for k in range(top)]
    earlier = (iota((tok_dev, tok_dev), 0) > iota((tok_dev, tok_dev), 1)).astype(bf16)
    before = dot(earlier, sum(named).astype(bf16), (1, 0))
    lane = iota((tok_dev, 2 * experts * cap), 1)
    take_x = jnp.zeros(lane.shape, f32)
    take_dy = jnp.zeros(lane.shape, f32)
    scale = jnp.zeros((2 * experts * cap, LANES), f32)
    for k in range(top):
        rank = jnp.sum(before * named[k], axis=1, keepdims=True).astype(jnp.int32)
        expert = ids[:, k : k + 1]
        if chunk_count > 1:
            chunk = expert ^ me
            slot = chunk * cap + rank
            x_lane = slot + chunk * cap
        else:
            slot = expert * cap + rank
            x_lane = slot
        slot_out[:, k : k + 1] = slot
        take_x += (lane == x_lane).astype(f32)
        here = (lane == x_lane + rows).astype(f32)
        take_dy += here
        weight = jnp.broadcast_to(route_weight[:, k : k + 1], (tok_dev, LANES))
        scale += dot(here.astype(bf16), weight, (0, 0))
    scale += dot(take_x.astype(bf16), jnp.ones((tok_dev, LANES), bf16), (0, 0))
    picked = dot(take_x.astype(bf16), tokens[...], (0, 0)) + dot(take_dy.astype(bf16), upstream[...], (0, 0))
    picked = picked * scale[:, :1]
    for c in range(chunk_count):
        chunks[c][...] = picked[2 * rows * c : 2 * rows * (c + 1)].astype(bf16)
    for copy in copies:
        copy.wait()


def expert_math(x_rows, d_rows, pieces):
    width = x_rows.shape[1]
    half = width // 2
    acts, mixed, gates = [], [], []
    prob = 0.0
    for first, second in pieces:
        hidden = first.shape[0] // 3
        both, down = pl.ds(0, 2 * hidden), pl.ds(2 * hidden, hidden)
        pre = dot(x_rows[:, :half], first[both], (1, 1)) + dot(x_rows[:, half:], second[both], (1, 1))
        d_act = dot(d_rows[:, :half], first[down], (1, 1)) + dot(d_rows[:, half:], second[down], (1, 1))
        gate_pre, up_pre = pre[:, :hidden], pre[:, hidden:]
        sig = jax.nn.sigmoid(gate_pre)
        silu = gate_pre * sig
        act = silu * up_pre
        prob = prob + jnp.sum(act * d_act, axis=1, keepdims=True)
        acts.append(act)
        mixed += [d_act * up_pre * sig * (1.0 + gate_pre * (1.0 - sig)), d_act * silu]
        gates.append((first[both], second[both]))
    mixed = jnp.concatenate(mixed, axis=1).astype(bf16)
    acts = jnp.concatenate(acts, axis=1).astype(bf16)
    dx = [dot(mixed, jnp.concatenate([g[j] for g in gates]), (1, 0)) for j in range(2)]
    return dx, prob, dot(acts, d_rows, (0, 0))


def early_kernel(chunk_count, piece_count, *refs):
    chunks, refs = refs[:chunk_count], refs[chunk_count:]
    pieces, refs = refs[:piece_count], refs[piece_count:]
    x_out, d_out, dx_out, grad_own, *grads = refs
    rows = chunks[0].shape[0] // 2
    values = [c[...].astype(f32) for c in chunks]
    x_out[...] = jnp.concatenate([v[:rows] for v in values]).astype(bf16)
    d_out[...] = jnp.concatenate([v[rows:] for v in values]).astype(bf16)
    pairs = [(pieces[i], pieces[i + 1]) for i in range(0, piece_count, 2)]
    dx, prob, grad = expert_math(x_out[...], d_out[...], pairs)
    width = x_out.shape[1]
    dx_out[:, : width // 2] = dx[0]
    dx_out[:, width // 2 : width] = dx[1]
    dx_out[:, width:] = jnp.broadcast_to(prob, (prob.shape[0], LANES))
    hidden = grad_own.shape[0]
    grad_own[...] = grad[:hidden]
    for i, out in enumerate(grads):
        out[...] = grad[hidden * (i + 1) : hidden * (i + 2)].astype(bf16)


def late_kernel(x_ref, d_ref, dx_ref, first, second, keep, give, grad_out):
    dx, prob, grad = expert_math(x_ref[...], d_ref[...], [(first, second)])
    half, slots = dx[0].shape[1], keep.shape[0]
    for j, value in enumerate((dx[0], dx[1], jnp.broadcast_to(prob, (prob.shape[0], LANES)))):
        columns = slice(j * half, j * half + value.shape[1])
        total = value + dx_ref[:, columns]
        keep[:, columns] = total[:slots]
        give[:, columns] = total[slots:].astype(bf16)
    grad_out[...] = grad.astype(bf16)


def add_kernel(keep, got, *chunks):
    rows = chunks[0].shape[0]
    total = keep[...] + got[...].astype(f32)
    for c, chunk in enumerate(chunks):
        chunk[...] = total[c * rows : (c + 1) * rows].astype(bf16)


def combine_kernel(chunk_count, *refs):
    chunks, (slot, route_weight, tokens_out, probs_out) = refs[:chunk_count], refs[chunk_count:]
    rows = chunks[0].shape[0]
    tok_dev, width = tokens_out.shape
    top = slot.shape[1]
    total = 0.0
    probs = [0.0] * top
    for c in range(chunk_count):
        slot_of_lane = iota((tok_dev, rows), 1) + c * rows
        hits = [(slot_of_lane == slot[:, k : k + 1]).astype(f32) for k in range(top)]
        total = total + dot(sum(hits).astype(bf16), chunks[c][:, :width], (1, 0))
        for k in range(top):
            probs[k] = probs[k] + dot(hits[k].astype(bf16), chunks[c][:, width:], (1, 0))
    tokens_out[...] = total.astype(bf16)
    for k in range(top):
        weight = route_weight[:, k : k + 1].astype(f32)
        probs_out[:, k : k + 1] = (probs[k][:, :1] / weight).astype(bf16)


def local(tokens, upstream, expert_ids, route_weight, gate_weight, up_weight, down_weight):
    tok_dev, width = tokens.shape
    top = expert_ids.shape[1]
    experts, shards, reps = lax.axis_size("ep"), lax.axis_size("dp"), lax.axis_size("rep")
    cap = 2 * ((5 * tok_dev * top + 8 * experts - 1) // (8 * experts))
    slots = experts * cap
    chunk_count = experts if experts <= 8 else 1
    rows = slots // chunk_count
    hidden = gate_weight.shape[1] // reps
    shape = jax.ShapeDtypeStruct
    in_vmem, anywhere = pl.BlockSpec(memory_space=pltpu.VMEM), pl.BlockSpec(memory_space=pl.ANY)

    *chunks, slot, first, second = kernel_call(
        functools.partial(dispatch_kernel, experts, cap, chunk_count),
        [tokens, upstream, expert_ids, route_weight, gate_weight, up_weight, down_weight],
        [shape((2 * rows, width), bf16)] * chunk_count
        + [shape((tok_dev, top), jnp.int32)]
        + [shape((3 * hidden, width // 2), bf16)] * 2,
        in_specs=[in_vmem] * 4 + [anywhere] * 3,
        scratch_shapes=[pltpu.SemaphoreType.DMA((6,))],
    )

    if shards == 4:
        near = [[swap(piece, "dp", m) for piece in (first, second)] for m in (1, 2)]
        diagonal = [swap(near[0][0], "dp", 2), swap(near[1][1], "dp", 1)]
        blocks = [[first, second]] + near + [diagonal]
    else:
        blocks = [[first, second]] + [[swap(p, "dp", m) for p in (first, second)] for m in range(1, shards)]

    if chunk_count > 1:
        chunks = [chunks[0]] + [swap(chunks[m], "ep", m) for m in range(1, experts)]
    else:
        moved = chunks[0].reshape(2, experts, cap, width)
        moved = lax.all_to_all(moved, "ep", split_axis=1, concat_axis=1, tiled=True)
        chunks = [moved.reshape(2 * rows, width)]
    chunks = chunks + [swap(c, "rep", 1) for c in chunks]

    pieces = [p for block in blocks[:-1] for p in block]
    wide = width + LANES
    flops = 14 * 2 * slots * width * hidden
    x_rows, d_rows, dx, grad_own, *grads = kernel_call(
        functools.partial(early_kernel, 2 * chunk_count, len(pieces)),
        chunks + pieces,
        [shape((2 * slots, width), bf16)] * 2
        + [shape((2 * slots, wide), f32), shape((hidden, width), f32)]
        + [shape((hidden, width), bf16)] * (shards - 2),
        flops=flops * (shards - 1),
    )
    keep, give, grad_last = kernel_call(
        late_kernel,
        [x_rows, d_rows, dx] + blocks[-1],
        [shape((slots, wide), f32), shape((slots, wide), bf16), shape((hidden, width), bf16)],
        flops=flops,
    )
    back = kernel_call(add_kernel, [keep, swap(give, "rep", 1)], [shape((rows, wide), bf16)] * chunk_count)
    if chunk_count > 1:
        back = [back[0]] + [swap(back[m], "ep", m) for m in range(1, experts)]
    else:
        moved = back[0].reshape(experts, cap, wide)
        moved = lax.all_to_all(moved, "ep", split_axis=0, concat_axis=0, tiled=True)
        back = [moved.reshape(rows, wide)]
    d_tokens, d_probs = kernel_call(
        functools.partial(combine_kernel, chunk_count),
        back + [slot, route_weight],
        [shape((tok_dev, width), bf16), shape((tok_dev, top), bf16)],
    )

    total = grad_own
    for m, grad in enumerate(grads + [grad_last]):
        total = total + swap(grad, "dp", m + 1).astype(f32)
    total = total.astype(bf16)
    theirs = swap(total, "rep", 1)
    lower = lax.axis_index("rep") == 0
    grad_total = jnp.concatenate([jnp.where(lower, total, theirs), jnp.where(lower, theirs, total)])
    return (d_tokens, d_probs, grad_total.astype(f32)[None])


def solution(mesh):
    rows = P(("rep", "ep", "dp"), None)
    weights = P("ep", "dp", None)
    return jax.shard_map(
        local,
        mesh=mesh,
        in_specs=(rows,) * 4 + (weights,) * 3,
        out_specs=(rows, rows, weights),
        check_vma=False,
    )
```

time: 77.2 us -> 66.5 us (0.86)
  waiting for transfers between devices: 34.6 us -> 26.1 us
  matrix products: 7.67 us -> 0 us
  Pallas kernels: 0 us -> 6.17 us
  other arithmetic: 6.96 us -> 1.07 us
  starting transfers between devices: 18.7 us -> 23.9 us
    ppermute x18 -> x21, waiting for transfers between devices: 34.6 us -> 26.1 us  [swap(): lax.ppermute(value, axis, [(i, i ^ mask) for i in range(lax.axis_size(axi...]
    dot_general x10 -> x0, matrix products: 7.67 us -> none  [the longest x3 1.9 us: contract_last(): lax.dot_general(left, right, (((1,), (1,)), ((), ())), preferred_element_...]
    unnamed x36 -> x15, local copies, waits for them, and re-layouts: 1.79 us -> 8.25 us
    pallas_call x0 -> x5, Pallas kernels: none -> 6.17 us  [kernel_call(): pl.pallas_call(body, out_shape=outputs, in_specs=kwargs.pop('in_specs', [...]
    ppermute x18 -> x21, starting transfers between devices: 18.7 us -> 23.9 us  [swap(): lax.ppermute(value, axis, [(i, i ^ mask) for i in range(lax.axis_size(axi...]
    slice x7 -> x0, local copies, waits for them, and re-layouts: 3.84 us -> none  [the longest x3 3.5 us: local(): gate = jnp.concatenate([b[:hidden] for b in blocks])]
    reshape x5 -> x0, local copies, waits for them, and re-layouts: 1.81 us -> none  [the longest x1 1.38 us: local(): dx.reshape(2 * experts, cap, width)]
    reduce_sum x4 -> x0, other arithmetic: 1.68 us -> none  [the longest x1 0.74 us: local(): named = jnp.sum(onehot, axis=1)]
  transfers between devices with their start and end apart: 18 -> 21, of which waited for: 11 -> 9; matrix products, arithmetic and copies ran while one was open for 7% -> 2% of each run, Pallas kernels for 0% -> 6%
where the time goes in v2:
time: 66.5 us; the launch traced here: 66.2 us
  waiting for transfers between devices  26.1 us (39%)
  starting transfers between devices  23.9 us (36%)
  local copies, waits for them, and re-layouts  8.25 us (12%)
  Pallas kernels  6.17 us (9%)
  other arithmetic  1.07 us (2%)
  between operations  0.74 us (1%)
    ppermute x21, waiting for transfers between devices, swap(): lax.ppermute(value, axis, [(i, i ^ mask) for i in range(lax.axis_size(axi...  26.1 us
    ppermute x21, starting transfers between devices, swap(): lax.ppermute(value, axis, [(i, i ^ mask) for i in range(lax.axis_size(axi...  23.9 us
    unnamed x15, local copies, waits for them, and re-layouts  8.25 us
    pallas_call x5, Pallas kernels, kernel_call(): pl.pallas_call(body, out_shape=outputs, in_specs=kwargs.pop('in_specs', [...  6.17 us
  transfers between devices with their start and end apart: 21, of which 9 were waited for; matrix products, arithmetic and copies ran while one was open for 2% of the time, Pallas kernels for 6%

profile of v2, /device:TPU:0, one launch (start us, length us, event | category | flops | bytes accessed | tf_op | source)
XLA Modules:
  0.0 66.2 jit_solution(7775913930678056228)
XLA Ops:
  0.6 0.8 %copy.11.refs_3_.refs_5_ = bf16[32,2]{1,0:T(8,128)(2,1)S(1)} copy(bf16[32,2]{0,1:T(2,128)(2,1)} %param.10) | data formatting | bytes 256 | tf_op args[3]
  1.4 0.8 %copy.10.refs_2_ = s32[32,2]{1,0:T(8,128)S(1)} copy(s32[32,2]{0,1:T(2,128)} %param.9) | data formatting | bytes 512 | tf_op args[2]
  2.1 1.0 %copy-done.1 = bf16[1,96,2048]{2,1,0:T(8,128)(2,1)S(1)} copy-done((bf16[1,96,2048]{2,1,0:T(8,128)(2,1)S(1)}, bf16[1,96,2048]{2,1,0:T(8,128)(2,1)}, u32[]{:S(2)}) %copy-start.1) | copy-done | bytes 393240
  3.1 1.0 %copy-done.2 = bf16[1,96,2048]{2,1,0:T(8,128)(2,1)S(1)} copy-done((bf16[1,96,2048]{2,1,0:T(8,128)(2,1)S(1)}, bf16[1,96,2048]{2,1,0:T(8,128)(2,1)}, u32[]{:S(2)}) %copy-start.2) | copy-done | bytes 393240
  4.1 1.0 %copy-done.3 = bf16[1,96,2048]{2,1,0:T(8,128)(2,1)S(1)} copy-done((bf16[1,96,2048]{2,1,0:T(8,128)(2,1)S(1)}, bf16[1,96,2048]{2,1,0:T(8,128)(2,1)}, u32[]{:S(2)}) %copy-start.3) | copy-done | bytes 393240
  5.1 0.9 %copy-done.4 = bf16[32,2048]{1,0:T(8,128)(2,1)S(1)} copy-done((bf16[32,2048]{1,0:T(8,128)(2,1)S(1)}, bf16[32,2048]{1,0:T(8,128)(2,1)}, u32[]{:S(2)}) %copy-start.4) | copy-done | bytes 131096
  6.0 0.9 %copy-done.5 = bf16[32,2048]{1,0:T(8,128)(2,1)S(1)} copy-done((bf16[32,2048]{1,0:T(8,128)(2,1)S(1)}, bf16[32,2048]{1,0:T(8,128)(2,1)}, u32[]{:S(2)}) %copy-start.5) | copy-done | bytes 131096
  6.9 1.1 %shard_map.94 = (bf16[40,2048]{1,0:T(8,128)(2,1)S(1)}, bf16[40,2048]{1,0:T(8,128)(2,1)S(1)}, bf16[40,2048]{1,0:T(8,128)(2,1)S(1)}, bf16[40,2048]{1,0:T(8,128)(2,...) custom-call(bf16[32,2048]{1,0:T(8,128)(2,1)S(1)} %copy-done.4, ...), custom_call_target="tpu_custom_call" | custom-call | bytes 2687616 | tf_op jit(solution)/shard_map/pallas_call | solution.py:26
  8.1 3.1 %collective-permute-start = (bf16[40,2048]{1,0:T(8,128)(2,1)S(1)}, bf16[40,2048]{1,0:T(8,128)(2,1)S(1)}, u32[]{:S(2)}, u32[]{:S(2)}) collective-permute-start(bf16[40,2048]{1,0:T(8,128)(2,1)S(1)} %get-tuple-element.26), channel_id=1, source_target_pairs={{0,4},{4,0},{8,12},{12,8},{1,5},{5,1},{9,13},{13,9},{2,6},{6,2},{1... | collective-permute-start | bytes 491528 | tf_op jit(solution)/shard_map/ppermute | solution.py:20
  11.2 2.6 %collective-permute-start.1 = (bf16[40,2048]{1,0:T(8,128)(2,1)S(1)}, bf16[40,2048]{1,0:T(8,128)(2,1)S(1)}, u32[]{:S(2)}, u32[]{:S(2)}) collective-permute-start(bf16[40,2048]{1,0:T(8,128)(2,1)S(1)} %get-tuple-element.27), channel_id=1, source_target_pairs={{0,8},{4,12},{8,0},{12,4},{1,9},{5,13},{9,1},{13,5},{2,10},{6,14},... | collective-permute-start | bytes 491528 | tf_op jit(solution)/shard_map/ppermute | solution.py:20
  13.8 1.5 %collective-permute-start.7 = (bf16[144,1024]{1,0:T(8,128)(2,1)S(1)}, bf16[144,1024]{1,0:T(8,128)(2,1)S(1)}, u32[]{:S(2)}, u32[]{:S(2)}) collective-permute-start(bf16[144,1024]{1,0:T(8,128)(2,1)S(1)} %get-tuple-element.29.refs_8_), channel_id=1, source_target_pairs={{0,1},{1,0},{2,3},{3,2},{4,5},{5,4},{6,7},{7,6},{8,9},{9,8},{10,11... | collective-permute-start | bytes 884744 | tf_op jit(solution)/shard_map/ppermute | solution.py:20
  15.3 1.5 %collective-permute-start.10 = (bf16[144,1024]{1,0:T(8,128)(2,1)S(1)}, bf16[144,1024]{1,0:T(8,128)(2,1)S(1)}, u32[]{:S(2)}, u32[]{:S(2)}) collective-permute-start(bf16[144,1024]{1,0:T(8,128)(2,1)S(1)} %get-tuple-element.30.refs_9_), channel_id=1, source_target_pairs={{0,2},{1,3},{2,0},{3,1},{4,6},{5,7},{6,4},{7,5},{8,10},{9,11},{10,... | collective-permute-start | bytes 884744 | tf_op jit(solution)/shard_map/ppermute | solution.py:20
  16.8 0.2 collective-permute-start.2
  17.0 1.4 %collective-permute-done.refs_1_ = bf16[40,2048]{1,0:T(8,128)(2,1)S(1)} collective-permute-done((bf16[40,2048]{1,0:T(8,128)(2,1)S(1)}, bf16[40,2048]{1,0:T(8,128)(2,1)S(1)}, u32[]{:S(2)}, u32[]{:S(2)}) %collective-permute-start) | collective-permute-done | bytes 163872 | tf_op jit(solution)/shard_map/ppermute | solution.py:20
  18.5 1.4 %collective-permute-start.8 = (bf16[144,1024]{1,0:T(8,128)(2,1)S(1)}, bf16[144,1024]{1,0:T(8,128)(2,1)S(1)}, u32[]{:S(2)}, u32[]{:S(2)}) collective-permute-start(bf16[144,1024]{1,0:T(8,128)(2,1)S(1)} %get-tuple-element.30.refs_9_), channel_id=1, source_target_pairs={{0,1},{1,0},{2,3},{3,2},{4,5},{5,4},{6,7},{7,6},{8,9},{9,8},{10,11... | collective-permute-start | bytes 884744 | tf_op jit(solution)/shard_map/ppermute | solution.py:20
  19.8 5.5 %collective-permute-done.1.refs_2_ = bf16[40,2048]{1,0:T(8,128)(2,1)S(1)} collective-permute-done((bf16[40,2048]{1,0:T(8,128)(2,1)S(1)}, bf16[40,2048]{1,0:T(8,128)(2,1)S(1)}, u32[]{:S(2)}, u32[]{:S(2)}) %collective-permute-start.1) | collective-permute-done | bytes 163872 | tf_op jit(solution)/shard_map/ppermute | solution.py:20
  25.3 2.1 %collective-permute-start.9 = (bf16[144,1024]{1,0:T(8,128)(2,1)S(1)}, bf16[144,1024]{1,0:T(8,128)(2,1)S(1)}, u32[]{:S(2)}, u32[]{:S(2)}) collective-permute-start(bf16[144,1024]{1,0:T(8,128)(2,1)S(1)} %get-tuple-element.29.refs_8_), channel_id=1, source_target_pairs={{0,2},{1,3},{2,0},{3,1},{4,6},{5,7},{6,4},{7,5},{8,10},{9,11},{10,... | collective-permute-start | bytes 884744 | tf_op jit(solution)/shard_map/ppermute | solution.py:20
  27.4 0.1 collective-permute-start.11
  27.5 1.9 %collective-permute-start.12 = (bf16[144,1024]{1,0:T(8,128)(2,1)S(1)}, bf16[144,1024]{1,0:T(8,128)(2,1)S(1)}, u32[]{:S(2)}, u32[]{:S(2)}) collective-permute-start(bf16[144,1024]{1,0:T(8,128)(2,1)S(1)} %collective-permute-done.10.refs_13_), channel_id=1, source_target_pairs={{0,1},{1,0},{2,3},{3,2},{4,5},{5,4},{6,7},{7,6},{8,9},{9,8},{10,11... | collective-permute-start | bytes 884744 | tf_op jit(solution)/shard_map/ppermute | solution.py:20
  29.4 0.0 collective-permute-done.3.refs_4_
  29.4 0.1 collective-permute-start.4
  29.6 0.0 collective-permute-done.8.refs_11_
  29.6 0.4 collective-permute-start.5
  29.9 4.7 %collective-permute-done.9.refs_12_ = bf16[144,1024]{1,0:T(8,128)(2,1)S(1)} collective-permute-done((bf16[144,1024]{1,0:T(8,128)(2,1)S(1)}, bf16[144,1024]{1,0:T(8,128)(2,1)S(1)}, u32[]{:S(2)}, u32[]{:S(2)}) %collective-permute-start.9) | collective-permute-done | bytes 294944 | tf_op jit(solution)/shard_map/ppermute | solution.py:20
  34.6 0.0 collective-permute-start.6
  34.6 1.4 %collective-permute-done.6.refs_7_ = bf16[40,2048]{1,0:T(8,128)(2,1)S(1)} collective-permute-done((bf16[40,2048]{1,0:T(8,128)(2,1)S(1)}, bf16[40,2048]{1,0:T(8,128)(2,1)S(1)}, u32[]{:S(2)}, u32[]{:S(2)}) %collective-permute-start.6) | collective-permute-done | bytes 163872 | tf_op jit(solution)/shard_map/ppermute | solution.py:20
  36.0 2.9 %shard_map.95 = (bf16[160,2048]{1,0:T(8,128)(2,1)S(1)}, bf16[160,2048]{1,0:T(8,128)(2,1)S(1)}, f32[160,2176]{1,0:T(8,128)}, f32[48,2048]{1,0:T(8,128)S(1)}, bf16...) custom-call(bf16[40,2048]{1,0:T(8,128)(2,1)S(1)} %get-tuple-element.25.refs_0_, ...), custom_call_target="tpu_custom_call" | custom-call | flops 660602880 | bytes 6569984 | tf_op jit(solution)/shard_map/pallas_call | solution.py:26
  38.9 1.9 %collective-permute-start.17 = (bf16[48,2048]{1,0:T(8,128)(2,1)S(1)}, bf16[48,2048]{1,0:T(8,128)(2,1)S(1)}, u32[]{:S(2)}, u32[]{:S(2)}) collective-permute-start(bf16[48,2048]{1,0:T(8,128)(2,1)S(1)} %get-tuple-element.44), channel_id=1, source_target_pairs={{0,1},{1,0},{2,3},{3,2},{4,5},{5,4},{6,7},{7,6},{8,9},{9,8},{10,11... | collective-permute-start | bytes 589832 | tf_op jit(solution)/shard_map/ppermute | solution.py:20
  40.8 2.5 %collective-permute-start.18 = (bf16[48,2048]{1,0:T(8,128)(2,1)S(1)}, bf16[48,2048]{1,0:T(8,128)(2,1)S(1)}, u32[]{:S(2)}, u32[]{:S(2)}) collective-permute-start(bf16[48,2048]{1,0:T(8,128)(2,1)S(1)} %get-tuple-element.45), channel_id=1, source_target_pairs={{0,2},{1,3},{2,0},{3,1},{4,6},{5,7},{6,4},{7,5},{8,10},{9,11},{10,... | collective-permute-start | bytes 589832 | tf_op jit(solution)/shard_map/ppermute | solution.py:20
  43.3 1.3 %copy-done = f32[160,2176]{1,0:T(8,128)S(1)} copy-done((f32[160,2176]{1,0:T(8,128)S(1)}, f32[160,2176]{1,0:T(8,128)}, u32[]{:S(2)}) %copy-start) | copy-done | bytes 1392664
  44.6 1.0 %shard_map.96 = (f32[80,2176]{1,0:T(8,128)S(1)}, bf16[80,2176]{1,0:T(8,128)(2,1)S(1)}, bf16[48,2048]{1,0:T(8,128)(2,1)S(1)}) custom-call(bf16[160,2048]{1,0:T(8,128)(2,1)S(1)} %get-tuple-element.31.x_ref, bf16[160,2048]{1,0:T(8,128)(2,1)S(1)} %get-tuple-element.32.d_ref, f32[160,2176]{1,0:T(8,128)S(1)} %copy-done, ...), custom_call_target="tpu_custom_call" | custom-call | flops 220200960 | bytes 4534272 | tf_op jit(solution)/shard_map/pallas_call | solution.py:26
  45.6 0.1 collective-permute-start.19
  45.7 0.1 collective-permute-start.13
  45.8 0.2 collective-permute-done.17
  46.0 5.7 %collective-permute-done.18 = bf16[48,2048]{1,0:T(8,128)(2,1)S(1)} collective-permute-done((bf16[48,2048]{1,0:T(8,128)(2,1)S(1)}, bf16[48,2048]{1,0:T(8,128)(2,1)S(1)}, u32[]{:S(2)}, u32[]{:S(2)}) %collective-permute-start.18) | collective-permute-done | bytes 196640 | tf_op jit(solution)/shard_map/ppermute | solution.py:20
  51.6 1.3 %collective-permute-done.19 = bf16[48,2048]{1,0:T(8,128)(2,1)S(1)} collective-permute-done((bf16[48,2048]{1,0:T(8,128)(2,1)S(1)}, bf16[48,2048]{1,0:T(8,128)(2,1)S(1)}, u32[]{:S(2)}, u32[]{:S(2)}) %collective-permute-start.19) | collective-permute-done | bytes 196640 | tf_op jit(solution)/shard_map/ppermute | solution.py:20
  53.0 0.1 add_convert_fusion
  53.1 0.1 collective-permute-start.20
  53.1 0.0 collective-permute-done.13.got
  53.2 0.1 shard_map.97
  53.3 0.1 collective-permute-start.14
  53.3 3.0 %collective-permute-start.15 = (bf16[20,2176]{1,0:T(8,128)(2,1)S(1)}, bf16[20,2176]{1,0:T(8,128)(2,1)S(1)}, u32[]{:S(2)}, u32[]{:S(2)}) collective-permute-start(bf16[20,2176]{1,0:T(8,128)(2,1)S(1)} %get-tuple-element.38), channel_id=1, source_target_pairs={{0,8},{4,12},{8,0},{12,4},{1,9},{5,13},{9,1},{13,5},{2,10},{6,14},... | collective-permute-start | bytes 261128 | tf_op jit(solution)/shard_map/ppermute | solution.py:20
  56.3 1.4 %collective-permute-start.16 = (bf16[20,2176]{1,0:T(8,128)(2,1)S(1)}, bf16[20,2176]{1,0:T(8,128)(2,1)S(1)}, u32[]{:S(2)}, u32[]{:S(2)}) collective-permute-start(bf16[20,2176]{1,0:T(8,128)(2,1)S(1)} %get-tuple-element.39), channel_id=1, source_target_pairs={{0,12},{4,8},{8,4},{12,0},{1,13},{5,9},{9,5},{13,1},{2,14},{6,10},... | collective-permute-start | bytes 261128 | tf_op jit(solution)/shard_map/ppermute | solution.py:20
  57.8 1.0 %maximum_convert_fusion = f32[1,96,2048]{2,1,0:T(8,128)} fusion(bf16[1,48,2048]{2,1,0:T(8,128)(2,1)S(1)} %get-tuple-element.51, bf16[1,48,2048]{2,1,0:T(8,128)(2,1)S(1)} %get-tuple-element.50), kind=kLoop, calls=%fused_computation | loop fusion | flops 786432 | bytes 1179648 | tf_op jit(solution)/shard_map/convert_element_type | solution.py:251
  58.7 1.8 %collective-permute-done.14.refs_1_ = bf16[20,2176]{1,0:T(8,128)(2,1)S(1)} collective-permute-done((bf16[20,2176]{1,0:T(8,128)(2,1)S(1)}, bf16[20,2176]{1,0:T(8,128)(2,1)S(1)}, u32[]{:S(2)}, u32[]{:S(2)}) %collective-permute-start.14) | collective-permute-done | bytes 87072 | tf_op jit(solution)/shard_map/ppermute | solution.py:20
  60.5 4.0 %collective-permute-done.15.refs_2_ = bf16[20,2176]{1,0:T(8,128)(2,1)S(1)} collective-permute-done((bf16[20,2176]{1,0:T(8,128)(2,1)S(1)}, bf16[20,2176]{1,0:T(8,128)(2,1)S(1)}, u32[]{:S(2)}, u32[]{:S(2)}) %collective-permute-start.15) | collective-permute-done | bytes 87072 | tf_op jit(solution)/shard_map/ppermute | solution.py:20
  64.6 1.0 %shard_map.98 = (bf16[32,2048]{1,0:T(8,128)(2,1)}, bf16[32,2]{1,0:T(8,128)(2,1)S(1)}) custom-call(bf16[20,2176]{1,0:T(8,128)(2,1)S(1)} %get-tuple-element.36.refs_0_, bf16[20,2176]{1,0:T(8,128)(2,1)S(1)} %collective-permute-done.14.refs_1_, bf16[20,2176]{1,0:T(8,128)(2,1)S(1)} %collective-permute-done.15.refs_2_, ...), custom_call_target="tpu_custom_call" | custom-call | bytes 479744 | tf_op jit(solution)/shard_map/pallas_call | solution.py:26
  65.6 0.6 copy.13
  (17 shorter events, 0.1 us)
Async XLA Ops:
  2.1 1.0 %copy-start.1 = (bf16[1,96,2048]{2,1,0:T(8,128)(2,1)S(1)}, bf16[1,96,2048]{2,1,0:T(8,128)(2,1)}, u32[]{:S(2)}) copy-start(bf16[1,96,2048]{2,1,0:T(8,128)(2,1)} %refs_4_.1) | copy-start | bytes 1179652
  3.1 1.0 %copy-start.2 = (bf16[1,96,2048]{2,1,0:T(8,128)(2,1)S(1)}, bf16[1,96,2048]{2,1,0:T(8,128)(2,1)}, u32[]{:S(2)}) copy-start(bf16[1,96,2048]{2,1,0:T(8,128)(2,1)} %refs_5_.2) | copy-start | bytes 1179652
  4.1 1.0 %copy-start.3 = (bf16[1,96,2048]{2,1,0:T(8,128)(2,1)S(1)}, bf16[1,96,2048]{2,1,0:T(8,128)(2,1)}, u32[]{:S(2)}) copy-start(bf16[1,96,2048]{2,1,0:T(8,128)(2,1)} %refs_6_.1) | copy-start | bytes 1179652
  5.1 0.9 %copy-start.4 = (bf16[32,2048]{1,0:T(8,128)(2,1)S(1)}, bf16[32,2048]{1,0:T(8,128)(2,1)}, u32[]{:S(2)}) copy-start(bf16[32,2048]{1,0:T(8,128)(2,1)} %refs_0_.1) | copy-start | bytes 393220
  6.0 0.9 %copy-start.5 = (bf16[32,2048]{1,0:T(8,128)(2,1)S(1)}, bf16[32,2048]{1,0:T(8,128)(2,1)}, u32[]{:S(2)}) copy-start(bf16[32,2048]{1,0:T(8,128)(2,1)} %refs_1_.1) | copy-start | bytes 393220
  8.1 10.4 %collective-permute-start = (bf16[40,2048]{1,0:T(8,128)(2,1)S(1)}, bf16[40,2048]{1,0:T(8,128)(2,1)S(1)}, u32[]{:S(2)}, u32[]{:S(2)}) collective-permute-start(bf16[40,2048]{1,0:T(8,128)(2,1)S(1)} %get-tuple-element.26), channel_id=1, source_target_pairs={{0,4},{4,0},{8,12},{12,8},{1,5},{5,1},{9,13},{13,9},{2,6},{6,2},{1... | collective-permute-start | bytes 491528 | tf_op jit(solution)/shard_map/ppermute | solution.py:20
  11.2 14.1 %collective-permute-start.1 = (bf16[40,2048]{1,0:T(8,128)(2,1)S(1)}, bf16[40,2048]{1,0:T(8,128)(2,1)S(1)}, u32[]{:S(2)}, u32[]{:S(2)}) collective-permute-start(bf16[40,2048]{1,0:T(8,128)(2,1)S(1)} %get-tuple-element.27), channel_id=1, source_target_pairs={{0,8},{4,12},{8,0},{12,4},{1,9},{5,13},{9,1},{13,5},{2,10},{6,14},... | collective-permute-start | bytes 491528 | tf_op jit(solution)/shard_map/ppermute | solution.py:20
  13.8 13.6 %collective-permute-start.7 = (bf16[144,1024]{1,0:T(8,128)(2,1)S(1)}, bf16[144,1024]{1,0:T(8,128)(2,1)S(1)}, u32[]{:S(2)}, u32[]{:S(2)}) collective-permute-start(bf16[144,1024]{1,0:T(8,128)(2,1)S(1)} %get-tuple-element.29.refs_8_), channel_id=1, source_target_pairs={{0,1},{1,0},{2,3},{3,2},{4,5},{5,4},{6,7},{7,6},{8,9},{9,8},{10,11... | collective-permute-start | bytes 884744 | tf_op jit(solution)/shard_map/ppermute | solution.py:20
  15.3 12.2 %collective-permute-start.10 = (bf16[144,1024]{1,0:T(8,128)(2,1)S(1)}, bf16[144,1024]{1,0:T(8,128)(2,1)S(1)}, u32[]{:S(2)}, u32[]{:S(2)}) collective-permute-start(bf16[144,1024]{1,0:T(8,128)(2,1)S(1)} %get-tuple-element.30.refs_9_), channel_id=1, source_target_pairs={{0,2},{1,3},{2,0},{3,1},{4,6},{5,7},{6,4},{7,5},{8,10},{9,11},{10,... | collective-permute-start | bytes 884744 | tf_op jit(solution)/shard_map/ppermute | solution.py:20
  16.8 10.6 %collective-permute-start.2 = (bf16[40,2048]{1,0:T(8,128)(2,1)S(1)}, bf16[40,2048]{1,0:T(8,128)(2,1)S(1)}, u32[]{:S(2)}, u32[]{:S(2)}) collective-permute-start(bf16[40,2048]{1,0:T(8,128)(2,1)S(1)} %get-tuple-element.28), channel_id=1, source_target_pairs={{0,12},{4,8},{8,4},{12,0},{1,13},{5,9},{9,5},{13,1},{2,14},{6,10},... | collective-permute-start | bytes 491528 | tf_op jit(solution)/shard_map/ppermute | solution.py:20
  18.5 11.1 %collective-permute-start.8 = (bf16[144,1024]{1,0:T(8,128)(2,1)S(1)}, bf16[144,1024]{1,0:T(8,128)(2,1)S(1)}, u32[]{:S(2)}, u32[]{:S(2)}) collective-permute-start(bf16[144,1024]{1,0:T(8,128)(2,1)S(1)} %get-tuple-element.30.refs_9_), channel_id=1, source_target_pairs={{0,1},{1,0},{2,3},{3,2},{4,5},{5,4},{6,7},{7,6},{8,9},{9,8},{10,11... | collective-permute-start | bytes 884744 | tf_op jit(solution)/shard_map/ppermute | solution.py:20
  25.3 9.3 %collective-permute-start.9 = (bf16[144,1024]{1,0:T(8,128)(2,1)S(1)}, bf16[144,1024]{1,0:T(8,128)(2,1)S(1)}, u32[]{:S(2)}, u32[]{:S(2)}) collective-permute-start(bf16[144,1024]{1,0:T(8,128)(2,1)S(1)} %get-tuple-element.29.refs_8_), channel_id=1, source_target_pairs={{0,2},{1,3},{2,0},{3,1},{4,6},{5,7},{6,4},{7,5},{8,10},{9,11},{10,... | collective-permute-start | bytes 884744 | tf_op jit(solution)/shard_map/ppermute | solution.py:20
  27.4 2.0 %collective-permute-start.3 = (bf16[40,2048]{1,0:T(8,128)(2,1)S(1)}, bf16[40,2048]{1,0:T(8,128)(2,1)S(1)}, u32[]{:S(2)}, u32[]{:S(2)}) collective-permute-start(bf16[40,2048]{1,0:T(8,128)(2,1)S(1)} %get-tuple-element.25.refs_0_), channel_id=1, source_target_pairs={{0,16},{16,0},{1,17},{17,1},{2,18},{18,2},{3,19},{19,3},{4,20},{20... | collective-permute-start | bytes 491528 | tf_op jit(solution)/shard_map/ppermute | solution.py:20
  27.4 15.8 %collective-permute-start.11 = (bf16[144,1024]{1,0:T(8,128)(2,1)S(1)}, bf16[144,1024]{1,0:T(8,128)(2,1)S(1)}, u32[]{:S(2)}, u32[]{:S(2)}) collective-permute-start(bf16[144,1024]{1,0:T(8,128)(2,1)S(1)} %collective-permute-done.7.refs_10_), channel_id=1, source_target_pairs={{0,2},{1,3},{2,0},{3,1},{4,6},{5,7},{6,4},{7,5},{8,10},{9,11},{10,... | collective-permute-start | bytes 884744 | tf_op jit(solution)/shard_map/ppermute | solution.py:20
  27.5 15.8 %collective-permute-start.12 = (bf16[144,1024]{1,0:T(8,128)(2,1)S(1)}, bf16[144,1024]{1,0:T(8,128)(2,1)S(1)}, u32[]{:S(2)}, u32[]{:S(2)}) collective-permute-start(bf16[144,1024]{1,0:T(8,128)(2,1)S(1)} %collective-permute-done.10.refs_13_), channel_id=1, source_target_pairs={{0,1},{1,0},{2,3},{3,2},{4,5},{5,4},{6,7},{7,6},{8,9},{9,8},{10,11... | collective-permute-start | bytes 884744 | tf_op jit(solution)/shard_map/ppermute | solution.py:20
  29.4 5.2 %collective-permute-start.4 = (bf16[40,2048]{1,0:T(8,128)(2,1)S(1)}, bf16[40,2048]{1,0:T(8,128)(2,1)S(1)}, u32[]{:S(2)}, u32[]{:S(2)}) collective-permute-start(bf16[40,2048]{1,0:T(8,128)(2,1)S(1)} %collective-permute-done.refs_1_), channel_id=1, source_target_pairs={{0,16},{16,0},{1,17},{17,1},{2,18},{18,2},{3,19},{19,3},{4,20},{20... | collective-permute-start | bytes 491528 | tf_op jit(solution)/shard_map/ppermute | solution.py:20
  29.6 5.0 %collective-permute-start.5 = (bf16[40,2048]{1,0:T(8,128)(2,1)S(1)}, bf16[40,2048]{1,0:T(8,128)(2,1)S(1)}, u32[]{:S(2)}, u32[]{:S(2)}) collective-permute-start(bf16[40,2048]{1,0:T(8,128)(2,1)S(1)} %collective-permute-done.1.refs_2_), channel_id=1, source_target_pairs={{0,16},{16,0},{1,17},{17,1},{2,18},{18,2},{3,19},{19,3},{4,20},{20... | collective-permute-start | bytes 491528 | tf_op jit(solution)/shard_map/ppermute | solution.py:20
  34.6 1.4 %collective-permute-start.6 = (bf16[40,2048]{1,0:T(8,128)(2,1)S(1)}, bf16[40,2048]{1,0:T(8,128)(2,1)S(1)}, u32[]{:S(2)}, u32[]{:S(2)}) collective-permute-start(bf16[40,2048]{1,0:T(8,128)(2,1)S(1)} %collective-permute-done.2.refs_3_), channel_id=1, source_target_pairs={{0,16},{16,0},{1,17},{17,1},{2,18},{18,2},{3,19},{19,3},{4,20},{20... | collective-permute-start | bytes 491528 | tf_op jit(solution)/shard_map/ppermute | solution.py:20
  38.9 7.1 %collective-permute-start.17 = (bf16[48,2048]{1,0:T(8,128)(2,1)S(1)}, bf16[48,2048]{1,0:T(8,128)(2,1)S(1)}, u32[]{:S(2)}, u32[]{:S(2)}) collective-permute-start(bf16[48,2048]{1,0:T(8,128)(2,1)S(1)} %get-tuple-element.44), channel_id=1, source_target_pairs={{0,1},{1,0},{2,3},{3,2},{4,5},{5,4},{6,7},{7,6},{8,9},{9,8},{10,11... | collective-permute-start | bytes 589832 | tf_op jit(solution)/shard_map/ppermute | solution.py:20
  40.8 10.9 %collective-permute-start.18 = (bf16[48,2048]{1,0:T(8,128)(2,1)S(1)}, bf16[48,2048]{1,0:T(8,128)(2,1)S(1)}, u32[]{:S(2)}, u32[]{:S(2)}) collective-permute-start(bf16[48,2048]{1,0:T(8,128)(2,1)S(1)} %get-tuple-element.45), channel_id=1, source_target_pairs={{0,2},{1,3},{2,0},{3,1},{4,6},{5,7},{6,4},{7,5},{8,10},{9,11},{10,... | collective-permute-start | bytes 589832 | tf_op jit(solution)/shard_map/ppermute | solution.py:20
  43.2 1.3 %copy-start = (f32[160,2176]{1,0:T(8,128)S(1)}, f32[160,2176]{1,0:T(8,128)}, u32[]{:S(2)}) copy-start(f32[160,2176]{1,0:T(8,128)} %get-tuple-element.33.dx_ref) | copy-start | bytes 4177924
  45.6 7.4 %collective-permute-start.19 = (bf16[48,2048]{1,0:T(8,128)(2,1)S(1)}, bf16[48,2048]{1,0:T(8,128)(2,1)S(1)}, u32[]{:S(2)}, u32[]{:S(2)}) collective-permute-start(bf16[48,2048]{1,0:T(8,128)(2,1)S(1)} %get-tuple-element.46), channel_id=1, source_target_pairs={{0,3},{1,2},{2,1},{3,0},{4,7},{5,6},{6,5},{7,4},{8,11},{9,10},{10,... | collective-permute-start | bytes 589832 | tf_op jit(solution)/shard_map/ppermute | solution.py:20
  45.7 7.5 %collective-permute-start.13 = (bf16[80,2176]{1,0:T(8,128)(2,1)S(1)}, bf16[80,2176]{1,0:T(8,128)(2,1)S(1)}, u32[]{:S(2)}, u32[]{:S(2)}) collective-permute-start(bf16[80,2176]{1,0:T(8,128)(2,1)S(1)} %get-tuple-element.35), channel_id=1, source_target_pairs={{0,16},{16,0},{1,17},{17,1},{2,18},{18,2},{3,19},{19,3},{4,20},{20... | collective-permute-start | bytes 1044488 | tf_op jit(solution)/shard_map/ppermute | solution.py:20
  53.1 4.7 %collective-permute-start.20 = (bf16[48,2048]{1,0:T(8,128)(2,1)S(1)}, bf16[48,2048]{1,0:T(8,128)(2,1)S(1)}, u32[]{:S(2)}, u32[]{:S(2)}) collective-permute-start(bf16[48,2048]{1,0:T(8,128)(2,1)S(1)} %add_convert_fusion), channel_id=1, source_target_pairs={{0,16},{16,0},{1,17},{17,1},{2,18},{18,2},{3,19},{19,3},{4,20},{20... | collective-permute-start | bytes 589832 | tf_op jit(solution)/shard_map/ppermute | solution.py:20
  53.3 7.3 %collective-permute-start.14 = (bf16[20,2176]{1,0:T(8,128)(2,1)S(1)}, bf16[20,2176]{1,0:T(8,128)(2,1)S(1)}, u32[]{:S(2)}, u32[]{:S(2)}) collective-permute-start(bf16[20,2176]{1,0:T(8,128)(2,1)S(1)} %get-tuple-element.37), channel_id=1, source_target_pairs={{0,4},{4,0},{8,12},{12,8},{1,5},{5,1},{9,13},{13,9},{2,6},{6,2},{1... | collective-permute-start | bytes 261128 | tf_op jit(solution)/shard_map/ppermute | solution.py:20
  53.3 11.2 %collective-permute-start.15 = (bf16[20,2176]{1,0:T(8,128)(2,1)S(1)}, bf16[20,2176]{1,0:T(8,128)(2,1)S(1)}, u32[]{:S(2)}, u32[]{:S(2)}) collective-permute-start(bf16[20,2176]{1,0:T(8,128)(2,1)S(1)} %get-tuple-element.38), channel_id=1, source_target_pairs={{0,8},{4,12},{8,0},{12,4},{1,9},{5,13},{9,1},{13,5},{2,10},{6,14},... | collective-permute-start | bytes 261128 | tf_op jit(solution)/shard_map/ppermute | solution.py:20
  56.3 8.3 %collective-permute-start.16 = (bf16[20,2176]{1,0:T(8,128)(2,1)S(1)}, bf16[20,2176]{1,0:T(8,128)(2,1)S(1)}, u32[]{:S(2)}, u32[]{:S(2)}) collective-permute-start(bf16[20,2176]{1,0:T(8,128)(2,1)S(1)} %get-tuple-element.39), channel_id=1, source_target_pairs={{0,12},{4,8},{8,4},{12,0},{1,13},{5,9},{9,5},{13,1},{2,14},{6,10},... | collective-permute-start | bytes 261128 | tf_op jit(solution)/shard_map/ppermute | solution.py:20

commit v3 on v2

--- a/solution.py
+++ b/solution.py
@@ -8,7 +8,7 @@
 from jax.sharding import PartitionSpec as P
 
 LANES = 128
-VMEM_BYTES = 48 * 1024 * 1024
+VMEM_BYTES = 32 * 1024 * 1024
 f32, bf16 = jnp.float32, jnp.bfloat16
 
 
@@ -39,57 +39,55 @@
 
 
 def dispatch_kernel(experts, cap, chunk_count, *refs):
-    tokens, upstream, ids, route_weight, gate, up, down = refs[:7]
-    chunks = refs[7 : 7 + chunk_count]
-    slot_out, first, second, sems = refs[7 + chunk_count :]
-    hidden, half = first.shape[0] // 3, first.shape[1]
+    small, (gate, up, down), refs = refs[:4], refs[4:7], refs[7:]
+    chunks, (slot_out, packed), refs = refs[:chunk_count], refs[chunk_count : chunk_count + 2], refs[chunk_count + 2 :]
+    held, sems = refs[:4], refs[4]
+    hidden = packed.shape[0] // 3
     rep = lax.axis_index("rep")
-    copies = []
-    for i, weight in enumerate((gate, up, down)):
-        for j, piece in enumerate((first, second)):
-            copies.append(
-                pltpu.make_async_copy(
-                    weight.at[0, pl.ds(pl.multiple_of(rep * hidden, hidden), hidden), pl.ds(j * half, half)],
-                    piece.at[pl.ds(i * hidden, hidden)],
-                    sems.at[2 * i + j],
-                )
-            )
-            copies[-1].start()
-
-    tok_dev, top = ids.shape
+    half = pl.ds(pl.multiple_of(rep * hidden, hidden), hidden)
+    loads = [pltpu.make_async_copy(*pair, sems.at[i]) for i, pair in enumerate(zip(small, held))]
+    packs = [
+        pltpu.make_async_copy(weight.at[0, half], packed.at[pl.ds(i * hidden, hidden)], sems.at[4 + i])
+        for i, weight in enumerate((gate, up, down))
+    ]
+    for copy in loads + packs:
+        copy.start()
+    for copy in loads:
+        copy.wait()
+
+    tokens, upstream, ids, route_weight = held
+    top, tok_dev = ids.shape
     rows = experts * cap // chunk_count
     me = lax.axis_index("ep")
-    wide = -(-experts // LANES) * LANES
-    expert_of_lane = iota((tok_dev, wide), 1)
-    named = [(expert_of_lane == ids[:, k : k + 1]).astype(f32) for k in range(top)]
-    earlier = (iota((tok_dev, tok_dev), 0) > iota((tok_dev, tok_dev), 1)).astype(bf16)
-    before = dot(earlier, sum(named).astype(bf16), (1, 0))
-    lane = iota((tok_dev, 2 * experts * cap), 1)
-    take_x = jnp.zeros(lane.shape, f32)
-    take_dy = jnp.zeros(lane.shape, f32)
-    scale = jnp.zeros((2 * experts * cap, LANES), f32)
+    expert_of_row = iota((experts, tok_dev), 0)
+    named = [(expert_of_row == ids[k : k + 1, :]).astype(f32) for k in range(top)]
+    earlier = (iota((tok_dev, tok_dev), 0) < iota((tok_dev, tok_dev), 1)).astype(bf16)
+    before = dot(sum(named).astype(bf16), earlier, (1, 0))
+    row = iota((2 * experts * cap, tok_dev), 0)
+    take_x = jnp.zeros(row.shape, f32)
+    take_dy = jnp.zeros(row.shape, f32)
+    scale = jnp.zeros(row.shape, f32)
     for k in range(top):
-        rank = jnp.sum(before * named[k], axis=1, keepdims=True).astype(jnp.int32)
-        expert = ids[:, k : k + 1]
+        rank = jnp.sum(before * named[k], axis=0, keepdims=True).astype(jnp.int32)
+        expert = ids[k : k + 1, :]
         if chunk_count > 1:
             chunk = expert ^ me
             slot = chunk * cap + rank
-            x_lane = slot + chunk * cap
+            x_row = slot + chunk * cap
         else:
             slot = expert * cap + rank
-            x_lane = slot
-        slot_out[:, k : k + 1] = slot
-        take_x += (lane == x_lane).astype(f32)
-        here = (lane == x_lane + rows).astype(f32)
-        take_dy += here
-        weight = jnp.broadcast_to(route_weight[:, k : k + 1], (tok_dev, LANES))
-        scale += dot(here.astype(bf16), weight, (0, 0))
-    scale += dot(take_x.astype(bf16), jnp.ones((tok_dev, LANES), bf16), (0, 0))
-    picked = dot(take_x.astype(bf16), tokens[...], (0, 0)) + dot(take_dy.astype(bf16), upstream[...], (0, 0))
-    picked = picked * scale[:, :1]
+            x_row = slot
+        slot_out[k : k + 1, :] = slot
+        here_x = (row == x_row).astype(f32)
+        here_dy = (row == x_row + rows).astype(f32)
+        take_x += here_x
+        take_dy += here_dy
+        scale += here_x + here_dy * route_weight[k : k + 1, :].astype(f32)
+    picked = dot(take_x.astype(bf16), tokens[...], (1, 0)) + dot(take_dy.astype(bf16), upstream[...], (1, 0))
+    picked = picked * jnp.sum(scale, axis=1, keepdims=True)
     for c in range(chunk_count):
         chunks[c][...] = picked[2 * rows * c : 2 * rows * (c + 1)].astype(bf16)
-    for copy in copies:
+    for copy in packs:
         copy.wait()
 
 
@@ -125,9 +123,9 @@
     values = [c[...].astype(f32) for c in chunks]
     x_out[...] = jnp.concatenate([v[:rows] for v in values]).astype(bf16)
     d_out[...] = jnp.concatenate([v[rows:] for v in values]).astype(bf16)
-    pairs = [(pieces[i], pieces[i + 1]) for i in range(0, piece_count, 2)]
+    width = x_out.shape[1]
+    pairs = [[p.at[:, pl.ds(j, width // 2)] for j in (0, width // 2)] for p in pieces]
     dx, prob, grad = expert_math(x_out[...], d_out[...], pairs)
-    width = x_out.shape[1]
     dx_out[:, : width // 2] = dx[0]
     dx_out[:, width // 2 : width] = dx[1]
     dx_out[:, width:] = jnp.broadcast_to(prob, (prob.shape[0], LANES))
@@ -159,19 +157,19 @@
     chunks, (slot, route_weight, tokens_out, probs_out) = refs[:chunk_count], refs[chunk_count:]
     rows = chunks[0].shape[0]
     tok_dev, width = tokens_out.shape
-    top = slot.shape[1]
+    top = slot.shape[0]
     total = 0.0
     probs = [0.0] * top
     for c in range(chunk_count):
-        slot_of_lane = iota((tok_dev, rows), 1) + c * rows
-        hits = [(slot_of_lane == slot[:, k : k + 1]).astype(f32) for k in range(top)]
-        total = total + dot(sum(hits).astype(bf16), chunks[c][:, :width], (1, 0))
+        slot_of_row = iota((rows, tok_dev), 0) + c * rows
+        hits = [(slot_of_row == slot[k : k + 1, :]).astype(f32) for k in range(top)]
+        total = total + dot(sum(hits).astype(bf16), chunks[c][:, :width], (0, 0))
+        prob = chunks[c][:, width : width + 1].astype(f32)
         for k in range(top):
-            probs[k] = probs[k] + dot(hits[k].astype(bf16), chunks[c][:, width:], (1, 0))
+            probs[k] = probs[k] + jnp.sum(hits[k] * prob, axis=0, keepdims=True)
     tokens_out[...] = total.astype(bf16)
     for k in range(top):
-        weight = route_weight[:, k : k + 1].astype(f32)
-        probs_out[:, k : k + 1] = (probs[k][:, :1] / weight).astype(bf16)
+        probs_out[k : k + 1, :] = (probs[k] / route_weight[k : k + 1, :].astype(f32)).astype(bf16)
 
 
 def local(tokens, upstream, expert_ids, route_weight, gate_weight, up_weight, down_weight):
@@ -184,24 +182,26 @@
     rows = slots // chunk_count
     hidden = gate_weight.shape[1] // reps
     shape = jax.ShapeDtypeStruct
-    in_vmem, anywhere = pl.BlockSpec(memory_space=pltpu.VMEM), pl.BlockSpec(memory_space=pl.ANY)
-
-    *chunks, slot, first, second = kernel_call(
+    in_hbm = pl.BlockSpec(memory_space=pltpu.HBM)
+
+    small = [tokens, upstream, expert_ids.T, route_weight.T]
+    *chunks, slot, packed = kernel_call(
         functools.partial(dispatch_kernel, experts, cap, chunk_count),
-        [tokens, upstream, expert_ids, route_weight, gate_weight, up_weight, down_weight],
+        [pltpu.with_memory_space_constraint(a, pltpu.HBM) for a in small + [gate_weight, up_weight, down_weight]],
         [shape((2 * rows, width), bf16)] * chunk_count
-        + [shape((tok_dev, top), jnp.int32)]
-        + [shape((3 * hidden, width // 2), bf16)] * 2,
-        in_specs=[in_vmem] * 4 + [anywhere] * 3,
-        scratch_shapes=[pltpu.SemaphoreType.DMA((6,))],
-    )
-
+        + [shape((top, tok_dev), jnp.int32), shape((3 * hidden, width), bf16)],
+        in_specs=[in_hbm] * 7,
+        scratch_shapes=[pltpu.VMEM(a.shape, a.dtype) for a in small] + [pltpu.SemaphoreType.DMA((7,))],
+    )
+
+    half = width // 2
     if shards == 4:
-        near = [[swap(piece, "dp", m) for piece in (first, second)] for m in (1, 2)]
-        diagonal = [swap(near[0][0], "dp", 2), swap(near[1][1], "dp", 1)]
-        blocks = [[first, second]] + near + [diagonal]
+        near = [packed] + [swap(packed, "dp", m) for m in (1, 2)]
+        last = [swap(near[1][:, :half], "dp", 2), swap(near[2][:, half:], "dp", 1)]
     else:
-        blocks = [[first, second]] + [[swap(p, "dp", m) for p in (first, second)] for m in range(1, shards)]
+        near = [packed] + [swap(packed, "dp", m) for m in range(1, shards - 1)]
+        last = swap(packed, "dp", shards - 1)
+        last = [last[:, :half], last[:, half:]]
 
     if chunk_count > 1:
         chunks = [chunks[0]] + [swap(chunks[m], "ep", m) for m in range(1, experts)]
@@ -211,12 +211,11 @@
         chunks = [moved.reshape(2 * rows, width)]
     chunks = chunks + [swap(c, "rep", 1) for c in chunks]
 
-    pieces = [p for block in blocks[:-1] for p in block]
     wide = width + LANES
     flops = 14 * 2 * slots * width * hidden
     x_rows, d_rows, dx, grad_own, *grads = kernel_call(
-        functools.partial(early_kernel, 2 * chunk_count, len(pieces)),
-        chunks + pieces,
+        functools.partial(early_kernel, 2 * chunk_count, len(near)),
+        chunks + near,
         [shape((2 * slots, width), bf16)] * 2
         + [shape((2 * slots, wide), f32), shape((hidden, width), f32)]
         + [shape((hidden, width), bf16)] * (shards - 2),
@@ -224,11 +223,12 @@
     )
     keep, give, grad_last = kernel_call(
         late_kernel,
-        [x_rows, d_rows, dx] + blocks[-1],
+        [x_rows, d_rows, dx] + last,
         [shape((slots, wide), f32), shape((slots, wide), bf16), shape((hidden, width), bf16)],
         flops=flops,
     )
     back = kernel_call(add_kernel, [keep, swap(give, "rep", 1)], [shape((rows, wide), bf16)] * chunk_count)
+    grad_last, back = lax.optimization_barrier((grad_last, back))
     if chunk_count > 1:
         back = [back[0]] + [swap(back[m], "ep", m) for m in range(1, experts)]
     else:
@@ -237,18 +237,17 @@
         back = [moved.reshape(rows, wide)]
     d_tokens, d_probs = kernel_call(
         functools.partial(combine_kernel, chunk_count),
-        back + [slot, route_weight],
-        [shape((tok_dev, width), bf16), shape((tok_dev, top), bf16)],
-    )
-
-    total = grad_own
-    for m, grad in enumerate(grads + [grad_last]):
-        total = total + swap(grad, "dp", m + 1).astype(f32)
-    total = total.astype(bf16)
+        back + [slot, route_weight.T],
+        [shape((tok_dev, width), bf16), shape((top, tok_dev), bf16)],
+    )
+
+    arrived = [swap(grad, "dp", m + 1) for m, grad in enumerate(grads + [grad_last])]
+    arrived, _ = lax.optimization_barrier((arrived, back[1:]))
+    total = (grad_own + sum(a.astype(f32) for a in arrived)).astype(bf16)
     theirs = swap(total, "rep", 1)
     lower = lax.axis_index("rep") == 0
     grad_total = jnp.concatenate([jnp.where(lower, total, theirs), jnp.where(lower, theirs, total)])
-    return (d_tokens, d_probs, grad_total.astype(f32)[None])
+    return (d_tokens, d_probs.T, grad_total.astype(f32)[None])
 
 
 def solution(mesh):

time: 66.5 us -> 49.2 us (0.74)
  local copies, waits for them, and re-layouts: 8.25 us -> 0.05 us
  waiting for transfers between devices: 26.1 us -> 18.5 us
  starting transfers between devices: 23.9 us -> 23 us
    unnamed x15 -> x2, local copies, waits for them, and re-layouts: 8.25 us -> 0.01 us
    ppermute x21 -> x19, waiting for transfers between devices: 26.1 us -> 18.5 us  [swap(): lax.ppermute(value, axis, [(i, i ^ mask) for i in range(lax.axis_size(axi...]
    ppermute x21 -> x19, starting transfers between devices: 23.9 us -> 23 us  [swap(): lax.ppermute(value, axis, [(i, i ^ mask) for i in range(lax.axis_size(axi...]
  transfers between devices with their start and end apart: 21 -> 19, of which waited for: 9 -> 10; matrix products, arithmetic and copies ran while one was open for 2% -> 0% of each run, Pallas kernels for 6% -> 6%
where the time goes in v3:
time: 49.2 us; the launch traced here: 49 us
  starting transfers between devices  23 us (47%)
  waiting for transfers between devices  18.5 us (38%)
  Pallas kernels  5.75 us (12%)
  other arithmetic  1.07 us (2%)
  between operations  0.74 us (2%)
    ppermute x19, starting transfers between devices, swap(): lax.ppermute(value, axis, [(i, i ^ mask) for i in range(lax.axis_size(axi...  23 us
    ppermute x19, waiting for transfers between devices, swap(): lax.ppermute(value, axis, [(i, i ^ mask) for i in range(lax.axis_size(axi...  18.5 us
    pallas_call x5, Pallas kernels, kernel_call(): pl.pallas_call(body, out_shape=outputs, in_specs=kwargs.pop('in_specs', [...  5.75 us
  transfers between devices with their start and end apart: 19, of which 10 were waited for; matrix products, arithmetic and copies ran while one was open for 0% of the time, Pallas kernels for 6%

profile of v3, /device:TPU:0, one launch (start us, length us, event | category | flops | bytes accessed | tf_op | source)
XLA Modules:
  0.0 49.0 jit_solution(13409542498531543770)
XLA Ops:
  0.6 1.7 %shard_map.94 = (bf16[40,2048]{1,0:T(8,128)(2,1)S(1)}, bf16[40,2048]{1,0:T(8,128)(2,1)S(1)}, bf16[40,2048]{1,0:T(8,128)(2,1)S(1)}, bf16[40,2048]{1,0:T(8,128)(2,...) custom-call(bf16[32,2048]{1,0:T(8,128)(2,1)} %refs_0_.1, bf16[32,2048]{1,0:T(8,128)(2,1)} %refs_1_.1, ...), custom_call_target="tpu_custom_call" | custom-call | bytes 2687616 | tf_op jit(solution)/shard_map/pallas_call | solution.py:26
  2.3 3.0 %collective-permute-start.8 = (bf16[144,2048]{1,0:T(8,128)(2,1)S(1)}, bf16[144,2048]{1,0:T(8,128)(2,1)S(1)}, u32[]{:S(2)}, u32[]{:S(2)}) collective-permute-start(bf16[144,2048]{1,0:T(8,128)(2,1)S(1)} %get-tuple-element.36.refs_8_), channel_id=1, source_target_pairs={{0,2},{1,3},{2,0},{3,1},{4,6},{5,7},{6,4},{7,5},{8,10},{9,11},{10,... | collective-permute-start | bytes 1769480 | tf_op jit(solution)/shard_map/ppermute | solution.py:20
  5.3 1.5 %collective-permute-start.7 = (bf16[144,2048]{1,0:T(8,128)(2,1)S(1)}, bf16[144,2048]{1,0:T(8,128)(2,1)S(1)}, u32[]{:S(2)}, u32[]{:S(2)}) collective-permute-start(bf16[144,2048]{1,0:T(8,128)(2,1)S(1)} %get-tuple-element.36.refs_8_), channel_id=1, source_target_pairs={{0,1},{1,0},{2,3},{3,2},{4,5},{5,4},{6,7},{7,6},{8,9},{9,8},{10,11... | collective-permute-start | bytes 1769480 | tf_op jit(solution)/shard_map/ppermute | solution.py:20
  6.8 1.6 %collective-permute-start = (bf16[40,2048]{1,0:T(8,128)(2,1)S(1)}, bf16[40,2048]{1,0:T(8,128)(2,1)S(1)}, u32[]{:S(2)}, u32[]{:S(2)}) collective-permute-start(bf16[40,2048]{1,0:T(8,128)(2,1)S(1)} %get-tuple-element.33), channel_id=1, source_target_pairs={{0,4},{4,0},{8,12},{12,8},{1,5},{5,1},{9,13},{13,9},{2,6},{6,2},{1... | collective-permute-start | bytes 491528 | tf_op jit(solution)/shard_map/ppermute | solution.py:20
  8.4 2.6 %collective-permute-start.1 = (bf16[40,2048]{1,0:T(8,128)(2,1)S(1)}, bf16[40,2048]{1,0:T(8,128)(2,1)S(1)}, u32[]{:S(2)}, u32[]{:S(2)}) collective-permute-start(bf16[40,2048]{1,0:T(8,128)(2,1)S(1)} %get-tuple-element.34), channel_id=1, source_target_pairs={{0,8},{4,12},{8,0},{12,4},{1,9},{5,13},{9,1},{13,5},{2,10},{6,14},... | collective-permute-start | bytes 491528 | tf_op jit(solution)/shard_map/ppermute | solution.py:20
  11.0 0.2 collective-permute-start.2
  11.2 7.4 %collective-permute-done.8.refs_10_ = bf16[144,2048]{1,0:T(8,128)(2,1)S(1)} collective-permute-done((bf16[144,2048]{1,0:T(8,128)(2,1)S(1)}, bf16[144,2048]{1,0:T(8,128)(2,1)S(1)}, u32[]{:S(2)}, u32[]{:S(2)}) %collective-permute-start.8) | collective-permute-done | bytes 589856 | tf_op jit(solution)/shard_map/ppermute | solution.py:20
  18.7 0.0 collective-permute-start.3
  18.7 1.4 %collective-permute-done.7.refs_9_ = bf16[144,2048]{1,0:T(8,128)(2,1)S(1)} collective-permute-done((bf16[144,2048]{1,0:T(8,128)(2,1)S(1)}, bf16[144,2048]{1,0:T(8,128)(2,1)S(1)}, u32[]{:S(2)}, u32[]{:S(2)}) %collective-permute-start.7) | collective-permute-done | bytes 589856 | tf_op jit(solution)/shard_map/ppermute | solution.py:20
  20.1 1.5 %collective-permute-start.10 = (bf16[144,1024]{1,0:T(8,128)(2,1)S(1)}, bf16[144,1024]{1,0:T(8,128)(2,1)S(1)}, u32[]{:S(2)}, u32[]{:S(2)}) collective-permute-start(bf16[144,1024]{1,0:T(8,128)(2,1)S(1)} %slice.9), channel_id=1, source_target_pairs={{0,1},{1,0},{2,3},{3,2},{4,5},{5,4},{6,7},{7,6},{8,9},{9,8},{10,11... | collective-permute-start | bytes 884744 | tf_op jit(solution)/shard_map/ppermute | solution.py:20
  21.6 0.0 collective-permute-done.refs_1_
  21.6 0.6 %collective-permute-start.9 = (bf16[144,1024]{1,0:T(8,128)(2,1)S(1)}, bf16[144,1024]{1,0:T(8,128)(2,1)S(1)}, u32[]{:S(2)}, u32[]{:S(2)}) collective-permute-start(bf16[144,1024]{1,0:T(8,128)(2,1)S(1)} %slice.8), channel_id=1, source_target_pairs={{0,2},{1,3},{2,0},{3,1},{4,6},{5,7},{6,4},{7,5},{8,10},{9,11},{10,... | collective-permute-start | bytes 884744 | tf_op jit(solution)/shard_map/ppermute | solution.py:20
  22.2 1.0 %collective-permute-done.1.refs_2_ = bf16[40,2048]{1,0:T(8,128)(2,1)S(1)} collective-permute-done((bf16[40,2048]{1,0:T(8,128)(2,1)S(1)}, bf16[40,2048]{1,0:T(8,128)(2,1)S(1)}, u32[]{:S(2)}, u32[]{:S(2)}) %collective-permute-start.1) | collective-permute-done | bytes 163872 | tf_op jit(solution)/shard_map/ppermute | solution.py:20
  23.2 0.0 collective-permute-start.4
  23.2 0.0 collective-permute-done.2.refs_3_
  23.2 0.5 %collective-permute-start.5 = (bf16[40,2048]{1,0:T(8,128)(2,1)S(1)}, bf16[40,2048]{1,0:T(8,128)(2,1)S(1)}, u32[]{:S(2)}, u32[]{:S(2)}) collective-permute-start(bf16[40,2048]{1,0:T(8,128)(2,1)S(1)} %collective-permute-done.1.refs_2_), channel_id=1, source_target_pairs={{0,16},{16,0},{1,17},{17,1},{2,18},{18,2},{3,19},{19,3},{4,20},{20... | collective-permute-start | bytes 491528 | tf_op jit(solution)/shard_map/ppermute | solution.py:20
  23.7 0.0 collective-permute-done.3.refs_4_
  23.7 0.1 collective-permute-start.6
  23.8 0.8 %collective-permute-done.4.refs_5_ = bf16[40,2048]{1,0:T(8,128)(2,1)S(1)} collective-permute-done((bf16[40,2048]{1,0:T(8,128)(2,1)S(1)}, bf16[40,2048]{1,0:T(8,128)(2,1)S(1)}, u32[]{:S(2)}, u32[]{:S(2)}) %collective-permute-start.4) | collective-permute-done | bytes 163872 | tf_op jit(solution)/shard_map/ppermute | solution.py:20
  24.6 0.2 collective-permute-done.5.refs_6_
  24.9 0.3 collective-permute-done.6.refs_7_
  25.1 2.0 %shard_map.95 = (bf16[160,2048]{1,0:T(8,128)(2,1)S(1)}, bf16[160,2048]{1,0:T(8,128)(2,1)S(1)}, f32[160,2176]{1,0:T(8,128)S(1)}, f32[48,2048]{1,0:T(8,128)S(1)}, ...) custom-call(bf16[40,2048]{1,0:T(8,128)(2,1)S(1)} %get-tuple-element.32.refs_0_, ...), custom_call_target="tpu_custom_call" | custom-call | flops 660602880 | bytes 6569984 | tf_op jit(solution)/shard_map/pallas_call | solution.py:26
  27.1 1.1 %collective-permute-done.10.second = bf16[144,1024]{1,0:T(8,128)(2,1)S(1)} collective-permute-done((bf16[144,1024]{1,0:T(8,128)(2,1)S(1)}, bf16[144,1024]{1,0:T(8,128)(2,1)S(1)}, u32[]{:S(2)}, u32[]{:S(2)}) %collective-permute-start.10) | collective-permute-done | bytes 294944 | tf_op jit(solution)/shard_map/ppermute | solution.py:20
  28.2 1.5 %collective-permute-done.9.first = bf16[144,1024]{1,0:T(8,128)(2,1)S(1)} collective-permute-done((bf16[144,1024]{1,0:T(8,128)(2,1)S(1)}, bf16[144,1024]{1,0:T(8,128)(2,1)S(1)}, u32[]{:S(2)}, u32[]{:S(2)}) %collective-permute-start.9) | collective-permute-done | bytes 294944 | tf_op jit(solution)/shard_map/ppermute | solution.py:20
  29.7 1.0 %shard_map.96 = (f32[80,2176]{1,0:T(8,128)S(1)}, bf16[80,2176]{1,0:T(8,128)(2,1)S(1)}, bf16[48,2048]{1,0:T(8,128)(2,1)S(1)}) custom-call(bf16[160,2048]{1,0:T(8,128)(2,1)S(1)} %get-tuple-element.37.x_ref, bf16[160,2048]{1,0:T(8,128)(2,1)S(1)} %get-tuple-element.38.d_ref, f32[160,2176]{1,0:T(8,128)S(1)} %get-tuple-element.39.dx_ref, ...), custom_call_target="tpu_custom_call" | custom-call | flops 220200960 | bytes 4534272 | tf_op jit(solution)/shard_map/pallas_call | solution.py:26
  30.7 0.0 copy-start
  30.8 0.1 collective-permute-start.11
  30.8 0.4 collective-permute-start.15
  31.2 1.7 %collective-permute-start.16 = (bf16[48,2048]{1,0:T(8,128)(2,1)S(1)}, bf16[48,2048]{1,0:T(8,128)(2,1)S(1)}, u32[]{:S(2)}, u32[]{:S(2)}) collective-permute-start(bf16[48,2048]{1,0:T(8,128)(2,1)S(1)} %get-tuple-element.56), channel_id=1, source_target_pairs={{0,2},{1,3},{2,0},{3,1},{4,6},{5,7},{6,4},{7,5},{8,10},{9,11},{10,... | collective-permute-start | bytes 589832 | tf_op jit(solution)/shard_map/ppermute | solution.py:20
  32.9 0.0 collective-permute-done.11.got
  33.0 0.1 shard_map.97
  33.1 1.5 %collective-permute-start.17 = (bf16[48,2048]{1,0:T(8,128)(2,1)S(1)}, bf16[48,2048]{1,0:T(8,128)(2,1)S(1)}, u32[]{:S(2)}, u32[]{:S(2)}) collective-permute-start(bf16[48,2048]{1,0:T(8,128)(2,1)S(1)} %get-tuple-element.57), channel_id=1, source_target_pairs={{0,3},{1,2},{2,1},{3,0},{4,7},{5,6},{6,5},{7,4},{8,11},{9,10},{10,... | collective-permute-start | bytes 589832 | tf_op jit(solution)/shard_map/ppermute | solution.py:20
  34.6 1.6 %collective-permute-start.12 = (bf16[20,2176]{1,0:T(8,128)(2,1)S(1)}, bf16[20,2176]{1,0:T(8,128)(2,1)S(1)}, u32[]{:S(2)}, u32[]{:S(2)}) collective-permute-start(bf16[20,2176]{1,0:T(8,128)(2,1)S(1)} %get-tuple-element.48), channel_id=1, source_target_pairs={{0,4},{4,0},{8,12},{12,8},{1,5},{5,1},{9,13},{13,9},{2,6},{6,2},{1... | collective-permute-start | bytes 261128 | tf_op jit(solution)/shard_map/ppermute | solution.py:20
  36.1 2.6 %collective-permute-start.13 = (bf16[20,2176]{1,0:T(8,128)(2,1)S(1)}, bf16[20,2176]{1,0:T(8,128)(2,1)S(1)}, u32[]{:S(2)}, u32[]{:S(2)}) collective-permute-start(bf16[20,2176]{1,0:T(8,128)(2,1)S(1)} %get-tuple-element.49), channel_id=1, source_target_pairs={{0,8},{4,12},{8,0},{12,4},{1,9},{5,13},{9,1},{13,5},{2,10},{6,14},... | collective-permute-start | bytes 261128 | tf_op jit(solution)/shard_map/ppermute | solution.py:20
  38.7 0.0 collective-permute-done.15
  38.7 3.5 %collective-permute-start.14 = (bf16[20,2176]{1,0:T(8,128)(2,1)S(1)}, bf16[20,2176]{1,0:T(8,128)(2,1)S(1)}, u32[]{:S(2)}, u32[]{:S(2)}) collective-permute-start(bf16[20,2176]{1,0:T(8,128)(2,1)S(1)} %get-tuple-element.50), channel_id=1, source_target_pairs={{0,12},{4,8},{8,4},{12,0},{1,13},{5,9},{9,5},{13,1},{2,14},{6,10},... | collective-permute-start | bytes 261128 | tf_op jit(solution)/shard_map/ppermute | solution.py:20
  42.2 0.0 collective-permute-done.16
  42.2 0.0 collective-permute-done.12.refs_1_
  42.2 4.2 %collective-permute-done.13.refs_2_ = bf16[20,2176]{1,0:T(8,128)(2,1)S(1)} collective-permute-done((bf16[20,2176]{1,0:T(8,128)(2,1)S(1)}, bf16[20,2176]{1,0:T(8,128)(2,1)S(1)}, u32[]{:S(2)}, u32[]{:S(2)}) %collective-permute-start.13) | collective-permute-done | bytes 87072 | tf_op jit(solution)/shard_map/ppermute | solution.py:20
  46.4 0.0 collective-permute-done.14.refs_3_
  46.4 0.0 collective-permute-done.17
  46.4 0.1 add_convert_fusion
  46.5 0.1 collective-permute-start.18
  46.6 0.0 copy-done
  46.6 1.0 %shard_map.98 = (bf16[32,2048]{1,0:T(8,128)(2,1)}, bf16[2,32]{1,0:T(2,128)(2,1)}) custom-call(bf16[20,2176]{1,0:T(8,128)(2,1)S(1)} %get-tuple-element.47.refs_0_, bf16[20,2176]{1,0:T(8,128)(2,1)S(1)} %collective-permute-done.12.refs_1_, bf16[20,2176]{1,0:T(8,128)(2,1)S(1)} %collective-permute-done.13.refs_2_, ...), custom_call_target="tpu_custom_call" | custom-call | bytes 479744 | tf_op jit(solution)/shard_map/pallas_call | solution.py:26
  47.6 0.4 collective-permute-done.18
  48.1 0.9 %maximum_convert_fusion = f32[1,96,2048]{2,1,0:T(8,128)} fusion(bf16[1,48,2048]{2,1,0:T(8,128)(2,1)S(1)} %get-tuple-element.62, bf16[1,48,2048]{2,1,0:T(8,128)(2,1)S(1)} %get-tuple-element.61), kind=kLoop, calls=%fused_computation | loop fusion | flops 786432 | bytes 1179648 | tf_op jit(solution)/shard_map/convert_element_type | solution.py:250
  (3 shorter events, 0.1 us)
Async XLA Ops:
  2.3 16.4 %collective-permute-start.8 = (bf16[144,2048]{1,0:T(8,128)(2,1)S(1)}, bf16[144,2048]{1,0:T(8,128)(2,1)S(1)}, u32[]{:S(2)}, u32[]{:S(2)}) collective-permute-start(bf16[144,2048]{1,0:T(8,128)(2,1)S(1)} %get-tuple-element.36.refs_8_), channel_id=1, source_target_pairs={{0,2},{1,3},{2,0},{3,1},{4,6},{5,7},{6,4},{7,5},{8,10},{9,11},{10,... | collective-permute-start | bytes 1769480 | tf_op jit(solution)/shard_map/ppermute | solution.py:20
  5.3 14.8 %collective-permute-start.7 = (bf16[144,2048]{1,0:T(8,128)(2,1)S(1)}, bf16[144,2048]{1,0:T(8,128)(2,1)S(1)}, u32[]{:S(2)}, u32[]{:S(2)}) collective-permute-start(bf16[144,2048]{1,0:T(8,128)(2,1)S(1)} %get-tuple-element.36.refs_8_), channel_id=1, source_target_pairs={{0,1},{1,0},{2,3},{3,2},{4,5},{5,4},{6,7},{7,6},{8,9},{9,8},{10,11... | collective-permute-start | bytes 1769480 | tf_op jit(solution)/shard_map/ppermute | solution.py:20
  6.8 14.8 %collective-permute-start = (bf16[40,2048]{1,0:T(8,128)(2,1)S(1)}, bf16[40,2048]{1,0:T(8,128)(2,1)S(1)}, u32[]{:S(2)}, u32[]{:S(2)}) collective-permute-start(bf16[40,2048]{1,0:T(8,128)(2,1)S(1)} %get-tuple-element.33), channel_id=1, source_target_pairs={{0,4},{4,0},{8,12},{12,8},{1,5},{5,1},{9,13},{13,9},{2,6},{6,2},{1... | collective-permute-start | bytes 491528 | tf_op jit(solution)/shard_map/ppermute | solution.py:20
  8.4 14.8 %collective-permute-start.1 = (bf16[40,2048]{1,0:T(8,128)(2,1)S(1)}, bf16[40,2048]{1,0:T(8,128)(2,1)S(1)}, u32[]{:S(2)}, u32[]{:S(2)}) collective-permute-start(bf16[40,2048]{1,0:T(8,128)(2,1)S(1)} %get-tuple-element.34), channel_id=1, source_target_pairs={{0,8},{4,12},{8,0},{12,4},{1,9},{5,13},{9,1},{13,5},{2,10},{6,14},... | collective-permute-start | bytes 491528 | tf_op jit(solution)/shard_map/ppermute | solution.py:20
  11.0 12.2 %collective-permute-start.2 = (bf16[40,2048]{1,0:T(8,128)(2,1)S(1)}, bf16[40,2048]{1,0:T(8,128)(2,1)S(1)}, u32[]{:S(2)}, u32[]{:S(2)}) collective-permute-start(bf16[40,2048]{1,0:T(8,128)(2,1)S(1)} %get-tuple-element.35), channel_id=1, source_target_pairs={{0,12},{4,8},{8,4},{12,0},{1,13},{5,9},{9,5},{13,1},{2,14},{6,10},... | collective-permute-start | bytes 491528 | tf_op jit(solution)/shard_map/ppermute | solution.py:20
  18.7 5.1 %collective-permute-start.3 = (bf16[40,2048]{1,0:T(8,128)(2,1)S(1)}, bf16[40,2048]{1,0:T(8,128)(2,1)S(1)}, u32[]{:S(2)}, u32[]{:S(2)}) collective-permute-start(bf16[40,2048]{1,0:T(8,128)(2,1)S(1)} %get-tuple-element.32.refs_0_), channel_id=1, source_target_pairs={{0,16},{16,0},{1,17},{17,1},{2,18},{18,2},{3,19},{19,3},{4,20},{20... | collective-permute-start | bytes 491528 | tf_op jit(solution)/shard_map/ppermute | solution.py:20
  20.1 8.1 %collective-permute-start.10 = (bf16[144,1024]{1,0:T(8,128)(2,1)S(1)}, bf16[144,1024]{1,0:T(8,128)(2,1)S(1)}, u32[]{:S(2)}, u32[]{:S(2)}) collective-permute-start(bf16[144,1024]{1,0:T(8,128)(2,1)S(1)} %slice.9), channel_id=1, source_target_pairs={{0,1},{1,0},{2,3},{3,2},{4,5},{5,4},{6,7},{7,6},{8,9},{9,8},{10,11... | collective-permute-start | bytes 884744 | tf_op jit(solution)/shard_map/ppermute | solution.py:20
  21.6 8.1 %collective-permute-start.9 = (bf16[144,1024]{1,0:T(8,128)(2,1)S(1)}, bf16[144,1024]{1,0:T(8,128)(2,1)S(1)}, u32[]{:S(2)}, u32[]{:S(2)}) collective-permute-start(bf16[144,1024]{1,0:T(8,128)(2,1)S(1)} %slice.8), channel_id=1, source_target_pairs={{0,2},{1,3},{2,0},{3,1},{4,6},{5,7},{6,4},{7,5},{8,10},{9,11},{10,... | collective-permute-start | bytes 884744 | tf_op jit(solution)/shard_map/ppermute | solution.py:20
  23.2 1.4 %collective-permute-start.4 = (bf16[40,2048]{1,0:T(8,128)(2,1)S(1)}, bf16[40,2048]{1,0:T(8,128)(2,1)S(1)}, u32[]{:S(2)}, u32[]{:S(2)}) collective-permute-start(bf16[40,2048]{1,0:T(8,128)(2,1)S(1)} %collective-permute-done.refs_1_), channel_id=1, source_target_pairs={{0,16},{16,0},{1,17},{17,1},{2,18},{18,2},{3,19},{19,3},{4,20},{20... | collective-permute-start | bytes 491528 | tf_op jit(solution)/shard_map/ppermute | solution.py:20
  23.2 1.6 %collective-permute-start.5 = (bf16[40,2048]{1,0:T(8,128)(2,1)S(1)}, bf16[40,2048]{1,0:T(8,128)(2,1)S(1)}, u32[]{:S(2)}, u32[]{:S(2)}) collective-permute-start(bf16[40,2048]{1,0:T(8,128)(2,1)S(1)} %collective-permute-done.1.refs_2_), channel_id=1, source_target_pairs={{0,16},{16,0},{1,17},{17,1},{2,18},{18,2},{3,19},{19,3},{4,20},{20... | collective-permute-start | bytes 491528 | tf_op jit(solution)/shard_map/ppermute | solution.py:20
  23.7 1.4 %collective-permute-start.6 = (bf16[40,2048]{1,0:T(8,128)(2,1)S(1)}, bf16[40,2048]{1,0:T(8,128)(2,1)S(1)}, u32[]{:S(2)}, u32[]{:S(2)}) collective-permute-start(bf16[40,2048]{1,0:T(8,128)(2,1)S(1)} %collective-permute-done.2.refs_3_), channel_id=1, source_target_pairs={{0,16},{16,0},{1,17},{17,1},{2,18},{18,2},{3,19},{19,3},{4,20},{20... | collective-permute-start | bytes 491528 | tf_op jit(solution)/shard_map/ppermute | solution.py:20
  30.7 15.9 %copy-start = (bf16[32,2]{0,1:T(2,128)(2,1)S(1)}, bf16[32,2]{0,1:T(2,128)(2,1)}, u32[]{:S(2)}) copy-start(bf16[32,2]{0,1:T(2,128)(2,1)} %param.10) | copy-start | bytes 388
  30.8 2.2 %collective-permute-start.11 = (bf16[80,2176]{1,0:T(8,128)(2,1)S(1)}, bf16[80,2176]{1,0:T(8,128)(2,1)S(1)}, u32[]{:S(2)}, u32[]{:S(2)}) collective-permute-start(bf16[80,2176]{1,0:T(8,128)(2,1)S(1)} %get-tuple-element.42), channel_id=1, source_target_pairs={{0,16},{16,0},{1,17},{17,1},{2,18},{18,2},{3,19},{19,3},{4,20},{20... | collective-permute-start | bytes 1044488 | tf_op jit(solution)/shard_map/ppermute | solution.py:20
  30.8 7.9 %collective-permute-start.15 = (bf16[48,2048]{1,0:T(8,128)(2,1)S(1)}, bf16[48,2048]{1,0:T(8,128)(2,1)S(1)}, u32[]{:S(2)}, u32[]{:S(2)}) collective-permute-start(bf16[48,2048]{1,0:T(8,128)(2,1)S(1)} %get-tuple-element.55), channel_id=1, source_target_pairs={{0,1},{1,0},{2,3},{3,2},{4,5},{5,4},{6,7},{7,6},{8,9},{9,8},{10,11... | collective-permute-start | bytes 589832 | tf_op jit(solution)/shard_map/ppermute | solution.py:20
  31.2 11.0 %collective-permute-start.16 = (bf16[48,2048]{1,0:T(8,128)(2,1)S(1)}, bf16[48,2048]{1,0:T(8,128)(2,1)S(1)}, u32[]{:S(2)}, u32[]{:S(2)}) collective-permute-start(bf16[48,2048]{1,0:T(8,128)(2,1)S(1)} %get-tuple-element.56), channel_id=1, source_target_pairs={{0,2},{1,3},{2,0},{3,1},{4,6},{5,7},{6,4},{7,5},{8,10},{9,11},{10,... | collective-permute-start | bytes 589832 | tf_op jit(solution)/shard_map/ppermute | solution.py:20
  33.1 13.4 %collective-permute-start.17 = (bf16[48,2048]{1,0:T(8,128)(2,1)S(1)}, bf16[48,2048]{1,0:T(8,128)(2,1)S(1)}, u32[]{:S(2)}, u32[]{:S(2)}) collective-permute-start(bf16[48,2048]{1,0:T(8,128)(2,1)S(1)} %get-tuple-element.57), channel_id=1, source_target_pairs={{0,3},{1,2},{2,1},{3,0},{4,7},{5,6},{6,5},{7,4},{8,11},{9,10},{10,... | collective-permute-start | bytes 589832 | tf_op jit(solution)/shard_map/ppermute | solution.py:20
  34.6 7.6 %collective-permute-start.12 = (bf16[20,2176]{1,0:T(8,128)(2,1)S(1)}, bf16[20,2176]{1,0:T(8,128)(2,1)S(1)}, u32[]{:S(2)}, u32[]{:S(2)}) collective-permute-start(bf16[20,2176]{1,0:T(8,128)(2,1)S(1)} %get-tuple-element.48), channel_id=1, source_target_pairs={{0,4},{4,0},{8,12},{12,8},{1,5},{5,1},{9,13},{13,9},{2,6},{6,2},{1... | collective-permute-start | bytes 261128 | tf_op jit(solution)/shard_map/ppermute | solution.py:20
  36.1 10.3 %collective-permute-start.13 = (bf16[20,2176]{1,0:T(8,128)(2,1)S(1)}, bf16[20,2176]{1,0:T(8,128)(2,1)S(1)}, u32[]{:S(2)}, u32[]{:S(2)}) collective-permute-start(bf16[20,2176]{1,0:T(8,128)(2,1)S(1)} %get-tuple-element.49), channel_id=1, source_target_pairs={{0,8},{4,12},{8,0},{12,4},{1,9},{5,13},{9,1},{13,5},{2,10},{6,14},... | collective-permute-start | bytes 261128 | tf_op jit(solution)/shard_map/ppermute | solution.py:20
  38.7 7.7 %collective-permute-start.14 = (bf16[20,2176]{1,0:T(8,128)(2,1)S(1)}, bf16[20,2176]{1,0:T(8,128)(2,1)S(1)}, u32[]{:S(2)}, u32[]{:S(2)}) collective-permute-start(bf16[20,2176]{1,0:T(8,128)(2,1)S(1)} %get-tuple-element.50), channel_id=1, source_target_pairs={{0,12},{4,8},{8,4},{12,0},{1,13},{5,9},{9,5},{13,1},{2,14},{6,10},... | collective-permute-start | bytes 261128 | tf_op jit(solution)/shard_map/ppermute | solution.py:20
  46.5 1.5 %collective-permute-start.18 = (bf16[48,2048]{1,0:T(8,128)(2,1)S(1)}, bf16[48,2048]{1,0:T(8,128)(2,1)S(1)}, u32[]{:S(2)}, u32[]{:S(2)}) collective-permute-start(bf16[48,2048]{1,0:T(8,128)(2,1)S(1)} %add_convert_fusion), channel_id=1, source_target_pairs={{0,16},{16,0},{1,17},{17,1},{2,18},{18,2},{3,19},{19,3},{4,20},{20... | collective-permute-start | bytes 589832 | tf_op jit(solution)/shard_map/ppermute | solution.py:20

commit v4 on v3

v4 whole, which is shorter than its diff:
```python
import functools

import jax
import jax.numpy as jnp
from jax import lax
from jax.experimental import pallas as pl
from jax.experimental.pallas import tpu as pltpu
from jax.sharding import PartitionSpec as P

LANES = 128
VMEM_BYTES = 32 * 1024 * 1024
f32, bf16 = jnp.float32, jnp.bfloat16


def dot(left, right, contract):
    return lax.dot_general(left, right, ((contract[0:1], contract[1:2]), ((), ())), preferred_element_type=f32)


def swap(value, axis, mask):
    return lax.ppermute(value, axis, [(i, i ^ mask) for i in range(lax.axis_size(axis))])


def kernel_call(body, inputs, outputs, flops=0, **kwargs):
    whole = pl.BlockSpec(memory_space=pltpu.VMEM)
    moved = sum(a.size * a.dtype.itemsize for a in inputs + outputs)
    return pl.pallas_call(
        body,
        out_shape=outputs,
        in_specs=kwargs.pop("in_specs", [whole] * len(inputs)),
        out_specs=[whole] * len(outputs),
        cost_estimate=pl.CostEstimate(flops=flops, bytes_accessed=moved, transcendentals=0),
        compiler_params=pltpu.CompilerParams(vmem_limit_bytes=VMEM_BYTES),
        **kwargs,
    )(*inputs)


def iota(shape, dim):
    return lax.broadcasted_iota(jnp.int32, shape, dim)


def dispatch_kernel(experts, cap, *refs):
    small, (gate, up, down), refs = refs[:4], refs[4:7], refs[7:]
    send, slot_out, packed, *held, sems = refs
    hidden = packed.shape[0] // 3
    rep = lax.axis_index("rep")
    half = pl.ds(pl.multiple_of(rep * hidden, hidden), hidden)
    loads = [pltpu.make_async_copy(*pair, sems.at[i]) for i, pair in enumerate(zip(small, held))]
    packs = [
        pltpu.make_async_copy(weight.at[0, half], packed.at[pl.ds(i * hidden, hidden)], sems.at[4 + i])
        for i, weight in enumerate((gate, up, down))
    ]
    for copy in loads + packs:
        copy.start()
    for copy in loads:
        copy.wait()

    tokens, upstream, ids, route_weight = held
    top, tok_dev = ids.shape
    expert_of_row = iota((experts, tok_dev), 0)
    named = [(expert_of_row == ids[k : k + 1, :]).astype(f32) for k in range(top)]
    earlier = (iota((tok_dev, tok_dev), 0) < iota((tok_dev, tok_dev), 1)).astype(bf16)
    before = dot(sum(named).astype(bf16), earlier, (1, 0))
    row = iota((2 * experts * cap, tok_dev), 0)
    take_x = jnp.zeros(row.shape, f32)
    take_dy = jnp.zeros(row.shape, f32)
    scale = jnp.zeros(row.shape, f32)
    for k in range(top):
        rank = jnp.sum(before * named[k], axis=0, keepdims=True).astype(jnp.int32)
        expert = ids[k : k + 1, :]
        slot = expert * cap + rank
        x_row = slot + expert * cap
        slot_out[k : k + 1, :] = slot
        here_x = (row == x_row).astype(f32)
        here_dy = (row == x_row + cap).astype(f32)
        take_x += here_x
        take_dy += here_dy
        scale += here_x + here_dy * route_weight[k : k + 1, :].astype(f32)
    picked = dot(take_x.astype(bf16), tokens[...], (1, 0)) + dot(take_dy.astype(bf16), upstream[...], (1, 0))
    picked = picked * jnp.sum(scale, axis=1, keepdims=True)
    send[...] = picked.astype(bf16)
    for copy in packs:
        copy.wait()


def expert_math(x_rows, d_rows, pieces):
    acts, mixed, held = [], [], []
    prob = 0.0
    for piece in pieces:
        hidden = piece[0].shape[0] // 3
        both, down = pl.ds(0, 2 * hidden), pl.ds(2 * hidden, hidden)
        pre = sum(dot(x, p[both], (1, 1)) for x, p in zip(x_rows, piece))
        d_act = sum(dot(d, p[down], (1, 1)) for d, p in zip(d_rows, piece))
        gate_pre, up_pre = pre[:, :hidden], pre[:, hidden:]
        sig = jax.nn.sigmoid(gate_pre)
        silu = gate_pre * sig
        act = silu * up_pre
        prob = prob + jnp.sum(act * d_act, axis=1, keepdims=True)
        acts.append(act)
        mixed += [d_act * up_pre * sig * (1.0 + gate_pre * (1.0 - sig)), d_act * silu]
        held.append([p[both] for p in piece])
    mixed = jnp.concatenate(mixed, axis=1).astype(bf16)
    acts = jnp.concatenate(acts, axis=1).astype(bf16)
    dx = [dot(mixed, jnp.concatenate([h[j] for h in held]), (1, 0)) for j in range(2)]
    return dx, prob, [dot(acts, d, (0, 0)) for d in d_rows]


def gather_kernel(*refs):
    chunks, *outs = refs
    rows, half = chunks.shape[1] // 2, outs[0].shape[1]
    values = [chunks[c].astype(f32) for c in range(chunks.shape[0])]
    for i, out in enumerate(outs):
        kind, side = slice(i // 2 * rows, (i // 2 + 1) * rows), slice(i % 2 * half, (i % 2 + 1) * half)
        out[...] = jnp.concatenate([v[kind, side] for v in values]).astype(bf16)


def both_cores(own, other):
    rows = [jnp.concatenate([a[...], b[...]]) for a, b in zip(own, other)]
    return rows[:2], rows[2:]


def early_kernel(*refs):
    x_rows, d_rows = both_cores(refs[:4], refs[4:8])
    count = (len(refs) - 9) // 2
    pieces, (dx_out, grad_own, *grads) = refs[8 : 8 + count], refs[8 + count :]
    half = x_rows[0].shape[1]
    sides = [slice(0, half), slice(half, 2 * half)]
    dx, prob, grad = expert_math(x_rows, d_rows, [[p.at[:, pl.ds(j * half, half)] for j in range(2)] for p in pieces])
    dx_out[:, 2 * half :] = jnp.broadcast_to(prob, (prob.shape[0], LANES))
    hidden = grad_own.shape[0]
    for j, side in enumerate(sides):
        dx_out[:, side] = dx[j]
        grad_own[:, side] = grad[j][:hidden]
        for i, out in enumerate(grads):
            out[:, side] = grad[j][hidden * (i + 1) : hidden * (i + 2)].astype(bf16)


def late_kernel(*refs):
    dx_ref, first, second, keep, give, grad_out = refs[8:]
    dx, prob, grad = expert_math(*both_cores(refs[:4], refs[4:8]), [(first, second)])
    half, slots = first.shape[1], keep.shape[0]
    for j, value in enumerate((dx[0], dx[1], jnp.broadcast_to(prob, (prob.shape[0], LANES)))):
        columns = slice(j * half, j * half + value.shape[1])
        total = value + dx_ref[:, columns]
        keep[:, columns] = total[:slots]
        give[:, columns] = total[slots:].astype(bf16)
    for j in range(2):
        grad_out[:, j * half : (j + 1) * half] = grad[j].astype(bf16)


def add_kernel(keep, got, out):
    out[...] = (keep[...] + got[...].astype(f32)).astype(bf16)


def combine_kernel(back, slot, route_weight, tokens_out, probs_out):
    slots = back.shape[0]
    tok_dev, width = tokens_out.shape
    top = slot.shape[0]
    slot_of_row = iota((slots, tok_dev), 0)
    hits = [(slot_of_row == slot[k : k + 1, :]).astype(f32) for k in range(top)]
    total = dot(sum(hits).astype(bf16), back[:, :width], (0, 0))
    prob = back[:, width : width + 1].astype(f32)
    probs = [jnp.sum(hit * prob, axis=0, keepdims=True) for hit in hits]
    tokens_out[...] = total.astype(bf16)
    for k in range(top):
        probs_out[k : k + 1, :] = (probs[k] / route_weight[k : k + 1, :].astype(f32)).astype(bf16)


def local(tokens, upstream, expert_ids, route_weight, gate_weight, up_weight, down_weight):
    tok_dev, width = tokens.shape
    top = expert_ids.shape[1]
    experts, shards, reps = lax.axis_size("ep"), lax.axis_size("dp"), lax.axis_size("rep")
    cap = 2 * ((5 * tok_dev * top + 8 * experts - 1) // (8 * experts))
    slots = experts * cap
    hidden = gate_weight.shape[1] // reps
    shape = jax.ShapeDtypeStruct
    in_hbm = pl.BlockSpec(memory_space=pltpu.HBM)

    small = [tokens, upstream, expert_ids.T, route_weight.T]
    send, slot, packed = kernel_call(
        functools.partial(dispatch_kernel, experts, cap),
        [pltpu.with_memory_space_constraint(a, pltpu.HBM) for a in small + [gate_weight, up_weight, down_weight]],
        [shape((2 * slots, width), bf16), shape((top, tok_dev), jnp.int32), shape((3 * hidden, width), bf16)],
        in_specs=[in_hbm] * 7,
        scratch_shapes=[pltpu.VMEM(a.shape, a.dtype) for a in small] + [pltpu.SemaphoreType.DMA((7,))],
    )

    half = width // 2
    if shards == 4:
        near = [packed] + [swap(packed, "dp", m) for m in (1, 2)]
        onward = [near[1][:, :half], near[2][:, half:]]
        last = [swap(onward[0], "dp", 2), swap(onward[1], "dp", 1)]
    else:
        near = [packed] + [swap(packed, "dp", m) for m in range(1, shards - 1)]
        onward = near
        last = swap(packed, "dp", shards - 1)
        last = [last[:, :half], last[:, half:]]

    moved = lax.all_to_all(send.reshape(experts, 2 * cap, width), "ep", split_axis=0, concat_axis=0, tiled=True)
    own = kernel_call(gather_kernel, [moved], [shape((slots, half), bf16)] * 4)
    other = [swap(part, "rep", 1) for part in own]

    wide = width + LANES
    flops = 14 * 2 * slots * width * hidden
    dx, grad_own, *grads = kernel_call(
        early_kernel,
        [*own, *other, *near],
        [shape((2 * slots, wide), f32), shape((hidden, width), f32)]
        + [shape((hidden, width), bf16)] * (shards - 2),
        flops=flops * (shards - 1),
    )
    keep, give, grad_last = kernel_call(
        late_kernel,
        [*own, *other, dx, *last],
        [shape((slots, wide), f32), shape((slots, wide), bf16), shape((hidden, width), bf16)],
        flops=flops,
    )
    (back,) = kernel_call(add_kernel, [keep, swap(give, "rep", 1)], [shape((slots, wide), bf16)])
    grads, grad_last, back = lax.optimization_barrier((grads, grad_last, back))
    back = lax.all_to_all(back.reshape(experts, cap, wide), "ep", split_axis=0, concat_axis=0, tiled=True)
    back = back.reshape(slots, wide)
    d_tokens, d_probs = kernel_call(
        combine_kernel,
        [back, slot, route_weight.T],
        [shape((tok_dev, width), bf16), shape((top, tok_dev), bf16)],
    )

    arrived = [swap(grad, "dp", m + 1) for m, grad in enumerate([*grads, grad_last])]
    arrived, _ = lax.optimization_barrier((arrived, back))
    total = (grad_own + sum(a.astype(f32) for a in arrived)).astype(bf16)
    theirs = swap(total, "rep", 1)
    lower = lax.axis_index("rep") == 0
    grad_total = jnp.concatenate([jnp.where(lower, total, theirs), jnp.where(lower, theirs, total)])
    return (d_tokens, d_probs.T, grad_total.astype(f32)[None])


def solution(mesh):
    rows = P(("rep", "ep", "dp"), None)
    weights = P("ep", "dp", None)
    return jax.shard_map(
        local,
        mesh=mesh,
        in_specs=(rows,) * 4 + (weights,) * 3,
        out_specs=(rows, rows, weights),
        check_vma=False,
    )
```

time: 49.2 us -> 60.7 us (1.23)
  waiting for transfers between devices: 18.5 us -> 30.9 us
  starting transfers between devices: 23 us -> 20.4 us
  local copies, waits for them, and re-layouts: 0.05 us -> 0.95 us
  Pallas kernels: 5.75 us -> 6.47 us
    all_to_all x0 -> x2, waiting for transfers between devices: none -> 23.5 us  [the longest x1 14.3 us: local(): lax.all_to_all(send.reshape(experts, 2 * cap, width), 'ep', split_axis=0,...]
    ppermute x19 -> x13, starting transfers between devices: 23 us -> 10.4 us  [swap(): lax.ppermute(value, axis, [(i, i ^ mask) for i in range(lax.axis_size(axi...]
    ppermute x19 -> x13, waiting for transfers between devices: 18.5 us -> 7.37 us  [swap(): lax.ppermute(value, axis, [(i, i ^ mask) for i in range(lax.axis_size(axi...]
    all_to_all x0 -> x2, starting transfers between devices: none -> 9.93 us  [the longest x1 6.33 us: local(): lax.all_to_all(send.reshape(experts, 2 * cap, width), 'ep', split_axis=0,...]
    reshape x0 -> x2, local copies, waits for them, and re-layouts: none -> 0.9 us  [the longest x1 0.83 us: local(): back.reshape(experts, cap, wide)]
    pallas_call x5 -> x6, Pallas kernels: 5.75 us -> 6.47 us  [kernel_call(): pl.pallas_call(body, out_shape=outputs, in_specs=kwargs.pop('in_specs', [...]
  transfers between devices with their start and end apart: 19 -> 15, of which waited for: 10 -> 9; matrix products, arithmetic and copies ran while one was open for 0% -> 0% of each run, Pallas kernels for 6% -> 5%
where the time goes in v4:
time: 60.7 us; the launch traced here: 60.5 us
  waiting for transfers between devices  30.9 us (51%)
  starting transfers between devices  20.4 us (34%)
  Pallas kernels  6.47 us (11%)
  other arithmetic  1.07 us (2%)
  local copies, waits for them, and re-layouts  0.95 us (2%)
  between operations  0.78 us (1%)
    all_to_all x1, waiting for transfers between devices, local(): lax.all_to_all(send.reshape(experts, 2 * cap, width), 'ep', split_axis=0,...  14.3 us
    ppermute x13, starting transfers between devices, swap(): lax.ppermute(value, axis, [(i, i ^ mask) for i in range(lax.axis_size(axi...  10.4 us
    all_to_all x1, waiting for transfers between devices, local(): lax.all_to_all(back.reshape(experts, cap, wide), 'ep', split_axis=0, conc...  9.2 us
    ppermute x13, waiting for transfers between devices, swap(): lax.ppermute(value, axis, [(i, i ^ mask) for i in range(lax.axis_size(axi...  7.37 us
    pallas_call x6, Pallas kernels, kernel_call(): pl.pallas_call(body, out_shape=outputs, in_specs=kwargs.pop('in_specs', [...  6.47 us
    all_to_all x1, starting transfers between devices, local(): lax.all_to_all(send.reshape(experts, 2 * cap, width), 'ep', split_axis=0,...  6.33 us
    all_to_all x1, starting transfers between devices, local(): lax.all_to_all(back.reshape(experts, cap, wide), 'ep', split_axis=0, conc...  3.59 us
  transfers between devices with their start and end apart: 15, of which 9 were waited for; matrix products, arithmetic and copies ran while one was open for 0% of the time, Pallas kernels for 5%

profile of v4, /device:TPU:0, one launch (start us, length us, event | category | flops | bytes accessed | tf_op | source)
XLA Modules:
  0.0 60.5 jit_solution(17626980416653279759)
XLA Ops:
  0.6 2.5 %shard_map.94 = (bf16[160,2048]{1,0:T(8,128)(2,1)}, s32[2,32]{1,0:T(2,128)S(1)}, bf16[144,2048]{1,0:T(8,128)(2,1)S(1)}) custom-call(bf16[32,2048]{1,0:T(8,128)(2,1)} %refs_0_.1, bf16[32,2048]{1,0:T(8,128)(2,1)} %refs_1_.1, s32[2,32]{1,0:T(2,128)} %bitcast.10, bf16[2,32]{1,0:T(2,128)(2,1)} %bitcast.8, bf16[1,96,2048]{2,1,0:T(8,128)(2,1)} %refs_4_.1, ...), custom_call_target="tpu_custom_call" | custom-call | bytes 2687616 | tf_op jit(solution)/shard_map/pallas_call | solution.py:26
  3.1 6.3 %all-to-all-start = ((bf16[4,40,2048]{2,1,0:T(8,128)(2,1)}), bf16[4,40,2048]{2,1,0:T(8,128)(2,1)S(1)}, u32[]{:S(2)}, u32[]{:S(2)}) async-start(bf16[4,40,2048]{2,1,0:T(8,128)(2,1)} %bitcast.2), calls=%async_computation | async-start | bytes 1310720 | tf_op jit(solution)/shard_map/all_to_all | solution.py:198
  9.5 1.5 %collective-permute-start.4 = (bf16[144,2048]{1,0:T(8,128)(2,1)S(1)}, bf16[144,2048]{1,0:T(8,128)(2,1)S(1)}, u32[]{:S(2)}, u32[]{:S(2)}) collective-permute-start(bf16[144,2048]{1,0:T(8,128)(2,1)S(1)} %get-tuple-element.31.refs_8_), channel_id=1, source_target_pairs={{0,1},{1,0},{2,3},{3,2},{4,5},{5,4},{6,7},{7,6},{8,9},{9,8},{10,11... | collective-permute-start | bytes 1769480 | tf_op jit(solution)/shard_map/ppermute | solution.py:20
  11.0 1.5 %collective-permute-start.5 = (bf16[144,2048]{1,0:T(8,128)(2,1)S(1)}, bf16[144,2048]{1,0:T(8,128)(2,1)S(1)}, u32[]{:S(2)}, u32[]{:S(2)}) collective-permute-start(bf16[144,2048]{1,0:T(8,128)(2,1)S(1)} %get-tuple-element.31.refs_8_), channel_id=1, source_target_pairs={{0,2},{1,3},{2,0},{3,1},{4,6},{5,7},{6,4},{7,5},{8,10},{9,11},{10,... | collective-permute-start | bytes 1769480 | tf_op jit(solution)/shard_map/ppermute | solution.py:20
  12.5 14.3 %all-to-all-done.refs_0_ = bf16[4,40,2048]{2,1,0:T(8,128)(2,1)S(1)} async-done(((bf16[4,40,2048]{2,1,0:T(8,128)(2,1)}), bf16[4,40,2048]{2,1,0:T(8,128)(2,1)S(1)}, u32[]{:S(2)}, u32[]{:S(2)}) %all-to-all-start) | async-done | bytes 655392 | tf_op jit(solution)/shard_map/all_to_all | solution.py:198
  26.8 0.1 shard_map.95
  26.9 0.1 collective-permute-start
  26.9 0.0 collective-permute-done.4.refs_9_
  27.0 1.6 %collective-permute-start.6 = (bf16[144,1024]{1,0:T(8,128)(2,1)S(1)}, bf16[144,1024]{1,0:T(8,128)(2,1)S(1)}, u32[]{:S(2)}, u32[]{:S(2)}) collective-permute-start(bf16[144,1024]{1,0:T(8,128)(2,1)S(1)} %slice.8), channel_id=1, source_target_pairs={{0,2},{1,3},{2,0},{3,1},{4,6},{5,7},{6,4},{7,5},{8,10},{9,11},{10,... | collective-permute-start | bytes 884744 | tf_op jit(solution)/shard_map/ppermute | solution.py:20
  28.6 0.0 collective-permute-done.5.refs_10_
  28.6 1.6 %collective-permute-start.7 = (bf16[144,1024]{1,0:T(8,128)(2,1)S(1)}, bf16[144,1024]{1,0:T(8,128)(2,1)S(1)}, u32[]{:S(2)}, u32[]{:S(2)}) collective-permute-start(bf16[144,1024]{1,0:T(8,128)(2,1)S(1)} %slice.9), channel_id=1, source_target_pairs={{0,1},{1,0},{2,3},{3,2},{4,5},{5,4},{6,7},{7,6},{8,9},{9,8},{10,11... | collective-permute-start | bytes 884744 | tf_op jit(solution)/shard_map/ppermute | solution.py:20
  30.2 0.0 collective-permute-start.1
  30.2 0.5 collective-permute-start.2
  30.7 0.0 collective-permute-done.refs_4_
  30.7 0.0 collective-permute-start.3
  30.7 0.9 %collective-permute-done.1.refs_5_ = bf16[80,1024]{1,0:T(8,128)(2,1)S(1)} collective-permute-done((bf16[80,1024]{1,0:T(8,128)(2,1)S(1)}, bf16[80,1024]{1,0:T(8,128)(2,1)S(1)}, u32[]{:S(2)}, u32[]{:S(2)}) %collective-permute-start.1) | collective-permute-done | bytes 163872 | tf_op jit(solution)/shard_map/ppermute | solution.py:20
  31.6 0.2 collective-permute-done.2.refs_6_
  31.8 0.3 collective-permute-done.3.refs_7_
  32.1 1.9 %shard_map.96 = (f32[160,2176]{1,0:T(8,128)S(1)}, f32[48,2048]{1,0:T(8,128)S(1)}, bf16[48,2048]{1,0:T(8,128)(2,1)S(1)}, bf16[48,2048]{1,0:T(8,128)(2,1)S(1)}) custom-call(bf16[80,1024]{1,0:T(8,128)(2,1)S(1)} %get-tuple-element.27.refs_0_, bf16[80,1024]{1,0:T(8,128)(2,1)S(1)} %get-tuple-element.28.refs_1_, bf16[80,1024]{1,0:T(8,128)(2,1)S(1)} %get-tuple-element.29.refs_2_, ...), custom_call_target="tpu_custom_call" | custom-call | flops 660602880 | bytes 5259264 | tf_op jit(solution)/shard_map/pallas_call | solution.py:26
  34.0 2.5 %collective-permute-done.6.refs_9_ = bf16[144,1024]{1,0:T(8,128)(2,1)S(1)} collective-permute-done((bf16[144,1024]{1,0:T(8,128)(2,1)S(1)}, bf16[144,1024]{1,0:T(8,128)(2,1)S(1)}, u32[]{:S(2)}, u32[]{:S(2)}) %collective-permute-start.6) | collective-permute-done | bytes 294944 | tf_op jit(solution)/shard_map/ppermute | solution.py:20
  36.4 1.3 %collective-permute-done.7.refs_10_ = bf16[144,1024]{1,0:T(8,128)(2,1)S(1)} collective-permute-done((bf16[144,1024]{1,0:T(8,128)(2,1)S(1)}, bf16[144,1024]{1,0:T(8,128)(2,1)S(1)}, u32[]{:S(2)}, u32[]{:S(2)}) %collective-permute-start.7) | collective-permute-done | bytes 294944 | tf_op jit(solution)/shard_map/ppermute | solution.py:20
  37.8 1.0 %shard_map.97 = (f32[80,2176]{1,0:T(8,128)S(1)}, bf16[80,2176]{1,0:T(8,128)(2,1)S(1)}, bf16[48,2048]{1,0:T(8,128)(2,1)S(1)}) custom-call(bf16[80,1024]{1,0:T(8,128)(2,1)S(1)} %get-tuple-element.27.refs_0_, bf16[80,1024]{1,0:T(8,128)(2,1)S(1)} %get-tuple-element.28.refs_1_, bf16[80,1024]{1,0:T(8,128)(2,1)S(1)} %get-tuple-element.29.refs_2_, ...), custom_call_target="tpu_custom_call" | custom-call | flops 220200960 | bytes 4534272 | tf_op jit(solution)/shard_map/pallas_call | solution.py:26
  38.8 0.1 collective-permute-start.8
  38.9 1.6 %collective-permute-done.8.got = bf16[80,2176]{1,0:T(8,128)(2,1)S(1)} collective-permute-done((bf16[80,2176]{1,0:T(8,128)(2,1)S(1)}, bf16[80,2176]{1,0:T(8,128)(2,1)S(1)}, u32[]{:S(2)}, u32[]{:S(2)}) %collective-permute-start.8) | collective-permute-done | bytes 348192 | tf_op jit(solution)/shard_map/ppermute | solution.py:20
  40.5 0.1 shard_map.98
  40.6 0.8 %reshape.45 = bf16[4,20,2176]{2,1,0:T(8,128)(2,1)} reshape(bf16[80,2176]{1,0:T(8,128)(2,1)S(1)} %shard_map.98) | data formatting | bytes 696320 | tf_op jit(solution)/shard_map/reshape | solution.py:219
  41.4 0.0 copy-start
  41.4 3.6 %all-to-all-start.1 = ((bf16[4,20,2176]{2,1,0:T(8,128)(2,1)}), bf16[4,20,2176]{2,1,0:T(8,128)(2,1)S(1)}, u32[]{:S(2)}, u32[]{:S(2)}) async-start(bf16[4,20,2176]{2,1,0:T(8,128)(2,1)} %reshape.45), calls=%async_computation.1 | async-start | bytes 835584 | tf_op jit(solution)/shard_map/all_to_all | solution.py:219
  45.0 0.6 collective-permute-start.10
  45.6 2.4 %collective-permute-start.11 = (bf16[48,2048]{1,0:T(8,128)(2,1)S(1)}, bf16[48,2048]{1,0:T(8,128)(2,1)S(1)}, u32[]{:S(2)}, u32[]{:S(2)}) collective-permute-start(bf16[48,2048]{1,0:T(8,128)(2,1)S(1)} %get-tuple-element.45), channel_id=1, source_target_pairs={{0,3},{1,2},{2,1},{3,0},{4,7},{5,6},{6,5},{7,4},{8,11},{9,10},{10,... | collective-permute-start | bytes 589832 | tf_op jit(solution)/shard_map/ppermute | solution.py:20
  48.1 0.5 collective-permute-start.9
  48.6 9.2 %all-to-all-done.1 = bf16[4,20,2176]{2,1,0:T(8,128)(2,1)S(1)} async-done(((bf16[4,20,2176]{2,1,0:T(8,128)(2,1)}), bf16[4,20,2176]{2,1,0:T(8,128)(2,1)S(1)}, u32[]{:S(2)}, u32[]{:S(2)}) %all-to-all-start.1) | async-done | bytes 348192 | tf_op jit(solution)/shard_map/all_to_all | solution.py:219
  57.8 0.1 reshape.46.back
  57.9 0.0 collective-permute-done.10
  57.9 0.0 collective-permute-done.11
  57.9 0.0 collective-permute-done.9
  57.9 0.1 add_convert_fusion
  58.0 0.1 collective-permute-start.12
  58.1 0.0 copy-done
  58.1 0.9 %shard_map.99 = (bf16[32,2048]{1,0:T(8,128)(2,1)}, bf16[2,32]{1,0:T(2,128)(2,1)}) custom-call(bf16[80,2176]{1,0:T(8,128)(2,1)S(1)} %reshape.46.back, s32[2,32]{1,0:T(2,128)S(1)} %get-tuple-element.39.slot, bf16[2,32]{1,0:T(2,128)(2,1)S(1)} %bitcast.9), custom_call_target="tpu_custom_call" | custom-call | bytes 479744 | tf_op jit(solution)/shard_map/pallas_call | solution.py:26
  59.0 0.5 collective-permute-done.12
  59.5 0.9 %maximum_convert_fusion = f32[1,96,2048]{2,1,0:T(8,128)} fusion(bf16[1,48,2048]{2,1,0:T(8,128)(2,1)S(1)} %get-tuple-element.50, bf16[1,48,2048]{2,1,0:T(8,128)(2,1)S(1)} %get-tuple-element.49), kind=kLoop, calls=%fused_computation | loop fusion | flops 786432 | bytes 1179648 | tf_op jit(solution)/shard_map/convert_element_type | solution.py:233
  (3 shorter events, 0.1 us)
Async XLA Ops:
  3.1 23.6 %all-to-all-start = ((bf16[4,40,2048]{2,1,0:T(8,128)(2,1)}), bf16[4,40,2048]{2,1,0:T(8,128)(2,1)S(1)}, u32[]{:S(2)}, u32[]{:S(2)}) async-start(bf16[4,40,2048]{2,1,0:T(8,128)(2,1)} %bitcast.2), calls=%async_computation | async-start | bytes 1310720 | tf_op jit(solution)/shard_map/all_to_all | solution.py:198
  9.5 17.5 %collective-permute-start.4 = (bf16[144,2048]{1,0:T(8,128)(2,1)S(1)}, bf16[144,2048]{1,0:T(8,128)(2,1)S(1)}, u32[]{:S(2)}, u32[]{:S(2)}) collective-permute-start(bf16[144,2048]{1,0:T(8,128)(2,1)S(1)} %get-tuple-element.31.refs_8_), channel_id=1, source_target_pairs={{0,1},{1,0},{2,3},{3,2},{4,5},{5,4},{6,7},{7,6},{8,9},{9,8},{10,11... | collective-permute-start | bytes 1769480 | tf_op jit(solution)/shard_map/ppermute | solution.py:20
  11.0 17.6 %collective-permute-start.5 = (bf16[144,2048]{1,0:T(8,128)(2,1)S(1)}, bf16[144,2048]{1,0:T(8,128)(2,1)S(1)}, u32[]{:S(2)}, u32[]{:S(2)}) collective-permute-start(bf16[144,2048]{1,0:T(8,128)(2,1)S(1)} %get-tuple-element.31.refs_8_), channel_id=1, source_target_pairs={{0,2},{1,3},{2,0},{3,1},{4,6},{5,7},{6,4},{7,5},{8,10},{9,11},{10,... | collective-permute-start | bytes 1769480 | tf_op jit(solution)/shard_map/ppermute | solution.py:20
  26.9 3.8 %collective-permute-start = (bf16[80,1024]{1,0:T(8,128)(2,1)S(1)}, bf16[80,1024]{1,0:T(8,128)(2,1)S(1)}, u32[]{:S(2)}, u32[]{:S(2)}) collective-permute-start(bf16[80,1024]{1,0:T(8,128)(2,1)S(1)} %get-tuple-element.27.refs_0_), channel_id=1, source_target_pairs={{0,16},{16,0},{1,17},{17,1},{2,18},{18,2},{3,19},{19,3},{4,20},{20... | collective-permute-start | bytes 491528 | tf_op jit(solution)/shard_map/ppermute | solution.py:20
  27.0 9.5 %collective-permute-start.6 = (bf16[144,1024]{1,0:T(8,128)(2,1)S(1)}, bf16[144,1024]{1,0:T(8,128)(2,1)S(1)}, u32[]{:S(2)}, u32[]{:S(2)}) collective-permute-start(bf16[144,1024]{1,0:T(8,128)(2,1)S(1)} %slice.8), channel_id=1, source_target_pairs={{0,2},{1,3},{2,0},{3,1},{4,6},{5,7},{6,4},{7,5},{8,10},{9,11},{10,... | collective-permute-start | bytes 884744 | tf_op jit(solution)/shard_map/ppermute | solution.py:20
  28.6 9.2 %collective-permute-start.7 = (bf16[144,1024]{1,0:T(8,128)(2,1)S(1)}, bf16[144,1024]{1,0:T(8,128)(2,1)S(1)}, u32[]{:S(2)}, u32[]{:S(2)}) collective-permute-start(bf16[144,1024]{1,0:T(8,128)(2,1)S(1)} %slice.9), channel_id=1, source_target_pairs={{0,1},{1,0},{2,3},{3,2},{4,5},{5,4},{6,7},{7,6},{8,9},{9,8},{10,11... | collective-permute-start | bytes 884744 | tf_op jit(solution)/shard_map/ppermute | solution.py:20
  30.2 1.4 %collective-permute-start.1 = (bf16[80,1024]{1,0:T(8,128)(2,1)S(1)}, bf16[80,1024]{1,0:T(8,128)(2,1)S(1)}, u32[]{:S(2)}, u32[]{:S(2)}) collective-permute-start(bf16[80,1024]{1,0:T(8,128)(2,1)S(1)} %get-tuple-element.28.refs_1_), channel_id=1, source_target_pairs={{0,16},{16,0},{1,17},{17,1},{2,18},{18,2},{3,19},{19,3},{4,20},{20... | collective-permute-start | bytes 491528 | tf_op jit(solution)/shard_map/ppermute | solution.py:20
  30.2 1.6 %collective-permute-start.2 = (bf16[80,1024]{1,0:T(8,128)(2,1)S(1)}, bf16[80,1024]{1,0:T(8,128)(2,1)S(1)}, u32[]{:S(2)}, u32[]{:S(2)}) collective-permute-start(bf16[80,1024]{1,0:T(8,128)(2,1)S(1)} %get-tuple-element.29.refs_2_), channel_id=1, source_target_pairs={{0,16},{16,0},{1,17},{17,1},{2,18},{18,2},{3,19},{19,3},{4,20},{20... | collective-permute-start | bytes 491528 | tf_op jit(solution)/shard_map/ppermute | solution.py:20
  30.7 1.4 %collective-permute-start.3 = (bf16[80,1024]{1,0:T(8,128)(2,1)S(1)}, bf16[80,1024]{1,0:T(8,128)(2,1)S(1)}, u32[]{:S(2)}, u32[]{:S(2)}) collective-permute-start(bf16[80,1024]{1,0:T(8,128)(2,1)S(1)} %get-tuple-element.30.refs_3_), channel_id=1, source_target_pairs={{0,16},{16,0},{1,17},{17,1},{2,18},{18,2},{3,19},{19,3},{4,20},{20... | collective-permute-start | bytes 491528 | tf_op jit(solution)/shard_map/ppermute | solution.py:20
  38.8 1.7 %collective-permute-start.8 = (bf16[80,2176]{1,0:T(8,128)(2,1)S(1)}, bf16[80,2176]{1,0:T(8,128)(2,1)S(1)}, u32[]{:S(2)}, u32[]{:S(2)}) collective-permute-start(bf16[80,2176]{1,0:T(8,128)(2,1)S(1)} %get-tuple-element.37), channel_id=1, source_target_pairs={{0,16},{16,0},{1,17},{17,1},{2,18},{18,2},{3,19},{19,3},{4,20},{20... | collective-permute-start | bytes 1044488 | tf_op jit(solution)/shard_map/ppermute | solution.py:20
  41.4 16.7 %copy-start = (bf16[32,2]{0,1:T(2,128)(2,1)S(1)}, bf16[32,2]{0,1:T(2,128)(2,1)}, u32[]{:S(2)}) copy-start(bf16[32,2]{0,1:T(2,128)(2,1)} %param.10) | copy-start | bytes 388
  41.4 16.4 %all-to-all-start.1 = ((bf16[4,20,2176]{2,1,0:T(8,128)(2,1)}), bf16[4,20,2176]{2,1,0:T(8,128)(2,1)S(1)}, u32[]{:S(2)}, u32[]{:S(2)}) async-start(bf16[4,20,2176]{2,1,0:T(8,128)(2,1)} %reshape.45), calls=%async_computation.1 | async-start | bytes 835584 | tf_op jit(solution)/shard_map/all_to_all | solution.py:219
  45.0 12.8 %collective-permute-start.10 = (bf16[48,2048]{1,0:T(8,128)(2,1)S(1)}, bf16[48,2048]{1,0:T(8,128)(2,1)S(1)}, u32[]{:S(2)}, u32[]{:S(2)}) collective-permute-start(bf16[48,2048]{1,0:T(8,128)(2,1)S(1)} %get-tuple-element.44), channel_id=1, source_target_pairs={{0,2},{1,3},{2,0},{3,1},{4,6},{5,7},{6,4},{7,5},{8,10},{9,11},{10,... | collective-permute-start | bytes 589832 | tf_op jit(solution)/shard_map/ppermute | solution.py:20
  45.6 12.3 %collective-permute-start.11 = (bf16[48,2048]{1,0:T(8,128)(2,1)S(1)}, bf16[48,2048]{1,0:T(8,128)(2,1)S(1)}, u32[]{:S(2)}, u32[]{:S(2)}) collective-permute-start(bf16[48,2048]{1,0:T(8,128)(2,1)S(1)} %get-tuple-element.45), channel_id=1, source_target_pairs={{0,3},{1,2},{2,1},{3,0},{4,7},{5,6},{6,5},{7,4},{8,11},{9,10},{10,... | collective-permute-start | bytes 589832 | tf_op jit(solution)/shard_map/ppermute | solution.py:20
  48.1 9.8 %collective-permute-start.9 = (bf16[48,2048]{1,0:T(8,128)(2,1)S(1)}, bf16[48,2048]{1,0:T(8,128)(2,1)S(1)}, u32[]{:S(2)}, u32[]{:S(2)}) collective-permute-start(bf16[48,2048]{1,0:T(8,128)(2,1)S(1)} %get-tuple-element.43), channel_id=1, source_target_pairs={{0,1},{1,0},{2,3},{3,2},{4,5},{5,4},{6,7},{7,6},{8,9},{9,8},{10,11... | collective-permute-start | bytes 589832 | tf_op jit(solution)/shard_map/ppermute | solution.py:20
  58.0 1.5 %collective-permute-start.12 = (bf16[48,2048]{1,0:T(8,128)(2,1)S(1)}, bf16[48,2048]{1,0:T(8,128)(2,1)S(1)}, u32[]{:S(2)}, u32[]{:S(2)}) collective-permute-start(bf16[48,2048]{1,0:T(8,128)(2,1)S(1)} %add_convert_fusion), channel_id=1, source_target_pairs={{0,16},{16,0},{1,17},{17,1},{2,18},{18,2},{3,19},{19,3},{4,20},{20... | collective-permute-start | bytes 589832 | tf_op jit(solution)/shard_map/ppermute | solution.py:20

commit v5 on v3

--- a/solution.py
+++ b/solution.py
@@ -18,6 +18,12 @@
 
 def swap(value, axis, mask):
     return lax.ppermute(value, axis, [(i, i ^ mask) for i in range(lax.axis_size(axis))])
+
+
+def swap_by_core(value, masks):
+    count = lax.axis_size("dp")
+    pairs = [(r * count + i, r * count + (i ^ mask)) for r, mask in enumerate(masks) for i in range(count)]
+    return lax.ppermute(value, ("rep", "dp"), pairs)
 
 
 def kernel_call(body, inputs, outputs, flops=0, **kwargs):
@@ -40,16 +46,18 @@
 
 def dispatch_kernel(experts, cap, chunk_count, *refs):
     small, (gate, up, down), refs = refs[:4], refs[4:7], refs[7:]
-    chunks, (slot_out, packed), refs = refs[:chunk_count], refs[chunk_count : chunk_count + 2], refs[chunk_count + 2 :]
-    held, sems = refs[:4], refs[4]
-    hidden = packed.shape[0] // 3
+    chunks, (slot_out, *held, sems) = refs[:chunk_count], refs[chunk_count:]
+    packed, held = held[:2], held[2:]
+    hidden = packed[0].shape[0] // 3
     rep = lax.axis_index("rep")
-    half = pl.ds(pl.multiple_of(rep * hidden, hidden), hidden)
     loads = [pltpu.make_async_copy(*pair, sems.at[i]) for i, pair in enumerate(zip(small, held))]
-    packs = [
-        pltpu.make_async_copy(weight.at[0, half], packed.at[pl.ds(i * hidden, hidden)], sems.at[4 + i])
-        for i, weight in enumerate((gate, up, down))
-    ]
+    packs = []
+    for j, half in enumerate((rep, 1 - rep)):
+        rows = pl.ds(pl.multiple_of(half * hidden, hidden), hidden)
+        packs += [
+            pltpu.make_async_copy(weight.at[0, rows], packed[j].at[pl.ds(i * hidden, hidden)], sems.at[4 + 3 * j + i])
+            for i, weight in enumerate((gate, up, down))
+        ]
     for copy in loads + packs:
         copy.start()
     for copy in loads:
@@ -92,15 +100,12 @@
 
 
 def expert_math(x_rows, d_rows, pieces):
-    width = x_rows.shape[1]
-    half = width // 2
-    acts, mixed, gates = [], [], []
+    acts, mixed = [], []
     prob = 0.0
-    for first, second in pieces:
-        hidden = first.shape[0] // 3
-        both, down = pl.ds(0, 2 * hidden), pl.ds(2 * hidden, hidden)
-        pre = dot(x_rows[:, :half], first[both], (1, 1)) + dot(x_rows[:, half:], second[both], (1, 1))
-        d_act = dot(d_rows[:, :half], first[down], (1, 1)) + dot(d_rows[:, half:], second[down], (1, 1))
+    for piece in pieces:
+        hidden = piece.shape[0] // 3
+        pre = dot(x_rows, piece[: 2 * hidden], (1, 1))
+        d_act = dot(d_rows, piece[2 * hidden :], (1, 1))
         gate_pre, up_pre = pre[:, :hidden], pre[:, hidden:]
         sig = jax.nn.sigmoid(gate_pre)
         silu = gate_pre * sig
@@ -108,42 +113,51 @@
         prob = prob + jnp.sum(act * d_act, axis=1, keepdims=True)
         acts.append(act)
         mixed += [d_act * up_pre * sig * (1.0 + gate_pre * (1.0 - sig)), d_act * silu]
-        gates.append((first[both], second[both]))
     mixed = jnp.concatenate(mixed, axis=1).astype(bf16)
     acts = jnp.concatenate(acts, axis=1).astype(bf16)
-    dx = [dot(mixed, jnp.concatenate([g[j] for g in gates]), (1, 0)) for j in range(2)]
-    return dx, prob, dot(acts, d_rows, (0, 0))
-
-
-def early_kernel(chunk_count, piece_count, *refs):
-    chunks, refs = refs[:chunk_count], refs[chunk_count:]
-    pieces, refs = refs[:piece_count], refs[piece_count:]
-    x_out, d_out, dx_out, grad_own, *grads = refs
+    gates = jnp.concatenate([piece[: 2 * hidden] for piece in pieces])
+    return dot(mixed, gates, (1, 0)), prob, dot(acts, d_rows, (0, 0))
+
+
+def early_kernel(chunk_count, *refs):
+    chunks, (own, near, x_out, d_out, dx_out, grad_own, grad_near) = refs[:chunk_count], refs[chunk_count:]
     rows = chunks[0].shape[0] // 2
     values = [c[...].astype(f32) for c in chunks]
     x_out[...] = jnp.concatenate([v[:rows] for v in values]).astype(bf16)
     d_out[...] = jnp.concatenate([v[rows:] for v in values]).astype(bf16)
-    width = x_out.shape[1]
-    pairs = [[p.at[:, pl.ds(j, width // 2)] for j in (0, width // 2)] for p in pieces]
-    dx, prob, grad = expert_math(x_out[...], d_out[...], pairs)
-    dx_out[:, : width // 2] = dx[0]
-    dx_out[:, width // 2 : width] = dx[1]
+    dx, prob, grad = expert_math(x_out[...], d_out[...], [own, near])
+    width, hidden = dx.shape[1], grad_own.shape[0]
+    dx_out[:, :width] = dx
     dx_out[:, width:] = jnp.broadcast_to(prob, (prob.shape[0], LANES))
-    hidden = grad_own.shape[0]
     grad_own[...] = grad[:hidden]
-    for i, out in enumerate(grads):
-        out[...] = grad[hidden * (i + 1) : hidden * (i + 2)].astype(bf16)
-
-
-def late_kernel(x_ref, d_ref, dx_ref, first, second, keep, give, grad_out):
-    dx, prob, grad = expert_math(x_ref[...], d_ref[...], [(first, second)])
-    half, slots = dx[0].shape[1], keep.shape[0]
-    for j, value in enumerate((dx[0], dx[1], jnp.broadcast_to(prob, (prob.shape[0], LANES)))):
-        columns = slice(j * half, j * half + value.shape[1])
-        total = value + dx_ref[:, columns]
-        keep[:, columns] = total[:slots]
-        give[:, columns] = total[slots:].astype(bf16)
-    grad_out[...] = grad.astype(bf16)
+    grad_near[...] = grad[hidden:].astype(bf16)
+
+
+def late_kernel(x_ref, d_ref, dx_ref, grad_ref, near, far, keep, give, grad_near, grad_far):
+    dx, prob, grad = expert_math(x_ref[...], d_ref[...], [near, far])
+    width, slots, hidden = dx.shape[1], keep.shape[0], grad_far.shape[0]
+    for side, value in ((slice(0, width), dx), (slice(width, None), jnp.broadcast_to(prob, (prob.shape[0], LANES)))):
+        total = value + dx_ref[:, side]
+        keep[:, side] = total[:slots]
+        give[:, side] = total[slots:].astype(bf16)
+    grad_near[:hidden] = grad_ref[...]
+    grad_near[hidden:] = grad[:hidden].astype(bf16)
+    grad_far[...] = grad[hidden:].astype(bf16)
+
+
+def grad_kernel(own, near, far, out):
+    hidden = own.shape[0]
+    out[:hidden] = (own[...] + near[:hidden].astype(f32) + far[...].astype(f32)).astype(bf16)
+    out[hidden:] = near[hidden:]
+
+
+def total_kernel(mine, theirs, out):
+    hidden = mine.shape[0] // 2
+    rep = lax.axis_index("rep")
+    for i, half in enumerate((rep, 1 - rep)):
+        here, there = slice(i * hidden, (i + 1) * hidden), slice((1 - i) * hidden, (2 - i) * hidden)
+        rows = pl.ds(pl.multiple_of(half * hidden, hidden), hidden)
+        out[0, rows] = mine[here].astype(f32) + theirs[there].astype(f32)
 
 
 def add_kernel(keep, got, *chunks):
@@ -175,7 +189,7 @@
 def local(tokens, upstream, expert_ids, route_weight, gate_weight, up_weight, down_weight):
     tok_dev, width = tokens.shape
     top = expert_ids.shape[1]
-    experts, shards, reps = lax.axis_size("ep"), lax.axis_size("dp"), lax.axis_size("rep")
+    experts, reps = lax.axis_size("ep"), lax.axis_size("rep")
     cap = 2 * ((5 * tok_dev * top + 8 * experts - 1) // (8 * experts))
     slots = experts * cap
     chunk_count = experts if experts <= 8 else 1
@@ -185,23 +199,19 @@
     in_hbm = pl.BlockSpec(memory_space=pltpu.HBM)
 
     small = [tokens, upstream, expert_ids.T, route_weight.T]
-    *chunks, slot, packed = kernel_call(
+    *chunks, slot, first, second = kernel_call(
         functools.partial(dispatch_kernel, experts, cap, chunk_count),
         [pltpu.with_memory_space_constraint(a, pltpu.HBM) for a in small + [gate_weight, up_weight, down_weight]],
         [shape((2 * rows, width), bf16)] * chunk_count
-        + [shape((top, tok_dev), jnp.int32), shape((3 * hidden, width), bf16)],
+        + [shape((top, tok_dev), jnp.int32)]
+        + [shape((3 * hidden, width), bf16)] * 2,
         in_specs=[in_hbm] * 7,
-        scratch_shapes=[pltpu.VMEM(a.shape, a.dtype) for a in small] + [pltpu.SemaphoreType.DMA((7,))],
-    )
-
-    half = width // 2
-    if shards == 4:
-        near = [packed] + [swap(packed, "dp", m) for m in (1, 2)]
-        last = [swap(near[1][:, :half], "dp", 2), swap(near[2][:, half:], "dp", 1)]
-    else:
-        near = [packed] + [swap(packed, "dp", m) for m in range(1, shards - 1)]
-        last = swap(packed, "dp", shards - 1)
-        last = [last[:, :half], last[:, half:]]
+        scratch_shapes=[pltpu.VMEM(a.shape, a.dtype) for a in small] + [pltpu.SemaphoreType.DMA((10,))],
+    )
+
+    along, across = (1, 2), (2, 1)
+    near = [swap_by_core(first, along), swap_by_core(second, along)]
+    far = swap_by_core(near[0], across)
 
     if chunk_count > 1:
         chunks = [chunks[0]] + [swap(chunks[m], "ep", m) for m in range(1, experts)]
@@ -212,23 +222,20 @@
     chunks = chunks + [swap(c, "rep", 1) for c in chunks]
 
     wide = width + LANES
-    flops = 14 * 2 * slots * width * hidden
-    x_rows, d_rows, dx, grad_own, *grads = kernel_call(
-        functools.partial(early_kernel, 2 * chunk_count, len(near)),
-        chunks + near,
+    x_rows, d_rows, dx, grad_own, grad_near = kernel_call(
+        functools.partial(early_kernel, 2 * chunk_count),
+        chunks + [first, near[0]],
         [shape((2 * slots, width), bf16)] * 2
-        + [shape((2 * slots, wide), f32), shape((hidden, width), f32)]
-        + [shape((hidden, width), bf16)] * (shards - 2),
-        flops=flops * (shards - 1),
-    )
-    keep, give, grad_last = kernel_call(
+        + [shape((2 * slots, wide), f32), shape((hidden, width), f32), shape((hidden, width), bf16)],
+        flops=4 * 10**9,
+    )
+    keep, give, grad_near, grad_far = kernel_call(
         late_kernel,
-        [x_rows, d_rows, dx] + last,
-        [shape((slots, wide), f32), shape((slots, wide), bf16), shape((hidden, width), bf16)],
-        flops=flops,
+        [x_rows, d_rows, dx, grad_near, near[1], far],
+        [shape((slots, wide), f32), shape((slots, wide), bf16)]
+        + [shape((2 * hidden, width), bf16), shape((hidden, width), bf16)],
     )
     back = kernel_call(add_kernel, [keep, swap(give, "rep", 1)], [shape((rows, wide), bf16)] * chunk_count)
-    grad_last, back = lax.optimization_barrier((grad_last, back))
     if chunk_count > 1:
         back = [back[0]] + [swap(back[m], "ep", m) for m in range(1, experts)]
     else:
@@ -241,13 +248,13 @@
         [shape((tok_dev, width), bf16), shape((top, tok_dev), bf16)],
     )
 
-    arrived = [swap(grad, "dp", m + 1) for m, grad in enumerate(grads + [grad_last])]
+    arrived = swap_by_core(grad_near, along), swap_by_core(grad_far, (3, 3))
     arrived, _ = lax.optimization_barrier((arrived, back[1:]))
-    total = (grad_own + sum(a.astype(f32) for a in arrived)).astype(bf16)
-    theirs = swap(total, "rep", 1)
-    lower = lax.axis_index("rep") == 0
-    grad_total = jnp.concatenate([jnp.where(lower, total, theirs), jnp.where(lower, theirs, total)])
-    return (d_tokens, d_probs.T, grad_total.astype(f32)[None])
+    (mine,) = kernel_call(grad_kernel, [grad_own, *arrived], [shape((2 * hidden, width), bf16)])
+    (grad_total,) = kernel_call(
+        total_kernel, [mine, swap(mine, "rep", 1)], [shape((1, 2 * hidden, width), f32)]
+    )
+    return d_tokens, d_probs.T, grad_total
 
 
 def solution(mesh):

time: 49.2 us -> 48.4 us (0.984)
  starting transfers between devices: 23 us -> 17.1 us
  waiting for transfers between devices: 18.5 us -> 23.9 us
  other arithmetic: 1.07 us -> 0 us
  Pallas kernels: 5.75 us -> 6.61 us
    ppermute x19 -> x12, starting transfers between devices: 23 us -> 9.56 us  [swap(): lax.ppermute(value, axis, [(i, i ^ mask) for i in range(lax.axis_size(axi...]
    ppermute x0 -> x5, waiting for transfers between devices: none -> 9.37 us  [swap_by_core(): return lax.ppermute(value, ('rep', 'dp'), pairs)]
    ppermute x0 -> x5, starting transfers between devices: none -> 7.51 us  [swap_by_core(): return lax.ppermute(value, ('rep', 'dp'), pairs)]
    ppermute x19 -> x12, waiting for transfers between devices: 18.5 us -> 14.5 us  [swap(): lax.ppermute(value, axis, [(i, i ^ mask) for i in range(lax.axis_size(axi...]
    convert_element_type x2 -> x0, other arithmetic: 1.04 us -> none  [the longest x1 0.95 us: local(): return (d_tokens, d_probs.T, grad_total.astype(f32)[None])]
    pallas_call x5 -> x7, Pallas kernels: 5.75 us -> 6.61 us  [kernel_call(): pl.pallas_call(body, out_shape=outputs, in_specs=kwargs.pop('in_specs', [...]
  transfers between devices with their start and end apart: 19 -> 17, of which waited for: 10 -> 9; matrix products, arithmetic and copies ran while one was open for 0% -> 0% of each run, Pallas kernels for 6% -> 5%
where the time goes in v5:
time: 48.4 us; the launch traced here: 48.3 us
  waiting for transfers between devices  23.9 us (49%)
  starting transfers between devices  17.1 us (35%)
  Pallas kernels  6.61 us (14%)
  between operations  0.71 us (1%)
    ppermute x12, waiting for transfers between devices, swap(): lax.ppermute(value, axis, [(i, i ^ mask) for i in range(lax.axis_size(axi...  14.5 us
    ppermute x12, starting transfers between devices, swap(): lax.ppermute(value, axis, [(i, i ^ mask) for i in range(lax.axis_size(axi...  9.56 us
    ppermute x5, waiting for transfers between devices, swap_by_core(): return lax.ppermute(value, ('rep', 'dp'), pairs)  9.37 us
    ppermute x5, starting transfers between devices, swap_by_core(): return lax.ppermute(value, ('rep', 'dp'), pairs)  7.51 us
    pallas_call x7, Pallas kernels, kernel_call(): pl.pallas_call(body, out_shape=outputs, in_specs=kwargs.pop('in_specs', [...  6.61 us
  transfers between devices with their start and end apart: 17, of which 9 were waited for; matrix products, arithmetic and copies ran while one was open for 0% of the time, Pallas kernels for 5%

profile of v5, /device:TPU:0, one launch (start us, length us, event | category | flops | bytes accessed | tf_op | source)
XLA Modules:
  0.0 48.3 jit_solution(18417962372284906908)
XLA Ops:
  0.6 1.7 %shard_map.94 = (bf16[40,2048]{1,0:T(8,128)(2,1)S(1)}, bf16[40,2048]{1,0:T(8,128)(2,1)S(1)}, bf16[40,2048]{1,0:T(8,128)(2,1)S(1)}, bf16[40,2048]{1,0:T(8,128)(2,...) custom-call(bf16[32,2048]{1,0:T(8,128)(2,1)} %refs_0_.1, ...), custom_call_target="tpu_custom_call" | custom-call | bytes 3277440 | tf_op jit(solution)/shard_map/pallas_call | solution.py:32
  2.3 3.0 %collective-permute-start.7 = (bf16[144,2048]{1,0:T(8,128)(2,1)S(1)}, bf16[144,2048]{1,0:T(8,128)(2,1)S(1)}, u32[]{:S(2)}, u32[]{:S(2)}) collective-permute-start(bf16[144,2048]{1,0:T(8,128)(2,1)S(1)} %get-tuple-element.31.refs_8_), channel_id=1, source_target_pairs={{0,1},{1,0},{2,3},{3,2},{16,18},{17,19},{18,16},{19,17},{4,5},{5,4... | collective-permute-start | bytes 1769480 | tf_op jit(solution)/shard_map/ppermute | solution.py:26
  5.3 1.6 %collective-permute-start = (bf16[40,2048]{1,0:T(8,128)(2,1)S(1)}, bf16[40,2048]{1,0:T(8,128)(2,1)S(1)}, u32[]{:S(2)}, u32[]{:S(2)}) collective-permute-start(bf16[40,2048]{1,0:T(8,128)(2,1)S(1)} %get-tuple-element.28), channel_id=1, source_target_pairs={{0,4},{4,0},{8,12},{12,8},{1,5},{5,1},{9,13},{13,9},{2,6},{6,2},{1... | collective-permute-start | bytes 491528 | tf_op jit(solution)/shard_map/ppermute | solution.py:20
  6.9 2.6 %collective-permute-start.1 = (bf16[40,2048]{1,0:T(8,128)(2,1)S(1)}, bf16[40,2048]{1,0:T(8,128)(2,1)S(1)}, u32[]{:S(2)}, u32[]{:S(2)}) collective-permute-start(bf16[40,2048]{1,0:T(8,128)(2,1)S(1)} %get-tuple-element.29), channel_id=1, source_target_pairs={{0,8},{4,12},{8,0},{12,4},{1,9},{5,13},{9,1},{13,5},{2,10},{6,14},... | collective-permute-start | bytes 491528 | tf_op jit(solution)/shard_map/ppermute | solution.py:20
  9.5 0.2 collective-permute-start.2
  9.7 0.0 collective-permute-start.3
  9.7 3.6 %collective-permute-done.refs_1_ = bf16[40,2048]{1,0:T(8,128)(2,1)S(1)} collective-permute-done((bf16[40,2048]{1,0:T(8,128)(2,1)S(1)}, bf16[40,2048]{1,0:T(8,128)(2,1)S(1)}, u32[]{:S(2)}, u32[]{:S(2)}) %collective-permute-start) | collective-permute-done | bytes 163872 | tf_op jit(solution)/shard_map/ppermute | solution.py:20
  13.3 2.3 %collective-permute-start.8 = (bf16[144,2048]{1,0:T(8,128)(2,1)S(1)}, bf16[144,2048]{1,0:T(8,128)(2,1)S(1)}, u32[]{:S(2)}, u32[]{:S(2)}) collective-permute-start(bf16[144,2048]{1,0:T(8,128)(2,1)S(1)} %get-tuple-element.36), channel_id=1, source_target_pairs={{0,1},{1,0},{2,3},{3,2},{16,18},{17,19},{18,16},{19,17},{4,5},{5,4... | collective-permute-start | bytes 1769480 | tf_op jit(solution)/shard_map/ppermute | solution.py:26
  15.6 0.0 collective-permute-done.7.refs_9_
  15.6 0.0 collective-permute-start.9
  15.6 6.4 %collective-permute-done.1.refs_2_ = bf16[40,2048]{1,0:T(8,128)(2,1)S(1)} collective-permute-done((bf16[40,2048]{1,0:T(8,128)(2,1)S(1)}, bf16[40,2048]{1,0:T(8,128)(2,1)S(1)}, u32[]{:S(2)}, u32[]{:S(2)}) %collective-permute-start.1) | collective-permute-done | bytes 163872 | tf_op jit(solution)/shard_map/ppermute | solution.py:20
  22.0 0.0 collective-permute-start.4
  22.0 0.0 collective-permute-done.2.refs_3_
  22.0 0.5 %collective-permute-start.5 = (bf16[40,2048]{1,0:T(8,128)(2,1)S(1)}, bf16[40,2048]{1,0:T(8,128)(2,1)S(1)}, u32[]{:S(2)}, u32[]{:S(2)}) collective-permute-start(bf16[40,2048]{1,0:T(8,128)(2,1)S(1)} %collective-permute-done.1.refs_2_), channel_id=1, source_target_pairs={{0,16},{16,0},{1,17},{17,1},{2,18},{18,2},{3,19},{19,3},{4,20},{20... | collective-permute-start | bytes 491528 | tf_op jit(solution)/shard_map/ppermute | solution.py:20
  22.5 0.0 collective-permute-done.3.refs_4_
  22.5 0.1 collective-permute-start.6
  22.6 0.8 %collective-permute-done.4.refs_5_ = bf16[40,2048]{1,0:T(8,128)(2,1)S(1)} collective-permute-done((bf16[40,2048]{1,0:T(8,128)(2,1)S(1)}, bf16[40,2048]{1,0:T(8,128)(2,1)S(1)}, u32[]{:S(2)}, u32[]{:S(2)}) %collective-permute-start.4) | collective-permute-done | bytes 163872 | tf_op jit(solution)/shard_map/ppermute | solution.py:20
  23.4 0.2 collective-permute-done.5.refs_6_
  23.6 0.3 collective-permute-done.6.refs_7_
  23.9 1.4 %shard_map.95 = (bf16[160,2048]{1,0:T(8,128)(2,1)S(1)}, bf16[160,2048]{1,0:T(8,128)(2,1)S(1)}, f32[160,2176]{1,0:T(8,128)S(1)}, f32[48,2048]{1,0:T(8,128)S(1)}, bf16[48,2048]{1,0:T(8,128)(2,1)S(1)}) custom-call(bf16[40,2048]{1,0:T(8,128)(2,1)S(1)} %get-tuple-element.27.refs_0_, bf16[40,2048]{1,0:T(8,128)(2,1)S(1)} %collective-permute-done.refs_1_, ...), custom_call_target="tpu_custom_call" | custom-call | flops 4000000000 | bytes 5783552 | tf_op jit(solution)/shard_map/pallas_call | solution.py:32
  25.3 4.0 %collective-permute-done.8.near = bf16[144,2048]{1,0:T(8,128)(2,1)S(1)} collective-permute-done((bf16[144,2048]{1,0:T(8,128)(2,1)S(1)}, bf16[144,2048]{1,0:T(8,128)(2,1)S(1)}, u32[]{:S(2)}, u32[]{:S(2)}) %collective-permute-start.8) | collective-permute-done | bytes 589856 | tf_op jit(solution)/shard_map/ppermute | solution.py:26
  29.2 0.0 collective-permute-done.9.far
  29.2 1.4 %shard_map.96 = (f32[80,2176]{1,0:T(8,128)S(1)}, bf16[80,2176]{1,0:T(8,128)(2,1)S(1)}, bf16[96,2048]{1,0:T(8,128)(2,1)S(1)}, bf16[48,2048]{1,0:T(8,128)(2,1)S(1)}) custom-call(bf16[160,2048]{1,0:T(8,128)(2,1)S(1)} %get-tuple-element.32.x_ref, bf16[160,2048]{1,0:T(8,128)(2,1)S(1)} %get-tuple-element.33.d_ref, f32[160,2176]{1,0:T(8,128)S(1)} %get-tuple-element.34.dx_ref, ...), custom_call_target="tpu_custom_call" | custom-call | bytes 5713920 | tf_op jit(solution)/shard_map/pallas_call | solution.py:32
  30.7 0.0 copy-start
  30.7 0.1 collective-permute-start.10
  30.8 1.8 %collective-permute-start.14 = (bf16[96,2048]{1,0:T(8,128)(2,1)S(1)}, bf16[96,2048]{1,0:T(8,128)(2,1)S(1)}, u32[]{:S(2)}, u32[]{:S(2)}) collective-permute-start(bf16[96,2048]{1,0:T(8,128)(2,1)S(1)} %get-tuple-element.47), channel_id=1, source_target_pairs={{0,1},{1,0},{2,3},{3,2},{16,18},{17,19},{18,16},{19,17},{4,5},{5,4... | collective-permute-start | bytes 1179656 | tf_op jit(solution)/shard_map/ppermute | solution.py:26
  32.6 0.4 collective-permute-start.15
  32.9 0.0 collective-permute-done.10.got
  32.9 0.1 shard_map.97
  33.1 1.2 %collective-permute-start.11 = (bf16[20,2176]{1,0:T(8,128)(2,1)S(1)}, bf16[20,2176]{1,0:T(8,128)(2,1)S(1)}, u32[]{:S(2)}, u32[]{:S(2)}) collective-permute-start(bf16[20,2176]{1,0:T(8,128)(2,1)S(1)} %get-tuple-element.40), channel_id=1, source_target_pairs={{0,4},{4,0},{8,12},{12,8},{1,5},{5,1},{9,13},{13,9},{2,6},{6,2},{1... | collective-permute-start | bytes 261128 | tf_op jit(solution)/shard_map/ppermute | solution.py:20
  34.3 2.9 %collective-permute-start.12 = (bf16[20,2176]{1,0:T(8,128)(2,1)S(1)}, bf16[20,2176]{1,0:T(8,128)(2,1)S(1)}, u32[]{:S(2)}, u32[]{:S(2)}) collective-permute-start(bf16[20,2176]{1,0:T(8,128)(2,1)S(1)} %get-tuple-element.41), channel_id=1, source_target_pairs={{0,8},{4,12},{8,0},{12,4},{1,9},{5,13},{9,1},{13,5},{2,10},{6,14},... | collective-permute-start | bytes 261128 | tf_op jit(solution)/shard_map/ppermute | solution.py:20
  37.2 0.3 collective-permute-start.13
  37.5 5.4 %collective-permute-done.15.far = bf16[48,2048]{1,0:T(8,128)(2,1)S(1)} collective-permute-done((bf16[48,2048]{1,0:T(8,128)(2,1)S(1)}, bf16[48,2048]{1,0:T(8,128)(2,1)S(1)}, u32[]{:S(2)}, u32[]{:S(2)}) %collective-permute-start.15) | collective-permute-done | bytes 196640 | tf_op jit(solution)/shard_map/ppermute | solution.py:26
  42.9 0.0 collective-permute-done.14.near
  42.9 0.0 collective-permute-done.11.refs_1_
  42.9 2.5 %collective-permute-done.12.refs_2_ = bf16[20,2176]{1,0:T(8,128)(2,1)S(1)} collective-permute-done((bf16[20,2176]{1,0:T(8,128)(2,1)S(1)}, bf16[20,2176]{1,0:T(8,128)(2,1)S(1)}, u32[]{:S(2)}, u32[]{:S(2)}) %collective-permute-start.12) | collective-permute-done | bytes 87072 | tf_op jit(solution)/shard_map/ppermute | solution.py:20
  45.4 0.0 collective-permute-done.13.refs_3_
  45.4 0.1 shard_map.99.mine
  45.5 0.1 collective-permute-start.16
  45.6 0.0 copy-done
  45.6 1.0 %shard_map.98 = (bf16[32,2048]{1,0:T(8,128)(2,1)}, bf16[2,32]{1,0:T(2,128)(2,1)}) custom-call(bf16[20,2176]{1,0:T(8,128)(2,1)S(1)} %get-tuple-element.39.refs_0_, bf16[20,2176]{1,0:T(8,128)(2,1)S(1)} %collective-permute-done.11.refs_1_, bf16[20,2176]{1,0:T(8,128)(2,1)S(1)} %collective-permute-done.12.refs_2_, ...), custom_call_target="tpu_custom_call" | custom-call | bytes 479744 | tf_op jit(solution)/shard_map/pallas_call | solution.py:32
  46.6 0.7 %collective-permute-done.16.theirs = bf16[96,2048]{1,0:T(8,128)(2,1)S(1)} collective-permute-done((bf16[96,2048]{1,0:T(8,128)(2,1)S(1)}, bf16[96,2048]{1,0:T(8,128)(2,1)S(1)}, u32[]{:S(2)}, u32[]{:S(2)}) %collective-permute-start.16) | collective-permute-done | bytes 393248 | tf_op jit(solution)/shard_map/ppermute | solution.py:20
  47.3 1.0 %shard_map.100 = f32[1,96,2048]{2,1,0:T(8,128)} custom-call(bf16[96,2048]{1,0:T(8,128)(2,1)S(1)} %shard_map.99.mine, bf16[96,2048]{1,0:T(8,128)(2,1)S(1)} %collective-permute-done.16.theirs), custom_call_target="tpu_custom_call" | custom-call | bytes 1572864 | tf_op jit(solution)/shard_map/pallas_call | solution.py:32
Async XLA Ops:
  2.3 13.3 %collective-permute-start.7 = (bf16[144,2048]{1,0:T(8,128)(2,1)S(1)}, bf16[144,2048]{1,0:T(8,128)(2,1)S(1)}, u32[]{:S(2)}, u32[]{:S(2)}) collective-permute-start(bf16[144,2048]{1,0:T(8,128)(2,1)S(1)} %get-tuple-element.31.refs_8_), channel_id=1, source_target_pairs={{0,1},{1,0},{2,3},{3,2},{16,18},{17,19},{18,16},{19,17},{4,5},{5,4... | collective-permute-start | bytes 1769480 | tf_op jit(solution)/shard_map/ppermute | solution.py:26
  5.3 7.9 %collective-permute-start = (bf16[40,2048]{1,0:T(8,128)(2,1)S(1)}, bf16[40,2048]{1,0:T(8,128)(2,1)S(1)}, u32[]{:S(2)}, u32[]{:S(2)}) collective-permute-start(bf16[40,2048]{1,0:T(8,128)(2,1)S(1)} %get-tuple-element.28), channel_id=1, source_target_pairs={{0,4},{4,0},{8,12},{12,8},{1,5},{5,1},{9,13},{13,9},{2,6},{6,2},{1... | collective-permute-start | bytes 491528 | tf_op jit(solution)/shard_map/ppermute | solution.py:20
  6.9 15.1 %collective-permute-start.1 = (bf16[40,2048]{1,0:T(8,128)(2,1)S(1)}, bf16[40,2048]{1,0:T(8,128)(2,1)S(1)}, u32[]{:S(2)}, u32[]{:S(2)}) collective-permute-start(bf16[40,2048]{1,0:T(8,128)(2,1)S(1)} %get-tuple-element.29), channel_id=1, source_target_pairs={{0,8},{4,12},{8,0},{12,4},{1,9},{5,13},{9,1},{13,5},{2,10},{6,14},... | collective-permute-start | bytes 491528 | tf_op jit(solution)/shard_map/ppermute | solution.py:20
  9.5 12.5 %collective-permute-start.2 = (bf16[40,2048]{1,0:T(8,128)(2,1)S(1)}, bf16[40,2048]{1,0:T(8,128)(2,1)S(1)}, u32[]{:S(2)}, u32[]{:S(2)}) collective-permute-start(bf16[40,2048]{1,0:T(8,128)(2,1)S(1)} %get-tuple-element.30), channel_id=1, source_target_pairs={{0,12},{4,8},{8,4},{12,0},{1,13},{5,9},{9,5},{13,1},{2,14},{6,10},... | collective-permute-start | bytes 491528 | tf_op jit(solution)/shard_map/ppermute | solution.py:20
  9.7 12.8 %collective-permute-start.3 = (bf16[40,2048]{1,0:T(8,128)(2,1)S(1)}, bf16[40,2048]{1,0:T(8,128)(2,1)S(1)}, u32[]{:S(2)}, u32[]{:S(2)}) collective-permute-start(bf16[40,2048]{1,0:T(8,128)(2,1)S(1)} %get-tuple-element.27.refs_0_), channel_id=1, source_target_pairs={{0,16},{16,0},{1,17},{17,1},{2,18},{18,2},{3,19},{19,3},{4,20},{20... | collective-permute-start | bytes 491528 | tf_op jit(solution)/shard_map/ppermute | solution.py:20
  13.3 15.9 %collective-permute-start.8 = (bf16[144,2048]{1,0:T(8,128)(2,1)S(1)}, bf16[144,2048]{1,0:T(8,128)(2,1)S(1)}, u32[]{:S(2)}, u32[]{:S(2)}) collective-permute-start(bf16[144,2048]{1,0:T(8,128)(2,1)S(1)} %get-tuple-element.36), channel_id=1, source_target_pairs={{0,1},{1,0},{2,3},{3,2},{16,18},{17,19},{18,16},{19,17},{4,5},{5,4... | collective-permute-start | bytes 1769480 | tf_op jit(solution)/shard_map/ppermute | solution.py:26
  15.6 13.6 %collective-permute-start.9 = (bf16[144,2048]{1,0:T(8,128)(2,1)S(1)}, bf16[144,2048]{1,0:T(8,128)(2,1)S(1)}, u32[]{:S(2)}, u32[]{:S(2)}) collective-permute-start(bf16[144,2048]{1,0:T(8,128)(2,1)S(1)} %collective-permute-done.7.refs_9_), channel_id=1, source_target_pairs={{0,2},{1,3},{2,0},{3,1},{16,17},{17,16},{18,19},{19,18},{4,6},{5,7... | collective-permute-start | bytes 1769480 | tf_op jit(solution)/shard_map/ppermute | solution.py:26
  22.0 1.4 %collective-permute-start.4 = (bf16[40,2048]{1,0:T(8,128)(2,1)S(1)}, bf16[40,2048]{1,0:T(8,128)(2,1)S(1)}, u32[]{:S(2)}, u32[]{:S(2)}) collective-permute-start(bf16[40,2048]{1,0:T(8,128)(2,1)S(1)} %collective-permute-done.refs_1_), channel_id=1, source_target_pairs={{0,16},{16,0},{1,17},{17,1},{2,18},{18,2},{3,19},{19,3},{4,20},{20... | collective-permute-start | bytes 491528 | tf_op jit(solution)/shard_map/ppermute | solution.py:20
  22.0 1.6 %collective-permute-start.5 = (bf16[40,2048]{1,0:T(8,128)(2,1)S(1)}, bf16[40,2048]{1,0:T(8,128)(2,1)S(1)}, u32[]{:S(2)}, u32[]{:S(2)}) collective-permute-start(bf16[40,2048]{1,0:T(8,128)(2,1)S(1)} %collective-permute-done.1.refs_2_), channel_id=1, source_target_pairs={{0,16},{16,0},{1,17},{17,1},{2,18},{18,2},{3,19},{19,3},{4,20},{20... | collective-permute-start | bytes 491528 | tf_op jit(solution)/shard_map/ppermute | solution.py:20
  22.5 1.4 %collective-permute-start.6 = (bf16[40,2048]{1,0:T(8,128)(2,1)S(1)}, bf16[40,2048]{1,0:T(8,128)(2,1)S(1)}, u32[]{:S(2)}, u32[]{:S(2)}) collective-permute-start(bf16[40,2048]{1,0:T(8,128)(2,1)S(1)} %collective-permute-done.2.refs_3_), channel_id=1, source_target_pairs={{0,16},{16,0},{1,17},{17,1},{2,18},{18,2},{3,19},{19,3},{4,20},{20... | collective-permute-start | bytes 491528 | tf_op jit(solution)/shard_map/ppermute | solution.py:20
  30.7 14.9 %copy-start = (bf16[32,2]{0,1:T(2,128)(2,1)S(1)}, bf16[32,2]{0,1:T(2,128)(2,1)}, u32[]{:S(2)}) copy-start(bf16[32,2]{0,1:T(2,128)(2,1)} %param.10) | copy-start | bytes 388
  30.7 2.3 %collective-permute-start.10 = (bf16[80,2176]{1,0:T(8,128)(2,1)S(1)}, bf16[80,2176]{1,0:T(8,128)(2,1)S(1)}, u32[]{:S(2)}, u32[]{:S(2)}) collective-permute-start(bf16[80,2176]{1,0:T(8,128)(2,1)S(1)} %get-tuple-element.38), channel_id=1, source_target_pairs={{0,16},{16,0},{1,17},{17,1},{2,18},{18,2},{3,19},{19,3},{4,20},{20... | collective-permute-start | bytes 1044488 | tf_op jit(solution)/shard_map/ppermute | solution.py:20
  30.8 12.1 %collective-permute-start.14 = (bf16[96,2048]{1,0:T(8,128)(2,1)S(1)}, bf16[96,2048]{1,0:T(8,128)(2,1)S(1)}, u32[]{:S(2)}, u32[]{:S(2)}) collective-permute-start(bf16[96,2048]{1,0:T(8,128)(2,1)S(1)} %get-tuple-element.47), channel_id=1, source_target_pairs={{0,1},{1,0},{2,3},{3,2},{16,18},{17,19},{18,16},{19,17},{4,5},{5,4... | collective-permute-start | bytes 1179656 | tf_op jit(solution)/shard_map/ppermute | solution.py:26
  32.6 10.3 %collective-permute-start.15 = (bf16[48,2048]{1,0:T(8,128)(2,1)S(1)}, bf16[48,2048]{1,0:T(8,128)(2,1)S(1)}, u32[]{:S(2)}, u32[]{:S(2)}) collective-permute-start(bf16[48,2048]{1,0:T(8,128)(2,1)S(1)} %get-tuple-element.48), channel_id=1, source_target_pairs={{0,3},{1,2},{2,1},{3,0},{16,19},{17,18},{18,17},{19,16},{4,7},{5,6... | collective-permute-start | bytes 589832 | tf_op jit(solution)/shard_map/ppermute | solution.py:26
  33.1 9.9 %collective-permute-start.11 = (bf16[20,2176]{1,0:T(8,128)(2,1)S(1)}, bf16[20,2176]{1,0:T(8,128)(2,1)S(1)}, u32[]{:S(2)}, u32[]{:S(2)}) collective-permute-start(bf16[20,2176]{1,0:T(8,128)(2,1)S(1)} %get-tuple-element.40), channel_id=1, source_target_pairs={{0,4},{4,0},{8,12},{12,8},{1,5},{5,1},{9,13},{13,9},{2,6},{6,2},{1... | collective-permute-start | bytes 261128 | tf_op jit(solution)/shard_map/ppermute | solution.py:20
  34.3 11.2 %collective-permute-start.12 = (bf16[20,2176]{1,0:T(8,128)(2,1)S(1)}, bf16[20,2176]{1,0:T(8,128)(2,1)S(1)}, u32[]{:S(2)}, u32[]{:S(2)}) collective-permute-start(bf16[20,2176]{1,0:T(8,128)(2,1)S(1)} %get-tuple-element.41), channel_id=1, source_target_pairs={{0,8},{4,12},{8,0},{12,4},{1,9},{5,13},{9,1},{13,5},{2,10},{6,14},... | collective-permute-start | bytes 261128 | tf_op jit(solution)/shard_map/ppermute | solution.py:20
  37.2 8.3 %collective-permute-start.13 = (bf16[20,2176]{1,0:T(8,128)(2,1)S(1)}, bf16[20,2176]{1,0:T(8,128)(2,1)S(1)}, u32[]{:S(2)}, u32[]{:S(2)}) collective-permute-start(bf16[20,2176]{1,0:T(8,128)(2,1)S(1)} %get-tuple-element.42), channel_id=1, source_target_pairs={{0,12},{4,8},{8,4},{12,0},{1,13},{5,9},{9,5},{13,1},{2,14},{6,10},... | collective-permute-start | bytes 261128 | tf_op jit(solution)/shard_map/ppermute | solution.py:20
  45.5 1.8 %collective-permute-start.16 = (bf16[96,2048]{1,0:T(8,128)(2,1)S(1)}, bf16[96,2048]{1,0:T(8,128)(2,1)S(1)}, u32[]{:S(2)}, u32[]{:S(2)}) collective-permute-start(bf16[96,2048]{1,0:T(8,128)(2,1)S(1)} %shard_map.99.mine), channel_id=1, source_target_pairs={{0,16},{16,0},{1,17},{17,1},{2,18},{18,2},{3,19},{19,3},{4,20},{20... | collective-permute-start | bytes 1179656 | tf_op jit(solution)/shard_map/ppermute | solution.py:20

commit v6 on v5

--- a/solution.py
+++ b/solution.py
@@ -18,6 +18,11 @@
 
 def swap(value, axis, mask):
     return lax.ppermute(value, axis, [(i, i ^ mask) for i in range(lax.axis_size(axis))])
+
+
+def exchange(chunks):
+    count = len(chunks)
+    return [chunks[0]] + [swap(chunks[c], "ep", count - c) for c in range(1, count)]
 
 
 def swap_by_core(value, masks):
@@ -79,7 +84,8 @@
         rank = jnp.sum(before * named[k], axis=0, keepdims=True).astype(jnp.int32)
         expert = ids[k : k + 1, :]
         if chunk_count > 1:
-            chunk = expert ^ me
+            mask = expert ^ me
+            chunk = jnp.where(mask == 0, 0, experts - mask)
             slot = chunk * cap + rank
             x_row = slot + chunk * cap
         else:
@@ -120,12 +126,12 @@
 
 
 def early_kernel(chunk_count, *refs):
-    chunks, (own, near, x_out, d_out, dx_out, grad_own, grad_near) = refs[:chunk_count], refs[chunk_count:]
+    chunks, (*pieces, x_out, d_out, dx_out, grad_own, grad_near) = refs[:chunk_count], refs[chunk_count:]
     rows = chunks[0].shape[0] // 2
     values = [c[...].astype(f32) for c in chunks]
     x_out[...] = jnp.concatenate([v[:rows] for v in values]).astype(bf16)
     d_out[...] = jnp.concatenate([v[rows:] for v in values]).astype(bf16)
-    dx, prob, grad = expert_math(x_out[...], d_out[...], [own, near])
+    dx, prob, grad = expert_math(x_out[...], d_out[...], pieces)
     width, hidden = dx.shape[1], grad_own.shape[0]
     dx_out[:, :width] = dx
     dx_out[:, width:] = jnp.broadcast_to(prob, (prob.shape[0], LANES))
@@ -133,16 +139,14 @@
     grad_near[...] = grad[hidden:].astype(bf16)
 
 
-def late_kernel(x_ref, d_ref, dx_ref, grad_ref, near, far, keep, give, grad_near, grad_far):
-    dx, prob, grad = expert_math(x_ref[...], d_ref[...], [near, far])
-    width, slots, hidden = dx.shape[1], keep.shape[0], grad_far.shape[0]
+def late_kernel(x_ref, d_ref, dx_ref, far, keep, give, grad_far):
+    dx, prob, grad = expert_math(x_ref[...], d_ref[...], [far])
+    width, slots = dx.shape[1], keep.shape[0]
     for side, value in ((slice(0, width), dx), (slice(width, None), jnp.broadcast_to(prob, (prob.shape[0], LANES)))):
         total = value + dx_ref[:, side]
         keep[:, side] = total[:slots]
         give[:, side] = total[slots:].astype(bf16)
-    grad_near[:hidden] = grad_ref[...]
-    grad_near[hidden:] = grad[:hidden].astype(bf16)
-    grad_far[...] = grad[hidden:].astype(bf16)
+    grad_far[...] = grad.astype(bf16)
 
 
 def grad_kernel(own, near, far, out):
@@ -214,7 +218,7 @@
     far = swap_by_core(near[0], across)
 
     if chunk_count > 1:
-        chunks = [chunks[0]] + [swap(chunks[m], "ep", m) for m in range(1, experts)]
+        chunks = exchange(chunks)
     else:
         moved = chunks[0].reshape(2, experts, cap, width)
         moved = lax.all_to_all(moved, "ep", split_axis=1, concat_axis=1, tiled=True)
@@ -224,20 +228,20 @@
     wide = width + LANES
     x_rows, d_rows, dx, grad_own, grad_near = kernel_call(
         functools.partial(early_kernel, 2 * chunk_count),
-        chunks + [first, near[0]],
+        chunks + [first, *near],
         [shape((2 * slots, width), bf16)] * 2
-        + [shape((2 * slots, wide), f32), shape((hidden, width), f32), shape((hidden, width), bf16)],
-        flops=4 * 10**9,
-    )
-    keep, give, grad_near, grad_far = kernel_call(
+        + [shape((2 * slots, wide), f32), shape((hidden, width), f32), shape((2 * hidden, width), bf16)],
+        flops=4*10**9,
+    )
+    keep, give, grad_far = kernel_call(
         late_kernel,
-        [x_rows, d_rows, dx, grad_near, near[1], far],
-        [shape((slots, wide), f32), shape((slots, wide), bf16)]
-        + [shape((2 * hidden, width), bf16), shape((hidden, width), bf16)],
+        [x_rows, d_rows, dx, far],
+        [shape((slots, wide), f32), shape((slots, wide), bf16), shape((hidden, width), bf16)],
     )
     back = kernel_call(add_kernel, [keep, swap(give, "rep", 1)], [shape((rows, wide), bf16)] * chunk_count)
+    grad_far, back = lax.optimization_barrier((grad_far, back))
     if chunk_count > 1:
-        back = [back[0]] + [swap(back[m], "ep", m) for m in range(1, experts)]
+        back = exchange(back)
     else:
         moved = back[0].reshape(experts, cap, wide)
         moved = lax.all_to_all(moved, "ep", split_axis=0, concat_axis=0, tiled=True)
@@ -246,10 +250,10 @@
         functools.partial(combine_kernel, chunk_count),
         back + [slot, route_weight.T],
         [shape((tok_dev, width), bf16), shape((top, tok_dev), bf16)],
+        flops=8*10**9,
     )
 
     arrived = swap_by_core(grad_near, along), swap_by_core(grad_far, (3, 3))
-    arrived, _ = lax.optimization_barrier((arrived, back[1:]))
     (mine,) = kernel_call(grad_kernel, [grad_own, *arrived], [shape((2 * hidden, width), bf16)])
     (grad_total,) = kernel_call(
         total_kernel, [mine, swap(mine, "rep", 1)], [shape((1, 2 * hidden, width), f32)]

time: 48.4 us -> 47.4 us (0.979)
  waiting for transfers between devices: 23.9 us -> 19 us
  starting transfers between devices: 17.1 us -> 20.8 us
    ppermute x5, waiting for transfers between devices: 9.37 us -> 2.48 us  [swap_by_core(): return lax.ppermute(value, ('rep', 'dp'), pairs)]
    ppermute x12, starting transfers between devices: 9.56 us -> 12 us  [swap(): lax.ppermute(value, axis, [(i, i ^ mask) for i in range(lax.axis_size(axi...]
    ppermute x12, waiting for transfers between devices: 14.5 us -> 16.6 us  [swap(): lax.ppermute(value, axis, [(i, i ^ mask) for i in range(lax.axis_size(axi...]
    ppermute x5, starting transfers between devices: 7.51 us -> 8.77 us  [swap_by_core(): return lax.ppermute(value, ('rep', 'dp'), pairs)]
  transfers between devices with their start and end apart: 17 -> 17, of which waited for: 9 -> 7; matrix products, arithmetic and copies ran while one was open for 0% -> 0% of each run, Pallas kernels for 5% -> 7%
where the time goes in v6:
time: 47.4 us; the launch traced here: 47.3 us
  starting transfers between devices  20.8 us (44%)
  waiting for transfers between devices  19 us (40%)
  Pallas kernels  6.76 us (14%)
  between operations  0.71 us (1%)
    ppermute x12, waiting for transfers between devices, swap(): lax.ppermute(value, axis, [(i, i ^ mask) for i in range(lax.axis_size(axi...  16.6 us
    ppermute x12, starting transfers between devices, swap(): lax.ppermute(value, axis, [(i, i ^ mask) for i in range(lax.axis_size(axi...  12 us
    ppermute x5, starting transfers between devices, swap_by_core(): return lax.ppermute(value, ('rep', 'dp'), pairs)  8.77 us
    pallas_call x7, Pallas kernels, kernel_call(): pl.pallas_call(body, out_shape=outputs, in_specs=kwargs.pop('in_specs', [...  6.76 us
    ppermute x5, waiting for transfers between devices, swap_by_core(): return lax.ppermute(value, ('rep', 'dp'), pairs)  2.48 us
  transfers between devices with their start and end apart: 17, of which 7 were waited for; matrix products, arithmetic and copies ran while one was open for 0% of the time, Pallas kernels for 7%

profile of v6, /device:TPU:0, one launch (start us, length us, event | category | flops | bytes accessed | tf_op | source)
XLA Modules:
  0.0 47.3 jit_solution(1553377660143358738)
XLA Ops:
  0.6 1.7 %shard_map.94 = (bf16[40,2048]{1,0:T(8,128)(2,1)S(1)}, bf16[40,2048]{1,0:T(8,128)(2,1)S(1)}, bf16[40,2048]{1,0:T(8,128)(2,1)S(1)}, bf16[40,2048]{1,0:T(8,128)(2,...) custom-call(bf16[32,2048]{1,0:T(8,128)(2,1)} %refs_0_.1, ...), custom_call_target="tpu_custom_call" | custom-call | bytes 3277440 | tf_op jit(solution)/shard_map/pallas_call | solution.py:37
  2.3 3.0 %collective-permute-start.7 = (bf16[144,2048]{1,0:T(8,128)(2,1)S(1)}, bf16[144,2048]{1,0:T(8,128)(2,1)S(1)}, u32[]{:S(2)}, u32[]{:S(2)}) collective-permute-start(bf16[144,2048]{1,0:T(8,128)(2,1)S(1)} %get-tuple-element.33.refs_8_), channel_id=1, source_target_pairs={{0,1},{1,0},{2,3},{3,2},{16,18},{17,19},{18,16},{19,17},{4,5},{5,4... | collective-permute-start | bytes 1769480 | tf_op jit(solution)/shard_map/ppermute | solution.py:31
  5.3 0.1 collective-permute-start.8
  5.4 4.1 %collective-permute-start = (bf16[40,2048]{1,0:T(8,128)(2,1)S(1)}, bf16[40,2048]{1,0:T(8,128)(2,1)S(1)}, u32[]{:S(2)}, u32[]{:S(2)}) collective-permute-start(bf16[40,2048]{1,0:T(8,128)(2,1)S(1)} %get-tuple-element.30), channel_id=1, source_target_pairs={{0,12},{4,8},{8,4},{12,0},{1,13},{5,9},{9,5},{13,1},{2,14},{6,10},... | collective-permute-start | bytes 491528 | tf_op jit(solution)/shard_map/ppermute | solution.py:20
  9.5 0.0 collective-permute-start.1
  9.5 0.6 %collective-permute-start.2 = (bf16[40,2048]{1,0:T(8,128)(2,1)S(1)}, bf16[40,2048]{1,0:T(8,128)(2,1)S(1)}, u32[]{:S(2)}, u32[]{:S(2)}) collective-permute-start(bf16[40,2048]{1,0:T(8,128)(2,1)S(1)} %get-tuple-element.32), channel_id=1, source_target_pairs={{0,4},{4,0},{8,12},{12,8},{1,5},{5,1},{9,13},{13,9},{2,6},{6,2},{1... | collective-permute-start | bytes 491528 | tf_op jit(solution)/shard_map/ppermute | solution.py:20
  10.0 4.6 %collective-permute-done.refs_1_ = bf16[40,2048]{1,0:T(8,128)(2,1)S(1)} collective-permute-done((bf16[40,2048]{1,0:T(8,128)(2,1)S(1)}, bf16[40,2048]{1,0:T(8,128)(2,1)S(1)}, u32[]{:S(2)}, u32[]{:S(2)}) %collective-permute-start) | collective-permute-done | bytes 163872 | tf_op jit(solution)/shard_map/ppermute | solution.py:20
  14.6 0.0 collective-permute-start.3
  14.6 0.0 collective-permute-done.7.refs_9_
  14.6 1.7 %collective-permute-start.9 = (bf16[144,2048]{1,0:T(8,128)(2,1)S(1)}, bf16[144,2048]{1,0:T(8,128)(2,1)S(1)}, u32[]{:S(2)}, u32[]{:S(2)}) collective-permute-start(bf16[144,2048]{1,0:T(8,128)(2,1)S(1)} %collective-permute-done.7.refs_9_), channel_id=1, source_target_pairs={{0,2},{1,3},{2,0},{3,1},{16,17},{17,16},{18,19},{19,18},{4,6},{5,7... | collective-permute-start | bytes 1769480 | tf_op jit(solution)/shard_map/ppermute | solution.py:31
  16.4 6.4 %collective-permute-done.1.refs_2_ = bf16[40,2048]{1,0:T(8,128)(2,1)S(1)} collective-permute-done((bf16[40,2048]{1,0:T(8,128)(2,1)S(1)}, bf16[40,2048]{1,0:T(8,128)(2,1)S(1)}, u32[]{:S(2)}, u32[]{:S(2)}) %collective-permute-start.1) | collective-permute-done | bytes 163872 | tf_op jit(solution)/shard_map/ppermute | solution.py:20
  22.8 0.0 collective-permute-start.4
  22.8 0.0 collective-permute-done.2.refs_3_
  22.8 0.5 %collective-permute-start.5 = (bf16[40,2048]{1,0:T(8,128)(2,1)S(1)}, bf16[40,2048]{1,0:T(8,128)(2,1)S(1)}, u32[]{:S(2)}, u32[]{:S(2)}) collective-permute-start(bf16[40,2048]{1,0:T(8,128)(2,1)S(1)} %collective-permute-done.1.refs_2_), channel_id=1, source_target_pairs={{0,16},{16,0},{1,17},{17,1},{2,18},{18,2},{3,19},{19,3},{4,20},{20... | collective-permute-start | bytes 491528 | tf_op jit(solution)/shard_map/ppermute | solution.py:20
  23.3 0.0 collective-permute-done.3.refs_4_
  23.3 0.1 collective-permute-start.6
  23.4 0.8 %collective-permute-done.4.refs_5_ = bf16[40,2048]{1,0:T(8,128)(2,1)S(1)} collective-permute-done((bf16[40,2048]{1,0:T(8,128)(2,1)S(1)}, bf16[40,2048]{1,0:T(8,128)(2,1)S(1)}, u32[]{:S(2)}, u32[]{:S(2)}) %collective-permute-start.4) | collective-permute-done | bytes 163872 | tf_op jit(solution)/shard_map/ppermute | solution.py:20
  24.2 0.2 collective-permute-done.5.refs_6_
  24.4 0.3 collective-permute-done.6.refs_7_
  24.7 0.0 collective-permute-done.8.refs_10_
  24.7 1.9 %shard_map.95 = (bf16[160,2048]{1,0:T(8,128)(2,1)S(1)}, bf16[160,2048]{1,0:T(8,128)(2,1)S(1)}, f32[160,2176]{1,0:T(8,128)S(1)}, f32[48,2048]{1,0:T(8,128)S(1)}, bf16[96,2048]{1,0:T(8,128)(2,1)S(1)}) custom-call(bf16[40,2048]{1,0:T(8,128)(2,1)S(1)} %get-tuple-element.29.refs_0_, bf16[40,2048]{1,0:T(8,128)(2,1)S(1)} %collective-permute-done.refs_1_, ...), custom_call_target="tpu_custom_call" | custom-call | flops 4000000000 | bytes 6569984 | tf_op jit(solution)/shard_map/pallas_call | solution.py:37
  26.7 0.0 collective-permute-done.9.far
  26.7 1.0 %shard_map.96 = (f32[80,2176]{1,0:T(8,128)S(1)}, bf16[80,2176]{1,0:T(8,128)(2,1)S(1)}, bf16[48,2048]{1,0:T(8,128)(2,1)S(1)}) custom-call(bf16[160,2048]{1,0:T(8,128)(2,1)S(1)} %get-tuple-element.35.x_ref, bf16[160,2048]{1,0:T(8,128)(2,1)S(1)} %get-tuple-element.36.d_ref, f32[160,2176]{1,0:T(8,128)S(1)} %get-tuple-element.37.dx_ref, ...), custom_call_target="tpu_custom_call" | custom-call | bytes 4534272 | tf_op jit(solution)/shard_map/pallas_call | solution.py:37
  27.7 0.0 copy-start
  27.7 0.3 collective-permute-start.10
  28.0 1.5 %collective-permute-start.14 = (bf16[96,2048]{1,0:T(8,128)(2,1)S(1)}, bf16[96,2048]{1,0:T(8,128)(2,1)S(1)}, u32[]{:S(2)}, u32[]{:S(2)}) collective-permute-start(bf16[96,2048]{1,0:T(8,128)(2,1)S(1)} %get-tuple-element.53), channel_id=1, source_target_pairs={{0,1},{1,0},{2,3},{3,2},{16,18},{17,19},{18,16},{19,17},{4,5},{5,4... | collective-permute-start | bytes 1179656 | tf_op jit(solution)/shard_map/ppermute | solution.py:31
  29.5 0.0 collective-permute-done.10.got
  29.5 0.1 shard_map.97
  29.6 2.4 %collective-permute-start.15 = (bf16[48,2048]{1,0:T(8,128)(2,1)S(1)}, bf16[48,2048]{1,0:T(8,128)(2,1)S(1)}, u32[]{:S(2)}, u32[]{:S(2)}) collective-permute-start(bf16[48,2048]{1,0:T(8,128)(2,1)S(1)} %get-tuple-element.54), channel_id=1, source_target_pairs={{0,3},{1,2},{2,1},{3,0},{16,19},{17,18},{18,17},{19,16},{4,7},{5,6... | collective-permute-start | bytes 589832 | tf_op jit(solution)/shard_map/ppermute | solution.py:31
  32.0 2.8 %collective-permute-start.11 = (bf16[20,2176]{1,0:T(8,128)(2,1)S(1)}, bf16[20,2176]{1,0:T(8,128)(2,1)S(1)}, u32[]{:S(2)}, u32[]{:S(2)}) collective-permute-start(bf16[20,2176]{1,0:T(8,128)(2,1)S(1)} %get-tuple-element.46), channel_id=1, source_target_pairs={{0,12},{4,8},{8,4},{12,0},{1,13},{5,9},{9,5},{13,1},{2,14},{6,10},... | collective-permute-start | bytes 261128 | tf_op jit(solution)/shard_map/ppermute | solution.py:20
  34.8 3.1 %collective-permute-start.12 = (bf16[20,2176]{1,0:T(8,128)(2,1)S(1)}, bf16[20,2176]{1,0:T(8,128)(2,1)S(1)}, u32[]{:S(2)}, u32[]{:S(2)}) collective-permute-start(bf16[20,2176]{1,0:T(8,128)(2,1)S(1)} %get-tuple-element.47), channel_id=1, source_target_pairs={{0,8},{4,12},{8,0},{12,4},{1,9},{5,13},{9,1},{13,5},{2,10},{6,14},... | collective-permute-start | bytes 261128 | tf_op jit(solution)/shard_map/ppermute | solution.py:20
  37.9 0.6 %collective-permute-start.13 = (bf16[20,2176]{1,0:T(8,128)(2,1)S(1)}, bf16[20,2176]{1,0:T(8,128)(2,1)S(1)}, u32[]{:S(2)}, u32[]{:S(2)}) collective-permute-start(bf16[20,2176]{1,0:T(8,128)(2,1)S(1)} %get-tuple-element.48), channel_id=1, source_target_pairs={{0,4},{4,0},{8,12},{12,8},{1,5},{5,1},{9,13},{13,9},{2,6},{6,2},{1... | collective-permute-start | bytes 261128 | tf_op jit(solution)/shard_map/ppermute | solution.py:20
  38.5 0.0 collective-permute-done.14.near
  38.5 2.5 %collective-permute-done.15.far = bf16[48,2048]{1,0:T(8,128)(2,1)S(1)} collective-permute-done((bf16[48,2048]{1,0:T(8,128)(2,1)S(1)}, bf16[48,2048]{1,0:T(8,128)(2,1)S(1)}, u32[]{:S(2)}, u32[]{:S(2)}) %collective-permute-start.15) | collective-permute-done | bytes 196640 | tf_op jit(solution)/shard_map/ppermute | solution.py:31
  41.0 0.1 shard_map.99.mine
  41.0 0.1 collective-permute-start.16
  41.1 0.0 collective-permute-done.11.refs_1_
  41.1 4.2 %collective-permute-done.12.refs_2_ = bf16[20,2176]{1,0:T(8,128)(2,1)S(1)} collective-permute-done((bf16[20,2176]{1,0:T(8,128)(2,1)S(1)}, bf16[20,2176]{1,0:T(8,128)(2,1)S(1)}, u32[]{:S(2)}, u32[]{:S(2)}) %collective-permute-start.12) | collective-permute-done | bytes 87072 | tf_op jit(solution)/shard_map/ppermute | solution.py:20
  45.3 0.0 collective-permute-done.13.refs_3_
  45.3 0.0 copy-done
  45.3 1.0 %shard_map.98 = (bf16[32,2048]{1,0:T(8,128)(2,1)}, bf16[2,32]{1,0:T(2,128)(2,1)}) custom-call(bf16[20,2176]{1,0:T(8,128)(2,1)S(1)} %get-tuple-element.45.refs_0_, bf16[20,2176]{1,0:T(8,128)(2,1)S(1)} %collective-permute-done.11.refs_1_, bf16[20,2176]{1,0:T(8,128)(2,1)S(1)} %collective-permute-done.12.refs_2_, ...), custom_call_target="tpu_custom_call" | custom-call | flops 8000000000 | bytes 479744 | tf_op jit(solution)/shard_map/pallas_call | solution.py:37
  46.3 0.0 collective-permute-done.16.theirs
  46.3 1.0 %shard_map.100 = f32[1,96,2048]{2,1,0:T(8,128)} custom-call(bf16[96,2048]{1,0:T(8,128)(2,1)S(1)} %shard_map.99.mine, bf16[96,2048]{1,0:T(8,128)(2,1)S(1)} %collective-permute-done.16.theirs), custom_call_target="tpu_custom_call" | custom-call | bytes 1572864 | tf_op jit(solution)/shard_map/pallas_call | solution.py:37
Async XLA Ops:
  2.3 12.3 %collective-permute-start.7 = (bf16[144,2048]{1,0:T(8,128)(2,1)S(1)}, bf16[144,2048]{1,0:T(8,128)(2,1)S(1)}, u32[]{:S(2)}, u32[]{:S(2)}) collective-permute-start(bf16[144,2048]{1,0:T(8,128)(2,1)S(1)} %get-tuple-element.33.refs_8_), channel_id=1, source_target_pairs={{0,1},{1,0},{2,3},{3,2},{16,18},{17,19},{18,16},{19,17},{4,5},{5,4... | collective-permute-start | bytes 1769480 | tf_op jit(solution)/shard_map/ppermute | solution.py:31
  5.3 19.4 %collective-permute-start.8 = (bf16[144,2048]{1,0:T(8,128)(2,1)S(1)}, bf16[144,2048]{1,0:T(8,128)(2,1)S(1)}, u32[]{:S(2)}, u32[]{:S(2)}) collective-permute-start(bf16[144,2048]{1,0:T(8,128)(2,1)S(1)} %get-tuple-element.34), channel_id=1, source_target_pairs={{0,1},{1,0},{2,3},{3,2},{16,18},{17,19},{18,16},{19,17},{4,5},{5,4... | collective-permute-start | bytes 1769480 | tf_op jit(solution)/shard_map/ppermute | solution.py:31
  5.4 9.2 %collective-permute-start = (bf16[40,2048]{1,0:T(8,128)(2,1)S(1)}, bf16[40,2048]{1,0:T(8,128)(2,1)S(1)}, u32[]{:S(2)}, u32[]{:S(2)}) collective-permute-start(bf16[40,2048]{1,0:T(8,128)(2,1)S(1)} %get-tuple-element.30), channel_id=1, source_target_pairs={{0,12},{4,8},{8,4},{12,0},{1,13},{5,9},{9,5},{13,1},{2,14},{6,10},... | collective-permute-start | bytes 491528 | tf_op jit(solution)/shard_map/ppermute | solution.py:20
  9.5 13.3 %collective-permute-start.1 = (bf16[40,2048]{1,0:T(8,128)(2,1)S(1)}, bf16[40,2048]{1,0:T(8,128)(2,1)S(1)}, u32[]{:S(2)}, u32[]{:S(2)}) collective-permute-start(bf16[40,2048]{1,0:T(8,128)(2,1)S(1)} %get-tuple-element.31), channel_id=1, source_target_pairs={{0,8},{4,12},{8,0},{12,4},{1,9},{5,13},{9,1},{13,5},{2,10},{6,14},... | collective-permute-start | bytes 491528 | tf_op jit(solution)/shard_map/ppermute | solution.py:20
  9.5 13.3 %collective-permute-start.2 = (bf16[40,2048]{1,0:T(8,128)(2,1)S(1)}, bf16[40,2048]{1,0:T(8,128)(2,1)S(1)}, u32[]{:S(2)}, u32[]{:S(2)}) collective-permute-start(bf16[40,2048]{1,0:T(8,128)(2,1)S(1)} %get-tuple-element.32), channel_id=1, source_target_pairs={{0,4},{4,0},{8,12},{12,8},{1,5},{5,1},{9,13},{13,9},{2,6},{6,2},{1... | collective-permute-start | bytes 491528 | tf_op jit(solution)/shard_map/ppermute | solution.py:20
  14.6 8.7 %collective-permute-start.3 = (bf16[40,2048]{1,0:T(8,128)(2,1)S(1)}, bf16[40,2048]{1,0:T(8,128)(2,1)S(1)}, u32[]{:S(2)}, u32[]{:S(2)}) collective-permute-start(bf16[40,2048]{1,0:T(8,128)(2,1)S(1)} %get-tuple-element.29.refs_0_), channel_id=1, source_target_pairs={{0,16},{16,0},{1,17},{17,1},{2,18},{18,2},{3,19},{19,3},{4,20},{20... | collective-permute-start | bytes 491528 | tf_op jit(solution)/shard_map/ppermute | solution.py:20
  14.6 12.0 %collective-permute-start.9 = (bf16[144,2048]{1,0:T(8,128)(2,1)S(1)}, bf16[144,2048]{1,0:T(8,128)(2,1)S(1)}, u32[]{:S(2)}, u32[]{:S(2)}) collective-permute-start(bf16[144,2048]{1,0:T(8,128)(2,1)S(1)} %collective-permute-done.7.refs_9_), channel_id=1, source_target_pairs={{0,2},{1,3},{2,0},{3,1},{16,17},{17,16},{18,19},{19,18},{4,6},{5,7... | collective-permute-start | bytes 1769480 | tf_op jit(solution)/shard_map/ppermute | solution.py:31
  22.8 1.4 %collective-permute-start.4 = (bf16[40,2048]{1,0:T(8,128)(2,1)S(1)}, bf16[40,2048]{1,0:T(8,128)(2,1)S(1)}, u32[]{:S(2)}, u32[]{:S(2)}) collective-permute-start(bf16[40,2048]{1,0:T(8,128)(2,1)S(1)} %collective-permute-done.refs_1_), channel_id=1, source_target_pairs={{0,16},{16,0},{1,17},{17,1},{2,18},{18,2},{3,19},{19,3},{4,20},{20... | collective-permute-start | bytes 491528 | tf_op jit(solution)/shard_map/ppermute | solution.py:20
  22.8 1.6 %collective-permute-start.5 = (bf16[40,2048]{1,0:T(8,128)(2,1)S(1)}, bf16[40,2048]{1,0:T(8,128)(2,1)S(1)}, u32[]{:S(2)}, u32[]{:S(2)}) collective-permute-start(bf16[40,2048]{1,0:T(8,128)(2,1)S(1)} %collective-permute-done.1.refs_2_), channel_id=1, source_target_pairs={{0,16},{16,0},{1,17},{17,1},{2,18},{18,2},{3,19},{19,3},{4,20},{20... | collective-permute-start | bytes 491528 | tf_op jit(solution)/shard_map/ppermute | solution.py:20
  23.3 1.4 %collective-permute-start.6 = (bf16[40,2048]{1,0:T(8,128)(2,1)S(1)}, bf16[40,2048]{1,0:T(8,128)(2,1)S(1)}, u32[]{:S(2)}, u32[]{:S(2)}) collective-permute-start(bf16[40,2048]{1,0:T(8,128)(2,1)S(1)} %collective-permute-done.2.refs_3_), channel_id=1, source_target_pairs={{0,16},{16,0},{1,17},{17,1},{2,18},{18,2},{3,19},{19,3},{4,20},{20... | collective-permute-start | bytes 491528 | tf_op jit(solution)/shard_map/ppermute | solution.py:20
  27.7 17.7 %copy-start = (bf16[32,2]{0,1:T(2,128)(2,1)S(1)}, bf16[32,2]{0,1:T(2,128)(2,1)}, u32[]{:S(2)}) copy-start(bf16[32,2]{0,1:T(2,128)(2,1)} %param.10) | copy-start | bytes 388
  27.7 1.8 %collective-permute-start.10 = (bf16[80,2176]{1,0:T(8,128)(2,1)S(1)}, bf16[80,2176]{1,0:T(8,128)(2,1)S(1)}, u32[]{:S(2)}, u32[]{:S(2)}) collective-permute-start(bf16[80,2176]{1,0:T(8,128)(2,1)S(1)} %get-tuple-element.40), channel_id=1, source_target_pairs={{0,16},{16,0},{1,17},{17,1},{2,18},{18,2},{3,19},{19,3},{4,20},{20... | collective-permute-start | bytes 1044488 | tf_op jit(solution)/shard_map/ppermute | solution.py:20
  28.0 10.5 %collective-permute-start.14 = (bf16[96,2048]{1,0:T(8,128)(2,1)S(1)}, bf16[96,2048]{1,0:T(8,128)(2,1)S(1)}, u32[]{:S(2)}, u32[]{:S(2)}) collective-permute-start(bf16[96,2048]{1,0:T(8,128)(2,1)S(1)} %get-tuple-element.53), channel_id=1, source_target_pairs={{0,1},{1,0},{2,3},{3,2},{16,18},{17,19},{18,16},{19,17},{4,5},{5,4... | collective-permute-start | bytes 1179656 | tf_op jit(solution)/shard_map/ppermute | solution.py:31
  29.6 11.4 %collective-permute-start.15 = (bf16[48,2048]{1,0:T(8,128)(2,1)S(1)}, bf16[48,2048]{1,0:T(8,128)(2,1)S(1)}, u32[]{:S(2)}, u32[]{:S(2)}) collective-permute-start(bf16[48,2048]{1,0:T(8,128)(2,1)S(1)} %get-tuple-element.54), channel_id=1, source_target_pairs={{0,3},{1,2},{2,1},{3,0},{16,19},{17,18},{18,17},{19,16},{4,7},{5,6... | collective-permute-start | bytes 589832 | tf_op jit(solution)/shard_map/ppermute | solution.py:31
  32.0 9.1 %collective-permute-start.11 = (bf16[20,2176]{1,0:T(8,128)(2,1)S(1)}, bf16[20,2176]{1,0:T(8,128)(2,1)S(1)}, u32[]{:S(2)}, u32[]{:S(2)}) collective-permute-start(bf16[20,2176]{1,0:T(8,128)(2,1)S(1)} %get-tuple-element.46), channel_id=1, source_target_pairs={{0,12},{4,8},{8,4},{12,0},{1,13},{5,9},{9,5},{13,1},{2,14},{6,10},... | collective-permute-start | bytes 261128 | tf_op jit(solution)/shard_map/ppermute | solution.py:20
  34.8 10.5 %collective-permute-start.12 = (bf16[20,2176]{1,0:T(8,128)(2,1)S(1)}, bf16[20,2176]{1,0:T(8,128)(2,1)S(1)}, u32[]{:S(2)}, u32[]{:S(2)}) collective-permute-start(bf16[20,2176]{1,0:T(8,128)(2,1)S(1)} %get-tuple-element.47), channel_id=1, source_target_pairs={{0,8},{4,12},{8,0},{12,4},{1,9},{5,13},{9,1},{13,5},{2,10},{6,14},... | collective-permute-start | bytes 261128 | tf_op jit(solution)/shard_map/ppermute | solution.py:20
  37.9 7.4 %collective-permute-start.13 = (bf16[20,2176]{1,0:T(8,128)(2,1)S(1)}, bf16[20,2176]{1,0:T(8,128)(2,1)S(1)}, u32[]{:S(2)}, u32[]{:S(2)}) collective-permute-start(bf16[20,2176]{1,0:T(8,128)(2,1)S(1)} %get-tuple-element.48), channel_id=1, source_target_pairs={{0,4},{4,0},{8,12},{12,8},{1,5},{5,1},{9,13},{13,9},{2,6},{6,2},{1... | collective-permute-start | bytes 261128 | tf_op jit(solution)/shard_map/ppermute | solution.py:20
  41.0 5.3 %collective-permute-start.16 = (bf16[96,2048]{1,0:T(8,128)(2,1)S(1)}, bf16[96,2048]{1,0:T(8,128)(2,1)S(1)}, u32[]{:S(2)}, u32[]{:S(2)}) collective-permute-start(bf16[96,2048]{1,0:T(8,128)(2,1)S(1)} %shard_map.99.mine), channel_id=1, source_target_pairs={{0,16},{16,0},{1,17},{17,1},{2,18},{18,2},{3,19},{19,3},{4,20},{20... | collective-permute-start | bytes 1179656 | tf_op jit(solution)/shard_map/ppermute | solution.py:20

commit v7 on v6

--- a/solution.py
+++ b/solution.py
@@ -20,9 +20,8 @@
     return lax.ppermute(value, axis, [(i, i ^ mask) for i in range(lax.axis_size(axis))])
 
 
-def exchange(chunks):
-    count = len(chunks)
-    return [chunks[0]] + [swap(chunks[c], "ep", count - c) for c in range(1, count)]
+def exchange(chunks, masks):
+    return [chunks[0]] + [swap(chunk, "ep", mask) for chunk, mask in zip(chunks[1:], masks[1:])]
 
 
 def swap_by_core(value, masks):
@@ -85,7 +84,7 @@
         expert = ids[k : k + 1, :]
         if chunk_count > 1:
             mask = expert ^ me
-            chunk = jnp.where(mask == 0, 0, experts - mask)
+            chunk = jnp.where(mask < 2, mask, experts + 1 - mask)
             slot = chunk * cap + rank
             x_row = slot + chunk * cap
         else:
@@ -178,8 +177,9 @@
     top = slot.shape[0]
     total = 0.0
     probs = [0.0] * top
-    for c in range(chunk_count):
-        slot_of_row = iota((rows, tok_dev), 0) + c * rows
+    places = [0, *range(2, chunk_count), 1][:chunk_count]
+    for c, place in enumerate(places):
+        slot_of_row = iota((rows, tok_dev), 0) + place * rows
         hits = [(slot_of_row == slot[k : k + 1, :]).astype(f32) for k in range(top)]
         total = total + dot(sum(hits).astype(bf16), chunks[c][:, :width], (0, 0))
         prob = chunks[c][:, width : width + 1].astype(f32)
@@ -198,6 +198,7 @@
     slots = experts * cap
     chunk_count = experts if experts <= 8 else 1
     rows = slots // chunk_count
+    masks = [0, 1, *range(experts - 1, 1, -1)]
     hidden = gate_weight.shape[1] // reps
     shape = jax.ShapeDtypeStruct
     in_hbm = pl.BlockSpec(memory_space=pltpu.HBM)
@@ -218,7 +219,7 @@
     far = swap_by_core(near[0], across)
 
     if chunk_count > 1:
-        chunks = exchange(chunks)
+        chunks = exchange(chunks, masks)
     else:
         moved = chunks[0].reshape(2, experts, cap, width)
         moved = lax.all_to_all(moved, "ep", split_axis=1, concat_axis=1, tiled=True)
@@ -231,7 +232,7 @@
         chunks + [first, *near],
         [shape((2 * slots, width), bf16)] * 2
         + [shape((2 * slots, wide), f32), shape((hidden, width), f32), shape((2 * hidden, width), bf16)],
-        flops=4*10**9,
+        flops=4 * 10**9,
     )
     keep, give, grad_far = kernel_call(
         late_kernel,
@@ -239,9 +240,9 @@
         [shape((slots, wide), f32), shape((slots, wide), bf16), shape((hidden, width), bf16)],
     )
     back = kernel_call(add_kernel, [keep, swap(give, "rep", 1)], [shape((rows, wide), bf16)] * chunk_count)
-    grad_far, back = lax.optimization_barrier((grad_far, back))
     if chunk_count > 1:
-        back = exchange(back)
+        back = exchange(back, masks)
+        back = [back[0], *back[2:], back[1]]
     else:
         moved = back[0].reshape(experts, cap, wide)
         moved = lax.all_to_all(moved, "ep", split_axis=0, concat_axis=0, tiled=True)
@@ -250,7 +251,7 @@
         functools.partial(combine_kernel, chunk_count),
         back + [slot, route_weight.T],
         [shape((tok_dev, width), bf16), shape((top, tok_dev), bf16)],
-        flops=8*10**9,
+        flops=8 * 10**9,
     )
 
     arrived = swap_by_core(grad_near, along), swap_by_core(grad_far, (3, 3))

time: 47.4 us -> 45.1 us (0.951)
  starting transfers between devices: 20.8 us -> 18.1 us
    ppermute x5, waiting for transfers between devices: 2.48 us -> 6.87 us  [swap_by_core(): return lax.ppermute(value, ('rep', 'dp'), pairs)]
    ppermute x12, waiting for transfers between devices: 16.6 us -> 12.5 us  [swap(): lax.ppermute(value, axis, [(i, i ^ mask) for i in range(lax.axis_size(axi...]
    ppermute x12, starting transfers between devices: 12 us -> 10 us  [swap(): lax.ppermute(value, axis, [(i, i ^ mask) for i in range(lax.axis_size(axi...]
    ppermute x5, starting transfers between devices: 8.77 us -> 8.11 us  [swap_by_core(): return lax.ppermute(value, ('rep', 'dp'), pairs)]
  transfers between devices with their start and end apart: 17 -> 17, of which waited for: 7 -> 9; matrix products, arithmetic and copies ran while one was open for 0% -> 0% of each run, Pallas kernels for 7% -> 7%
where the time goes in v7:
time: 45.1 us; the launch traced here: 45 us
  waiting for transfers between devices  19.3 us (43%)
  starting transfers between devices  18.1 us (40%)
  Pallas kernels  6.79 us (15%)
  between operations  0.71 us (2%)
    ppermute x12, waiting for transfers between devices, swap(): lax.ppermute(value, axis, [(i, i ^ mask) for i in range(lax.axis_size(axi...  12.5 us
    ppermute x12, starting transfers between devices, swap(): lax.ppermute(value, axis, [(i, i ^ mask) for i in range(lax.axis_size(axi...  10 us
    ppermute x5, starting transfers between devices, swap_by_core(): return lax.ppermute(value, ('rep', 'dp'), pairs)  8.11 us
    ppermute x5, waiting for transfers between devices, swap_by_core(): return lax.ppermute(value, ('rep', 'dp'), pairs)  6.87 us
    pallas_call x7, Pallas kernels, kernel_call(): pl.pallas_call(body, out_shape=outputs, in_specs=kwargs.pop('in_specs', [...  6.79 us
  transfers between devices with their start and end apart: 17, of which 9 were waited for; matrix products, arithmetic and copies ran while one was open for 0% of the time, Pallas kernels for 7%

profile of v7, /device:TPU:0, one launch (start us, length us, event | category | flops | bytes accessed | tf_op | source)
XLA Modules:
  0.0 45.0 jit_solution(6490056676241669577)
XLA Ops:
  0.6 1.7 %shard_map.94 = (bf16[40,2048]{1,0:T(8,128)(2,1)S(1)}, bf16[40,2048]{1,0:T(8,128)(2,1)S(1)}, bf16[40,2048]{1,0:T(8,128)(2,1)S(1)}, bf16[40,2048]{1,0:T(8,128)(2,...) custom-call(bf16[32,2048]{1,0:T(8,128)(2,1)} %refs_0_.1, ...), custom_call_target="tpu_custom_call" | custom-call | bytes 3277440 | tf_op jit(solution)/shard_map/pallas_call | solution.py:36
  2.3 3.0 %collective-permute-start.7 = (bf16[144,2048]{1,0:T(8,128)(2,1)S(1)}, bf16[144,2048]{1,0:T(8,128)(2,1)S(1)}, u32[]{:S(2)}, u32[]{:S(2)}) collective-permute-start(bf16[144,2048]{1,0:T(8,128)(2,1)S(1)} %get-tuple-element.28.refs_8_), channel_id=1, source_target_pairs={{0,1},{1,0},{2,3},{3,2},{16,18},{17,19},{18,16},{19,17},{4,5},{5,4... | collective-permute-start | bytes 1769480 | tf_op jit(solution)/shard_map/ppermute | solution.py:30
  5.3 0.1 collective-permute-start.8
  5.4 2.0 %collective-permute-start = (bf16[40,2048]{1,0:T(8,128)(2,1)S(1)}, bf16[40,2048]{1,0:T(8,128)(2,1)S(1)}, u32[]{:S(2)}, u32[]{:S(2)}) collective-permute-start(bf16[40,2048]{1,0:T(8,128)(2,1)S(1)} %get-tuple-element.25), channel_id=1, source_target_pairs={{0,4},{4,0},{8,12},{12,8},{1,5},{5,1},{9,13},{13,9},{2,6},{6,2},{1... | collective-permute-start | bytes 491528 | tf_op jit(solution)/shard_map/ppermute | solution.py:20
  7.4 2.5 %collective-permute-start.1 = (bf16[40,2048]{1,0:T(8,128)(2,1)S(1)}, bf16[40,2048]{1,0:T(8,128)(2,1)S(1)}, u32[]{:S(2)}, u32[]{:S(2)}) collective-permute-start(bf16[40,2048]{1,0:T(8,128)(2,1)S(1)} %get-tuple-element.26), channel_id=1, source_target_pairs={{0,12},{4,8},{8,4},{12,0},{1,13},{5,9},{9,5},{13,1},{2,14},{6,10},... | collective-permute-start | bytes 491528 | tf_op jit(solution)/shard_map/ppermute | solution.py:20
  9.9 0.1 collective-permute-start.2
  10.0 1.7 %collective-permute-done.refs_1_ = bf16[40,2048]{1,0:T(8,128)(2,1)S(1)} collective-permute-done((bf16[40,2048]{1,0:T(8,128)(2,1)S(1)}, bf16[40,2048]{1,0:T(8,128)(2,1)S(1)}, u32[]{:S(2)}, u32[]{:S(2)}) %collective-permute-start) | collective-permute-done | bytes 163872 | tf_op jit(solution)/shard_map/ppermute | solution.py:20
  11.7 0.0 collective-permute-start.3
  11.7 1.5 %collective-permute-done.7.refs_9_ = bf16[144,2048]{1,0:T(8,128)(2,1)S(1)} collective-permute-done((bf16[144,2048]{1,0:T(8,128)(2,1)S(1)}, bf16[144,2048]{1,0:T(8,128)(2,1)S(1)}, u32[]{:S(2)}, u32[]{:S(2)}) %collective-permute-start.7) | collective-permute-done | bytes 589856 | tf_op jit(solution)/shard_map/ppermute | solution.py:30
  13.2 2.0 %collective-permute-start.9 = (bf16[144,2048]{1,0:T(8,128)(2,1)S(1)}, bf16[144,2048]{1,0:T(8,128)(2,1)S(1)}, u32[]{:S(2)}, u32[]{:S(2)}) collective-permute-start(bf16[144,2048]{1,0:T(8,128)(2,1)S(1)} %collective-permute-done.7.refs_9_), channel_id=1, source_target_pairs={{0,2},{1,3},{2,0},{3,1},{16,17},{17,16},{18,19},{19,18},{4,6},{5,7... | collective-permute-start | bytes 1769480 | tf_op jit(solution)/shard_map/ppermute | solution.py:30
  15.2 3.4 %collective-permute-done.1.refs_2_ = bf16[40,2048]{1,0:T(8,128)(2,1)S(1)} collective-permute-done((bf16[40,2048]{1,0:T(8,128)(2,1)S(1)}, bf16[40,2048]{1,0:T(8,128)(2,1)S(1)}, u32[]{:S(2)}, u32[]{:S(2)}) %collective-permute-start.1) | collective-permute-done | bytes 163872 | tf_op jit(solution)/shard_map/ppermute | solution.py:20
  18.6 0.0 collective-permute-start.4
  18.6 5.3 %collective-permute-done.2.refs_3_ = bf16[40,2048]{1,0:T(8,128)(2,1)S(1)} collective-permute-done((bf16[40,2048]{1,0:T(8,128)(2,1)S(1)}, bf16[40,2048]{1,0:T(8,128)(2,1)S(1)}, u32[]{:S(2)}, u32[]{:S(2)}) %collective-permute-start.2) | collective-permute-done | bytes 163872 | tf_op jit(solution)/shard_map/ppermute | solution.py:20
  23.9 0.0 collective-permute-start.5
  23.9 0.0 collective-permute-done.3.refs_4_
  23.9 0.5 %collective-permute-start.6 = (bf16[40,2048]{1,0:T(8,128)(2,1)S(1)}, bf16[40,2048]{1,0:T(8,128)(2,1)S(1)}, u32[]{:S(2)}, u32[]{:S(2)}) collective-permute-start(bf16[40,2048]{1,0:T(8,128)(2,1)S(1)} %collective-permute-done.2.refs_3_), channel_id=1, source_target_pairs={{0,16},{16,0},{1,17},{17,1},{2,18},{18,2},{3,19},{19,3},{4,20},{20... | collective-permute-start | bytes 491528 | tf_op jit(solution)/shard_map/ppermute | solution.py:20
  24.4 0.0 collective-permute-done.4.refs_5_
  24.4 0.9 %collective-permute-done.5.refs_6_ = bf16[40,2048]{1,0:T(8,128)(2,1)S(1)} collective-permute-done((bf16[40,2048]{1,0:T(8,128)(2,1)S(1)}, bf16[40,2048]{1,0:T(8,128)(2,1)S(1)}, u32[]{:S(2)}, u32[]{:S(2)}) %collective-permute-start.5) | collective-permute-done | bytes 163872 | tf_op jit(solution)/shard_map/ppermute | solution.py:20
  25.3 0.2 collective-permute-done.6.refs_7_
  25.6 0.0 collective-permute-done.8.refs_10_
  25.6 1.9 %shard_map.95 = (bf16[160,2048]{1,0:T(8,128)(2,1)S(1)}, bf16[160,2048]{1,0:T(8,128)(2,1)S(1)}, f32[160,2176]{1,0:T(8,128)S(1)}, f32[48,2048]{1,0:T(8,128)S(1)}, bf16[96,2048]{1,0:T(8,128)(2,1)S(1)}) custom-call(bf16[40,2048]{1,0:T(8,128)(2,1)S(1)} %get-tuple-element.24.refs_0_, bf16[40,2048]{1,0:T(8,128)(2,1)S(1)} %collective-permute-done.refs_1_, ...), custom_call_target="tpu_custom_call" | custom-call | flops 4000000000 | bytes 6569984 | tf_op jit(solution)/shard_map/pallas_call | solution.py:36
  27.5 0.0 collective-permute-done.9.far
  27.5 1.0 %shard_map.96 = (f32[80,2176]{1,0:T(8,128)S(1)}, bf16[80,2176]{1,0:T(8,128)(2,1)S(1)}, bf16[48,2048]{1,0:T(8,128)(2,1)S(1)}) custom-call(bf16[160,2048]{1,0:T(8,128)(2,1)S(1)} %get-tuple-element.30.x_ref, bf16[160,2048]{1,0:T(8,128)(2,1)S(1)} %get-tuple-element.31.d_ref, f32[160,2176]{1,0:T(8,128)S(1)} %get-tuple-element.32.dx_ref, ...), custom_call_target="tpu_custom_call" | custom-call | bytes 4534272 | tf_op jit(solution)/shard_map/pallas_call | solution.py:36
  28.5 0.0 copy-start
  28.6 0.3 collective-permute-start.10
  28.9 1.5 %collective-permute-start.14 = (bf16[96,2048]{1,0:T(8,128)(2,1)S(1)}, bf16[96,2048]{1,0:T(8,128)(2,1)S(1)}, u32[]{:S(2)}, u32[]{:S(2)}) collective-permute-start(bf16[96,2048]{1,0:T(8,128)(2,1)S(1)} %get-tuple-element.43), channel_id=1, source_target_pairs={{0,1},{1,0},{2,3},{3,2},{16,18},{17,19},{18,16},{19,17},{4,5},{5,4... | collective-permute-start | bytes 1179656 | tf_op jit(solution)/shard_map/ppermute | solution.py:30
  30.4 1.5 %collective-permute-start.15 = (bf16[48,2048]{1,0:T(8,128)(2,1)S(1)}, bf16[48,2048]{1,0:T(8,128)(2,1)S(1)}, u32[]{:S(2)}, u32[]{:S(2)}) collective-permute-start(bf16[48,2048]{1,0:T(8,128)(2,1)S(1)} %get-tuple-element.44), channel_id=1, source_target_pairs={{0,3},{1,2},{2,1},{3,0},{16,19},{17,18},{18,17},{19,16},{4,7},{5,6... | collective-permute-start | bytes 589832 | tf_op jit(solution)/shard_map/ppermute | solution.py:30
  31.9 0.0 collective-permute-done.10.got
  31.9 0.1 shard_map.97
  32.0 2.7 %collective-permute-start.11 = (bf16[20,2176]{1,0:T(8,128)(2,1)S(1)}, bf16[20,2176]{1,0:T(8,128)(2,1)S(1)}, u32[]{:S(2)}, u32[]{:S(2)}) collective-permute-start(bf16[20,2176]{1,0:T(8,128)(2,1)S(1)} %get-tuple-element.36), channel_id=1, source_target_pairs={{0,12},{4,8},{8,4},{12,0},{1,13},{5,9},{9,5},{13,1},{2,14},{6,10},... | collective-permute-start | bytes 261128 | tf_op jit(solution)/shard_map/ppermute | solution.py:20
  34.7 0.0 collective-permute-start.12
  34.7 1.7 %collective-permute-start.13 = (bf16[20,2176]{1,0:T(8,128)(2,1)S(1)}, bf16[20,2176]{1,0:T(8,128)(2,1)S(1)}, u32[]{:S(2)}, u32[]{:S(2)}) collective-permute-start(bf16[20,2176]{1,0:T(8,128)(2,1)S(1)} %get-tuple-element.38), channel_id=1, source_target_pairs={{0,4},{4,0},{8,12},{12,8},{1,5},{5,1},{9,13},{13,9},{2,6},{6,2},{1... | collective-permute-start | bytes 261128 | tf_op jit(solution)/shard_map/ppermute | solution.py:20
  36.4 2.3 %collective-permute-done.14.near = bf16[96,2048]{1,0:T(8,128)(2,1)S(1)} collective-permute-done((bf16[96,2048]{1,0:T(8,128)(2,1)S(1)}, bf16[96,2048]{1,0:T(8,128)(2,1)S(1)}, u32[]{:S(2)}, u32[]{:S(2)}) %collective-permute-start.14) | collective-permute-done | bytes 393248 | tf_op jit(solution)/shard_map/ppermute | solution.py:30
  38.8 3.1 %collective-permute-done.15.far = bf16[48,2048]{1,0:T(8,128)(2,1)S(1)} collective-permute-done((bf16[48,2048]{1,0:T(8,128)(2,1)S(1)}, bf16[48,2048]{1,0:T(8,128)(2,1)S(1)}, u32[]{:S(2)}, u32[]{:S(2)}) %collective-permute-start.15) | collective-permute-done | bytes 196640 | tf_op jit(solution)/shard_map/ppermute | solution.py:30
  41.8 0.1 shard_map.99.mine
  41.9 0.1 collective-permute-start.16
  42.0 0.0 collective-permute-done.11.refs_1_
  42.0 1.0 %collective-permute-done.12.refs_2_ = bf16[20,2176]{1,0:T(8,128)(2,1)S(1)} collective-permute-done((bf16[20,2176]{1,0:T(8,128)(2,1)S(1)}, bf16[20,2176]{1,0:T(8,128)(2,1)S(1)}, u32[]{:S(2)}, u32[]{:S(2)}) %collective-permute-start.12) | collective-permute-done | bytes 87072 | tf_op jit(solution)/shard_map/ppermute | solution.py:20
  43.0 0.0 collective-permute-done.13.refs_3_
  43.0 0.0 copy-done
  43.0 1.0 %shard_map.98 = (bf16[32,2048]{1,0:T(8,128)(2,1)}, bf16[2,32]{1,0:T(2,128)(2,1)}) custom-call(bf16[20,2176]{1,0:T(8,128)(2,1)S(1)} %get-tuple-element.35.refs_0_, bf16[20,2176]{1,0:T(8,128)(2,1)S(1)} %collective-permute-done.11.refs_1_, bf16[20,2176]{1,0:T(8,128)(2,1)S(1)} %collective-permute-done.12.refs_2_, ...), custom_call_target="tpu_custom_call" | custom-call | flops 8000000000 | bytes 479744 | tf_op jit(solution)/shard_map/pallas_call | solution.py:36
  44.0 0.0 collective-permute-done.16.theirs
  44.0 1.0 %shard_map.100 = f32[1,96,2048]{2,1,0:T(8,128)} custom-call(bf16[96,2048]{1,0:T(8,128)(2,1)S(1)} %shard_map.99.mine, bf16[96,2048]{1,0:T(8,128)(2,1)S(1)} %collective-permute-done.16.theirs), custom_call_target="tpu_custom_call" | custom-call | bytes 1572864 | tf_op jit(solution)/shard_map/pallas_call | solution.py:36
Async XLA Ops:
  2.3 10.9 %collective-permute-start.7 = (bf16[144,2048]{1,0:T(8,128)(2,1)S(1)}, bf16[144,2048]{1,0:T(8,128)(2,1)S(1)}, u32[]{:S(2)}, u32[]{:S(2)}) collective-permute-start(bf16[144,2048]{1,0:T(8,128)(2,1)S(1)} %get-tuple-element.28.refs_8_), channel_id=1, source_target_pairs={{0,1},{1,0},{2,3},{3,2},{16,18},{17,19},{18,16},{19,17},{4,5},{5,4... | collective-permute-start | bytes 1769480 | tf_op jit(solution)/shard_map/ppermute | solution.py:30
  5.3 20.2 %collective-permute-start.8 = (bf16[144,2048]{1,0:T(8,128)(2,1)S(1)}, bf16[144,2048]{1,0:T(8,128)(2,1)S(1)}, u32[]{:S(2)}, u32[]{:S(2)}) collective-permute-start(bf16[144,2048]{1,0:T(8,128)(2,1)S(1)} %get-tuple-element.29), channel_id=1, source_target_pairs={{0,1},{1,0},{2,3},{3,2},{16,18},{17,19},{18,16},{19,17},{4,5},{5,4... | collective-permute-start | bytes 1769480 | tf_op jit(solution)/shard_map/ppermute | solution.py:30
  5.4 6.3 %collective-permute-start = (bf16[40,2048]{1,0:T(8,128)(2,1)S(1)}, bf16[40,2048]{1,0:T(8,128)(2,1)S(1)}, u32[]{:S(2)}, u32[]{:S(2)}) collective-permute-start(bf16[40,2048]{1,0:T(8,128)(2,1)S(1)} %get-tuple-element.25), channel_id=1, source_target_pairs={{0,4},{4,0},{8,12},{12,8},{1,5},{5,1},{9,13},{13,9},{2,6},{6,2},{1... | collective-permute-start | bytes 491528 | tf_op jit(solution)/shard_map/ppermute | solution.py:20
  7.4 11.2 %collective-permute-start.1 = (bf16[40,2048]{1,0:T(8,128)(2,1)S(1)}, bf16[40,2048]{1,0:T(8,128)(2,1)S(1)}, u32[]{:S(2)}, u32[]{:S(2)}) collective-permute-start(bf16[40,2048]{1,0:T(8,128)(2,1)S(1)} %get-tuple-element.26), channel_id=1, source_target_pairs={{0,12},{4,8},{8,4},{12,0},{1,13},{5,9},{9,5},{13,1},{2,14},{6,10},... | collective-permute-start | bytes 491528 | tf_op jit(solution)/shard_map/ppermute | solution.py:20
  9.9 14.0 %collective-permute-start.2 = (bf16[40,2048]{1,0:T(8,128)(2,1)S(1)}, bf16[40,2048]{1,0:T(8,128)(2,1)S(1)}, u32[]{:S(2)}, u32[]{:S(2)}) collective-permute-start(bf16[40,2048]{1,0:T(8,128)(2,1)S(1)} %get-tuple-element.27), channel_id=1, source_target_pairs={{0,8},{4,12},{8,0},{12,4},{1,9},{5,13},{9,1},{13,5},{2,10},{6,14},... | collective-permute-start | bytes 491528 | tf_op jit(solution)/shard_map/ppermute | solution.py:20
  11.7 12.2 %collective-permute-start.3 = (bf16[40,2048]{1,0:T(8,128)(2,1)S(1)}, bf16[40,2048]{1,0:T(8,128)(2,1)S(1)}, u32[]{:S(2)}, u32[]{:S(2)}) collective-permute-start(bf16[40,2048]{1,0:T(8,128)(2,1)S(1)} %get-tuple-element.24.refs_0_), channel_id=1, source_target_pairs={{0,16},{16,0},{1,17},{17,1},{2,18},{18,2},{3,19},{19,3},{4,20},{20... | collective-permute-start | bytes 491528 | tf_op jit(solution)/shard_map/ppermute | solution.py:20
  13.2 14.3 %collective-permute-start.9 = (bf16[144,2048]{1,0:T(8,128)(2,1)S(1)}, bf16[144,2048]{1,0:T(8,128)(2,1)S(1)}, u32[]{:S(2)}, u32[]{:S(2)}) collective-permute-start(bf16[144,2048]{1,0:T(8,128)(2,1)S(1)} %collective-permute-done.7.refs_9_), channel_id=1, source_target_pairs={{0,2},{1,3},{2,0},{3,1},{16,17},{17,16},{18,19},{19,18},{4,6},{5,7... | collective-permute-start | bytes 1769480 | tf_op jit(solution)/shard_map/ppermute | solution.py:30
  18.6 5.8 %collective-permute-start.4 = (bf16[40,2048]{1,0:T(8,128)(2,1)S(1)}, bf16[40,2048]{1,0:T(8,128)(2,1)S(1)}, u32[]{:S(2)}, u32[]{:S(2)}) collective-permute-start(bf16[40,2048]{1,0:T(8,128)(2,1)S(1)} %collective-permute-done.refs_1_), channel_id=1, source_target_pairs={{0,16},{16,0},{1,17},{17,1},{2,18},{18,2},{3,19},{19,3},{4,20},{20... | collective-permute-start | bytes 491528 | tf_op jit(solution)/shard_map/ppermute | solution.py:20
  23.9 1.4 %collective-permute-start.5 = (bf16[40,2048]{1,0:T(8,128)(2,1)S(1)}, bf16[40,2048]{1,0:T(8,128)(2,1)S(1)}, u32[]{:S(2)}, u32[]{:S(2)}) collective-permute-start(bf16[40,2048]{1,0:T(8,128)(2,1)S(1)} %collective-permute-done.1.refs_2_), channel_id=1, source_target_pairs={{0,16},{16,0},{1,17},{17,1},{2,18},{18,2},{3,19},{19,3},{4,20},{20... | collective-permute-start | bytes 491528 | tf_op jit(solution)/shard_map/ppermute | solution.py:20
  23.9 1.6 %collective-permute-start.6 = (bf16[40,2048]{1,0:T(8,128)(2,1)S(1)}, bf16[40,2048]{1,0:T(8,128)(2,1)S(1)}, u32[]{:S(2)}, u32[]{:S(2)}) collective-permute-start(bf16[40,2048]{1,0:T(8,128)(2,1)S(1)} %collective-permute-done.2.refs_3_), channel_id=1, source_target_pairs={{0,16},{16,0},{1,17},{17,1},{2,18},{18,2},{3,19},{19,3},{4,20},{20... | collective-permute-start | bytes 491528 | tf_op jit(solution)/shard_map/ppermute | solution.py:20
  28.5 14.4 %copy-start = (bf16[32,2]{0,1:T(2,128)(2,1)S(1)}, bf16[32,2]{0,1:T(2,128)(2,1)}, u32[]{:S(2)}) copy-start(bf16[32,2]{0,1:T(2,128)(2,1)} %param.10) | copy-start | bytes 388
  28.6 3.3 %collective-permute-start.10 = (bf16[80,2176]{1,0:T(8,128)(2,1)S(1)}, bf16[80,2176]{1,0:T(8,128)(2,1)S(1)}, u32[]{:S(2)}, u32[]{:S(2)}) collective-permute-start(bf16[80,2176]{1,0:T(8,128)(2,1)S(1)} %get-tuple-element.34), channel_id=1, source_target_pairs={{0,16},{16,0},{1,17},{17,1},{2,18},{18,2},{3,19},{19,3},{4,20},{20... | collective-permute-start | bytes 1044488 | tf_op jit(solution)/shard_map/ppermute | solution.py:20
  28.9 9.9 %collective-permute-start.14 = (bf16[96,2048]{1,0:T(8,128)(2,1)S(1)}, bf16[96,2048]{1,0:T(8,128)(2,1)S(1)}, u32[]{:S(2)}, u32[]{:S(2)}) collective-permute-start(bf16[96,2048]{1,0:T(8,128)(2,1)S(1)} %get-tuple-element.43), channel_id=1, source_target_pairs={{0,1},{1,0},{2,3},{3,2},{16,18},{17,19},{18,16},{19,17},{4,5},{5,4... | collective-permute-start | bytes 1179656 | tf_op jit(solution)/shard_map/ppermute | solution.py:30
  30.4 11.4 %collective-permute-start.15 = (bf16[48,2048]{1,0:T(8,128)(2,1)S(1)}, bf16[48,2048]{1,0:T(8,128)(2,1)S(1)}, u32[]{:S(2)}, u32[]{:S(2)}) collective-permute-start(bf16[48,2048]{1,0:T(8,128)(2,1)S(1)} %get-tuple-element.44), channel_id=1, source_target_pairs={{0,3},{1,2},{2,1},{3,0},{16,19},{17,18},{18,17},{19,16},{4,7},{5,6... | collective-permute-start | bytes 589832 | tf_op jit(solution)/shard_map/ppermute | solution.py:30
  32.0 10.0 %collective-permute-start.11 = (bf16[20,2176]{1,0:T(8,128)(2,1)S(1)}, bf16[20,2176]{1,0:T(8,128)(2,1)S(1)}, u32[]{:S(2)}, u32[]{:S(2)}) collective-permute-start(bf16[20,2176]{1,0:T(8,128)(2,1)S(1)} %get-tuple-element.36), channel_id=1, source_target_pairs={{0,12},{4,8},{8,4},{12,0},{1,13},{5,9},{9,5},{13,1},{2,14},{6,10},... | collective-permute-start | bytes 261128 | tf_op jit(solution)/shard_map/ppermute | solution.py:20
  34.7 8.3 %collective-permute-start.12 = (bf16[20,2176]{1,0:T(8,128)(2,1)S(1)}, bf16[20,2176]{1,0:T(8,128)(2,1)S(1)}, u32[]{:S(2)}, u32[]{:S(2)}) collective-permute-start(bf16[20,2176]{1,0:T(8,128)(2,1)S(1)} %get-tuple-element.37), channel_id=1, source_target_pairs={{0,8},{4,12},{8,0},{12,4},{1,9},{5,13},{9,1},{13,5},{2,10},{6,14},... | collective-permute-start | bytes 261128 | tf_op jit(solution)/shard_map/ppermute | solution.py:20
  34.7 8.3 %collective-permute-start.13 = (bf16[20,2176]{1,0:T(8,128)(2,1)S(1)}, bf16[20,2176]{1,0:T(8,128)(2,1)S(1)}, u32[]{:S(2)}, u32[]{:S(2)}) collective-permute-start(bf16[20,2176]{1,0:T(8,128)(2,1)S(1)} %get-tuple-element.38), channel_id=1, source_target_pairs={{0,4},{4,0},{8,12},{12,8},{1,5},{5,1},{9,13},{13,9},{2,6},{6,2},{1... | collective-permute-start | bytes 261128 | tf_op jit(solution)/shard_map/ppermute | solution.py:20
  41.9 2.1 %collective-permute-start.16 = (bf16[96,2048]{1,0:T(8,128)(2,1)S(1)}, bf16[96,2048]{1,0:T(8,128)(2,1)S(1)}, u32[]{:S(2)}, u32[]{:S(2)}) collective-permute-start(bf16[96,2048]{1,0:T(8,128)(2,1)S(1)} %shard_map.99.mine), channel_id=1, source_target_pairs={{0,16},{16,0},{1,17},{17,1},{2,18},{18,2},{3,19},{19,3},{4,20},{20... | collective-permute-start | bytes 1179656 | tf_op jit(solution)/shard_map/ppermute | solution.py:20

commit v8 on v7

--- a/solution.py
+++ b/solution.py
@@ -48,26 +48,32 @@
     return lax.broadcasted_iota(jnp.int32, shape, dim)
 
 
-def dispatch_kernel(experts, cap, chunk_count, *refs):
-    small, (gate, up, down), refs = refs[:4], refs[4:7], refs[7:]
-    chunks, (slot_out, *held, sems) = refs[:chunk_count], refs[chunk_count:]
-    packed, held = held[:2], held[2:]
-    hidden = packed[0].shape[0] // 3
+def pack_kernel(gate, up, down, first, second, sems):
+    hidden = first.shape[0] // 3
     rep = lax.axis_index("rep")
-    loads = [pltpu.make_async_copy(*pair, sems.at[i]) for i, pair in enumerate(zip(small, held))]
-    packs = []
-    for j, half in enumerate((rep, 1 - rep)):
+    copies = []
+    for j, (half, packed) in enumerate(((rep, first), (1 - rep, second))):
         rows = pl.ds(pl.multiple_of(half * hidden, hidden), hidden)
-        packs += [
-            pltpu.make_async_copy(weight.at[0, rows], packed[j].at[pl.ds(i * hidden, hidden)], sems.at[4 + 3 * j + i])
+        copies += [
+            pltpu.make_async_copy(weight.at[0, rows], packed.at[pl.ds(i * hidden, hidden)], sems.at[3 * j + i])
             for i, weight in enumerate((gate, up, down))
         ]
-    for copy in loads + packs:
+    for copy in copies:
         copy.start()
+    for copy in copies:
+        copy.wait()
+
+
+def dispatch_kernel(experts, cap, chunk_count, *refs):
+    given, refs = refs[:4], refs[4:]
+    chunks, (slot_out, ids, route_weight, tokens, upstream, sems) = refs[:chunk_count], refs[chunk_count:]
+    held = (ids, route_weight, tokens, upstream)
+    loads = [pltpu.make_async_copy(*pair, sems.at[i]) for i, pair in enumerate(zip(given, held))]
     for copy in loads:
+        copy.start()
+    for copy in loads[:2]:
         copy.wait()
 
-    tokens, upstream, ids, route_weight = held
     top, tok_dev = ids.shape
     rows = experts * cap // chunk_count
     me = lax.axis_index("ep")
@@ -96,38 +102,40 @@
         take_x += here_x
         take_dy += here_dy
         scale += here_x + here_dy * route_weight[k : k + 1, :].astype(f32)
-    picked = dot(take_x.astype(bf16), tokens[...], (1, 0)) + dot(take_dy.astype(bf16), upstream[...], (1, 0))
-    picked = picked * jnp.sum(scale, axis=1, keepdims=True)
+    scale = jnp.sum(scale, axis=1, keepdims=True)
+    take_x, take_dy = take_x.astype(bf16), take_dy.astype(bf16)
+    for copy in loads[2:]:
+        copy.wait()
+    picked = dot(take_x, tokens[...], (1, 0)) + dot(take_dy, upstream[...], (1, 0))
+    picked = picked * scale
     for c in range(chunk_count):
         chunks[c][...] = picked[2 * rows * c : 2 * rows * (c + 1)].astype(bf16)
-    for copy in packs:
-        copy.wait()
 
 
 def expert_math(x_rows, d_rows, pieces):
-    acts, mixed = [], []
-    prob = 0.0
-    for piece in pieces:
-        hidden = piece.shape[0] // 3
-        pre = dot(x_rows, piece[: 2 * hidden], (1, 1))
-        d_act = dot(d_rows, piece[2 * hidden :], (1, 1))
-        gate_pre, up_pre = pre[:, :hidden], pre[:, hidden:]
-        sig = jax.nn.sigmoid(gate_pre)
-        silu = gate_pre * sig
-        act = silu * up_pre
-        prob = prob + jnp.sum(act * d_act, axis=1, keepdims=True)
-        acts.append(act)
-        mixed += [d_act * up_pre * sig * (1.0 + gate_pre * (1.0 - sig)), d_act * silu]
-    mixed = jnp.concatenate(mixed, axis=1).astype(bf16)
-    acts = jnp.concatenate(acts, axis=1).astype(bf16)
-    gates = jnp.concatenate([piece[: 2 * hidden] for piece in pieces])
-    return dot(mixed, gates, (1, 0)), prob, dot(acts, d_rows, (0, 0))
+    hidden = pieces[0].shape[0] // 3
+    gate, up, down = [[piece[i * hidden : (i + 1) * hidden] for piece in pieces] for i in range(3)]
+    mixers = jnp.concatenate(gate + up)
+    pre = dot(x_rows, mixers, (1, 1))
+    d_act = dot(d_rows, jnp.concatenate(down), (1, 1))
+    gate_pre, up_pre = pre[:, : hidden * len(pieces)], pre[:, hidden * len(pieces) :]
+    sig = jax.nn.sigmoid(gate_pre)
+    silu = gate_pre * sig
+    act = silu * up_pre
+    prob = jnp.sum(act * d_act, axis=1, keepdims=True)
+    d_gate = d_act * up_pre * sig * (1.0 + gate_pre * (1.0 - sig))
+    d_pre = jnp.concatenate([d_gate, d_act * silu], axis=1).astype(bf16)
+    return dot(d_pre, mixers, (1, 0)), prob, dot(act.astype(bf16), d_rows, (0, 0))
+
+
+def join_kernel(one, two, out):
+    out[...] = jnp.concatenate([one[...].astype(f32), two[...].astype(f32)]).astype(bf16)
 
 
 def early_kernel(chunk_count, *refs):
     chunks, (*pieces, x_out, d_out, dx_out, grad_own, grad_near) = refs[:chunk_count], refs[chunk_count:]
     rows = chunks[0].shape[0] // 2
-    values = [c[...].astype(f32) for c in chunks]
+    values = [c[i : i + 2 * rows] for c in [c[...].astype(f32) for c in chunks] for i in range(0, c.shape[0], 2 * rows)]
     x_out[...] = jnp.concatenate([v[:rows] for v in values]).astype(bf16)
     d_out[...] = jnp.concatenate([v[rows:] for v in values]).astype(bf16)
     dx, prob, grad = expert_math(x_out[...], d_out[...], pieces)
@@ -203,15 +211,20 @@
     shape = jax.ShapeDtypeStruct
     in_hbm = pl.BlockSpec(memory_space=pltpu.HBM)
 
-    small = [tokens, upstream, expert_ids.T, route_weight.T]
-    *chunks, slot, first, second = kernel_call(
+    first, second = kernel_call(
+        pack_kernel,
+        [pltpu.with_memory_space_constraint(a, pltpu.HBM) for a in (gate_weight, up_weight, down_weight)],
+        [shape((3 * hidden, width), bf16)] * 2,
+        in_specs=[in_hbm] * 3,
+        scratch_shapes=[pltpu.SemaphoreType.DMA((6,))],
+    )
+    given = [expert_ids.T, route_weight.T, tokens, upstream]
+    *chunks, slot = kernel_call(
         functools.partial(dispatch_kernel, experts, cap, chunk_count),
-        [pltpu.with_memory_space_constraint(a, pltpu.HBM) for a in small + [gate_weight, up_weight, down_weight]],
-        [shape((2 * rows, width), bf16)] * chunk_count
-        + [shape((top, tok_dev), jnp.int32)]
-        + [shape((3 * hidden, width), bf16)] * 2,
-        in_specs=[in_hbm] * 7,
-        scratch_shapes=[pltpu.VMEM(a.shape, a.dtype) for a in small] + [pltpu.SemaphoreType.DMA((10,))],
+        [pltpu.with_memory_space_constraint(a, pltpu.HBM) for a in given],
+        [shape((2 * rows, width), bf16)] * chunk_count + [shape((top, tok_dev), jnp.int32)],
+        in_specs=[in_hbm] * 4,
+        scratch_shapes=[pltpu.VMEM(a.shape, a.dtype) for a in given] + [pltpu.SemaphoreType.DMA((4,))],
     )
 
     along, across = (1, 2), (2, 1)
@@ -224,11 +237,14 @@
         moved = chunks[0].reshape(2, experts, cap, width)
         moved = lax.all_to_all(moved, "ep", split_axis=1, concat_axis=1, tiled=True)
         chunks = [moved.reshape(2 * rows, width)]
-    chunks = chunks + [swap(c, "rep", 1) for c in chunks]
+    early = chunks[:2]
+    if len(early) > 1:
+        early = kernel_call(join_kernel, early, [shape((4 * rows, width), bf16)])
+    chunks = chunks + [swap(c, "rep", 1) for c in [*early, *chunks[2:]]]
 
     wide = width + LANES
     x_rows, d_rows, dx, grad_own, grad_near = kernel_call(
-        functools.partial(early_kernel, 2 * chunk_count),
+        functools.partial(early_kernel, len(chunks)),
         chunks + [first, *near],
         [shape((2 * slots, width), bf16)] * 2
         + [shape((2 * slots, wide), f32), shape((hidden, width), f32), shape((2 * hidden, width), bf16)],

time: 45.1 us -> 45.6 us (1.011)
  Pallas kernels: 6.79 us -> 7.63 us
  starting transfers between devices: 18.1 us -> 17.4 us
    ppermute x12 -> x11, waiting for transfers between devices: 12.5 us -> 14.3 us  [swap(): lax.ppermute(value, axis, [(i, i ^ mask) for i in range(lax.axis_size(axi...]
    ppermute x5, waiting for transfers between devices: 6.87 us -> 5.41 us  [swap_by_core(): return lax.ppermute(value, ('rep', 'dp'), pairs)]
    pallas_call x7 -> x9, Pallas kernels: 6.79 us -> 7.63 us  [kernel_call(): pl.pallas_call(body, out_shape=outputs, in_specs=kwargs.pop('in_specs', [...]
    ppermute x12 -> x11, starting transfers between devices: 10 us -> 9.5 us  [swap(): lax.ppermute(value, axis, [(i, i ^ mask) for i in range(lax.axis_size(axi...]
  transfers between devices with their start and end apart: 17 -> 16, of which waited for: 9 -> 7; matrix products, arithmetic and copies ran while one was open for 0% -> 0% of each run, Pallas kernels for 7% -> 9%
where the time goes in v8:
time: 45.6 us; the launch traced here: 45.4 us
  waiting for transfers between devices  19.7 us (43%)
  starting transfers between devices  17.4 us (38%)
  Pallas kernels  7.63 us (17%)
  between operations  0.73 us (2%)
    ppermute x11, waiting for transfers between devices, swap(): lax.ppermute(value, axis, [(i, i ^ mask) for i in range(lax.axis_size(axi...  14.3 us
    ppermute x11, starting transfers between devices, swap(): lax.ppermute(value, axis, [(i, i ^ mask) for i in range(lax.axis_size(axi...  9.5 us
    ppermute x5, starting transfers between devices, swap_by_core(): return lax.ppermute(value, ('rep', 'dp'), pairs)  7.88 us
    pallas_call x9, Pallas kernels, kernel_call(): pl.pallas_call(body, out_shape=outputs, in_specs=kwargs.pop('in_specs', [...  7.63 us
    ppermute x5, waiting for transfers between devices, swap_by_core(): return lax.ppermute(value, ('rep', 'dp'), pairs)  5.41 us
  transfers between devices with their start and end apart: 16, of which 7 were waited for; matrix products, arithmetic and copies ran while one was open for 0% of the time, Pallas kernels for 9%

profile of v8, /device:TPU:0, one launch (start us, length us, event | category | flops | bytes accessed | tf_op | source)
XLA Modules:
  0.0 45.4 jit_solution(15880757530250919789)
XLA Ops:
  0.6 1.4 %shard_map.96 = (bf16[144,2048]{1,0:T(8,128)(2,1)S(1)}, bf16[144,2048]{1,0:T(8,128)(2,1)S(1)}) custom-call(bf16[1,96,2048]{2,1,0:T(8,128)(2,1)} %gate.1, bf16[1,96,2048]{2,1,0:T(8,128)(2,1)} %up.1, bf16[1,96,2048]{2,1,0:T(8,128)(2,1)} %down.1), custom_call_target="tpu_custom_call" | custom-call | bytes 2359296 | tf_op jit(solution)/shard_map/pallas_call | solution.py:36
  2.0 3.0 %collective-permute-start.6 = (bf16[144,2048]{1,0:T(8,128)(2,1)S(1)}, bf16[144,2048]{1,0:T(8,128)(2,1)S(1)}, u32[]{:S(2)}, u32[]{:S(2)}) collective-permute-start(bf16[144,2048]{1,0:T(8,128)(2,1)S(1)} %get-tuple-element.28.refs_7_), channel_id=1, source_target_pairs={{0,1},{1,0},{2,3},{3,2},{16,18},{17,19},{18,16},{19,17},{4,5},{5,4... | collective-permute-start | bytes 1769480 | tf_op jit(solution)/shard_map/ppermute | solution.py:30
  5.0 0.1 collective-permute-start.7
  5.1 1.5 %shard_map.94 = (bf16[40,2048]{1,0:T(8,128)(2,1)S(1)}, bf16[40,2048]{1,0:T(8,128)(2,1)S(1)}, bf16[40,2048]{1,0:T(8,128)(2,1)S(1)}, bf16[40,2048]{1,0:T(8,128)(2,1)S(1)}, s32[2,32]{1,0:T(2,128)S(1)}) custom-call(s32[2,32]{1,0:T(2,128)} %bitcast.5, bf16[2,32]{1,0:T(2,128)(2,1)} %bitcast.3, bf16[32,2048]{1,0:T(8,128)(2,1)} %refs_2_.1, bf16[32,2048]{1,0:T(8,128)(2,1)} %refs_3_.1), custom_call_target="tpu_custom_call" | custom-call | bytes 918144 | tf_op jit(solution)/shard_map/pallas_call | solution.py:36
  6.6 2.1 %collective-permute-start = (bf16[40,2048]{1,0:T(8,128)(2,1)S(1)}, bf16[40,2048]{1,0:T(8,128)(2,1)S(1)}, u32[]{:S(2)}, u32[]{:S(2)}) collective-permute-start(bf16[40,2048]{1,0:T(8,128)(2,1)S(1)} %get-tuple-element.25), channel_id=1, source_target_pairs={{0,4},{4,0},{8,12},{12,8},{1,5},{5,1},{9,13},{13,9},{2,6},{6,2},{1... | collective-permute-start | bytes 491528 | tf_op jit(solution)/shard_map/ppermute | solution.py:20
  8.7 2.5 %collective-permute-start.1 = (bf16[40,2048]{1,0:T(8,128)(2,1)S(1)}, bf16[40,2048]{1,0:T(8,128)(2,1)S(1)}, u32[]{:S(2)}, u32[]{:S(2)}) collective-permute-start(bf16[40,2048]{1,0:T(8,128)(2,1)S(1)} %get-tuple-element.26), channel_id=1, source_target_pairs={{0,12},{4,8},{8,4},{12,0},{1,13},{5,9},{9,5},{13,1},{2,14},{6,10},... | collective-permute-start | bytes 491528 | tf_op jit(solution)/shard_map/ppermute | solution.py:20
  11.2 0.1 collective-permute-start.2
  11.3 1.7 %collective-permute-done.two.refs_1_ = bf16[40,2048]{1,0:T(8,128)(2,1)S(1)} collective-permute-done((bf16[40,2048]{1,0:T(8,128)(2,1)S(1)}, bf16[40,2048]{1,0:T(8,128)(2,1)S(1)}, u32[]{:S(2)}, u32[]{:S(2)}) %collective-permute-start) | collective-permute-done | bytes 163872 | tf_op jit(solution)/shard_map/ppermute | solution.py:20
  13.0 0.1 collective-permute-start.3
  13.1 0.0 collective-permute-done.6.refs_8_
  13.1 1.8 %collective-permute-start.8 = (bf16[144,2048]{1,0:T(8,128)(2,1)S(1)}, bf16[144,2048]{1,0:T(8,128)(2,1)S(1)}, u32[]{:S(2)}, u32[]{:S(2)}) collective-permute-start(bf16[144,2048]{1,0:T(8,128)(2,1)S(1)} %collective-permute-done.6.refs_8_), channel_id=1, source_target_pairs={{0,2},{1,3},{2,0},{3,1},{16,17},{17,16},{18,19},{19,18},{4,6},{5,7... | collective-permute-start | bytes 1769480 | tf_op jit(solution)/shard_map/ppermute | solution.py:30
  15.0 5.0 %collective-permute-done.1.refs_2_ = bf16[40,2048]{1,0:T(8,128)(2,1)S(1)} collective-permute-done((bf16[40,2048]{1,0:T(8,128)(2,1)S(1)}, bf16[40,2048]{1,0:T(8,128)(2,1)S(1)}, u32[]{:S(2)}, u32[]{:S(2)}) %collective-permute-start.1) | collective-permute-done | bytes 163872 | tf_op jit(solution)/shard_map/ppermute | solution.py:20
  19.9 0.0 collective-permute-start.4
  19.9 5.3 %collective-permute-done.2.refs_3_ = bf16[40,2048]{1,0:T(8,128)(2,1)S(1)} collective-permute-done((bf16[40,2048]{1,0:T(8,128)(2,1)S(1)}, bf16[40,2048]{1,0:T(8,128)(2,1)S(1)}, u32[]{:S(2)}, u32[]{:S(2)}) %collective-permute-start.2) | collective-permute-done | bytes 163872 | tf_op jit(solution)/shard_map/ppermute | solution.py:20
  25.2 0.0 collective-permute-start.5
  25.2 0.0 collective-permute-done.4.refs_5_
  25.2 1.4 %collective-permute-done.5.refs_6_ = bf16[40,2048]{1,0:T(8,128)(2,1)S(1)} collective-permute-done((bf16[40,2048]{1,0:T(8,128)(2,1)S(1)}, bf16[40,2048]{1,0:T(8,128)(2,1)S(1)}, u32[]{:S(2)}, u32[]{:S(2)}) %collective-permute-start.5) | collective-permute-done | bytes 163872 | tf_op jit(solution)/shard_map/ppermute | solution.py:20
  26.6 0.0 collective-permute-done.3.refs_4_
  26.6 0.0 collective-permute-done.7.refs_9_
  26.6 1.6 %shard_map.97 = (bf16[160,2048]{1,0:T(8,128)(2,1)S(1)}, bf16[160,2048]{1,0:T(8,128)(2,1)S(1)}, f32[160,2176]{1,0:T(8,128)S(1)}, f32[48,2048]{1,0:T(8,128)S(1)}, bf16[96,2048]{1,0:T(8,128)(2,1)S(1)}) custom-call(bf16[40,2048]{1,0:T(8,128)(2,1)S(1)} %get-tuple-element.24.one.refs_0_, bf16[40,2048]{1,0:T(8,128)(2,1)S(1)} %collective-permute-done.two.refs_1_, ...), custom_call_target="tpu_custom_call" | custom-call | flops 4000000000 | bytes 6569984 | tf_op jit(solution)/shard_map/pallas_call | solution.py:36
  28.2 0.0 collective-permute-done.8.far
  28.2 1.0 %shard_map.98 = (f32[80,2176]{1,0:T(8,128)S(1)}, bf16[80,2176]{1,0:T(8,128)(2,1)S(1)}, bf16[48,2048]{1,0:T(8,128)(2,1)S(1)}) custom-call(bf16[160,2048]{1,0:T(8,128)(2,1)S(1)} %get-tuple-element.30.x_ref, bf16[160,2048]{1,0:T(8,128)(2,1)S(1)} %get-tuple-element.31.d_ref, f32[160,2176]{1,0:T(8,128)S(1)} %get-tuple-element.32.dx_ref, ...), custom_call_target="tpu_custom_call" | custom-call | bytes 4534272 | tf_op jit(solution)/shard_map/pallas_call | solution.py:36
  29.2 0.0 copy-start
  29.2 0.2 collective-permute-start.9
  29.4 1.5 %collective-permute-start.13 = (bf16[96,2048]{1,0:T(8,128)(2,1)S(1)}, bf16[96,2048]{1,0:T(8,128)(2,1)S(1)}, u32[]{:S(2)}, u32[]{:S(2)}) collective-permute-start(bf16[96,2048]{1,0:T(8,128)(2,1)S(1)} %get-tuple-element.43), channel_id=1, source_target_pairs={{0,1},{1,0},{2,3},{3,2},{16,18},{17,19},{18,16},{19,17},{4,5},{5,4... | collective-permute-start | bytes 1179656 | tf_op jit(solution)/shard_map/ppermute | solution.py:30
  30.9 1.5 %collective-permute-start.14 = (bf16[48,2048]{1,0:T(8,128)(2,1)S(1)}, bf16[48,2048]{1,0:T(8,128)(2,1)S(1)}, u32[]{:S(2)}, u32[]{:S(2)}) collective-permute-start(bf16[48,2048]{1,0:T(8,128)(2,1)S(1)} %get-tuple-element.44), channel_id=1, source_target_pairs={{0,3},{1,2},{2,1},{3,0},{16,19},{17,18},{18,17},{19,16},{4,7},{5,6... | collective-permute-start | bytes 589832 | tf_op jit(solution)/shard_map/ppermute | solution.py:30
  32.4 0.0 collective-permute-done.9.got
  32.4 0.1 shard_map.99
  32.5 2.7 %collective-permute-start.10 = (bf16[20,2176]{1,0:T(8,128)(2,1)S(1)}, bf16[20,2176]{1,0:T(8,128)(2,1)S(1)}, u32[]{:S(2)}, u32[]{:S(2)}) collective-permute-start(bf16[20,2176]{1,0:T(8,128)(2,1)S(1)} %get-tuple-element.36), channel_id=1, source_target_pairs={{0,12},{4,8},{8,4},{12,0},{1,13},{5,9},{9,5},{13,1},{2,14},{6,10},... | collective-permute-start | bytes 261128 | tf_op jit(solution)/shard_map/ppermute | solution.py:20
  35.2 0.0 collective-permute-start.11
  35.3 1.7 %collective-permute-start.12 = (bf16[20,2176]{1,0:T(8,128)(2,1)S(1)}, bf16[20,2176]{1,0:T(8,128)(2,1)S(1)}, u32[]{:S(2)}, u32[]{:S(2)}) collective-permute-start(bf16[20,2176]{1,0:T(8,128)(2,1)S(1)} %get-tuple-element.38), channel_id=1, source_target_pairs={{0,4},{4,0},{8,12},{12,8},{1,5},{5,1},{9,13},{13,9},{2,6},{6,2},{1... | collective-permute-start | bytes 261128 | tf_op jit(solution)/shard_map/ppermute | solution.py:20
  37.0 2.3 %collective-permute-done.13.near = bf16[96,2048]{1,0:T(8,128)(2,1)S(1)} collective-permute-done((bf16[96,2048]{1,0:T(8,128)(2,1)S(1)}, bf16[96,2048]{1,0:T(8,128)(2,1)S(1)}, u32[]{:S(2)}, u32[]{:S(2)}) %collective-permute-start.13) | collective-permute-done | bytes 393248 | tf_op jit(solution)/shard_map/ppermute | solution.py:30
  39.3 3.1 %collective-permute-done.14.far = bf16[48,2048]{1,0:T(8,128)(2,1)S(1)} collective-permute-done((bf16[48,2048]{1,0:T(8,128)(2,1)S(1)}, bf16[48,2048]{1,0:T(8,128)(2,1)S(1)}, u32[]{:S(2)}, u32[]{:S(2)}) %collective-permute-start.14) | collective-permute-done | bytes 196640 | tf_op jit(solution)/shard_map/ppermute | solution.py:30
  42.4 0.1 shard_map.101.mine
  42.5 0.1 collective-permute-start.15
  42.5 0.0 collective-permute-done.10.refs_1_
  42.6 0.9 %collective-permute-done.11.refs_2_ = bf16[20,2176]{1,0:T(8,128)(2,1)S(1)} collective-permute-done((bf16[20,2176]{1,0:T(8,128)(2,1)S(1)}, bf16[20,2176]{1,0:T(8,128)(2,1)S(1)}, u32[]{:S(2)}, u32[]{:S(2)}) %collective-permute-start.11) | collective-permute-done | bytes 87072 | tf_op jit(solution)/shard_map/ppermute | solution.py:20
  43.5 0.0 collective-permute-done.12.refs_3_
  43.5 0.0 copy-done
  43.5 1.0 %shard_map.100 = (bf16[32,2048]{1,0:T(8,128)(2,1)}, bf16[2,32]{1,0:T(2,128)(2,1)}) custom-call(bf16[20,2176]{1,0:T(8,128)(2,1)S(1)} %get-tuple-element.35.refs_0_, bf16[20,2176]{1,0:T(8,128)(2,1)S(1)} %collective-permute-done.10.refs_1_, bf16[20,2176]{1,0:T(8,128)(2,1)S(1)} %collective-permute-done.11.refs_2_, ...), custom_call_target="tpu_custom_call" | custom-call | flops 8000000000 | bytes 479744 | tf_op jit(solution)/shard_map/pallas_call | solution.py:36
  44.5 0.0 collective-permute-done.15.theirs
  44.5 1.0 %shard_map.102 = f32[1,96,2048]{2,1,0:T(8,128)} custom-call(bf16[96,2048]{1,0:T(8,128)(2,1)S(1)} %shard_map.101.mine, bf16[96,2048]{1,0:T(8,128)(2,1)S(1)} %collective-permute-done.15.theirs), custom_call_target="tpu_custom_call" | custom-call | bytes 1572864 | tf_op jit(solution)/shard_map/pallas_call | solution.py:36
  (1 shorter events, 0.0 us)
Async XLA Ops:
  2.0 11.1 %collective-permute-start.6 = (bf16[144,2048]{1,0:T(8,128)(2,1)S(1)}, bf16[144,2048]{1,0:T(8,128)(2,1)S(1)}, u32[]{:S(2)}, u32[]{:S(2)}) collective-permute-start(bf16[144,2048]{1,0:T(8,128)(2,1)S(1)} %get-tuple-element.28.refs_7_), channel_id=1, source_target_pairs={{0,1},{1,0},{2,3},{3,2},{16,18},{17,19},{18,16},{19,17},{4,5},{5,4... | collective-permute-start | bytes 1769480 | tf_op jit(solution)/shard_map/ppermute | solution.py:30
  5.0 21.6 %collective-permute-start.7 = (bf16[144,2048]{1,0:T(8,128)(2,1)S(1)}, bf16[144,2048]{1,0:T(8,128)(2,1)S(1)}, u32[]{:S(2)}, u32[]{:S(2)}) collective-permute-start(bf16[144,2048]{1,0:T(8,128)(2,1)S(1)} %get-tuple-element.29), channel_id=1, source_target_pairs={{0,1},{1,0},{2,3},{3,2},{16,18},{17,19},{18,16},{19,17},{4,5},{5,4... | collective-permute-start | bytes 1769480 | tf_op jit(solution)/shard_map/ppermute | solution.py:30
  6.6 6.4 %collective-permute-start = (bf16[40,2048]{1,0:T(8,128)(2,1)S(1)}, bf16[40,2048]{1,0:T(8,128)(2,1)S(1)}, u32[]{:S(2)}, u32[]{:S(2)}) collective-permute-start(bf16[40,2048]{1,0:T(8,128)(2,1)S(1)} %get-tuple-element.25), channel_id=1, source_target_pairs={{0,4},{4,0},{8,12},{12,8},{1,5},{5,1},{9,13},{13,9},{2,6},{6,2},{1... | collective-permute-start | bytes 491528 | tf_op jit(solution)/shard_map/ppermute | solution.py:20
  8.7 11.2 %collective-permute-start.1 = (bf16[40,2048]{1,0:T(8,128)(2,1)S(1)}, bf16[40,2048]{1,0:T(8,128)(2,1)S(1)}, u32[]{:S(2)}, u32[]{:S(2)}) collective-permute-start(bf16[40,2048]{1,0:T(8,128)(2,1)S(1)} %get-tuple-element.26), channel_id=1, source_target_pairs={{0,12},{4,8},{8,4},{12,0},{1,13},{5,9},{9,5},{13,1},{2,14},{6,10},... | collective-permute-start | bytes 491528 | tf_op jit(solution)/shard_map/ppermute | solution.py:20
  11.2 14.0 %collective-permute-start.2 = (bf16[40,2048]{1,0:T(8,128)(2,1)S(1)}, bf16[40,2048]{1,0:T(8,128)(2,1)S(1)}, u32[]{:S(2)}, u32[]{:S(2)}) collective-permute-start(bf16[40,2048]{1,0:T(8,128)(2,1)S(1)} %get-tuple-element.27), channel_id=1, source_target_pairs={{0,8},{4,12},{8,0},{12,4},{1,9},{5,13},{9,1},{13,5},{2,10},{6,14},... | collective-permute-start | bytes 491528 | tf_op jit(solution)/shard_map/ppermute | solution.py:20
  13.0 13.6 %collective-permute-start.3 = (bf16[80,2048]{1,0:T(8,128)(2,1)S(1)}, bf16[80,2048]{1,0:T(8,128)(2,1)S(1)}, u32[]{:S(2)}, u32[]{:S(2)}) collective-permute-start(bf16[80,2048]{1,0:T(8,128)(2,1)S(1)} %shard_map.95), channel_id=1, source_target_pairs={{0,16},{16,0},{1,17},{17,1},{2,18},{18,2},{3,19},{19,3},{4,20},{20... | collective-permute-start | bytes 983048 | tf_op jit(solution)/shard_map/ppermute | solution.py:20
  13.1 15.1 %collective-permute-start.8 = (bf16[144,2048]{1,0:T(8,128)(2,1)S(1)}, bf16[144,2048]{1,0:T(8,128)(2,1)S(1)}, u32[]{:S(2)}, u32[]{:S(2)}) collective-permute-start(bf16[144,2048]{1,0:T(8,128)(2,1)S(1)} %collective-permute-done.6.refs_8_), channel_id=1, source_target_pairs={{0,2},{1,3},{2,0},{3,1},{16,17},{17,16},{18,19},{19,18},{4,6},{5,7... | collective-permute-start | bytes 1769480 | tf_op jit(solution)/shard_map/ppermute | solution.py:30
  19.9 5.3 %collective-permute-start.4 = (bf16[40,2048]{1,0:T(8,128)(2,1)S(1)}, bf16[40,2048]{1,0:T(8,128)(2,1)S(1)}, u32[]{:S(2)}, u32[]{:S(2)}) collective-permute-start(bf16[40,2048]{1,0:T(8,128)(2,1)S(1)} %collective-permute-done.1.refs_2_), channel_id=1, source_target_pairs={{0,16},{16,0},{1,17},{17,1},{2,18},{18,2},{3,19},{19,3},{4,20},{20... | collective-permute-start | bytes 491528 | tf_op jit(solution)/shard_map/ppermute | solution.py:20
  25.2 1.4 %collective-permute-start.5 = (bf16[40,2048]{1,0:T(8,128)(2,1)S(1)}, bf16[40,2048]{1,0:T(8,128)(2,1)S(1)}, u32[]{:S(2)}, u32[]{:S(2)}) collective-permute-start(bf16[40,2048]{1,0:T(8,128)(2,1)S(1)} %collective-permute-done.2.refs_3_), channel_id=1, source_target_pairs={{0,16},{16,0},{1,17},{17,1},{2,18},{18,2},{3,19},{19,3},{4,20},{20... | collective-permute-start | bytes 491528 | tf_op jit(solution)/shard_map/ppermute | solution.py:20
  29.2 14.3 %copy-start = (bf16[32,2]{0,1:T(2,128)(2,1)S(1)}, bf16[32,2]{0,1:T(2,128)(2,1)}, u32[]{:S(2)}) copy-start(bf16[32,2]{0,1:T(2,128)(2,1)} %param.10) | copy-start | bytes 388
  29.2 3.2 %collective-permute-start.9 = (bf16[80,2176]{1,0:T(8,128)(2,1)S(1)}, bf16[80,2176]{1,0:T(8,128)(2,1)S(1)}, u32[]{:S(2)}, u32[]{:S(2)}) collective-permute-start(bf16[80,2176]{1,0:T(8,128)(2,1)S(1)} %get-tuple-element.34), channel_id=1, source_target_pairs={{0,16},{16,0},{1,17},{17,1},{2,18},{18,2},{3,19},{19,3},{4,20},{20... | collective-permute-start | bytes 1044488 | tf_op jit(solution)/shard_map/ppermute | solution.py:20
  29.4 9.9 %collective-permute-start.13 = (bf16[96,2048]{1,0:T(8,128)(2,1)S(1)}, bf16[96,2048]{1,0:T(8,128)(2,1)S(1)}, u32[]{:S(2)}, u32[]{:S(2)}) collective-permute-start(bf16[96,2048]{1,0:T(8,128)(2,1)S(1)} %get-tuple-element.43), channel_id=1, source_target_pairs={{0,1},{1,0},{2,3},{3,2},{16,18},{17,19},{18,16},{19,17},{4,5},{5,4... | collective-permute-start | bytes 1179656 | tf_op jit(solution)/shard_map/ppermute | solution.py:30
  30.9 11.4 %collective-permute-start.14 = (bf16[48,2048]{1,0:T(8,128)(2,1)S(1)}, bf16[48,2048]{1,0:T(8,128)(2,1)S(1)}, u32[]{:S(2)}, u32[]{:S(2)}) collective-permute-start(bf16[48,2048]{1,0:T(8,128)(2,1)S(1)} %get-tuple-element.44), channel_id=1, source_target_pairs={{0,3},{1,2},{2,1},{3,0},{16,19},{17,18},{18,17},{19,16},{4,7},{5,6... | collective-permute-start | bytes 589832 | tf_op jit(solution)/shard_map/ppermute | solution.py:30
  32.5 10.0 %collective-permute-start.10 = (bf16[20,2176]{1,0:T(8,128)(2,1)S(1)}, bf16[20,2176]{1,0:T(8,128)(2,1)S(1)}, u32[]{:S(2)}, u32[]{:S(2)}) collective-permute-start(bf16[20,2176]{1,0:T(8,128)(2,1)S(1)} %get-tuple-element.36), channel_id=1, source_target_pairs={{0,12},{4,8},{8,4},{12,0},{1,13},{5,9},{9,5},{13,1},{2,14},{6,10},... | collective-permute-start | bytes 261128 | tf_op jit(solution)/shard_map/ppermute | solution.py:20
  35.2 8.2 %collective-permute-start.11 = (bf16[20,2176]{1,0:T(8,128)(2,1)S(1)}, bf16[20,2176]{1,0:T(8,128)(2,1)S(1)}, u32[]{:S(2)}, u32[]{:S(2)}) collective-permute-start(bf16[20,2176]{1,0:T(8,128)(2,1)S(1)} %get-tuple-element.37), channel_id=1, source_target_pairs={{0,8},{4,12},{8,0},{12,4},{1,9},{5,13},{9,1},{13,5},{2,10},{6,14},... | collective-permute-start | bytes 261128 | tf_op jit(solution)/shard_map/ppermute | solution.py:20
  35.3 8.2 %collective-permute-start.12 = (bf16[20,2176]{1,0:T(8,128)(2,1)S(1)}, bf16[20,2176]{1,0:T(8,128)(2,1)S(1)}, u32[]{:S(2)}, u32[]{:S(2)}) collective-permute-start(bf16[20,2176]{1,0:T(8,128)(2,1)S(1)} %get-tuple-element.38), channel_id=1, source_target_pairs={{0,4},{4,0},{8,12},{12,8},{1,5},{5,1},{9,13},{13,9},{2,6},{6,2},{1... | collective-permute-start | bytes 261128 | tf_op jit(solution)/shard_map/ppermute | solution.py:20
  42.5 2.0 %collective-permute-start.15 = (bf16[96,2048]{1,0:T(8,128)(2,1)S(1)}, bf16[96,2048]{1,0:T(8,128)(2,1)S(1)}, u32[]{:S(2)}, u32[]{:S(2)}) collective-permute-start(bf16[96,2048]{1,0:T(8,128)(2,1)S(1)} %shard_map.101.mine), channel_id=1, source_target_pairs={{0,16},{16,0},{1,17},{17,1},{2,18},{18,2},{3,19},{19,3},{4,20},{20... | collective-permute-start | bytes 1179656 | tf_op jit(solution)/shard_map/ppermute | solution.py:20

commit v9 on v7

--- a/solution.py
+++ b/solution.py
@@ -49,25 +49,24 @@
 
 
 def dispatch_kernel(experts, cap, chunk_count, *refs):
-    small, (gate, up, down), refs = refs[:4], refs[4:7], refs[7:]
-    chunks, (slot_out, *held, sems) = refs[:chunk_count], refs[chunk_count:]
-    packed, held = held[:2], held[2:]
+    given, weights, refs = refs[:4], refs[4:7], refs[7:]
+    chunks, (slot_out, *packed), (*held, sems) = refs[:chunk_count], refs[chunk_count:-5], refs[-5:]
     hidden = packed[0].shape[0] // 3
     rep = lax.axis_index("rep")
-    loads = [pltpu.make_async_copy(*pair, sems.at[i]) for i, pair in enumerate(zip(small, held))]
+    loads = [pltpu.make_async_copy(*pair, sems.at[i]) for i, pair in enumerate(zip(given, held))]
     packs = []
     for j, half in enumerate((rep, 1 - rep)):
         rows = pl.ds(pl.multiple_of(half * hidden, hidden), hidden)
         packs += [
             pltpu.make_async_copy(weight.at[0, rows], packed[j].at[pl.ds(i * hidden, hidden)], sems.at[4 + 3 * j + i])
-            for i, weight in enumerate((gate, up, down))
+            for i, weight in enumerate(weights)
         ]
     for copy in loads + packs:
         copy.start()
-    for copy in loads:
+    for copy in loads[:2]:
         copy.wait()
 
-    tokens, upstream, ids, route_weight = held
+    ids, route_weight, tokens, upstream = held
     top, tok_dev = ids.shape
     rows = experts * cap // chunk_count
     me = lax.axis_index("ep")
@@ -84,7 +83,7 @@
         expert = ids[k : k + 1, :]
         if chunk_count > 1:
             mask = expert ^ me
-            chunk = jnp.where(mask < 2, mask, experts + 1 - mask)
+            chunk = jnp.where(mask == 0, 0, experts - mask)
             slot = chunk * cap + rank
             x_row = slot + chunk * cap
         else:
@@ -96,8 +95,12 @@
         take_x += here_x
         take_dy += here_dy
         scale += here_x + here_dy * route_weight[k : k + 1, :].astype(f32)
-    picked = dot(take_x.astype(bf16), tokens[...], (1, 0)) + dot(take_dy.astype(bf16), upstream[...], (1, 0))
-    picked = picked * jnp.sum(scale, axis=1, keepdims=True)
+    scale = jnp.sum(scale, axis=1, keepdims=True)
+    take_x, take_dy = take_x.astype(bf16), take_dy.astype(bf16)
+    for copy in loads[2:]:
+        copy.wait()
+    picked = dot(take_x, tokens[...], (1, 0)) + dot(take_dy, upstream[...], (1, 0))
+    picked = picked * scale
     for c in range(chunk_count):
         chunks[c][...] = picked[2 * rows * c : 2 * rows * (c + 1)].astype(bf16)
     for copy in packs:
@@ -105,32 +108,36 @@
 
 
 def expert_math(x_rows, d_rows, pieces):
-    acts, mixed = [], []
-    prob = 0.0
-    for piece in pieces:
-        hidden = piece.shape[0] // 3
-        pre = dot(x_rows, piece[: 2 * hidden], (1, 1))
-        d_act = dot(d_rows, piece[2 * hidden :], (1, 1))
-        gate_pre, up_pre = pre[:, :hidden], pre[:, hidden:]
-        sig = jax.nn.sigmoid(gate_pre)
-        silu = gate_pre * sig
-        act = silu * up_pre
-        prob = prob + jnp.sum(act * d_act, axis=1, keepdims=True)
-        acts.append(act)
-        mixed += [d_act * up_pre * sig * (1.0 + gate_pre * (1.0 - sig)), d_act * silu]
-    mixed = jnp.concatenate(mixed, axis=1).astype(bf16)
-    acts = jnp.concatenate(acts, axis=1).astype(bf16)
-    gates = jnp.concatenate([piece[: 2 * hidden] for piece in pieces])
-    return dot(mixed, gates, (1, 0)), prob, dot(acts, d_rows, (0, 0))
-
-
-def early_kernel(chunk_count, *refs):
-    chunks, (*pieces, x_out, d_out, dx_out, grad_own, grad_near) = refs[:chunk_count], refs[chunk_count:]
+    hidden = pieces[0].shape[0] // 3
+    gate, up, down = [[piece[i * hidden : (i + 1) * hidden] for piece in pieces] for i in range(3)]
+    mixers = jnp.concatenate(gate + up)
+    pre = dot(x_rows, mixers, (1, 1))
+    d_act = dot(d_rows, jnp.concatenate(down), (1, 1))
+    gate_pre, up_pre = pre[:, : hidden * len(pieces)], pre[:, hidden * len(pieces) :]
+    sig = jax.nn.sigmoid(gate_pre)
+    silu = gate_pre * sig
+    act = silu * up_pre
+    prob = jnp.sum(act * d_act, axis=1, keepdims=True)
+    d_gate = d_act * up_pre * sig * (1.0 + gate_pre * (1.0 - sig))
+    d_pre = jnp.concatenate([d_gate, d_act * silu], axis=1).astype(bf16)
+    return dot(d_pre, mixers, (1, 0)), prob, dot(act.astype(bf16), d_rows, (0, 0))
+
+
+def gather_kernel(*refs):
+    *chunks, x_out, d_out = refs
     rows = chunks[0].shape[0] // 2
     values = [c[...].astype(f32) for c in chunks]
     x_out[...] = jnp.concatenate([v[:rows] for v in values]).astype(bf16)
     d_out[...] = jnp.concatenate([v[rows:] for v in values]).astype(bf16)
-    dx, prob, grad = expert_math(x_out[...], d_out[...], pieces)
+
+
+def both_cores(x_own, d_own, x_other, d_other):
+    return [jnp.concatenate([a[...], b[...]]) for a, b in ((x_own, x_other), (d_own, d_other))]
+
+
+def early_kernel(*refs):
+    *pieces, dx_out, grad_own, grad_near = refs[4:]
+    dx, prob, grad = expert_math(*both_cores(*refs[:4]), pieces)
     width, hidden = dx.shape[1], grad_own.shape[0]
     dx_out[:, :width] = dx
     dx_out[:, width:] = jnp.broadcast_to(prob, (prob.shape[0], LANES))
@@ -138,8 +145,9 @@
     grad_near[...] = grad[hidden:].astype(bf16)
 
 
-def late_kernel(x_ref, d_ref, dx_ref, far, keep, give, grad_far):
-    dx, prob, grad = expert_math(x_ref[...], d_ref[...], [far])
+def late_kernel(*refs):
+    dx_ref, far, keep, give, grad_far = refs[4:]
+    dx, prob, grad = expert_math(*both_cores(*refs[:4]), [far])
     width, slots = dx.shape[1], keep.shape[0]
     for side, value in ((slice(0, width), dx), (slice(width, None), jnp.broadcast_to(prob, (prob.shape[0], LANES)))):
         total = value + dx_ref[:, side]
@@ -163,21 +171,20 @@
         out[0, rows] = mine[here].astype(f32) + theirs[there].astype(f32)
 
 
-def add_kernel(keep, got, *chunks):
+def add_kernel(places, keep, got, *chunks):
     rows = chunks[0].shape[0]
     total = keep[...] + got[...].astype(f32)
-    for c, chunk in enumerate(chunks):
-        chunk[...] = total[c * rows : (c + 1) * rows].astype(bf16)
-
-
-def combine_kernel(chunk_count, *refs):
-    chunks, (slot, route_weight, tokens_out, probs_out) = refs[:chunk_count], refs[chunk_count:]
+    for place, chunk in zip(places, chunks):
+        chunk[...] = total[place * rows : (place + 1) * rows].astype(bf16)
+
+
+def combine_kernel(places, *refs):
+    chunks, (slot, route_weight, tokens_out, probs_out) = refs[: len(places)], refs[len(places) :]
     rows = chunks[0].shape[0]
     tok_dev, width = tokens_out.shape
     top = slot.shape[0]
     total = 0.0
     probs = [0.0] * top
-    places = [0, *range(2, chunk_count), 1][:chunk_count]
     for c, place in enumerate(places):
         slot_of_row = iota((rows, tok_dev), 0) + place * rows
         hits = [(slot_of_row == slot[k : k + 1, :]).astype(f32) for k in range(top)]
@@ -198,20 +205,20 @@
     slots = experts * cap
     chunk_count = experts if experts <= 8 else 1
     rows = slots // chunk_count
-    masks = [0, 1, *range(experts - 1, 1, -1)]
+    masks = [0, *range(experts - 1, 0, -1)]
     hidden = gate_weight.shape[1] // reps
     shape = jax.ShapeDtypeStruct
     in_hbm = pl.BlockSpec(memory_space=pltpu.HBM)
 
-    small = [tokens, upstream, expert_ids.T, route_weight.T]
+    given = [expert_ids.T, route_weight.T, tokens, upstream]
     *chunks, slot, first, second = kernel_call(
         functools.partial(dispatch_kernel, experts, cap, chunk_count),
-        [pltpu.with_memory_space_constraint(a, pltpu.HBM) for a in small + [gate_weight, up_weight, down_weight]],
+        [pltpu.with_memory_space_constraint(a, pltpu.HBM) for a in [*given, gate_weight, up_weight, down_weight]],
         [shape((2 * rows, width), bf16)] * chunk_count
         + [shape((top, tok_dev), jnp.int32)]
         + [shape((3 * hidden, width), bf16)] * 2,
         in_specs=[in_hbm] * 7,
-        scratch_shapes=[pltpu.VMEM(a.shape, a.dtype) for a in small] + [pltpu.SemaphoreType.DMA((10,))],
+        scratch_shapes=[pltpu.VMEM(a.shape, a.dtype) for a in given] + [pltpu.SemaphoreType.DMA((10,))],
     )
 
     along, across = (1, 2), (2, 1)
@@ -224,31 +231,35 @@
         moved = chunks[0].reshape(2, experts, cap, width)
         moved = lax.all_to_all(moved, "ep", split_axis=1, concat_axis=1, tiled=True)
         chunks = [moved.reshape(2 * rows, width)]
-    chunks = chunks + [swap(c, "rep", 1) for c in chunks]
+    own = kernel_call(gather_kernel, chunks, [shape((slots, width), bf16)] * 2, flops=2 * 10**9)
+    other = [swap(part, "rep", 1) for part in own]
 
     wide = width + LANES
-    x_rows, d_rows, dx, grad_own, grad_near = kernel_call(
-        functools.partial(early_kernel, 2 * chunk_count),
-        chunks + [first, *near],
-        [shape((2 * slots, width), bf16)] * 2
-        + [shape((2 * slots, wide), f32), shape((hidden, width), f32), shape((2 * hidden, width), bf16)],
-        flops=4 * 10**9,
+    dx, grad_own, grad_near = kernel_call(
+        early_kernel,
+        [*own, *other, first, *near],
+        [shape((2 * slots, wide), f32), shape((hidden, width), f32), shape((2 * hidden, width), bf16)],
+        flops=2 * 10**9,
     )
     keep, give, grad_far = kernel_call(
         late_kernel,
-        [x_rows, d_rows, dx, far],
+        [*own, *other, dx, far],
         [shape((slots, wide), f32), shape((slots, wide), bf16), shape((hidden, width), bf16)],
     )
-    back = kernel_call(add_kernel, [keep, swap(give, "rep", 1)], [shape((rows, wide), bf16)] * chunk_count)
+    places = [0, chunk_count - 1, *range(1, chunk_count - 1)][:chunk_count]
+    back = kernel_call(
+        functools.partial(add_kernel, places),
+        [keep, swap(give, "rep", 1)],
+        [shape((rows, wide), bf16)] * chunk_count,
+    )
     if chunk_count > 1:
-        back = exchange(back, masks)
-        back = [back[0], *back[2:], back[1]]
+        back = exchange(back, [masks[place] for place in places])
     else:
         moved = back[0].reshape(experts, cap, wide)
         moved = lax.all_to_all(moved, "ep", split_axis=0, concat_axis=0, tiled=True)
         back = [moved.reshape(rows, wide)]
     d_tokens, d_probs = kernel_call(
-        functools.partial(combine_kernel, chunk_count),
+        functools.partial(combine_kernel, places),
         back + [slot, route_weight.T],
         [shape((tok_dev, width), bf16), shape((top, tok_dev), bf16)],
         flops=8 * 10**9,

time: 45.1 us -> 45 us (level)
  waiting for transfers between devices: 19.3 us -> 19.9 us
    ppermute x5, waiting for transfers between devices: 6.87 us -> 8.57 us  [swap_by_core(): return lax.ppermute(value, ('rep', 'dp'), pairs)]
    ppermute x12 -> x10, waiting for transfers between devices: 12.5 us -> 11.4 us  [swap(): lax.ppermute(value, axis, [(i, i ^ mask) for i in range(lax.axis_size(axi...]
    pallas_call x7 -> x8, Pallas kernels: 6.79 us -> 6.36 us  [kernel_call(): pl.pallas_call(body, out_shape=outputs, in_specs=kwargs.pop('in_specs', [...]
    ppermute x12 -> x10, starting transfers between devices: 10 us -> 9.68 us  [swap(): lax.ppermute(value, axis, [(i, i ^ mask) for i in range(lax.axis_size(axi...]
  transfers between devices with their start and end apart: 17 -> 15, of which waited for: 9 -> 7; matrix products, arithmetic and copies ran while one was open for 0% -> 0% of each run, Pallas kernels for 7% -> 6%
where the time goes in v9:
time: 45 us; the launch traced here: 44.9 us
  waiting for transfers between devices  19.9 us (44%)
  starting transfers between devices  17.8 us (40%)
  Pallas kernels  6.36 us (14%)
  between operations  0.72 us (2%)
    ppermute x10, waiting for transfers between devices, swap(): lax.ppermute(value, axis, [(i, i ^ mask) for i in range(lax.axis_size(axi...  11.4 us
    ppermute x10, starting transfers between devices, swap(): lax.ppermute(value, axis, [(i, i ^ mask) for i in range(lax.axis_size(axi...  9.68 us
    ppermute x5, waiting for transfers between devices, swap_by_core(): return lax.ppermute(value, ('rep', 'dp'), pairs)  8.57 us
    ppermute x5, starting transfers between devices, swap_by_core(): return lax.ppermute(value, ('rep', 'dp'), pairs)  8.16 us
    pallas_call x8, Pallas kernels, kernel_call(): pl.pallas_call(body, out_shape=outputs, in_specs=kwargs.pop('in_specs', [...  6.36 us
  transfers between devices with their start and end apart: 15, of which 7 were waited for; matrix products, arithmetic and copies ran while one was open for 0% of the time, Pallas kernels for 6%

profile of v9, /device:TPU:0, one launch (start us, length us, event | category | flops | bytes accessed | tf_op | source)
XLA Modules:
  0.0 44.9 jit_solution(1109267006858874082)
XLA Ops:
  0.6 1.6 %shard_map.94 = (bf16[40,2048]{1,0:T(8,128)(2,1)S(1)}, bf16[40,2048]{1,0:T(8,128)(2,1)S(1)}, bf16[40,2048]{1,0:T(8,128)(2,1)S(1)}, bf16[40,2048]{1,0:T(8,128)(2,...) custom-call(s32[2,32]{1,0:T(2,128)} %bitcast.5, bf16[2,32]{1,0:T(2,128)(2,1)} %bitcast.3, ...), custom_call_target="tpu_custom_call" | custom-call | bytes 3277440 | tf_op jit(solution)/shard_map/pallas_call | solution.py:36
  2.2 3.0 %collective-permute-start.5 = (bf16[144,2048]{1,0:T(8,128)(2,1)S(1)}, bf16[144,2048]{1,0:T(8,128)(2,1)S(1)}, u32[]{:S(2)}, u32[]{:S(2)}) collective-permute-start(bf16[144,2048]{1,0:T(8,128)(2,1)S(1)} %get-tuple-element.30.refs_4_), channel_id=1, source_target_pairs={{0,1},{1,0},{2,3},{3,2},{16,18},{17,19},{18,16},{19,17},{4,5},{5,4... | collective-permute-start | bytes 1769480 | tf_op jit(solution)/shard_map/ppermute | solution.py:30
  5.2 3.6 %collective-permute-start = (bf16[40,2048]{1,0:T(8,128)(2,1)S(1)}, bf16[40,2048]{1,0:T(8,128)(2,1)S(1)}, u32[]{:S(2)}, u32[]{:S(2)}) collective-permute-start(bf16[40,2048]{1,0:T(8,128)(2,1)S(1)} %get-tuple-element.25), channel_id=1, source_target_pairs={{0,12},{4,8},{8,4},{12,0},{1,13},{5,9},{9,5},{13,1},{2,14},{6,10},... | collective-permute-start | bytes 491528 | tf_op jit(solution)/shard_map/ppermute | solution.py:20
  8.8 0.0 collective-permute-start.1
  8.8 0.8 %collective-permute-start.2 = (bf16[40,2048]{1,0:T(8,128)(2,1)S(1)}, bf16[40,2048]{1,0:T(8,128)(2,1)S(1)}, u32[]{:S(2)}, u32[]{:S(2)}) collective-permute-start(bf16[40,2048]{1,0:T(8,128)(2,1)S(1)} %get-tuple-element.27), channel_id=1, source_target_pairs={{0,4},{4,0},{8,12},{12,8},{1,5},{5,1},{9,13},{13,9},{2,6},{6,2},{1... | collective-permute-start | bytes 491528 | tf_op jit(solution)/shard_map/ppermute | solution.py:20
  9.6 0.3 collective-permute-start.6
  9.9 3.2 %collective-permute-done.5.refs_5_ = bf16[144,2048]{1,0:T(8,128)(2,1)S(1)} collective-permute-done((bf16[144,2048]{1,0:T(8,128)(2,1)S(1)}, bf16[144,2048]{1,0:T(8,128)(2,1)S(1)}, u32[]{:S(2)}, u32[]{:S(2)}) %collective-permute-start.5) | collective-permute-done | bytes 589856 | tf_op jit(solution)/shard_map/ppermute | solution.py:30
  13.1 2.1 %collective-permute-start.7 = (bf16[144,2048]{1,0:T(8,128)(2,1)S(1)}, bf16[144,2048]{1,0:T(8,128)(2,1)S(1)}, u32[]{:S(2)}, u32[]{:S(2)}) collective-permute-start(bf16[144,2048]{1,0:T(8,128)(2,1)S(1)} %collective-permute-done.5.refs_5_), channel_id=1, source_target_pairs={{0,2},{1,3},{2,0},{3,1},{16,17},{17,16},{18,19},{19,18},{4,6},{5,7... | collective-permute-start | bytes 1769480 | tf_op jit(solution)/shard_map/ppermute | solution.py:30
  15.1 0.0 collective-permute-done.refs_1_
  15.1 7.3 %collective-permute-done.1.refs_2_ = bf16[40,2048]{1,0:T(8,128)(2,1)S(1)} collective-permute-done((bf16[40,2048]{1,0:T(8,128)(2,1)S(1)}, bf16[40,2048]{1,0:T(8,128)(2,1)S(1)}, u32[]{:S(2)}, u32[]{:S(2)}) %collective-permute-start.1) | collective-permute-done | bytes 163872 | tf_op jit(solution)/shard_map/ppermute | solution.py:20
  22.5 0.0 collective-permute-done.2.refs_3_
  22.5 0.1 shard_map.95
  22.6 0.1 collective-permute-start.3
  22.6 0.5 %collective-permute-start.4 = (bf16[80,2048]{1,0:T(8,128)(2,1)S(1)}, bf16[80,2048]{1,0:T(8,128)(2,1)S(1)}, u32[]{:S(2)}, u32[]{:S(2)}) collective-permute-start(bf16[80,2048]{1,0:T(8,128)(2,1)S(1)} %get-tuple-element.29.refs_1_), channel_id=1, source_target_pairs={{0,16},{16,0},{1,17},{17,1},{2,18},{18,2},{3,19},{19,3},{4,20},{20... | collective-permute-start | bytes 983048 | tf_op jit(solution)/shard_map/ppermute | solution.py:20
  23.1 1.1 %collective-permute-done.3.refs_2_ = bf16[80,2048]{1,0:T(8,128)(2,1)S(1)} collective-permute-done((bf16[80,2048]{1,0:T(8,128)(2,1)S(1)}, bf16[80,2048]{1,0:T(8,128)(2,1)S(1)}, u32[]{:S(2)}, u32[]{:S(2)}) %collective-permute-start.3) | collective-permute-done | bytes 327712 | tf_op jit(solution)/shard_map/ppermute | solution.py:20
  24.3 0.5 %collective-permute-done.4.refs_3_ = bf16[80,2048]{1,0:T(8,128)(2,1)S(1)} collective-permute-done((bf16[80,2048]{1,0:T(8,128)(2,1)S(1)}, bf16[80,2048]{1,0:T(8,128)(2,1)S(1)}, u32[]{:S(2)}, u32[]{:S(2)}) %collective-permute-start.4) | collective-permute-done | bytes 327712 | tf_op jit(solution)/shard_map/ppermute | solution.py:20
  24.7 0.0 collective-permute-done.6.refs_6_
  24.7 1.5 %shard_map.96 = (f32[160,2176]{1,0:T(8,128)S(1)}, f32[48,2048]{1,0:T(8,128)S(1)}, bf16[96,2048]{1,0:T(8,128)(2,1)S(1)}) custom-call(bf16[80,2048]{1,0:T(8,128)(2,1)S(1)} %get-tuple-element.28.refs_0_, bf16[80,2048]{1,0:T(8,128)(2,1)S(1)} %get-tuple-element.29.refs_1_, bf16[80,2048]{1,0:T(8,128)(2,1)S(1)} %collective-permute-done.3.refs_2_, ...), custom_call_target="tpu_custom_call" | custom-call | flops 2000000000 | bytes 5259264 | tf_op jit(solution)/shard_map/pallas_call | solution.py:36
  26.3 0.0 collective-permute-done.7.refs_5_
  26.3 1.0 %shard_map.97 = (f32[80,2176]{1,0:T(8,128)S(1)}, bf16[80,2176]{1,0:T(8,128)(2,1)S(1)}, bf16[48,2048]{1,0:T(8,128)(2,1)S(1)}) custom-call(bf16[80,2048]{1,0:T(8,128)(2,1)S(1)} %get-tuple-element.28.refs_0_, bf16[80,2048]{1,0:T(8,128)(2,1)S(1)} %get-tuple-element.29.refs_1_, bf16[80,2048]{1,0:T(8,128)(2,1)S(1)} %collective-permute-done.3.refs_2_, ...), custom_call_target="tpu_custom_call" | custom-call | bytes 4534272 | tf_op jit(solution)/shard_map/pallas_call | solution.py:36
  27.3 0.0 copy-start
  27.3 0.2 collective-permute-start.8
  27.5 1.5 %collective-permute-start.12 = (bf16[96,2048]{1,0:T(8,128)(2,1)S(1)}, bf16[96,2048]{1,0:T(8,128)(2,1)S(1)}, u32[]{:S(2)}, u32[]{:S(2)}) collective-permute-start(bf16[96,2048]{1,0:T(8,128)(2,1)S(1)} %get-tuple-element.43), channel_id=1, source_target_pairs={{0,1},{1,0},{2,3},{3,2},{16,18},{17,19},{18,16},{19,17},{4,5},{5,4... | collective-permute-start | bytes 1179656 | tf_op jit(solution)/shard_map/ppermute | solution.py:30
  29.0 1.3 %collective-permute-start.13 = (bf16[48,2048]{1,0:T(8,128)(2,1)S(1)}, bf16[48,2048]{1,0:T(8,128)(2,1)S(1)}, u32[]{:S(2)}, u32[]{:S(2)}) collective-permute-start(bf16[48,2048]{1,0:T(8,128)(2,1)S(1)} %get-tuple-element.44), channel_id=1, source_target_pairs={{0,3},{1,2},{2,1},{3,0},{16,19},{17,18},{18,17},{19,16},{4,7},{5,6... | collective-permute-start | bytes 589832 | tf_op jit(solution)/shard_map/ppermute | solution.py:30
  30.3 0.0 collective-permute-done.8.got
  30.3 0.1 shard_map.98
  30.4 3.7 %collective-permute-start.10 = (bf16[20,2176]{1,0:T(8,128)(2,1)S(1)}, bf16[20,2176]{1,0:T(8,128)(2,1)S(1)}, u32[]{:S(2)}, u32[]{:S(2)}) collective-permute-start(bf16[20,2176]{1,0:T(8,128)(2,1)S(1)} %get-tuple-element.37), channel_id=1, source_target_pairs={{0,12},{4,8},{8,4},{12,0},{1,13},{5,9},{9,5},{13,1},{2,14},{6,10},... | collective-permute-start | bytes 261128 | tf_op jit(solution)/shard_map/ppermute | solution.py:20
  34.1 0.0 collective-permute-start.11
  34.1 0.8 %collective-permute-start.9 = (bf16[20,2176]{1,0:T(8,128)(2,1)S(1)}, bf16[20,2176]{1,0:T(8,128)(2,1)S(1)}, u32[]{:S(2)}, u32[]{:S(2)}) collective-permute-start(bf16[20,2176]{1,0:T(8,128)(2,1)S(1)} %get-tuple-element.36), channel_id=1, source_target_pairs={{0,4},{4,0},{8,12},{12,8},{1,5},{5,1},{9,13},{13,9},{2,6},{6,2},{1... | collective-permute-start | bytes 261128 | tf_op jit(solution)/shard_map/ppermute | solution.py:20
  34.9 2.5 %collective-permute-done.12.near = bf16[96,2048]{1,0:T(8,128)(2,1)S(1)} collective-permute-done((bf16[96,2048]{1,0:T(8,128)(2,1)S(1)}, bf16[96,2048]{1,0:T(8,128)(2,1)S(1)}, u32[]{:S(2)}, u32[]{:S(2)}) %collective-permute-start.12) | collective-permute-done | bytes 393248 | tf_op jit(solution)/shard_map/ppermute | solution.py:30
  37.4 2.9 %collective-permute-done.13.far = bf16[48,2048]{1,0:T(8,128)(2,1)S(1)} collective-permute-done((bf16[48,2048]{1,0:T(8,128)(2,1)S(1)}, bf16[48,2048]{1,0:T(8,128)(2,1)S(1)}, u32[]{:S(2)}, u32[]{:S(2)}) %collective-permute-start.13) | collective-permute-done | bytes 196640 | tf_op jit(solution)/shard_map/ppermute | solution.py:30
  40.3 0.1 shard_map.100.mine
  40.4 0.1 collective-permute-start.14
  40.4 0.0 collective-permute-done.10.refs_2_
  40.5 2.5 %collective-permute-done.11.refs_3_ = bf16[20,2176]{1,0:T(8,128)(2,1)S(1)} collective-permute-done((bf16[20,2176]{1,0:T(8,128)(2,1)S(1)}, bf16[20,2176]{1,0:T(8,128)(2,1)S(1)}, u32[]{:S(2)}, u32[]{:S(2)}) %collective-permute-start.11) | collective-permute-done | bytes 87072 | tf_op jit(solution)/shard_map/ppermute | solution.py:20
  42.9 0.0 collective-permute-done.9.refs_1_
  42.9 0.0 copy-done
  42.9 1.0 %shard_map.99 = (bf16[32,2048]{1,0:T(8,128)(2,1)}, bf16[2,32]{1,0:T(2,128)(2,1)}) custom-call(bf16[20,2176]{1,0:T(8,128)(2,1)S(1)} %get-tuple-element.35.refs_0_, bf16[20,2176]{1,0:T(8,128)(2,1)S(1)} %collective-permute-done.9.refs_1_, bf16[20,2176]{1,0:T(8,128)(2,1)S(1)} %collective-permute-done.10.refs_2_, ...), custom_call_target="tpu_custom_call" | custom-call | flops 8000000000 | bytes 479744 | tf_op jit(solution)/shard_map/pallas_call | solution.py:36
  43.9 0.0 collective-permute-done.14.theirs
  43.9 1.0 %shard_map.101 = f32[1,96,2048]{2,1,0:T(8,128)} custom-call(bf16[96,2048]{1,0:T(8,128)(2,1)S(1)} %shard_map.100.mine, bf16[96,2048]{1,0:T(8,128)(2,1)S(1)} %collective-permute-done.14.theirs), custom_call_target="tpu_custom_call" | custom-call | bytes 1572864 | tf_op jit(solution)/shard_map/pallas_call | solution.py:36
Async XLA Ops:
  2.2 10.9 %collective-permute-start.5 = (bf16[144,2048]{1,0:T(8,128)(2,1)S(1)}, bf16[144,2048]{1,0:T(8,128)(2,1)S(1)}, u32[]{:S(2)}, u32[]{:S(2)}) collective-permute-start(bf16[144,2048]{1,0:T(8,128)(2,1)S(1)} %get-tuple-element.30.refs_4_), channel_id=1, source_target_pairs={{0,1},{1,0},{2,3},{3,2},{16,18},{17,19},{18,16},{19,17},{4,5},{5,4... | collective-permute-start | bytes 1769480 | tf_op jit(solution)/shard_map/ppermute | solution.py:30
  5.2 9.9 %collective-permute-start = (bf16[40,2048]{1,0:T(8,128)(2,1)S(1)}, bf16[40,2048]{1,0:T(8,128)(2,1)S(1)}, u32[]{:S(2)}, u32[]{:S(2)}) collective-permute-start(bf16[40,2048]{1,0:T(8,128)(2,1)S(1)} %get-tuple-element.25), channel_id=1, source_target_pairs={{0,12},{4,8},{8,4},{12,0},{1,13},{5,9},{9,5},{13,1},{2,14},{6,10},... | collective-permute-start | bytes 491528 | tf_op jit(solution)/shard_map/ppermute | solution.py:20
  8.8 13.6 %collective-permute-start.1 = (bf16[40,2048]{1,0:T(8,128)(2,1)S(1)}, bf16[40,2048]{1,0:T(8,128)(2,1)S(1)}, u32[]{:S(2)}, u32[]{:S(2)}) collective-permute-start(bf16[40,2048]{1,0:T(8,128)(2,1)S(1)} %get-tuple-element.26), channel_id=1, source_target_pairs={{0,8},{4,12},{8,0},{12,4},{1,9},{5,13},{9,1},{13,5},{2,10},{6,14},... | collective-permute-start | bytes 491528 | tf_op jit(solution)/shard_map/ppermute | solution.py:20
  8.8 13.6 %collective-permute-start.2 = (bf16[40,2048]{1,0:T(8,128)(2,1)S(1)}, bf16[40,2048]{1,0:T(8,128)(2,1)S(1)}, u32[]{:S(2)}, u32[]{:S(2)}) collective-permute-start(bf16[40,2048]{1,0:T(8,128)(2,1)S(1)} %get-tuple-element.27), channel_id=1, source_target_pairs={{0,4},{4,0},{8,12},{12,8},{1,5},{5,1},{9,13},{13,9},{2,6},{6,2},{1... | collective-permute-start | bytes 491528 | tf_op jit(solution)/shard_map/ppermute | solution.py:20
  9.6 15.1 %collective-permute-start.6 = (bf16[144,2048]{1,0:T(8,128)(2,1)S(1)}, bf16[144,2048]{1,0:T(8,128)(2,1)S(1)}, u32[]{:S(2)}, u32[]{:S(2)}) collective-permute-start(bf16[144,2048]{1,0:T(8,128)(2,1)S(1)} %get-tuple-element.31), channel_id=1, source_target_pairs={{0,1},{1,0},{2,3},{3,2},{16,18},{17,19},{18,16},{19,17},{4,5},{5,4... | collective-permute-start | bytes 1769480 | tf_op jit(solution)/shard_map/ppermute | solution.py:30
  13.1 13.2 %collective-permute-start.7 = (bf16[144,2048]{1,0:T(8,128)(2,1)S(1)}, bf16[144,2048]{1,0:T(8,128)(2,1)S(1)}, u32[]{:S(2)}, u32[]{:S(2)}) collective-permute-start(bf16[144,2048]{1,0:T(8,128)(2,1)S(1)} %collective-permute-done.5.refs_5_), channel_id=1, source_target_pairs={{0,2},{1,3},{2,0},{3,1},{16,17},{17,16},{18,19},{19,18},{4,6},{5,7... | collective-permute-start | bytes 1769480 | tf_op jit(solution)/shard_map/ppermute | solution.py:30
  22.6 1.7 %collective-permute-start.3 = (bf16[80,2048]{1,0:T(8,128)(2,1)S(1)}, bf16[80,2048]{1,0:T(8,128)(2,1)S(1)}, u32[]{:S(2)}, u32[]{:S(2)}) collective-permute-start(bf16[80,2048]{1,0:T(8,128)(2,1)S(1)} %get-tuple-element.28.refs_0_), channel_id=1, source_target_pairs={{0,16},{16,0},{1,17},{17,1},{2,18},{18,2},{3,19},{19,3},{4,20},{20... | collective-permute-start | bytes 983048 | tf_op jit(solution)/shard_map/ppermute | solution.py:20
  22.6 2.1 %collective-permute-start.4 = (bf16[80,2048]{1,0:T(8,128)(2,1)S(1)}, bf16[80,2048]{1,0:T(8,128)(2,1)S(1)}, u32[]{:S(2)}, u32[]{:S(2)}) collective-permute-start(bf16[80,2048]{1,0:T(8,128)(2,1)S(1)} %get-tuple-element.29.refs_1_), channel_id=1, source_target_pairs={{0,16},{16,0},{1,17},{17,1},{2,18},{18,2},{3,19},{19,3},{4,20},{20... | collective-permute-start | bytes 983048 | tf_op jit(solution)/shard_map/ppermute | solution.py:20
  27.3 15.6 %copy-start = (bf16[32,2]{0,1:T(2,128)(2,1)S(1)}, bf16[32,2]{0,1:T(2,128)(2,1)}, u32[]{:S(2)}) copy-start(bf16[32,2]{0,1:T(2,128)(2,1)} %param.10) | copy-start | bytes 388
  27.3 3.0 %collective-permute-start.8 = (bf16[80,2176]{1,0:T(8,128)(2,1)S(1)}, bf16[80,2176]{1,0:T(8,128)(2,1)S(1)}, u32[]{:S(2)}, u32[]{:S(2)}) collective-permute-start(bf16[80,2176]{1,0:T(8,128)(2,1)S(1)} %get-tuple-element.34), channel_id=1, source_target_pairs={{0,16},{16,0},{1,17},{17,1},{2,18},{18,2},{3,19},{19,3},{4,20},{20... | collective-permute-start | bytes 1044488 | tf_op jit(solution)/shard_map/ppermute | solution.py:20
  27.5 9.9 %collective-permute-start.12 = (bf16[96,2048]{1,0:T(8,128)(2,1)S(1)}, bf16[96,2048]{1,0:T(8,128)(2,1)S(1)}, u32[]{:S(2)}, u32[]{:S(2)}) collective-permute-start(bf16[96,2048]{1,0:T(8,128)(2,1)S(1)} %get-tuple-element.43), channel_id=1, source_target_pairs={{0,1},{1,0},{2,3},{3,2},{16,18},{17,19},{18,16},{19,17},{4,5},{5,4... | collective-permute-start | bytes 1179656 | tf_op jit(solution)/shard_map/ppermute | solution.py:30
  29.0 11.3 %collective-permute-start.13 = (bf16[48,2048]{1,0:T(8,128)(2,1)S(1)}, bf16[48,2048]{1,0:T(8,128)(2,1)S(1)}, u32[]{:S(2)}, u32[]{:S(2)}) collective-permute-start(bf16[48,2048]{1,0:T(8,128)(2,1)S(1)} %get-tuple-element.44), channel_id=1, source_target_pairs={{0,3},{1,2},{2,1},{3,0},{16,19},{17,18},{18,17},{19,16},{4,7},{5,6... | collective-permute-start | bytes 589832 | tf_op jit(solution)/shard_map/ppermute | solution.py:30
  30.4 10.0 %collective-permute-start.10 = (bf16[20,2176]{1,0:T(8,128)(2,1)S(1)}, bf16[20,2176]{1,0:T(8,128)(2,1)S(1)}, u32[]{:S(2)}, u32[]{:S(2)}) collective-permute-start(bf16[20,2176]{1,0:T(8,128)(2,1)S(1)} %get-tuple-element.37), channel_id=1, source_target_pairs={{0,12},{4,8},{8,4},{12,0},{1,13},{5,9},{9,5},{13,1},{2,14},{6,10},... | collective-permute-start | bytes 261128 | tf_op jit(solution)/shard_map/ppermute | solution.py:20
  34.1 8.8 %collective-permute-start.11 = (bf16[20,2176]{1,0:T(8,128)(2,1)S(1)}, bf16[20,2176]{1,0:T(8,128)(2,1)S(1)}, u32[]{:S(2)}, u32[]{:S(2)}) collective-permute-start(bf16[20,2176]{1,0:T(8,128)(2,1)S(1)} %get-tuple-element.38), channel_id=1, source_target_pairs={{0,8},{4,12},{8,0},{12,4},{1,9},{5,13},{9,1},{13,5},{2,10},{6,14},... | collective-permute-start | bytes 261128 | tf_op jit(solution)/shard_map/ppermute | solution.py:20
  34.1 8.8 %collective-permute-start.9 = (bf16[20,2176]{1,0:T(8,128)(2,1)S(1)}, bf16[20,2176]{1,0:T(8,128)(2,1)S(1)}, u32[]{:S(2)}, u32[]{:S(2)}) collective-permute-start(bf16[20,2176]{1,0:T(8,128)(2,1)S(1)} %get-tuple-element.36), channel_id=1, source_target_pairs={{0,4},{4,0},{8,12},{12,8},{1,5},{5,1},{9,13},{13,9},{2,6},{6,2},{1... | collective-permute-start | bytes 261128 | tf_op jit(solution)/shard_map/ppermute | solution.py:20
  40.4 3.5 %collective-permute-start.14 = (bf16[96,2048]{1,0:T(8,128)(2,1)S(1)}, bf16[96,2048]{1,0:T(8,128)(2,1)S(1)}, u32[]{:S(2)}, u32[]{:S(2)}) collective-permute-start(bf16[96,2048]{1,0:T(8,128)(2,1)S(1)} %shard_map.100.mine), channel_id=1, source_target_pairs={{0,16},{16,0},{1,17},{17,1},{2,18},{18,2},{3,19},{19,3},{4,20},{20... | collective-permute-start | bytes 1179656 | tf_op jit(solution)/shard_map/ppermute | solution.py:20

commit v10 on v9

--- a/solution.py
+++ b/solution.py
@@ -20,8 +20,8 @@
     return lax.ppermute(value, axis, [(i, i ^ mask) for i in range(lax.axis_size(axis))])
 
 
-def exchange(chunks, masks):
-    return [chunks[0]] + [swap(chunk, "ep", mask) for chunk, mask in zip(chunks[1:], masks[1:])]
+def exchange(chunks):
+    return chunks[:1] + [swap(chunks[c], "ep", c) for c in range(1, len(chunks))]
 
 
 def swap_by_core(value, masks):
@@ -82,8 +82,7 @@
         rank = jnp.sum(before * named[k], axis=0, keepdims=True).astype(jnp.int32)
         expert = ids[k : k + 1, :]
         if chunk_count > 1:
-            mask = expert ^ me
-            chunk = jnp.where(mask == 0, 0, experts - mask)
+            chunk = expert ^ me
             slot = chunk * cap + rank
             x_row = slot + chunk * cap
         else:
@@ -126,7 +125,7 @@
 def gather_kernel(*refs):
     *chunks, x_out, d_out = refs
     rows = chunks[0].shape[0] // 2
-    values = [c[...].astype(f32) for c in chunks]
+    values = [c[...].astype(f32) for c in reversed(chunks)]
     x_out[...] = jnp.concatenate([v[:rows] for v in values]).astype(bf16)
     d_out[...] = jnp.concatenate([v[rows:] for v in values]).astype(bf16)
 
@@ -146,13 +145,15 @@
 
 
 def late_kernel(*refs):
-    dx_ref, far, keep, give, grad_far = refs[4:]
+    dx_ref, far, keep, *gives, grad_far = refs[4:]
     dx, prob, grad = expert_math(*both_cores(*refs[:4]), [far])
     width, slots = dx.shape[1], keep.shape[0]
     for side, value in ((slice(0, width), dx), (slice(width, None), jnp.broadcast_to(prob, (prob.shape[0], LANES)))):
         total = value + dx_ref[:, side]
         keep[:, side] = total[:slots]
-        give[:, side] = total[slots:].astype(bf16)
+        for i, give in enumerate(gives):
+            rows = give.shape[0]
+            give[:, side] = total[slots + rows * i : slots + rows * (i + 1)].astype(bf16)
     grad_far[...] = grad.astype(bf16)
 
 
@@ -171,22 +172,22 @@
         out[0, rows] = mine[here].astype(f32) + theirs[there].astype(f32)
 
 
-def add_kernel(places, keep, got, *chunks):
+def add_kernel(start, keep, got, *chunks):
     rows = chunks[0].shape[0]
-    total = keep[...] + got[...].astype(f32)
-    for place, chunk in zip(places, chunks):
-        chunk[...] = total[place * rows : (place + 1) * rows].astype(bf16)
-
-
-def combine_kernel(places, *refs):
-    chunks, (slot, route_weight, tokens_out, probs_out) = refs[: len(places)], refs[len(places) :]
+    total = keep[start : start + got.shape[0]] + got[...].astype(f32)
+    for c, chunk in enumerate(chunks):
+        chunk[...] = total[c * rows : (c + 1) * rows].astype(bf16)
+
+
+def combine_kernel(chunk_count, *refs):
+    chunks, (slot, route_weight, tokens_out, probs_out) = refs[:chunk_count], refs[chunk_count:]
     rows = chunks[0].shape[0]
     tok_dev, width = tokens_out.shape
     top = slot.shape[0]
     total = 0.0
     probs = [0.0] * top
-    for c, place in enumerate(places):
-        slot_of_row = iota((rows, tok_dev), 0) + place * rows
+    for c in range(chunk_count):
+        slot_of_row = iota((rows, tok_dev), 0) + c * rows
         hits = [(slot_of_row == slot[k : k + 1, :]).astype(f32) for k in range(top)]
         total = total + dot(sum(hits).astype(bf16), chunks[c][:, :width], (0, 0))
         prob = chunks[c][:, width : width + 1].astype(f32)
@@ -205,7 +206,6 @@
     slots = experts * cap
     chunk_count = experts if experts <= 8 else 1
     rows = slots // chunk_count
-    masks = [0, *range(experts - 1, 0, -1)]
     hidden = gate_weight.shape[1] // reps
     shape = jax.ShapeDtypeStruct
     in_hbm = pl.BlockSpec(memory_space=pltpu.HBM)
@@ -226,12 +226,12 @@
     far = swap_by_core(near[0], across)
 
     if chunk_count > 1:
-        chunks = exchange(chunks, masks)
+        chunks = exchange(chunks)
     else:
         moved = chunks[0].reshape(2, experts, cap, width)
         moved = lax.all_to_all(moved, "ep", split_axis=1, concat_axis=1, tiled=True)
         chunks = [moved.reshape(2 * rows, width)]
-    own = kernel_call(gather_kernel, chunks, [shape((slots, width), bf16)] * 2, flops=2 * 10**9)
+    own = kernel_call(gather_kernel, chunks[::-1], [shape((slots, width), bf16)] * 2, flops=2 * 10**9)
     other = [swap(part, "rep", 1) for part in own]
 
     wide = width + LANES
@@ -239,27 +239,31 @@
         early_kernel,
         [*own, *other, first, *near],
         [shape((2 * slots, wide), f32), shape((hidden, width), f32), shape((2 * hidden, width), bf16)],
-        flops=2 * 10**9,
-    )
-    keep, give, grad_far = kernel_call(
+        flops=10**9,
+    )
+    parts = 2 if chunk_count % 2 == 0 else 1
+    keep, *gives, grad_far = kernel_call(
         late_kernel,
         [*own, *other, dx, far],
-        [shape((slots, wide), f32), shape((slots, wide), bf16), shape((hidden, width), bf16)],
-    )
-    places = [0, chunk_count - 1, *range(1, chunk_count - 1)][:chunk_count]
-    back = kernel_call(
-        functools.partial(add_kernel, places),
-        [keep, swap(give, "rep", 1)],
-        [shape((rows, wide), bf16)] * chunk_count,
-    )
+        [shape((slots, wide), f32)]
+        + [shape((slots // parts, wide), bf16)] * parts
+        + [shape((hidden, width), bf16)],
+    )
+    back = []
+    for i, give in enumerate(gives):
+        back += kernel_call(
+            functools.partial(add_kernel, i * slots // parts),
+            [keep, swap(give, "rep", 1)],
+            [shape((rows, wide), bf16)] * (chunk_count // parts),
+        )
     if chunk_count > 1:
-        back = exchange(back, [masks[place] for place in places])
+        back = exchange(back)
     else:
         moved = back[0].reshape(experts, cap, wide)
         moved = lax.all_to_all(moved, "ep", split_axis=0, concat_axis=0, tiled=True)
         back = [moved.reshape(rows, wide)]
     d_tokens, d_probs = kernel_call(
-        functools.partial(combine_kernel, places),
+        functools.partial(combine_kernel, chunk_count),
         back + [slot, route_weight.T],
         [shape((tok_dev, width), bf16), shape((top, tok_dev), bf16)],
         flops=8 * 10**9,

time: 45 us -> 44.6 us (level)
  waiting for transfers between devices: 19.9 us -> 19.1 us
    ppermute x5, waiting for transfers between devices: 8.57 us -> 7.11 us  [swap_by_core(): return lax.ppermute(value, ('rep', 'dp'), pairs)]
    ppermute x10 -> x11, waiting for transfers between devices: 11.4 us -> 12 us  [swap(): lax.ppermute(value, axis, [(i, i ^ mask) for i in range(lax.axis_size(axi...]
    ppermute x10 -> x11, starting transfers between devices: 9.68 us -> 9.89 us  [swap(): lax.ppermute(value, axis, [(i, i ^ mask) for i in range(lax.axis_size(axi...]
    pallas_call x8 -> x9, Pallas kernels: 6.36 us -> 6.37 us  [kernel_call(): pl.pallas_call(body, out_shape=outputs, in_specs=kwargs.pop('in_specs', [...]
  transfers between devices with their start and end apart: 15 -> 16, of which waited for: 7 -> 7; matrix products, arithmetic and copies ran while one was open for 0% -> 0% of each run, Pallas kernels for 6% -> 9%
where the time goes in v10:
time: 44.6 us; the launch traced here: 44.4 us
  waiting for transfers between devices  19.1 us (43%)
  starting transfers between devices  18.2 us (41%)
  Pallas kernels  6.37 us (14%)
  between operations  0.71 us (2%)
    ppermute x11, waiting for transfers between devices, swap(): lax.ppermute(value, axis, [(i, i ^ mask) for i in range(lax.axis_size(axi...  12 us
    ppermute x11, starting transfers between devices, swap(): lax.ppermute(value, axis, [(i, i ^ mask) for i in range(lax.axis_size(axi...  9.89 us
    ppermute x5, starting transfers between devices, swap_by_core(): return lax.ppermute(value, ('rep', 'dp'), pairs)  8.29 us
    ppermute x5, waiting for transfers between devices, swap_by_core(): return lax.ppermute(value, ('rep', 'dp'), pairs)  7.11 us
    pallas_call x9, Pallas kernels, kernel_call(): pl.pallas_call(body, out_shape=outputs, in_specs=kwargs.pop('in_specs', [...  6.37 us
  transfers between devices with their start and end apart: 16, of which 7 were waited for; matrix products, arithmetic and copies ran while one was open for 0% of the time, Pallas kernels for 9%

profile of v10, /device:TPU:0, one launch (start us, length us, event | category | flops | bytes accessed | tf_op | source)
XLA Modules:
  0.0 44.4 jit_solution(1723851997840025661)
XLA Ops:
  0.6 1.6 %shard_map.94 = (bf16[40,2048]{1,0:T(8,128)(2,1)S(1)}, bf16[40,2048]{1,0:T(8,128)(2,1)S(1)}, bf16[40,2048]{1,0:T(8,128)(2,1)S(1)}, bf16[40,2048]{1,0:T(8,128)(2,...) custom-call(s32[2,32]{1,0:T(2,128)} %bitcast.5, bf16[2,32]{1,0:T(2,128)(2,1)} %bitcast.3, ...), custom_call_target="tpu_custom_call" | custom-call | bytes 3277440 | tf_op jit(solution)/shard_map/pallas_call | solution.py:36
  2.2 3.0 %collective-permute-start.5 = (bf16[144,2048]{1,0:T(8,128)(2,1)S(1)}, bf16[144,2048]{1,0:T(8,128)(2,1)S(1)}, u32[]{:S(2)}, u32[]{:S(2)}) collective-permute-start(bf16[144,2048]{1,0:T(8,128)(2,1)S(1)} %get-tuple-element.31.refs_4_), channel_id=1, source_target_pairs={{0,1},{1,0},{2,3},{3,2},{16,18},{17,19},{18,16},{19,17},{4,5},{5,4... | collective-permute-start | bytes 1769480 | tf_op jit(solution)/shard_map/ppermute | solution.py:30
  5.2 3.6 %collective-permute-start = (bf16[40,2048]{1,0:T(8,128)(2,1)S(1)}, bf16[40,2048]{1,0:T(8,128)(2,1)S(1)}, u32[]{:S(2)}, u32[]{:S(2)}) collective-permute-start(bf16[40,2048]{1,0:T(8,128)(2,1)S(1)} %get-tuple-element.25), channel_id=1, source_target_pairs={{0,12},{4,8},{8,4},{12,0},{1,13},{5,9},{9,5},{13,1},{2,14},{6,10},... | collective-permute-start | bytes 491528 | tf_op jit(solution)/shard_map/ppermute | solution.py:20
  8.8 0.0 collective-permute-start.1
  8.8 0.8 %collective-permute-start.2 = (bf16[40,2048]{1,0:T(8,128)(2,1)S(1)}, bf16[40,2048]{1,0:T(8,128)(2,1)S(1)}, u32[]{:S(2)}, u32[]{:S(2)}) collective-permute-start(bf16[40,2048]{1,0:T(8,128)(2,1)S(1)} %get-tuple-element.27), channel_id=1, source_target_pairs={{0,4},{4,0},{8,12},{12,8},{1,5},{5,1},{9,13},{13,9},{2,6},{6,2},{1... | collective-permute-start | bytes 491528 | tf_op jit(solution)/shard_map/ppermute | solution.py:20
  9.6 0.3 collective-permute-start.6
  9.9 3.2 %collective-permute-done.5.refs_5_ = bf16[144,2048]{1,0:T(8,128)(2,1)S(1)} collective-permute-done((bf16[144,2048]{1,0:T(8,128)(2,1)S(1)}, bf16[144,2048]{1,0:T(8,128)(2,1)S(1)}, u32[]{:S(2)}, u32[]{:S(2)}) %collective-permute-start.5) | collective-permute-done | bytes 589856 | tf_op jit(solution)/shard_map/ppermute | solution.py:30
  13.1 2.1 %collective-permute-start.7 = (bf16[144,2048]{1,0:T(8,128)(2,1)S(1)}, bf16[144,2048]{1,0:T(8,128)(2,1)S(1)}, u32[]{:S(2)}, u32[]{:S(2)}) collective-permute-start(bf16[144,2048]{1,0:T(8,128)(2,1)S(1)} %collective-permute-done.5.refs_5_), channel_id=1, source_target_pairs={{0,2},{1,3},{2,0},{3,1},{16,17},{17,16},{18,19},{19,18},{4,6},{5,7... | collective-permute-start | bytes 1769480 | tf_op jit(solution)/shard_map/ppermute | solution.py:30
  15.1 0.0 collective-permute-done.refs_0_
  15.1 7.3 %collective-permute-done.1.refs_1_ = bf16[40,2048]{1,0:T(8,128)(2,1)S(1)} collective-permute-done((bf16[40,2048]{1,0:T(8,128)(2,1)S(1)}, bf16[40,2048]{1,0:T(8,128)(2,1)S(1)}, u32[]{:S(2)}, u32[]{:S(2)}) %collective-permute-start.1) | collective-permute-done | bytes 163872 | tf_op jit(solution)/shard_map/ppermute | solution.py:20
  22.5 0.0 collective-permute-done.2.refs_2_
  22.5 0.1 shard_map.95
  22.6 0.1 collective-permute-start.3
  22.6 0.5 %collective-permute-start.4 = (bf16[80,2048]{1,0:T(8,128)(2,1)S(1)}, bf16[80,2048]{1,0:T(8,128)(2,1)S(1)}, u32[]{:S(2)}, u32[]{:S(2)}) collective-permute-start(bf16[80,2048]{1,0:T(8,128)(2,1)S(1)} %get-tuple-element.30.refs_1_), channel_id=1, source_target_pairs={{0,16},{16,0},{1,17},{17,1},{2,18},{18,2},{3,19},{19,3},{4,20},{20... | collective-permute-start | bytes 983048 | tf_op jit(solution)/shard_map/ppermute | solution.py:20
  23.1 1.1 %collective-permute-done.3.refs_2_ = bf16[80,2048]{1,0:T(8,128)(2,1)S(1)} collective-permute-done((bf16[80,2048]{1,0:T(8,128)(2,1)S(1)}, bf16[80,2048]{1,0:T(8,128)(2,1)S(1)}, u32[]{:S(2)}, u32[]{:S(2)}) %collective-permute-start.3) | collective-permute-done | bytes 327712 | tf_op jit(solution)/shard_map/ppermute | solution.py:20
  24.3 0.5 %collective-permute-done.4.refs_3_ = bf16[80,2048]{1,0:T(8,128)(2,1)S(1)} collective-permute-done((bf16[80,2048]{1,0:T(8,128)(2,1)S(1)}, bf16[80,2048]{1,0:T(8,128)(2,1)S(1)}, u32[]{:S(2)}, u32[]{:S(2)}) %collective-permute-start.4) | collective-permute-done | bytes 327712 | tf_op jit(solution)/shard_map/ppermute | solution.py:20
  24.7 0.0 collective-permute-done.6.refs_6_
  24.7 1.5 %shard_map.96 = (f32[160,2176]{1,0:T(8,128)S(1)}, f32[48,2048]{1,0:T(8,128)S(1)}, bf16[96,2048]{1,0:T(8,128)(2,1)S(1)}) custom-call(bf16[80,2048]{1,0:T(8,128)(2,1)S(1)} %get-tuple-element.29.refs_0_, bf16[80,2048]{1,0:T(8,128)(2,1)S(1)} %get-tuple-element.30.refs_1_, bf16[80,2048]{1,0:T(8,128)(2,1)S(1)} %collective-permute-done.3.refs_2_, ...), custom_call_target="tpu_custom_call" | custom-call | flops 1000000000 | bytes 5259264 | tf_op jit(solution)/shard_map/pallas_call | solution.py:36
  26.3 1.6 %collective-permute-start.13 = (bf16[96,2048]{1,0:T(8,128)(2,1)S(1)}, bf16[96,2048]{1,0:T(8,128)(2,1)S(1)}, u32[]{:S(2)}, u32[]{:S(2)}) collective-permute-start(bf16[96,2048]{1,0:T(8,128)(2,1)S(1)} %get-tuple-element.45), channel_id=1, source_target_pairs={{0,1},{1,0},{2,3},{3,2},{16,18},{17,19},{18,16},{19,17},{4,5},{5,4... | collective-permute-start | bytes 1179656 | tf_op jit(solution)/shard_map/ppermute | solution.py:30
  27.8 0.0 collective-permute-done.7.refs_5_
  27.8 1.0 %shard_map.97 = (f32[80,2176]{1,0:T(8,128)S(1)}, bf16[40,2176]{1,0:T(8,128)(2,1)S(1)}, bf16[40,2176]{1,0:T(8,128)(2,1)S(1)}, bf16[48,2048]{1,0:T(8,128)(2,1)S(1)}) custom-call(bf16[80,2048]{1,0:T(8,128)(2,1)S(1)} %get-tuple-element.29.refs_0_, bf16[80,2048]{1,0:T(8,128)(2,1)S(1)} %get-tuple-element.30.refs_1_, ...), custom_call_target="tpu_custom_call" | custom-call | bytes 4534272 | tf_op jit(solution)/shard_map/pallas_call | solution.py:36
  28.9 0.1 collective-permute-start.10
  28.9 0.5 %collective-permute-start.8 = (bf16[40,2176]{1,0:T(8,128)(2,1)S(1)}, bf16[40,2176]{1,0:T(8,128)(2,1)S(1)}, u32[]{:S(2)}, u32[]{:S(2)}) collective-permute-start(bf16[40,2176]{1,0:T(8,128)(2,1)S(1)} %get-tuple-element.35), channel_id=1, source_target_pairs={{0,16},{16,0},{1,17},{17,1},{2,18},{18,2},{3,19},{19,3},{4,20},{20... | collective-permute-start | bytes 522248 | tf_op jit(solution)/shard_map/ppermute | solution.py:20
  29.4 1.4 %collective-permute-start.14 = (bf16[48,2048]{1,0:T(8,128)(2,1)S(1)}, bf16[48,2048]{1,0:T(8,128)(2,1)S(1)}, u32[]{:S(2)}, u32[]{:S(2)}) collective-permute-start(bf16[48,2048]{1,0:T(8,128)(2,1)S(1)} %get-tuple-element.46), channel_id=1, source_target_pairs={{0,3},{1,2},{2,1},{3,0},{16,19},{17,18},{18,17},{19,16},{4,7},{5,6... | collective-permute-start | bytes 589832 | tf_op jit(solution)/shard_map/ppermute | solution.py:30
  30.8 0.0 collective-permute-done.10.got
  30.8 0.0 copy-start
  30.8 0.1 shard_map.99
  30.9 2.6 %collective-permute-start.11 = (bf16[20,2176]{1,0:T(8,128)(2,1)S(1)}, bf16[20,2176]{1,0:T(8,128)(2,1)S(1)}, u32[]{:S(2)}, u32[]{:S(2)}) collective-permute-start(bf16[20,2176]{1,0:T(8,128)(2,1)S(1)} %get-tuple-element.39), channel_id=1, source_target_pairs={{0,8},{4,12},{8,0},{12,4},{1,9},{5,13},{9,1},{13,5},{2,10},{6,14},... | collective-permute-start | bytes 261128 | tf_op jit(solution)/shard_map/ppermute | solution.py:20
  33.5 1.4 %collective-permute-start.12 = (bf16[20,2176]{1,0:T(8,128)(2,1)S(1)}, bf16[20,2176]{1,0:T(8,128)(2,1)S(1)}, u32[]{:S(2)}, u32[]{:S(2)}) collective-permute-start(bf16[20,2176]{1,0:T(8,128)(2,1)S(1)} %get-tuple-element.40), channel_id=1, source_target_pairs={{0,12},{4,8},{8,4},{12,0},{1,13},{5,9},{9,5},{13,1},{2,14},{6,10},... | collective-permute-start | bytes 261128 | tf_op jit(solution)/shard_map/ppermute | solution.py:20
  34.9 0.0 collective-permute-done.8.got
  34.9 0.1 shard_map.98
  34.9 0.3 collective-permute-start.9
  35.2 0.0 collective-permute-done.13.near
  35.3 3.9 %collective-permute-done.14.far = bf16[48,2048]{1,0:T(8,128)(2,1)S(1)} collective-permute-done((bf16[48,2048]{1,0:T(8,128)(2,1)S(1)}, bf16[48,2048]{1,0:T(8,128)(2,1)S(1)}, u32[]{:S(2)}, u32[]{:S(2)}) %collective-permute-start.14) | collective-permute-done | bytes 196640 | tf_op jit(solution)/shard_map/ppermute | solution.py:30
  39.2 0.1 shard_map.101.mine
  39.3 0.1 collective-permute-start.15
  39.3 2.8 %collective-permute-done.11.refs_2_ = bf16[20,2176]{1,0:T(8,128)(2,1)S(1)} collective-permute-done((bf16[20,2176]{1,0:T(8,128)(2,1)S(1)}, bf16[20,2176]{1,0:T(8,128)(2,1)S(1)}, u32[]{:S(2)}, u32[]{:S(2)}) %collective-permute-start.11) | collective-permute-done | bytes 87072 | tf_op jit(solution)/shard_map/ppermute | solution.py:20
  42.1 0.0 collective-permute-done.12.refs_3_
  42.1 0.3 collective-permute-done.9.refs_1_
  42.5 0.0 copy-done
  42.5 1.0 %shard_map.100 = (bf16[32,2048]{1,0:T(8,128)(2,1)}, bf16[2,32]{1,0:T(2,128)(2,1)}) custom-call(bf16[20,2176]{1,0:T(8,128)(2,1)S(1)} %get-tuple-element.36.refs_0_, bf16[20,2176]{1,0:T(8,128)(2,1)S(1)} %collective-permute-done.9.refs_1_, bf16[20,2176]{1,0:T(8,128)(2,1)S(1)} %collective-permute-done.11.refs_2_, ...), custom_call_target="tpu_custom_call" | custom-call | flops 8000000000 | bytes 479744 | tf_op jit(solution)/shard_map/pallas_call | solution.py:36
  43.4 0.0 collective-permute-done.15.theirs
  43.4 1.0 %shard_map.102 = f32[1,96,2048]{2,1,0:T(8,128)} custom-call(bf16[96,2048]{1,0:T(8,128)(2,1)S(1)} %shard_map.101.mine, bf16[96,2048]{1,0:T(8,128)(2,1)S(1)} %collective-permute-done.15.theirs), custom_call_target="tpu_custom_call" | custom-call | bytes 1572864 | tf_op jit(solution)/shard_map/pallas_call | solution.py:36
Async XLA Ops:
  2.2 10.9 %collective-permute-start.5 = (bf16[144,2048]{1,0:T(8,128)(2,1)S(1)}, bf16[144,2048]{1,0:T(8,128)(2,1)S(1)}, u32[]{:S(2)}, u32[]{:S(2)}) collective-permute-start(bf16[144,2048]{1,0:T(8,128)(2,1)S(1)} %get-tuple-element.31.refs_4_), channel_id=1, source_target_pairs={{0,1},{1,0},{2,3},{3,2},{16,18},{17,19},{18,16},{19,17},{4,5},{5,4... | collective-permute-start | bytes 1769480 | tf_op jit(solution)/shard_map/ppermute | solution.py:30
  5.2 9.9 %collective-permute-start = (bf16[40,2048]{1,0:T(8,128)(2,1)S(1)}, bf16[40,2048]{1,0:T(8,128)(2,1)S(1)}, u32[]{:S(2)}, u32[]{:S(2)}) collective-permute-start(bf16[40,2048]{1,0:T(8,128)(2,1)S(1)} %get-tuple-element.25), channel_id=1, source_target_pairs={{0,12},{4,8},{8,4},{12,0},{1,13},{5,9},{9,5},{13,1},{2,14},{6,10},... | collective-permute-start | bytes 491528 | tf_op jit(solution)/shard_map/ppermute | solution.py:20
  8.8 13.6 %collective-permute-start.1 = (bf16[40,2048]{1,0:T(8,128)(2,1)S(1)}, bf16[40,2048]{1,0:T(8,128)(2,1)S(1)}, u32[]{:S(2)}, u32[]{:S(2)}) collective-permute-start(bf16[40,2048]{1,0:T(8,128)(2,1)S(1)} %get-tuple-element.26), channel_id=1, source_target_pairs={{0,8},{4,12},{8,0},{12,4},{1,9},{5,13},{9,1},{13,5},{2,10},{6,14},... | collective-permute-start | bytes 491528 | tf_op jit(solution)/shard_map/ppermute | solution.py:20
  8.8 13.6 %collective-permute-start.2 = (bf16[40,2048]{1,0:T(8,128)(2,1)S(1)}, bf16[40,2048]{1,0:T(8,128)(2,1)S(1)}, u32[]{:S(2)}, u32[]{:S(2)}) collective-permute-start(bf16[40,2048]{1,0:T(8,128)(2,1)S(1)} %get-tuple-element.27), channel_id=1, source_target_pairs={{0,4},{4,0},{8,12},{12,8},{1,5},{5,1},{9,13},{13,9},{2,6},{6,2},{1... | collective-permute-start | bytes 491528 | tf_op jit(solution)/shard_map/ppermute | solution.py:20
  9.6 15.1 %collective-permute-start.6 = (bf16[144,2048]{1,0:T(8,128)(2,1)S(1)}, bf16[144,2048]{1,0:T(8,128)(2,1)S(1)}, u32[]{:S(2)}, u32[]{:S(2)}) collective-permute-start(bf16[144,2048]{1,0:T(8,128)(2,1)S(1)} %get-tuple-element.32), channel_id=1, source_target_pairs={{0,1},{1,0},{2,3},{3,2},{16,18},{17,19},{18,16},{19,17},{4,5},{5,4... | collective-permute-start | bytes 1769480 | tf_op jit(solution)/shard_map/ppermute | solution.py:30
  13.1 14.8 %collective-permute-start.7 = (bf16[144,2048]{1,0:T(8,128)(2,1)S(1)}, bf16[144,2048]{1,0:T(8,128)(2,1)S(1)}, u32[]{:S(2)}, u32[]{:S(2)}) collective-permute-start(bf16[144,2048]{1,0:T(8,128)(2,1)S(1)} %collective-permute-done.5.refs_5_), channel_id=1, source_target_pairs={{0,2},{1,3},{2,0},{3,1},{16,17},{17,16},{18,19},{19,18},{4,6},{5,7... | collective-permute-start | bytes 1769480 | tf_op jit(solution)/shard_map/ppermute | solution.py:30
  22.6 1.7 %collective-permute-start.3 = (bf16[80,2048]{1,0:T(8,128)(2,1)S(1)}, bf16[80,2048]{1,0:T(8,128)(2,1)S(1)}, u32[]{:S(2)}, u32[]{:S(2)}) collective-permute-start(bf16[80,2048]{1,0:T(8,128)(2,1)S(1)} %get-tuple-element.29.refs_0_), channel_id=1, source_target_pairs={{0,16},{16,0},{1,17},{17,1},{2,18},{18,2},{3,19},{19,3},{4,20},{20... | collective-permute-start | bytes 983048 | tf_op jit(solution)/shard_map/ppermute | solution.py:20
  22.6 2.1 %collective-permute-start.4 = (bf16[80,2048]{1,0:T(8,128)(2,1)S(1)}, bf16[80,2048]{1,0:T(8,128)(2,1)S(1)}, u32[]{:S(2)}, u32[]{:S(2)}) collective-permute-start(bf16[80,2048]{1,0:T(8,128)(2,1)S(1)} %get-tuple-element.30.refs_1_), channel_id=1, source_target_pairs={{0,16},{16,0},{1,17},{17,1},{2,18},{18,2},{3,19},{19,3},{4,20},{20... | collective-permute-start | bytes 983048 | tf_op jit(solution)/shard_map/ppermute | solution.py:20
  26.3 9.0 %collective-permute-start.13 = (bf16[96,2048]{1,0:T(8,128)(2,1)S(1)}, bf16[96,2048]{1,0:T(8,128)(2,1)S(1)}, u32[]{:S(2)}, u32[]{:S(2)}) collective-permute-start(bf16[96,2048]{1,0:T(8,128)(2,1)S(1)} %get-tuple-element.45), channel_id=1, source_target_pairs={{0,1},{1,0},{2,3},{3,2},{16,18},{17,19},{18,16},{19,17},{4,5},{5,4... | collective-permute-start | bytes 1179656 | tf_op jit(solution)/shard_map/ppermute | solution.py:30
  28.9 1.9 %collective-permute-start.10 = (bf16[40,2176]{1,0:T(8,128)(2,1)S(1)}, bf16[40,2176]{1,0:T(8,128)(2,1)S(1)}, u32[]{:S(2)}, u32[]{:S(2)}) collective-permute-start(bf16[40,2176]{1,0:T(8,128)(2,1)S(1)} %get-tuple-element.38), channel_id=1, source_target_pairs={{0,16},{16,0},{1,17},{17,1},{2,18},{18,2},{3,19},{19,3},{4,20},{20... | collective-permute-start | bytes 522248 | tf_op jit(solution)/shard_map/ppermute | solution.py:20
  28.9 5.9 %collective-permute-start.8 = (bf16[40,2176]{1,0:T(8,128)(2,1)S(1)}, bf16[40,2176]{1,0:T(8,128)(2,1)S(1)}, u32[]{:S(2)}, u32[]{:S(2)}) collective-permute-start(bf16[40,2176]{1,0:T(8,128)(2,1)S(1)} %get-tuple-element.35), channel_id=1, source_target_pairs={{0,16},{16,0},{1,17},{17,1},{2,18},{18,2},{3,19},{19,3},{4,20},{20... | collective-permute-start | bytes 522248 | tf_op jit(solution)/shard_map/ppermute | solution.py:20
  29.4 9.7 %collective-permute-start.14 = (bf16[48,2048]{1,0:T(8,128)(2,1)S(1)}, bf16[48,2048]{1,0:T(8,128)(2,1)S(1)}, u32[]{:S(2)}, u32[]{:S(2)}) collective-permute-start(bf16[48,2048]{1,0:T(8,128)(2,1)S(1)} %get-tuple-element.46), channel_id=1, source_target_pairs={{0,3},{1,2},{2,1},{3,0},{16,19},{17,18},{18,17},{19,16},{4,7},{5,6... | collective-permute-start | bytes 589832 | tf_op jit(solution)/shard_map/ppermute | solution.py:30
  30.8 11.6 %copy-start = (bf16[32,2]{0,1:T(2,128)(2,1)S(1)}, bf16[32,2]{0,1:T(2,128)(2,1)}, u32[]{:S(2)}) copy-start(bf16[32,2]{0,1:T(2,128)(2,1)} %param.10) | copy-start | bytes 388
  30.9 11.2 %collective-permute-start.11 = (bf16[20,2176]{1,0:T(8,128)(2,1)S(1)}, bf16[20,2176]{1,0:T(8,128)(2,1)S(1)}, u32[]{:S(2)}, u32[]{:S(2)}) collective-permute-start(bf16[20,2176]{1,0:T(8,128)(2,1)S(1)} %get-tuple-element.39), channel_id=1, source_target_pairs={{0,8},{4,12},{8,0},{12,4},{1,9},{5,13},{9,1},{13,5},{2,10},{6,14},... | collective-permute-start | bytes 261128 | tf_op jit(solution)/shard_map/ppermute | solution.py:20
  33.5 8.6 %collective-permute-start.12 = (bf16[20,2176]{1,0:T(8,128)(2,1)S(1)}, bf16[20,2176]{1,0:T(8,128)(2,1)S(1)}, u32[]{:S(2)}, u32[]{:S(2)}) collective-permute-start(bf16[20,2176]{1,0:T(8,128)(2,1)S(1)} %get-tuple-element.40), channel_id=1, source_target_pairs={{0,12},{4,8},{8,4},{12,0},{1,13},{5,9},{9,5},{13,1},{2,14},{6,10},... | collective-permute-start | bytes 261128 | tf_op jit(solution)/shard_map/ppermute | solution.py:20
  34.9 7.5 %collective-permute-start.9 = (bf16[20,2176]{1,0:T(8,128)(2,1)S(1)}, bf16[20,2176]{1,0:T(8,128)(2,1)S(1)}, u32[]{:S(2)}, u32[]{:S(2)}) collective-permute-start(bf16[20,2176]{1,0:T(8,128)(2,1)S(1)} %get-tuple-element.37), channel_id=1, source_target_pairs={{0,4},{4,0},{8,12},{12,8},{1,5},{5,1},{9,13},{13,9},{2,6},{6,2},{1... | collective-permute-start | bytes 261128 | tf_op jit(solution)/shard_map/ppermute | solution.py:20
  39.3 4.2 %collective-permute-start.15 = (bf16[96,2048]{1,0:T(8,128)(2,1)S(1)}, bf16[96,2048]{1,0:T(8,128)(2,1)S(1)}, u32[]{:S(2)}, u32[]{:S(2)}) collective-permute-start(bf16[96,2048]{1,0:T(8,128)(2,1)S(1)} %shard_map.101.mine), channel_id=1, source_target_pairs={{0,16},{16,0},{1,17},{17,1},{2,18},{18,2},{3,19},{19,3},{4,20},{20... | collective-permute-start | bytes 1179656 | tf_op jit(solution)/shard_map/ppermute | solution.py:20

commit v11 on v9

--- a/solution.py
+++ b/solution.py
@@ -48,19 +48,28 @@
     return lax.broadcasted_iota(jnp.int32, shape, dim)
 
 
+def pack_copies(weights, packed, half, sems):
+    hidden = packed.shape[0] // 3
+    rows = pl.ds(pl.multiple_of(half * hidden, hidden), hidden)
+    return [
+        pltpu.make_async_copy(weight.at[0, rows], packed.at[pl.ds(i * hidden, hidden)], sems.at[i])
+        for i, weight in enumerate(weights)
+    ]
+
+
+def pack_kernel(gate, up, down, packed, sems):
+    copies = pack_copies((gate, up, down), packed, lax.axis_index("rep"), sems)
+    for copy in copies:
+        copy.start()
+    for copy in copies:
+        copy.wait()
+
+
 def dispatch_kernel(experts, cap, chunk_count, *refs):
     given, weights, refs = refs[:4], refs[4:7], refs[7:]
-    chunks, (slot_out, *packed), (*held, sems) = refs[:chunk_count], refs[chunk_count:-5], refs[-5:]
-    hidden = packed[0].shape[0] // 3
-    rep = lax.axis_index("rep")
-    loads = [pltpu.make_async_copy(*pair, sems.at[i]) for i, pair in enumerate(zip(given, held))]
-    packs = []
-    for j, half in enumerate((rep, 1 - rep)):
-        rows = pl.ds(pl.multiple_of(half * hidden, hidden), hidden)
-        packs += [
-            pltpu.make_async_copy(weight.at[0, rows], packed[j].at[pl.ds(i * hidden, hidden)], sems.at[4 + 3 * j + i])
-            for i, weight in enumerate(weights)
-        ]
+    chunks, (slot_out, packed, *held), sems = refs[:chunk_count], refs[chunk_count:-1], refs[-1]
+    loads = [pltpu.make_async_copy(*pair, sems.at[3 + i]) for i, pair in enumerate(zip(given, held))]
+    packs = pack_copies(weights, packed, 1 - lax.axis_index("rep"), sems)
     for copy in loads + packs:
         copy.start()
     for copy in loads[:2]:
@@ -120,7 +129,7 @@
     prob = jnp.sum(act * d_act, axis=1, keepdims=True)
     d_gate = d_act * up_pre * sig * (1.0 + gate_pre * (1.0 - sig))
     d_pre = jnp.concatenate([d_gate, d_act * silu], axis=1).astype(bf16)
-    return dot(d_pre, mixers, (1, 0)), prob, dot(act.astype(bf16), d_rows, (0, 0))
+    return dot(d_pre, mixers, (1, 0)), prob, act.astype(bf16)
 
 
 def gather_kernel(*refs):
@@ -136,24 +145,29 @@
 
 
 def early_kernel(*refs):
-    *pieces, dx_out, grad_own, grad_near = refs[4:]
-    dx, prob, grad = expert_math(*both_cores(*refs[:4]), pieces)
-    width, hidden = dx.shape[1], grad_own.shape[0]
+    *pieces, dx_out, act_out = refs[4:]
+    dx, prob, act_out[...] = expert_math(*both_cores(*refs[:4]), pieces)
+    width = dx.shape[1]
     dx_out[:, :width] = dx
     dx_out[:, width:] = jnp.broadcast_to(prob, (prob.shape[0], LANES))
-    grad_own[...] = grad[:hidden]
-    grad_near[...] = grad[hidden:].astype(bf16)
 
 
 def late_kernel(*refs):
-    dx_ref, far, keep, give, grad_far = refs[4:]
-    dx, prob, grad = expert_math(*both_cores(*refs[:4]), [far])
+    dx_ref, far, keep, give, act_out = refs[4:]
+    dx, prob, act_out[...] = expert_math(*both_cores(*refs[:4]), [far])
     width, slots = dx.shape[1], keep.shape[0]
     for side, value in ((slice(0, width), dx), (slice(width, None), jnp.broadcast_to(prob, (prob.shape[0], LANES)))):
         total = value + dx_ref[:, side]
         keep[:, side] = total[:slots]
         give[:, side] = total[slots:].astype(bf16)
-    grad_far[...] = grad.astype(bf16)
+
+
+def down_kernel(act, d_own, d_other, *grads):
+    total = dot(act[...], jnp.concatenate([d_own[...], d_other[...]]), (0, 0))
+    start = 0
+    for grad in grads:
+        grad[...] = total[start : start + grad.shape[0]].astype(grad.dtype)
+        start += grad.shape[0]
 
 
 def grad_kernel(own, near, far, out):
@@ -211,14 +225,24 @@
     in_hbm = pl.BlockSpec(memory_space=pltpu.HBM)
 
     given = [expert_ids.T, route_weight.T, tokens, upstream]
-    *chunks, slot, first, second = kernel_call(
+    given, weights = [
+        [pltpu.with_memory_space_constraint(a, pltpu.HBM) for a in arrays]
+        for arrays in (given, (gate_weight, up_weight, down_weight))
+    ]
+    (first,) = kernel_call(
+        pack_kernel,
+        weights,
+        [shape((3 * hidden, width), bf16)],
+        in_specs=[in_hbm] * 3,
+        scratch_shapes=[pltpu.SemaphoreType.DMA((3,))],
+    )
+    *chunks, slot, second = kernel_call(
         functools.partial(dispatch_kernel, experts, cap, chunk_count),
-        [pltpu.with_memory_space_constraint(a, pltpu.HBM) for a in [*given, gate_weight, up_weight, down_weight]],
+        given + weights,
         [shape((2 * rows, width), bf16)] * chunk_count
-        + [shape((top, tok_dev), jnp.int32)]
-        + [shape((3 * hidden, width), bf16)] * 2,
+        + [shape((top, tok_dev), jnp.int32), shape((3 * hidden, width), bf16)],
         in_specs=[in_hbm] * 7,
-        scratch_shapes=[pltpu.VMEM(a.shape, a.dtype) for a in given] + [pltpu.SemaphoreType.DMA((10,))],
+        scratch_shapes=[pltpu.VMEM(a.shape, a.dtype) for a in given] + [pltpu.SemaphoreType.DMA((7,))],
     )
 
     along, across = (1, 2), (2, 1)
@@ -235,17 +259,21 @@
     other = [swap(part, "rep", 1) for part in own]
 
     wide = width + LANES
-    dx, grad_own, grad_near = kernel_call(
+    dx, act = kernel_call(
         early_kernel,
         [*own, *other, first, *near],
-        [shape((2 * slots, wide), f32), shape((hidden, width), f32), shape((2 * hidden, width), bf16)],
+        [shape((2 * slots, wide), f32), shape((2 * slots, 3 * hidden), bf16)],
         flops=2 * 10**9,
     )
-    keep, give, grad_far = kernel_call(
+    grad_own, grad_near = kernel_call(
+        down_kernel, [act, own[1], other[1]], [shape((hidden, width), f32), shape((2 * hidden, width), bf16)]
+    )
+    keep, give, act = kernel_call(
         late_kernel,
         [*own, *other, dx, far],
-        [shape((slots, wide), f32), shape((slots, wide), bf16), shape((hidden, width), bf16)],
-    )
+        [shape((slots, wide), f32), shape((slots, wide), bf16), shape((2 * slots, hidden), bf16)],
+    )
+    (grad_far,) = kernel_call(down_kernel, [act, own[1], other[1]], [shape((hidden, width), bf16)])
     places = [0, chunk_count - 1, *range(1, chunk_count - 1)][:chunk_count]
     back = kernel_call(
         functools.partial(add_kernel, places),

time: 45 us -> 46.4 us (1.031)
  Pallas kernels: 6.36 us -> 7.71 us
    pallas_call x8 -> x11, Pallas kernels: 6.36 us -> 7.71 us  [kernel_call(): pl.pallas_call(body, out_shape=outputs, in_specs=kwargs.pop('in_specs', [...]
    ppermute x5, waiting for transfers between devices: 8.57 us -> 7.45 us  [swap_by_core(): return lax.ppermute(value, ('rep', 'dp'), pairs)]
    ppermute x10, waiting for transfers between devices: 11.4 us -> 12.3 us  [swap(): lax.ppermute(value, axis, [(i, i ^ mask) for i in range(lax.axis_size(axi...]
  transfers between devices with their start and end apart: 15 -> 15, of which waited for: 7 -> 9; matrix products, arithmetic and copies ran while one was open for 0% -> 0% of each run, Pallas kernels for 6% -> 10%
where the time goes in v11:
time: 46.4 us; the launch traced here: 46.2 us
  waiting for transfers between devices  19.7 us (42%)
  starting transfers between devices  18 us (39%)
  Pallas kernels  7.71 us (17%)
  between operations  0.75 us (2%)
    ppermute x10, waiting for transfers between devices, swap(): lax.ppermute(value, axis, [(i, i ^ mask) for i in range(lax.axis_size(axi...  12.3 us
    ppermute x10, starting transfers between devices, swap(): lax.ppermute(value, axis, [(i, i ^ mask) for i in range(lax.axis_size(axi...  9.62 us
    ppermute x5, starting transfers between devices, swap_by_core(): return lax.ppermute(value, ('rep', 'dp'), pairs)  8.43 us
    pallas_call x11, Pallas kernels, kernel_call(): pl.pallas_call(body, out_shape=outputs, in_specs=kwargs.pop('in_specs', [...  7.71 us
    ppermute x5, waiting for transfers between devices, swap_by_core(): return lax.ppermute(value, ('rep', 'dp'), pairs)  7.45 us
  transfers between devices with their start and end apart: 15, of which 9 were waited for; matrix products, arithmetic and copies ran while one was open for 0% of the time, Pallas kernels for 10%

profile of v11, /device:TPU:0, one launch (start us, length us, event | category | flops | bytes accessed | tf_op | source)
XLA Modules:
  0.0 46.2 jit_solution(10018209734397493780)
XLA Ops:
  0.6 1.2 %shard_map.96.refs_4_ = bf16[144,2048]{1,0:T(8,128)(2,1)S(1)} custom-call(bf16[1,96,2048]{2,1,0:T(8,128)(2,1)} %gate.1, bf16[1,96,2048]{2,1,0:T(8,128)(2,1)} %up.1, bf16[1,96,2048]{2,1,0:T(8,128)(2,1)} %down.1), custom_call_target="tpu_custom_call" | custom-call | bytes 1769472 | tf_op jit(solution)/shard_map/pallas_call | solution.py:36
  1.8 3.0 %collective-permute-start.5 = (bf16[144,2048]{1,0:T(8,128)(2,1)S(1)}, bf16[144,2048]{1,0:T(8,128)(2,1)S(1)}, u32[]{:S(2)}, u32[]{:S(2)}) collective-permute-start(bf16[144,2048]{1,0:T(8,128)(2,1)S(1)} %shard_map.96.refs_4_), channel_id=1, source_target_pairs={{0,1},{1,0},{2,3},{3,2},{16,18},{17,19},{18,16},{19,17},{4,5},{5,4... | collective-permute-start | bytes 1769480 | tf_op jit(solution)/shard_map/ppermute | solution.py:30
  4.8 1.5 %shard_map.94 = (bf16[40,2048]{1,0:T(8,128)(2,1)S(1)}, bf16[40,2048]{1,0:T(8,128)(2,1)S(1)}, bf16[40,2048]{1,0:T(8,128)(2,1)S(1)}, bf16[40,2048]{1,0:T(8,128)(2,...) custom-call(s32[2,32]{1,0:T(2,128)} %bitcast.5, bf16[2,32]{1,0:T(2,128)(2,1)} %bitcast.3, ...), custom_call_target="tpu_custom_call" | custom-call | bytes 2687616 | tf_op jit(solution)/shard_map/pallas_call | solution.py:36
  6.3 3.7 %collective-permute-start = (bf16[40,2048]{1,0:T(8,128)(2,1)S(1)}, bf16[40,2048]{1,0:T(8,128)(2,1)S(1)}, u32[]{:S(2)}, u32[]{:S(2)}) collective-permute-start(bf16[40,2048]{1,0:T(8,128)(2,1)S(1)} %get-tuple-element.25), channel_id=1, source_target_pairs={{0,12},{4,8},{8,4},{12,0},{1,13},{5,9},{9,5},{13,1},{2,14},{6,10},... | collective-permute-start | bytes 491528 | tf_op jit(solution)/shard_map/ppermute | solution.py:20
  10.0 0.0 collective-permute-start.1
  10.0 0.8 %collective-permute-start.2 = (bf16[40,2048]{1,0:T(8,128)(2,1)S(1)}, bf16[40,2048]{1,0:T(8,128)(2,1)S(1)}, u32[]{:S(2)}, u32[]{:S(2)}) collective-permute-start(bf16[40,2048]{1,0:T(8,128)(2,1)S(1)} %get-tuple-element.27), channel_id=1, source_target_pairs={{0,4},{4,0},{8,12},{12,8},{1,5},{5,1},{9,13},{13,9},{2,6},{6,2},{1... | collective-permute-start | bytes 491528 | tf_op jit(solution)/shard_map/ppermute | solution.py:20
  10.8 0.4 collective-permute-start.6
  11.2 1.5 %collective-permute-done.5.refs_5_ = bf16[144,2048]{1,0:T(8,128)(2,1)S(1)} collective-permute-done((bf16[144,2048]{1,0:T(8,128)(2,1)S(1)}, bf16[144,2048]{1,0:T(8,128)(2,1)S(1)}, u32[]{:S(2)}, u32[]{:S(2)}) %collective-permute-start.5) | collective-permute-done | bytes 589856 | tf_op jit(solution)/shard_map/ppermute | solution.py:30
  12.7 2.0 %collective-permute-start.7 = (bf16[144,2048]{1,0:T(8,128)(2,1)S(1)}, bf16[144,2048]{1,0:T(8,128)(2,1)S(1)}, u32[]{:S(2)}, u32[]{:S(2)}) collective-permute-start(bf16[144,2048]{1,0:T(8,128)(2,1)S(1)} %collective-permute-done.5.refs_5_), channel_id=1, source_target_pairs={{0,2},{1,3},{2,0},{3,1},{16,17},{17,16},{18,19},{19,18},{4,6},{5,7... | collective-permute-start | bytes 1769480 | tf_op jit(solution)/shard_map/ppermute | solution.py:30
  14.7 0.7 %collective-permute-done.refs_1_ = bf16[40,2048]{1,0:T(8,128)(2,1)S(1)} collective-permute-done((bf16[40,2048]{1,0:T(8,128)(2,1)S(1)}, bf16[40,2048]{1,0:T(8,128)(2,1)S(1)}, u32[]{:S(2)}, u32[]{:S(2)}) %collective-permute-start) | collective-permute-done | bytes 163872 | tf_op jit(solution)/shard_map/ppermute | solution.py:20
  15.4 8.3 %collective-permute-done.1.refs_2_ = bf16[40,2048]{1,0:T(8,128)(2,1)S(1)} collective-permute-done((bf16[40,2048]{1,0:T(8,128)(2,1)S(1)}, bf16[40,2048]{1,0:T(8,128)(2,1)S(1)}, u32[]{:S(2)}, u32[]{:S(2)}) %collective-permute-start.1) | collective-permute-done | bytes 163872 | tf_op jit(solution)/shard_map/ppermute | solution.py:20
  23.6 0.0 collective-permute-done.2.refs_3_
  23.6 0.1 shard_map.95
  23.8 0.1 collective-permute-start.4
  23.8 0.5 %collective-permute-start.3 = (bf16[80,2048]{1,0:T(8,128)(2,1)S(1)}, bf16[80,2048]{1,0:T(8,128)(2,1)S(1)}, u32[]{:S(2)}, u32[]{:S(2)}) collective-permute-start(bf16[80,2048]{1,0:T(8,128)(2,1)S(1)} %get-tuple-element.28.refs_0_), channel_id=1, source_target_pairs={{0,16},{16,0},{1,17},{17,1},{2,18},{18,2},{3,19},{19,3},{4,20},{20... | collective-permute-start | bytes 983048 | tf_op jit(solution)/shard_map/ppermute | solution.py:20
  24.3 1.1 %collective-permute-done.4.refs_3_.d_other = bf16[80,2048]{1,0:T(8,128)(2,1)S(1)} collective-permute-done((bf16[80,2048]{1,0:T(8,128)(2,1)S(1)}, bf16[80,2048]{1,0:T(8,128)(2,1)S(1)}, u32[]{:S(2)}, u32[]{:S(2)}) %collective-permute-start.4) | collective-permute-done | bytes 327712 | tf_op jit(solution)/shard_map/ppermute | solution.py:20
  25.4 0.5 %collective-permute-done.3.refs_2_ = bf16[80,2048]{1,0:T(8,128)(2,1)S(1)} collective-permute-done((bf16[80,2048]{1,0:T(8,128)(2,1)S(1)}, bf16[80,2048]{1,0:T(8,128)(2,1)S(1)}, u32[]{:S(2)}, u32[]{:S(2)}) %collective-permute-start.3) | collective-permute-done | bytes 327712 | tf_op jit(solution)/shard_map/ppermute | solution.py:20
  25.9 0.9 %collective-permute-done.6.refs_6_ = bf16[144,2048]{1,0:T(8,128)(2,1)S(1)} collective-permute-done((bf16[144,2048]{1,0:T(8,128)(2,1)S(1)}, bf16[144,2048]{1,0:T(8,128)(2,1)S(1)}, u32[]{:S(2)}, u32[]{:S(2)}) %collective-permute-start.6) | collective-permute-done | bytes 589856 | tf_op jit(solution)/shard_map/ppermute | solution.py:30
  26.8 1.4 %shard_map.97 = (f32[160,2176]{1,0:T(8,128)S(1)}, bf16[160,144]{1,0:T(8,128)(2,1)S(1)}) custom-call(bf16[80,2048]{1,0:T(8,128)(2,1)S(1)} %get-tuple-element.28.refs_0_, bf16[80,2048]{1,0:T(8,128)(2,1)S(1)} %get-tuple-element.29.refs_1_.d_own, bf16[80,2048]{1,0:T(8,128)(2,1)S(1)} %collective-permute-done.3.refs_2_, ...), custom_call_target="tpu_custom_call" | custom-call | flops 2000000000 | bytes 4518912 | tf_op jit(solution)/shard_map/pallas_call | solution.py:36
  28.2 0.0 collective-permute-done.7.refs_5_
  28.2 0.8 %shard_map.98 = (f32[80,2176]{1,0:T(8,128)S(1)}, bf16[80,2176]{1,0:T(8,128)(2,1)S(1)}, bf16[160,48]{1,0:T(8,128)(2,1)S(1)}) custom-call(bf16[80,2048]{1,0:T(8,128)(2,1)S(1)} %get-tuple-element.28.refs_0_, bf16[80,2048]{1,0:T(8,128)(2,1)S(1)} %get-tuple-element.29.refs_1_.d_own, bf16[80,2048]{1,0:T(8,128)(2,1)S(1)} %collective-permute-done.3.refs_2_, ...), custom_call_target="tpu_custom_call" | custom-call | bytes 4353024 | tf_op jit(solution)/shard_map/pallas_call | solution.py:36
  29.1 0.1 collective-permute-start.8
  29.1 0.3 shard_map.101
  29.5 0.8 %collective-permute-start.12 = (bf16[96,2048]{1,0:T(8,128)(2,1)S(1)}, bf16[96,2048]{1,0:T(8,128)(2,1)S(1)}, u32[]{:S(2)}, u32[]{:S(2)}) collective-permute-start(bf16[96,2048]{1,0:T(8,128)(2,1)S(1)} %get-tuple-element.43), channel_id=1, source_target_pairs={{0,1},{1,0},{2,3},{3,2},{16,18},{17,19},{18,16},{19,17},{4,5},{5,4... | collective-permute-start | bytes 1179656 | tf_op jit(solution)/shard_map/ppermute | solution.py:30
  30.3 0.2 shard_map.102
  30.5 0.0 copy-start
  30.5 2.2 %collective-permute-start.13 = (bf16[48,2048]{1,0:T(8,128)(2,1)S(1)}, bf16[48,2048]{1,0:T(8,128)(2,1)S(1)}, u32[]{:S(2)}, u32[]{:S(2)}) collective-permute-start(bf16[48,2048]{1,0:T(8,128)(2,1)S(1)} %shard_map.102), channel_id=1, source_target_pairs={{0,3},{1,2},{2,1},{3,0},{16,19},{17,18},{18,17},{19,16},{4,7},{5,6... | collective-permute-start | bytes 589832 | tf_op jit(solution)/shard_map/ppermute | solution.py:30
  32.7 0.0 collective-permute-done.8.got
  32.7 0.1 shard_map.99
  32.8 3.6 %collective-permute-start.10 = (bf16[20,2176]{1,0:T(8,128)(2,1)S(1)}, bf16[20,2176]{1,0:T(8,128)(2,1)S(1)}, u32[]{:S(2)}, u32[]{:S(2)}) collective-permute-start(bf16[20,2176]{1,0:T(8,128)(2,1)S(1)} %get-tuple-element.36), channel_id=1, source_target_pairs={{0,12},{4,8},{8,4},{12,0},{1,13},{5,9},{9,5},{13,1},{2,14},{6,10},... | collective-permute-start | bytes 261128 | tf_op jit(solution)/shard_map/ppermute | solution.py:20
  36.5 0.0 collective-permute-start.11
  36.5 0.8 %collective-permute-start.9 = (bf16[20,2176]{1,0:T(8,128)(2,1)S(1)}, bf16[20,2176]{1,0:T(8,128)(2,1)S(1)}, u32[]{:S(2)}, u32[]{:S(2)}) collective-permute-start(bf16[20,2176]{1,0:T(8,128)(2,1)S(1)} %get-tuple-element.35), channel_id=1, source_target_pairs={{0,4},{4,0},{8,12},{12,8},{1,5},{5,1},{9,13},{13,9},{2,6},{6,2},{1... | collective-permute-start | bytes 261128 | tf_op jit(solution)/shard_map/ppermute | solution.py:20
  37.3 2.1 %collective-permute-done.12.near = bf16[96,2048]{1,0:T(8,128)(2,1)S(1)} collective-permute-done((bf16[96,2048]{1,0:T(8,128)(2,1)S(1)}, bf16[96,2048]{1,0:T(8,128)(2,1)S(1)}, u32[]{:S(2)}, u32[]{:S(2)}) %collective-permute-start.12) | collective-permute-done | bytes 393248 | tf_op jit(solution)/shard_map/ppermute | solution.py:30
  39.4 2.9 %collective-permute-done.13.far = bf16[48,2048]{1,0:T(8,128)(2,1)S(1)} collective-permute-done((bf16[48,2048]{1,0:T(8,128)(2,1)S(1)}, bf16[48,2048]{1,0:T(8,128)(2,1)S(1)}, u32[]{:S(2)}, u32[]{:S(2)}) %collective-permute-start.13) | collective-permute-done | bytes 196640 | tf_op jit(solution)/shard_map/ppermute | solution.py:30
  42.4 0.1 shard_map.103.mine
  42.4 0.1 collective-permute-start.14
  42.5 0.0 collective-permute-done.10.refs_2_
  42.5 1.7 %collective-permute-done.11.refs_3_ = bf16[20,2176]{1,0:T(8,128)(2,1)S(1)} collective-permute-done((bf16[20,2176]{1,0:T(8,128)(2,1)S(1)}, bf16[20,2176]{1,0:T(8,128)(2,1)S(1)}, u32[]{:S(2)}, u32[]{:S(2)}) %collective-permute-start.11) | collective-permute-done | bytes 87072 | tf_op jit(solution)/shard_map/ppermute | solution.py:20
  44.3 0.0 collective-permute-done.9.refs_1_
  44.3 0.0 copy-done
  44.3 1.0 %shard_map.100 = (bf16[32,2048]{1,0:T(8,128)(2,1)}, bf16[2,32]{1,0:T(2,128)(2,1)}) custom-call(bf16[20,2176]{1,0:T(8,128)(2,1)S(1)} %get-tuple-element.34.refs_0_, bf16[20,2176]{1,0:T(8,128)(2,1)S(1)} %collective-permute-done.9.refs_1_, bf16[20,2176]{1,0:T(8,128)(2,1)S(1)} %collective-permute-done.10.refs_2_, ...), custom_call_target="tpu_custom_call" | custom-call | flops 8000000000 | bytes 479744 | tf_op jit(solution)/shard_map/pallas_call | solution.py:36
  45.2 0.0 collective-permute-done.14.theirs
  45.3 1.0 %shard_map.104 = f32[1,96,2048]{2,1,0:T(8,128)} custom-call(bf16[96,2048]{1,0:T(8,128)(2,1)S(1)} %shard_map.103.mine, bf16[96,2048]{1,0:T(8,128)(2,1)S(1)} %collective-permute-done.14.theirs), custom_call_target="tpu_custom_call" | custom-call | bytes 1572864 | tf_op jit(solution)/shard_map/pallas_call | solution.py:36
Async XLA Ops:
  1.8 10.9 %collective-permute-start.5 = (bf16[144,2048]{1,0:T(8,128)(2,1)S(1)}, bf16[144,2048]{1,0:T(8,128)(2,1)S(1)}, u32[]{:S(2)}, u32[]{:S(2)}) collective-permute-start(bf16[144,2048]{1,0:T(8,128)(2,1)S(1)} %shard_map.96.refs_4_), channel_id=1, source_target_pairs={{0,1},{1,0},{2,3},{3,2},{16,18},{17,19},{18,16},{19,17},{4,5},{5,4... | collective-permute-start | bytes 1769480 | tf_op jit(solution)/shard_map/ppermute | solution.py:30
  6.3 9.0 %collective-permute-start = (bf16[40,2048]{1,0:T(8,128)(2,1)S(1)}, bf16[40,2048]{1,0:T(8,128)(2,1)S(1)}, u32[]{:S(2)}, u32[]{:S(2)}) collective-permute-start(bf16[40,2048]{1,0:T(8,128)(2,1)S(1)} %get-tuple-element.25), channel_id=1, source_target_pairs={{0,12},{4,8},{8,4},{12,0},{1,13},{5,9},{9,5},{13,1},{2,14},{6,10},... | collective-permute-start | bytes 491528 | tf_op jit(solution)/shard_map/ppermute | solution.py:20
  10.0 13.6 %collective-permute-start.1 = (bf16[40,2048]{1,0:T(8,128)(2,1)S(1)}, bf16[40,2048]{1,0:T(8,128)(2,1)S(1)}, u32[]{:S(2)}, u32[]{:S(2)}) collective-permute-start(bf16[40,2048]{1,0:T(8,128)(2,1)S(1)} %get-tuple-element.26), channel_id=1, source_target_pairs={{0,8},{4,12},{8,0},{12,4},{1,9},{5,13},{9,1},{13,5},{2,10},{6,14},... | collective-permute-start | bytes 491528 | tf_op jit(solution)/shard_map/ppermute | solution.py:20
  10.0 13.6 %collective-permute-start.2 = (bf16[40,2048]{1,0:T(8,128)(2,1)S(1)}, bf16[40,2048]{1,0:T(8,128)(2,1)S(1)}, u32[]{:S(2)}, u32[]{:S(2)}) collective-permute-start(bf16[40,2048]{1,0:T(8,128)(2,1)S(1)} %get-tuple-element.27), channel_id=1, source_target_pairs={{0,4},{4,0},{8,12},{12,8},{1,5},{5,1},{9,13},{13,9},{2,6},{6,2},{1... | collective-permute-start | bytes 491528 | tf_op jit(solution)/shard_map/ppermute | solution.py:20
  10.8 16.0 %collective-permute-start.6 = (bf16[144,2048]{1,0:T(8,128)(2,1)S(1)}, bf16[144,2048]{1,0:T(8,128)(2,1)S(1)}, u32[]{:S(2)}, u32[]{:S(2)}) collective-permute-start(bf16[144,2048]{1,0:T(8,128)(2,1)S(1)} %get-tuple-element.30), channel_id=1, source_target_pairs={{0,1},{1,0},{2,3},{3,2},{16,18},{17,19},{18,16},{19,17},{4,5},{5,4... | collective-permute-start | bytes 1769480 | tf_op jit(solution)/shard_map/ppermute | solution.py:30
  12.7 15.5 %collective-permute-start.7 = (bf16[144,2048]{1,0:T(8,128)(2,1)S(1)}, bf16[144,2048]{1,0:T(8,128)(2,1)S(1)}, u32[]{:S(2)}, u32[]{:S(2)}) collective-permute-start(bf16[144,2048]{1,0:T(8,128)(2,1)S(1)} %collective-permute-done.5.refs_5_), channel_id=1, source_target_pairs={{0,2},{1,3},{2,0},{3,1},{16,17},{17,16},{18,19},{19,18},{4,6},{5,7... | collective-permute-start | bytes 1769480 | tf_op jit(solution)/shard_map/ppermute | solution.py:30
  23.8 1.7 %collective-permute-start.4 = (bf16[80,2048]{1,0:T(8,128)(2,1)S(1)}, bf16[80,2048]{1,0:T(8,128)(2,1)S(1)}, u32[]{:S(2)}, u32[]{:S(2)}) collective-permute-start(bf16[80,2048]{1,0:T(8,128)(2,1)S(1)} %get-tuple-element.29.refs_1_.d_own), channel_id=1, source_target_pairs={{0,16},{16,0},{1,17},{17,1},{2,18},{18,2},{3,19},{19,3},{4,20},{20... | collective-permute-start | bytes 983048 | tf_op jit(solution)/shard_map/ppermute | solution.py:20
  23.8 2.1 %collective-permute-start.3 = (bf16[80,2048]{1,0:T(8,128)(2,1)S(1)}, bf16[80,2048]{1,0:T(8,128)(2,1)S(1)}, u32[]{:S(2)}, u32[]{:S(2)}) collective-permute-start(bf16[80,2048]{1,0:T(8,128)(2,1)S(1)} %get-tuple-element.28.refs_0_), channel_id=1, source_target_pairs={{0,16},{16,0},{1,17},{17,1},{2,18},{18,2},{3,19},{19,3},{4,20},{20... | collective-permute-start | bytes 983048 | tf_op jit(solution)/shard_map/ppermute | solution.py:20
  29.1 3.7 %collective-permute-start.8 = (bf16[80,2176]{1,0:T(8,128)(2,1)S(1)}, bf16[80,2176]{1,0:T(8,128)(2,1)S(1)}, u32[]{:S(2)}, u32[]{:S(2)}) collective-permute-start(bf16[80,2176]{1,0:T(8,128)(2,1)S(1)} %get-tuple-element.33), channel_id=1, source_target_pairs={{0,16},{16,0},{1,17},{17,1},{2,18},{18,2},{3,19},{19,3},{4,20},{20... | collective-permute-start | bytes 1044488 | tf_op jit(solution)/shard_map/ppermute | solution.py:20
  29.5 9.9 %collective-permute-start.12 = (bf16[96,2048]{1,0:T(8,128)(2,1)S(1)}, bf16[96,2048]{1,0:T(8,128)(2,1)S(1)}, u32[]{:S(2)}, u32[]{:S(2)}) collective-permute-start(bf16[96,2048]{1,0:T(8,128)(2,1)S(1)} %get-tuple-element.43), channel_id=1, source_target_pairs={{0,1},{1,0},{2,3},{3,2},{16,18},{17,19},{18,16},{19,17},{4,5},{5,4... | collective-permute-start | bytes 1179656 | tf_op jit(solution)/shard_map/ppermute | solution.py:30
  30.5 13.7 %copy-start = (bf16[32,2]{0,1:T(2,128)(2,1)S(1)}, bf16[32,2]{0,1:T(2,128)(2,1)}, u32[]{:S(2)}) copy-start(bf16[32,2]{0,1:T(2,128)(2,1)} %param.10) | copy-start | bytes 388
  30.5 11.8 %collective-permute-start.13 = (bf16[48,2048]{1,0:T(8,128)(2,1)S(1)}, bf16[48,2048]{1,0:T(8,128)(2,1)S(1)}, u32[]{:S(2)}, u32[]{:S(2)}) collective-permute-start(bf16[48,2048]{1,0:T(8,128)(2,1)S(1)} %shard_map.102), channel_id=1, source_target_pairs={{0,3},{1,2},{2,1},{3,0},{16,19},{17,18},{18,17},{19,16},{4,7},{5,6... | collective-permute-start | bytes 589832 | tf_op jit(solution)/shard_map/ppermute | solution.py:30
  32.8 9.7 %collective-permute-start.10 = (bf16[20,2176]{1,0:T(8,128)(2,1)S(1)}, bf16[20,2176]{1,0:T(8,128)(2,1)S(1)}, u32[]{:S(2)}, u32[]{:S(2)}) collective-permute-start(bf16[20,2176]{1,0:T(8,128)(2,1)S(1)} %get-tuple-element.36), channel_id=1, source_target_pairs={{0,12},{4,8},{8,4},{12,0},{1,13},{5,9},{9,5},{13,1},{2,14},{6,10},... | collective-permute-start | bytes 261128 | tf_op jit(solution)/shard_map/ppermute | solution.py:20
  36.5 7.8 %collective-permute-start.11 = (bf16[20,2176]{1,0:T(8,128)(2,1)S(1)}, bf16[20,2176]{1,0:T(8,128)(2,1)S(1)}, u32[]{:S(2)}, u32[]{:S(2)}) collective-permute-start(bf16[20,2176]{1,0:T(8,128)(2,1)S(1)} %get-tuple-element.37), channel_id=1, source_target_pairs={{0,8},{4,12},{8,0},{12,4},{1,9},{5,13},{9,1},{13,5},{2,10},{6,14},... | collective-permute-start | bytes 261128 | tf_op jit(solution)/shard_map/ppermute | solution.py:20
  36.5 7.8 %collective-permute-start.9 = (bf16[20,2176]{1,0:T(8,128)(2,1)S(1)}, bf16[20,2176]{1,0:T(8,128)(2,1)S(1)}, u32[]{:S(2)}, u32[]{:S(2)}) collective-permute-start(bf16[20,2176]{1,0:T(8,128)(2,1)S(1)} %get-tuple-element.35), channel_id=1, source_target_pairs={{0,4},{4,0},{8,12},{12,8},{1,5},{5,1},{9,13},{13,9},{2,6},{6,2},{1... | collective-permute-start | bytes 261128 | tf_op jit(solution)/shard_map/ppermute | solution.py:20
  42.4 2.8 %collective-permute-start.14 = (bf16[96,2048]{1,0:T(8,128)(2,1)S(1)}, bf16[96,2048]{1,0:T(8,128)(2,1)S(1)}, u32[]{:S(2)}, u32[]{:S(2)}) collective-permute-start(bf16[96,2048]{1,0:T(8,128)(2,1)S(1)} %shard_map.103.mine), channel_id=1, source_target_pairs={{0,16},{16,0},{1,17},{17,1},{2,18},{18,2},{3,19},{19,3},{4,20},{20... | collective-permute-start | bytes 1179656 | tf_op jit(solution)/shard_map/ppermute | solution.py:20

commit v12 on v10

--- a/solution.py
+++ b/solution.py
@@ -144,6 +144,16 @@
     grad_near[...] = grad[hidden:].astype(bf16)
 
 
+def middle_kernel(*refs):
+    dx_ref, grad_ref, piece, dx_out, grad_out = refs[4:]
+    dx, prob, grad = expert_math(*both_cores(*refs[:4]), [piece])
+    width, hidden = dx.shape[1], grad.shape[0]
+    dx_out[:, :width] = dx_ref[:, :width] + dx
+    dx_out[:, width:] = dx_ref[:, width:] + prob
+    grad_out[:hidden] = grad_ref[...]
+    grad_out[hidden:] = grad.astype(bf16)
+
+
 def late_kernel(*refs):
     dx_ref, far, keep, *gives, grad_far = refs[4:]
     dx, prob, grad = expert_math(*both_cores(*refs[:4]), [far])
@@ -151,7 +161,7 @@
     for side, value in ((slice(0, width), dx), (slice(width, None), jnp.broadcast_to(prob, (prob.shape[0], LANES)))):
         total = value + dx_ref[:, side]
         keep[:, side] = total[:slots]
-        for i, give in enumerate(gives):
+        for i, give in enumerate(reversed(gives)):
             rows = give.shape[0]
             give[:, side] = total[slots + rows * i : slots + rows * (i + 1)].astype(bf16)
     grad_far[...] = grad.astype(bf16)
@@ -186,8 +196,8 @@
     top = slot.shape[0]
     total = 0.0
     probs = [0.0] * top
-    for c in range(chunk_count):
-        slot_of_row = iota((rows, tok_dev), 0) + c * rows
+    for c, place in enumerate(reversed(range(chunk_count))):
+        slot_of_row = iota((rows, tok_dev), 0) + place * rows
         hits = [(slot_of_row == slot[k : k + 1, :]).astype(f32) for k in range(top)]
         total = total + dot(sum(hits).astype(bf16), chunks[c][:, :width], (0, 0))
         prob = chunks[c][:, width : width + 1].astype(f32)
@@ -237,9 +247,15 @@
     wide = width + LANES
     dx, grad_own, grad_near = kernel_call(
         early_kernel,
-        [*own, *other, first, *near],
-        [shape((2 * slots, wide), f32), shape((hidden, width), f32), shape((2 * hidden, width), bf16)],
+        [*own, *other, first, near[0]],
+        [shape((2 * slots, wide), f32), shape((hidden, width), f32), shape((hidden, width), bf16)],
         flops=10**9,
+    )
+    dx, grad_near = kernel_call(
+        middle_kernel,
+        [*own, *other, dx, grad_near, near[1]],
+        [shape((2 * slots, wide), f32), shape((2 * hidden, width), bf16)],
+        flops=0,
     )
     parts = 2 if chunk_count % 2 == 0 else 1
     keep, *gives, grad_far = kernel_call(
@@ -251,11 +267,12 @@
     )
     back = []
     for i, give in enumerate(gives):
-        back += kernel_call(
-            functools.partial(add_kernel, i * slots // parts),
+        sums = kernel_call(
+            functools.partial(add_kernel, (parts - 1 - i) * slots // parts),
             [keep, swap(give, "rep", 1)],
             [shape((rows, wide), bf16)] * (chunk_count // parts),
         )
+        back = [*sums, *back]
     if chunk_count > 1:
         back = exchange(back)
     else:
@@ -264,7 +281,7 @@
         back = [moved.reshape(rows, wide)]
     d_tokens, d_probs = kernel_call(
         functools.partial(combine_kernel, chunk_count),
-        back + [slot, route_weight.T],
+        back[::-1] + [slot, route_weight.T],
         [shape((tok_dev, width), bf16), shape((top, tok_dev), bf16)],
         flops=8 * 10**9,
     )

time: 44.6 us -> 44.8 us (level)
    ppermute x11, waiting for transfers between devices: 12 us -> 12.8 us  [swap(): lax.ppermute(value, axis, [(i, i ^ mask) for i in range(lax.axis_size(axi...]
    ppermute x5, waiting for transfers between devices: 7.11 us -> 6.49 us  [swap_by_core(): return lax.ppermute(value, ('rep', 'dp'), pairs)]
    ppermute x5, starting transfers between devices: 8.29 us -> 7.8 us  [swap_by_core(): return lax.ppermute(value, ('rep', 'dp'), pairs)]
    pallas_call x9 -> x10, Pallas kernels: 6.37 us -> 6.79 us  [kernel_call(): pl.pallas_call(body, out_shape=outputs, in_specs=kwargs.pop('in_specs', [...]
  transfers between devices with their start and end apart: 16 -> 16, of which waited for: 7 -> 7; matrix products, arithmetic and copies ran while one was open for 0% -> 0% of each run, Pallas kernels for 9% -> 10%
where the time goes in v12:
time: 44.8 us; the launch traced here: 44.7 us
  waiting for transfers between devices  19.2 us (43%)
  starting transfers between devices  17.9 us (40%)
  Pallas kernels  6.79 us (15%)
  between operations  0.72 us (2%)
    ppermute x11, waiting for transfers between devices, swap(): lax.ppermute(value, axis, [(i, i ^ mask) for i in range(lax.axis_size(axi...  12.8 us
    ppermute x11, starting transfers between devices, swap(): lax.ppermute(value, axis, [(i, i ^ mask) for i in range(lax.axis_size(axi...  10.1 us
    ppermute x5, starting transfers between devices, swap_by_core(): return lax.ppermute(value, ('rep', 'dp'), pairs)  7.8 us
    pallas_call x10, Pallas kernels, kernel_call(): pl.pallas_call(body, out_shape=outputs, in_specs=kwargs.pop('in_specs', [...  6.79 us
    ppermute x5, waiting for transfers between devices, swap_by_core(): return lax.ppermute(value, ('rep', 'dp'), pairs)  6.49 us
  transfers between devices with their start and end apart: 16, of which 7 were waited for; matrix products, arithmetic and copies ran while one was open for 0% of the time, Pallas kernels for 10%

profile of v12, /device:TPU:0, one launch (start us, length us, event | category | flops | bytes accessed | tf_op | source)
XLA Modules:
  0.0 44.7 jit_solution(10529638044276908233)
XLA Ops:
  0.6 1.6 %shard_map.94 = (bf16[40,2048]{1,0:T(8,128)(2,1)S(1)}, bf16[40,2048]{1,0:T(8,128)(2,1)S(1)}, bf16[40,2048]{1,0:T(8,128)(2,1)S(1)}, bf16[40,2048]{1,0:T(8,128)(2,...) custom-call(s32[2,32]{1,0:T(2,128)} %bitcast.5, bf16[2,32]{1,0:T(2,128)(2,1)} %bitcast.3, ...), custom_call_target="tpu_custom_call" | custom-call | bytes 3277440 | tf_op jit(solution)/shard_map/pallas_call | solution.py:36
  2.2 3.0 %collective-permute-start.5 = (bf16[144,2048]{1,0:T(8,128)(2,1)S(1)}, bf16[144,2048]{1,0:T(8,128)(2,1)S(1)}, u32[]{:S(2)}, u32[]{:S(2)}) collective-permute-start(bf16[144,2048]{1,0:T(8,128)(2,1)S(1)} %get-tuple-element.33.refs_4_), channel_id=1, source_target_pairs={{0,1},{1,0},{2,3},{3,2},{16,18},{17,19},{18,16},{19,17},{4,5},{5,4... | collective-permute-start | bytes 1769480 | tf_op jit(solution)/shard_map/ppermute | solution.py:30
  5.2 3.6 %collective-permute-start = (bf16[40,2048]{1,0:T(8,128)(2,1)S(1)}, bf16[40,2048]{1,0:T(8,128)(2,1)S(1)}, u32[]{:S(2)}, u32[]{:S(2)}) collective-permute-start(bf16[40,2048]{1,0:T(8,128)(2,1)S(1)} %get-tuple-element.27), channel_id=1, source_target_pairs={{0,12},{4,8},{8,4},{12,0},{1,13},{5,9},{9,5},{13,1},{2,14},{6,10},... | collective-permute-start | bytes 491528 | tf_op jit(solution)/shard_map/ppermute | solution.py:20
  8.8 0.0 collective-permute-start.1
  8.8 0.8 %collective-permute-start.2 = (bf16[40,2048]{1,0:T(8,128)(2,1)S(1)}, bf16[40,2048]{1,0:T(8,128)(2,1)S(1)}, u32[]{:S(2)}, u32[]{:S(2)}) collective-permute-start(bf16[40,2048]{1,0:T(8,128)(2,1)S(1)} %get-tuple-element.29), channel_id=1, source_target_pairs={{0,4},{4,0},{8,12},{12,8},{1,5},{5,1},{9,13},{13,9},{2,6},{6,2},{1... | collective-permute-start | bytes 491528 | tf_op jit(solution)/shard_map/ppermute | solution.py:20
  9.6 0.3 collective-permute-start.6
  9.9 3.2 %collective-permute-done.5.refs_5_ = bf16[144,2048]{1,0:T(8,128)(2,1)S(1)} collective-permute-done((bf16[144,2048]{1,0:T(8,128)(2,1)S(1)}, bf16[144,2048]{1,0:T(8,128)(2,1)S(1)}, u32[]{:S(2)}, u32[]{:S(2)}) %collective-permute-start.5) | collective-permute-done | bytes 589856 | tf_op jit(solution)/shard_map/ppermute | solution.py:30
  13.1 2.1 %collective-permute-start.7 = (bf16[144,2048]{1,0:T(8,128)(2,1)S(1)}, bf16[144,2048]{1,0:T(8,128)(2,1)S(1)}, u32[]{:S(2)}, u32[]{:S(2)}) collective-permute-start(bf16[144,2048]{1,0:T(8,128)(2,1)S(1)} %collective-permute-done.5.refs_5_), channel_id=1, source_target_pairs={{0,2},{1,3},{2,0},{3,1},{16,17},{17,16},{18,19},{19,18},{4,6},{5,7... | collective-permute-start | bytes 1769480 | tf_op jit(solution)/shard_map/ppermute | solution.py:30
  15.1 0.0 collective-permute-done.refs_0_
  15.1 7.3 %collective-permute-done.1.refs_1_ = bf16[40,2048]{1,0:T(8,128)(2,1)S(1)} collective-permute-done((bf16[40,2048]{1,0:T(8,128)(2,1)S(1)}, bf16[40,2048]{1,0:T(8,128)(2,1)S(1)}, u32[]{:S(2)}, u32[]{:S(2)}) %collective-permute-start.1) | collective-permute-done | bytes 163872 | tf_op jit(solution)/shard_map/ppermute | solution.py:20
  22.5 0.0 collective-permute-done.2.refs_2_
  22.5 0.1 shard_map.95
  22.6 0.1 collective-permute-start.3
  22.6 0.5 %collective-permute-start.4 = (bf16[80,2048]{1,0:T(8,128)(2,1)S(1)}, bf16[80,2048]{1,0:T(8,128)(2,1)S(1)}, u32[]{:S(2)}, u32[]{:S(2)}) collective-permute-start(bf16[80,2048]{1,0:T(8,128)(2,1)S(1)} %get-tuple-element.32.refs_1_), channel_id=1, source_target_pairs={{0,16},{16,0},{1,17},{17,1},{2,18},{18,2},{3,19},{19,3},{4,20},{20... | collective-permute-start | bytes 983048 | tf_op jit(solution)/shard_map/ppermute | solution.py:20
  23.1 1.1 %collective-permute-done.3.refs_2_ = bf16[80,2048]{1,0:T(8,128)(2,1)S(1)} collective-permute-done((bf16[80,2048]{1,0:T(8,128)(2,1)S(1)}, bf16[80,2048]{1,0:T(8,128)(2,1)S(1)}, u32[]{:S(2)}, u32[]{:S(2)}) %collective-permute-start.3) | collective-permute-done | bytes 327712 | tf_op jit(solution)/shard_map/ppermute | solution.py:20
  24.3 0.5 %collective-permute-done.4.refs_3_ = bf16[80,2048]{1,0:T(8,128)(2,1)S(1)} collective-permute-done((bf16[80,2048]{1,0:T(8,128)(2,1)S(1)}, bf16[80,2048]{1,0:T(8,128)(2,1)S(1)}, u32[]{:S(2)}, u32[]{:S(2)}) %collective-permute-start.4) | collective-permute-done | bytes 327712 | tf_op jit(solution)/shard_map/ppermute | solution.py:20
  24.7 1.1 %shard_map.96 = (f32[160,2176]{1,0:T(8,128)S(1)}, f32[48,2048]{1,0:T(8,128)S(1)}, bf16[48,2048]{1,0:T(8,128)(2,1)S(1)}) custom-call(bf16[80,2048]{1,0:T(8,128)(2,1)S(1)} %get-tuple-element.31.refs_0_, bf16[80,2048]{1,0:T(8,128)(2,1)S(1)} %get-tuple-element.32.refs_1_, bf16[80,2048]{1,0:T(8,128)(2,1)S(1)} %collective-permute-done.3.refs_2_, ...), custom_call_target="tpu_custom_call" | custom-call | flops 1000000000 | bytes 4472832 | tf_op jit(solution)/shard_map/pallas_call | solution.py:36
  25.8 0.0 collective-permute-done.6.refs_6_
  25.8 0.9 %shard_map.97 = (f32[160,2176]{1,0:T(8,128)S(1)}, bf16[96,2048]{1,0:T(8,128)(2,1)S(1)}) custom-call(bf16[80,2048]{1,0:T(8,128)(2,1)S(1)} %get-tuple-element.31.refs_0_, bf16[80,2048]{1,0:T(8,128)(2,1)S(1)} %get-tuple-element.32.refs_1_, bf16[80,2048]{1,0:T(8,128)(2,1)S(1)} %collective-permute-done.3.refs_2_, ...), custom_call_target="tpu_custom_call" | custom-call | bytes 5275648 | tf_op jit(solution)/shard_map/pallas_call | solution.py:36
  26.7 1.5 %collective-permute-start.13 = (bf16[96,2048]{1,0:T(8,128)(2,1)S(1)}, bf16[96,2048]{1,0:T(8,128)(2,1)S(1)}, u32[]{:S(2)}, u32[]{:S(2)}) collective-permute-start(bf16[96,2048]{1,0:T(8,128)(2,1)S(1)} %get-tuple-element.49), channel_id=1, source_target_pairs={{0,1},{1,0},{2,3},{3,2},{16,18},{17,19},{18,16},{19,17},{4,5},{5,4... | collective-permute-start | bytes 1179656 | tf_op jit(solution)/shard_map/ppermute | solution.py:30
  28.3 0.0 collective-permute-done.7.refs_5_
  28.3 1.0 %shard_map.98 = (f32[80,2176]{1,0:T(8,128)S(1)}, bf16[40,2176]{1,0:T(8,128)(2,1)S(1)}, bf16[40,2176]{1,0:T(8,128)(2,1)S(1)}, bf16[48,2048]{1,0:T(8,128)(2,1)S(1)}) custom-call(bf16[80,2048]{1,0:T(8,128)(2,1)S(1)} %get-tuple-element.31.refs_0_, bf16[80,2048]{1,0:T(8,128)(2,1)S(1)} %get-tuple-element.32.refs_1_, ...), custom_call_target="tpu_custom_call" | custom-call | bytes 4534272 | tf_op jit(solution)/shard_map/pallas_call | solution.py:36
  29.3 0.1 collective-permute-start.8
  29.4 0.5 %collective-permute-start.11 = (bf16[40,2176]{1,0:T(8,128)(2,1)S(1)}, bf16[40,2176]{1,0:T(8,128)(2,1)S(1)}, u32[]{:S(2)}, u32[]{:S(2)}) collective-permute-start(bf16[40,2176]{1,0:T(8,128)(2,1)S(1)} %get-tuple-element.42), channel_id=1, source_target_pairs={{0,16},{16,0},{1,17},{17,1},{2,18},{18,2},{3,19},{19,3},{4,20},{20... | collective-permute-start | bytes 522248 | tf_op jit(solution)/shard_map/ppermute | solution.py:20
  29.9 0.9 %collective-permute-start.14 = (bf16[48,2048]{1,0:T(8,128)(2,1)S(1)}, bf16[48,2048]{1,0:T(8,128)(2,1)S(1)}, u32[]{:S(2)}, u32[]{:S(2)}) collective-permute-start(bf16[48,2048]{1,0:T(8,128)(2,1)S(1)} %get-tuple-element.50), channel_id=1, source_target_pairs={{0,3},{1,2},{2,1},{3,0},{16,19},{17,18},{18,17},{19,16},{4,7},{5,6... | collective-permute-start | bytes 589832 | tf_op jit(solution)/shard_map/ppermute | solution.py:30
  30.8 0.0 collective-permute-done.8.got
  30.8 0.0 copy-start
  30.8 3.1 %collective-permute-start.9 = (bf16[20,2176]{1,0:T(8,128)(2,1)S(1)}, bf16[20,2176]{1,0:T(8,128)(2,1)S(1)}, u32[]{:S(2)}, u32[]{:S(2)}) collective-permute-start(bf16[20,2176]{1,0:T(8,128)(2,1)S(1)} %get-tuple-element.40), channel_id=1, source_target_pairs={{0,12},{4,8},{8,4},{12,0},{1,13},{5,9},{9,5},{13,1},{2,14},{6,10},... | collective-permute-start | bytes 261128 | tf_op jit(solution)/shard_map/ppermute | solution.py:20
  33.9 0.0 collective-permute-start.10
  33.9 0.0 collective-permute-done.11.got
  33.9 0.1 shard_map.100
  34.0 1.4 %collective-permute-start.12 = (bf16[20,2176]{1,0:T(8,128)(2,1)S(1)}, bf16[20,2176]{1,0:T(8,128)(2,1)S(1)}, u32[]{:S(2)}, u32[]{:S(2)}) collective-permute-start(bf16[20,2176]{1,0:T(8,128)(2,1)S(1)} %get-tuple-element.43), channel_id=1, source_target_pairs={{0,4},{4,0},{8,12},{12,8},{1,5},{5,1},{9,13},{13,9},{2,6},{6,2},{1... | collective-permute-start | bytes 261128 | tf_op jit(solution)/shard_map/ppermute | solution.py:20
  35.4 1.2 %collective-permute-done.13.near = bf16[96,2048]{1,0:T(8,128)(2,1)S(1)} collective-permute-done((bf16[96,2048]{1,0:T(8,128)(2,1)S(1)}, bf16[96,2048]{1,0:T(8,128)(2,1)S(1)}, u32[]{:S(2)}, u32[]{:S(2)}) %collective-permute-start.13) | collective-permute-done | bytes 393248 | tf_op jit(solution)/shard_map/ppermute | solution.py:30
  36.6 2.1 %collective-permute-done.14.far = bf16[48,2048]{1,0:T(8,128)(2,1)S(1)} collective-permute-done((bf16[48,2048]{1,0:T(8,128)(2,1)S(1)}, bf16[48,2048]{1,0:T(8,128)(2,1)S(1)}, u32[]{:S(2)}, u32[]{:S(2)}) %collective-permute-start.14) | collective-permute-done | bytes 196640 | tf_op jit(solution)/shard_map/ppermute | solution.py:30
  38.7 0.1 shard_map.102.mine
  38.8 0.1 collective-permute-start.15
  38.9 0.0 collective-permute-done.9.refs_0_
  38.9 3.8 %collective-permute-done.10.refs_1_ = bf16[20,2176]{1,0:T(8,128)(2,1)S(1)} collective-permute-done((bf16[20,2176]{1,0:T(8,128)(2,1)S(1)}, bf16[20,2176]{1,0:T(8,128)(2,1)S(1)}, u32[]{:S(2)}, u32[]{:S(2)}) %collective-permute-start.10) | collective-permute-done | bytes 87072 | tf_op jit(solution)/shard_map/ppermute | solution.py:20
  42.7 0.0 collective-permute-done.12.refs_2_
  42.7 0.0 copy-done
  42.7 1.0 %shard_map.101 = (bf16[32,2048]{1,0:T(8,128)(2,1)}, bf16[2,32]{1,0:T(2,128)(2,1)}) custom-call(bf16[20,2176]{1,0:T(8,128)(2,1)S(1)} %collective-permute-done.9.refs_0_, bf16[20,2176]{1,0:T(8,128)(2,1)S(1)} %collective-permute-done.10.refs_1_, bf16[20,2176]{1,0:T(8,128)(2,1)S(1)} %collective-permute-done.12.refs_2_, ...), custom_call_target="tpu_custom_call" | custom-call | flops 8000000000 | bytes 479744 | tf_op jit(solution)/shard_map/pallas_call | solution.py:36
  43.7 0.0 collective-permute-done.15.theirs
  43.7 1.0 %shard_map.103 = f32[1,96,2048]{2,1,0:T(8,128)} custom-call(bf16[96,2048]{1,0:T(8,128)(2,1)S(1)} %shard_map.102.mine, bf16[96,2048]{1,0:T(8,128)(2,1)S(1)} %collective-permute-done.15.theirs), custom_call_target="tpu_custom_call" | custom-call | bytes 1572864 | tf_op jit(solution)/shard_map/pallas_call | solution.py:36
  (1 shorter events, 0.0 us)
Async XLA Ops:
  2.2 10.9 %collective-permute-start.5 = (bf16[144,2048]{1,0:T(8,128)(2,1)S(1)}, bf16[144,2048]{1,0:T(8,128)(2,1)S(1)}, u32[]{:S(2)}, u32[]{:S(2)}) collective-permute-start(bf16[144,2048]{1,0:T(8,128)(2,1)S(1)} %get-tuple-element.33.refs_4_), channel_id=1, source_target_pairs={{0,1},{1,0},{2,3},{3,2},{16,18},{17,19},{18,16},{19,17},{4,5},{5,4... | collective-permute-start | bytes 1769480 | tf_op jit(solution)/shard_map/ppermute | solution.py:30
  5.2 9.9 %collective-permute-start = (bf16[40,2048]{1,0:T(8,128)(2,1)S(1)}, bf16[40,2048]{1,0:T(8,128)(2,1)S(1)}, u32[]{:S(2)}, u32[]{:S(2)}) collective-permute-start(bf16[40,2048]{1,0:T(8,128)(2,1)S(1)} %get-tuple-element.27), channel_id=1, source_target_pairs={{0,12},{4,8},{8,4},{12,0},{1,13},{5,9},{9,5},{13,1},{2,14},{6,10},... | collective-permute-start | bytes 491528 | tf_op jit(solution)/shard_map/ppermute | solution.py:20
  8.8 13.6 %collective-permute-start.1 = (bf16[40,2048]{1,0:T(8,128)(2,1)S(1)}, bf16[40,2048]{1,0:T(8,128)(2,1)S(1)}, u32[]{:S(2)}, u32[]{:S(2)}) collective-permute-start(bf16[40,2048]{1,0:T(8,128)(2,1)S(1)} %get-tuple-element.28), channel_id=1, source_target_pairs={{0,8},{4,12},{8,0},{12,4},{1,9},{5,13},{9,1},{13,5},{2,10},{6,14},... | collective-permute-start | bytes 491528 | tf_op jit(solution)/shard_map/ppermute | solution.py:20
  8.8 13.6 %collective-permute-start.2 = (bf16[40,2048]{1,0:T(8,128)(2,1)S(1)}, bf16[40,2048]{1,0:T(8,128)(2,1)S(1)}, u32[]{:S(2)}, u32[]{:S(2)}) collective-permute-start(bf16[40,2048]{1,0:T(8,128)(2,1)S(1)} %get-tuple-element.29), channel_id=1, source_target_pairs={{0,4},{4,0},{8,12},{12,8},{1,5},{5,1},{9,13},{13,9},{2,6},{6,2},{1... | collective-permute-start | bytes 491528 | tf_op jit(solution)/shard_map/ppermute | solution.py:20
  9.6 16.2 %collective-permute-start.6 = (bf16[144,2048]{1,0:T(8,128)(2,1)S(1)}, bf16[144,2048]{1,0:T(8,128)(2,1)S(1)}, u32[]{:S(2)}, u32[]{:S(2)}) collective-permute-start(bf16[144,2048]{1,0:T(8,128)(2,1)S(1)} %get-tuple-element.36), channel_id=1, source_target_pairs={{0,1},{1,0},{2,3},{3,2},{16,18},{17,19},{18,16},{19,17},{4,5},{5,4... | collective-permute-start | bytes 1769480 | tf_op jit(solution)/shard_map/ppermute | solution.py:30
  13.1 15.2 %collective-permute-start.7 = (bf16[144,2048]{1,0:T(8,128)(2,1)S(1)}, bf16[144,2048]{1,0:T(8,128)(2,1)S(1)}, u32[]{:S(2)}, u32[]{:S(2)}) collective-permute-start(bf16[144,2048]{1,0:T(8,128)(2,1)S(1)} %collective-permute-done.5.refs_5_), channel_id=1, source_target_pairs={{0,2},{1,3},{2,0},{3,1},{16,17},{17,16},{18,19},{19,18},{4,6},{5,7... | collective-permute-start | bytes 1769480 | tf_op jit(solution)/shard_map/ppermute | solution.py:30
  22.6 1.7 %collective-permute-start.3 = (bf16[80,2048]{1,0:T(8,128)(2,1)S(1)}, bf16[80,2048]{1,0:T(8,128)(2,1)S(1)}, u32[]{:S(2)}, u32[]{:S(2)}) collective-permute-start(bf16[80,2048]{1,0:T(8,128)(2,1)S(1)} %get-tuple-element.31.refs_0_), channel_id=1, source_target_pairs={{0,16},{16,0},{1,17},{17,1},{2,18},{18,2},{3,19},{19,3},{4,20},{20... | collective-permute-start | bytes 983048 | tf_op jit(solution)/shard_map/ppermute | solution.py:20
  22.6 2.1 %collective-permute-start.4 = (bf16[80,2048]{1,0:T(8,128)(2,1)S(1)}, bf16[80,2048]{1,0:T(8,128)(2,1)S(1)}, u32[]{:S(2)}, u32[]{:S(2)}) collective-permute-start(bf16[80,2048]{1,0:T(8,128)(2,1)S(1)} %get-tuple-element.32.refs_1_), channel_id=1, source_target_pairs={{0,16},{16,0},{1,17},{17,1},{2,18},{18,2},{3,19},{19,3},{4,20},{20... | collective-permute-start | bytes 983048 | tf_op jit(solution)/shard_map/ppermute | solution.py:20
  26.7 9.8 %collective-permute-start.13 = (bf16[96,2048]{1,0:T(8,128)(2,1)S(1)}, bf16[96,2048]{1,0:T(8,128)(2,1)S(1)}, u32[]{:S(2)}, u32[]{:S(2)}) collective-permute-start(bf16[96,2048]{1,0:T(8,128)(2,1)S(1)} %get-tuple-element.49), channel_id=1, source_target_pairs={{0,1},{1,0},{2,3},{3,2},{16,18},{17,19},{18,16},{19,17},{4,5},{5,4... | collective-permute-start | bytes 1179656 | tf_op jit(solution)/shard_map/ppermute | solution.py:30
  29.3 1.5 %collective-permute-start.8 = (bf16[40,2176]{1,0:T(8,128)(2,1)S(1)}, bf16[40,2176]{1,0:T(8,128)(2,1)S(1)}, u32[]{:S(2)}, u32[]{:S(2)}) collective-permute-start(bf16[40,2176]{1,0:T(8,128)(2,1)S(1)} %get-tuple-element.39), channel_id=1, source_target_pairs={{0,16},{16,0},{1,17},{17,1},{2,18},{18,2},{3,19},{19,3},{4,20},{20... | collective-permute-start | bytes 522248 | tf_op jit(solution)/shard_map/ppermute | solution.py:20
  29.4 4.5 %collective-permute-start.11 = (bf16[40,2176]{1,0:T(8,128)(2,1)S(1)}, bf16[40,2176]{1,0:T(8,128)(2,1)S(1)}, u32[]{:S(2)}, u32[]{:S(2)}) collective-permute-start(bf16[40,2176]{1,0:T(8,128)(2,1)S(1)} %get-tuple-element.42), channel_id=1, source_target_pairs={{0,16},{16,0},{1,17},{17,1},{2,18},{18,2},{3,19},{19,3},{4,20},{20... | collective-permute-start | bytes 522248 | tf_op jit(solution)/shard_map/ppermute | solution.py:20
  29.9 8.8 %collective-permute-start.14 = (bf16[48,2048]{1,0:T(8,128)(2,1)S(1)}, bf16[48,2048]{1,0:T(8,128)(2,1)S(1)}, u32[]{:S(2)}, u32[]{:S(2)}) collective-permute-start(bf16[48,2048]{1,0:T(8,128)(2,1)S(1)} %get-tuple-element.50), channel_id=1, source_target_pairs={{0,3},{1,2},{2,1},{3,0},{16,19},{17,18},{18,17},{19,16},{4,7},{5,6... | collective-permute-start | bytes 589832 | tf_op jit(solution)/shard_map/ppermute | solution.py:30
  30.8 11.9 %copy-start = (bf16[32,2]{0,1:T(2,128)(2,1)S(1)}, bf16[32,2]{0,1:T(2,128)(2,1)}, u32[]{:S(2)}) copy-start(bf16[32,2]{0,1:T(2,128)(2,1)} %param.10) | copy-start | bytes 388
  30.8 8.0 %collective-permute-start.9 = (bf16[20,2176]{1,0:T(8,128)(2,1)S(1)}, bf16[20,2176]{1,0:T(8,128)(2,1)S(1)}, u32[]{:S(2)}, u32[]{:S(2)}) collective-permute-start(bf16[20,2176]{1,0:T(8,128)(2,1)S(1)} %get-tuple-element.40), channel_id=1, source_target_pairs={{0,12},{4,8},{8,4},{12,0},{1,13},{5,9},{9,5},{13,1},{2,14},{6,10},... | collective-permute-start | bytes 261128 | tf_op jit(solution)/shard_map/ppermute | solution.py:20
  33.9 8.8 %collective-permute-start.10 = (bf16[20,2176]{1,0:T(8,128)(2,1)S(1)}, bf16[20,2176]{1,0:T(8,128)(2,1)S(1)}, u32[]{:S(2)}, u32[]{:S(2)}) collective-permute-start(bf16[20,2176]{1,0:T(8,128)(2,1)S(1)} %get-tuple-element.41), channel_id=1, source_target_pairs={{0,8},{4,12},{8,0},{12,4},{1,9},{5,13},{9,1},{13,5},{2,10},{6,14},... | collective-permute-start | bytes 261128 | tf_op jit(solution)/shard_map/ppermute | solution.py:20
  34.0 8.8 %collective-permute-start.12 = (bf16[20,2176]{1,0:T(8,128)(2,1)S(1)}, bf16[20,2176]{1,0:T(8,128)(2,1)S(1)}, u32[]{:S(2)}, u32[]{:S(2)}) collective-permute-start(bf16[20,2176]{1,0:T(8,128)(2,1)S(1)} %get-tuple-element.43), channel_id=1, source_target_pairs={{0,4},{4,0},{8,12},{12,8},{1,5},{5,1},{9,13},{13,9},{2,6},{6,2},{1... | collective-permute-start | bytes 261128 | tf_op jit(solution)/shard_map/ppermute | solution.py:20
  38.8 4.9 %collective-permute-start.15 = (bf16[96,2048]{1,0:T(8,128)(2,1)S(1)}, bf16[96,2048]{1,0:T(8,128)(2,1)S(1)}, u32[]{:S(2)}, u32[]{:S(2)}) collective-permute-start(bf16[96,2048]{1,0:T(8,128)(2,1)S(1)} %shard_map.102.mine), channel_id=1, source_target_pairs={{0,16},{16,0},{1,17},{17,1},{2,18},{18,2},{3,19},{19,3},{4,20},{20... | collective-permute-start | bytes 1179656 | tf_op jit(solution)/shard_map/ppermute | solution.py:20

commit v13 on v12

--- a/solution.py
+++ b/solution.py
@@ -8,6 +8,7 @@
 from jax.sharding import PartitionSpec as P
 
 LANES = 128
+FOLD = 256
 VMEM_BYTES = 32 * 1024 * 1024
 f32, bf16 = jnp.float32, jnp.bfloat16
 
@@ -182,16 +183,21 @@
         out[0, rows] = mine[here].astype(f32) + theirs[there].astype(f32)
 
 
-def add_kernel(start, keep, got, *chunks):
-    rows = chunks[0].shape[0]
+def add_kernel(start, rows, keep, got, *chunks):
     total = keep[start : start + got.shape[0]] + got[...].astype(f32)
+    width = total.shape[1] - LANES
     for c, chunk in enumerate(chunks):
-        chunk[...] = total[c * rows : (c + 1) * rows].astype(bf16)
-
-
-def combine_kernel(chunk_count, *refs):
+        value = total[c * rows : (c + 1) * rows]
+        if chunk.shape[0] > rows:
+            blocks = [value[:, i : i + FOLD] for i in range(0, width, FOLD)]
+            diagonal = iota((rows, FOLD), 0) == iota((rows, FOLD), 1)
+            prob = jnp.sum(jnp.where(diagonal, value[:, width : width + 1], 0.0), axis=0, keepdims=True)
+            value = jnp.concatenate([*blocks, jnp.broadcast_to(prob, (8, FOLD))])
+        chunk[...] = value.astype(bf16)
+
+
+def combine_kernel(chunk_count, rows, *refs):
     chunks, (slot, route_weight, tokens_out, probs_out) = refs[:chunk_count], refs[chunk_count:]
-    rows = chunks[0].shape[0]
     tok_dev, width = tokens_out.shape
     top = slot.shape[0]
     total = 0.0
@@ -199,8 +205,16 @@
     for c, place in enumerate(reversed(range(chunk_count))):
         slot_of_row = iota((rows, tok_dev), 0) + place * rows
         hits = [(slot_of_row == slot[k : k + 1, :]).astype(f32) for k in range(top)]
-        total = total + dot(sum(hits).astype(bf16), chunks[c][:, :width], (0, 0))
-        prob = chunks[c][:, width : width + 1].astype(f32)
+        value = chunks[c][...].astype(f32)
+        if value.shape[0] > rows:
+            blocks = [value[i : i + rows] for i in range(0, width // FOLD * rows, rows)]
+            diagonal = iota((rows, FOLD), 0) == iota((rows, FOLD), 1)
+            prob = value[width // FOLD * rows :][:1]
+            prob = jnp.sum(jnp.where(diagonal, prob, 0.0), axis=1, keepdims=True)
+            value = jnp.concatenate(blocks, axis=1)
+        else:
+            prob = value[:, width : width + 1]
+        total = total + dot(sum(hits).astype(bf16), value[:, :width].astype(bf16), (0, 0))
         for k in range(top):
             probs[k] = probs[k] + jnp.sum(hits[k] * prob, axis=0, keepdims=True)
     tokens_out[...] = total.astype(bf16)
@@ -265,12 +279,14 @@
         + [shape((slots // parts, wide), bf16)] * parts
         + [shape((hidden, width), bf16)],
     )
+    folds = chunk_count > 1 and rows <= FOLD and width % FOLD == 0 and rows * width // FOLD % 8 == 0
+    returned = shape((rows * width // FOLD + 8, FOLD) if folds else (rows, wide), bf16)
     back = []
     for i, give in enumerate(gives):
         sums = kernel_call(
-            functools.partial(add_kernel, (parts - 1 - i) * slots // parts),
+            functools.partial(add_kernel, (parts - 1 - i) * slots // parts, rows),
             [keep, swap(give, "rep", 1)],
-            [shape((rows, wide), bf16)] * (chunk_count // parts),
+            [returned] * (chunk_count // parts),
         )
         back = [*sums, *back]
     if chunk_count > 1:
@@ -280,7 +296,7 @@
         moved = lax.all_to_all(moved, "ep", split_axis=0, concat_axis=0, tiled=True)
         back = [moved.reshape(rows, wide)]
     d_tokens, d_probs = kernel_call(
-        functools.partial(combine_kernel, chunk_count),
+        functools.partial(combine_kernel, chunk_count, rows),
         back[::-1] + [slot, route_weight.T],
         [shape((tok_dev, width), bf16), shape((top, tok_dev), bf16)],
         flops=8 * 10**9,

time: 44.8 us -> 43.5 us (0.971)
  waiting for transfers between devices: 19.2 us -> 17.8 us
    ppermute x11, waiting for transfers between devices: 12.8 us -> 11.4 us  [swap(): lax.ppermute(value, axis, [(i, i ^ mask) for i in range(lax.axis_size(axi...]
where the time goes in v13:
time: 43.5 us; the launch traced here: 43.3 us
  starting transfers between devices  17.9 us (41%)
  waiting for transfers between devices  17.8 us (41%)
  Pallas kernels  6.87 us (16%)
  between operations  0.72 us (2%)
    ppermute x11, waiting for transfers between devices, swap(): lax.ppermute(value, axis, [(i, i ^ mask) for i in range(lax.axis_size(axi...  11.4 us
    ppermute x11, starting transfers between devices, swap(): lax.ppermute(value, axis, [(i, i ^ mask) for i in range(lax.axis_size(axi...  10.1 us
    ppermute x5, starting transfers between devices, swap_by_core(): return lax.ppermute(value, ('rep', 'dp'), pairs)  7.8 us
    pallas_call x10, Pallas kernels, kernel_call(): pl.pallas_call(body, out_shape=outputs, in_specs=kwargs.pop('in_specs', [...  6.87 us
    ppermute x5, waiting for transfers between devices, swap_by_core(): return lax.ppermute(value, ('rep', 'dp'), pairs)  6.41 us
  transfers between devices with their start and end apart: 16, of which 7 were waited for; matrix products, arithmetic and copies ran while one was open for 0% of the time, Pallas kernels for 10%

profile of v13, /device:TPU:0, one launch (start us, length us, event | category | flops | bytes accessed | tf_op | source)
XLA Modules:
  0.0 43.3 jit_solution(12870756024314699867)
XLA Ops:
  0.6 1.6 %shard_map.94 = (bf16[40,2048]{1,0:T(8,128)(2,1)S(1)}, bf16[40,2048]{1,0:T(8,128)(2,1)S(1)}, bf16[40,2048]{1,0:T(8,128)(2,1)S(1)}, bf16[40,2048]{1,0:T(8,128)(2,...) custom-call(s32[2,32]{1,0:T(2,128)} %bitcast.5, bf16[2,32]{1,0:T(2,128)(2,1)} %bitcast.3, ...), custom_call_target="tpu_custom_call" | custom-call | bytes 3277440 | tf_op jit(solution)/shard_map/pallas_call | solution.py:37
  2.2 3.0 %collective-permute-start.5 = (bf16[144,2048]{1,0:T(8,128)(2,1)S(1)}, bf16[144,2048]{1,0:T(8,128)(2,1)S(1)}, u32[]{:S(2)}, u32[]{:S(2)}) collective-permute-start(bf16[144,2048]{1,0:T(8,128)(2,1)S(1)} %get-tuple-element.33.refs_4_), channel_id=1, source_target_pairs={{0,1},{1,0},{2,3},{3,2},{16,18},{17,19},{18,16},{19,17},{4,5},{5,4... | collective-permute-start | bytes 1769480 | tf_op jit(solution)/shard_map/ppermute | solution.py:31
  5.2 3.6 %collective-permute-start = (bf16[40,2048]{1,0:T(8,128)(2,1)S(1)}, bf16[40,2048]{1,0:T(8,128)(2,1)S(1)}, u32[]{:S(2)}, u32[]{:S(2)}) collective-permute-start(bf16[40,2048]{1,0:T(8,128)(2,1)S(1)} %get-tuple-element.27), channel_id=1, source_target_pairs={{0,12},{4,8},{8,4},{12,0},{1,13},{5,9},{9,5},{13,1},{2,14},{6,10},... | collective-permute-start | bytes 491528 | tf_op jit(solution)/shard_map/ppermute | solution.py:21
  8.8 0.0 collective-permute-start.1
  8.8 0.8 %collective-permute-start.2 = (bf16[40,2048]{1,0:T(8,128)(2,1)S(1)}, bf16[40,2048]{1,0:T(8,128)(2,1)S(1)}, u32[]{:S(2)}, u32[]{:S(2)}) collective-permute-start(bf16[40,2048]{1,0:T(8,128)(2,1)S(1)} %get-tuple-element.29), channel_id=1, source_target_pairs={{0,4},{4,0},{8,12},{12,8},{1,5},{5,1},{9,13},{13,9},{2,6},{6,2},{1... | collective-permute-start | bytes 491528 | tf_op jit(solution)/shard_map/ppermute | solution.py:21
  9.6 0.3 collective-permute-start.6
  9.9 3.2 %collective-permute-done.5.refs_5_ = bf16[144,2048]{1,0:T(8,128)(2,1)S(1)} collective-permute-done((bf16[144,2048]{1,0:T(8,128)(2,1)S(1)}, bf16[144,2048]{1,0:T(8,128)(2,1)S(1)}, u32[]{:S(2)}, u32[]{:S(2)}) %collective-permute-start.5) | collective-permute-done | bytes 589856 | tf_op jit(solution)/shard_map/ppermute | solution.py:31
  13.1 2.1 %collective-permute-start.7 = (bf16[144,2048]{1,0:T(8,128)(2,1)S(1)}, bf16[144,2048]{1,0:T(8,128)(2,1)S(1)}, u32[]{:S(2)}, u32[]{:S(2)}) collective-permute-start(bf16[144,2048]{1,0:T(8,128)(2,1)S(1)} %collective-permute-done.5.refs_5_), channel_id=1, source_target_pairs={{0,2},{1,3},{2,0},{3,1},{16,17},{17,16},{18,19},{19,18},{4,6},{5,7... | collective-permute-start | bytes 1769480 | tf_op jit(solution)/shard_map/ppermute | solution.py:31
  15.1 0.0 collective-permute-done.refs_0_
  15.1 7.3 %collective-permute-done.1.refs_1_ = bf16[40,2048]{1,0:T(8,128)(2,1)S(1)} collective-permute-done((bf16[40,2048]{1,0:T(8,128)(2,1)S(1)}, bf16[40,2048]{1,0:T(8,128)(2,1)S(1)}, u32[]{:S(2)}, u32[]{:S(2)}) %collective-permute-start.1) | collective-permute-done | bytes 163872 | tf_op jit(solution)/shard_map/ppermute | solution.py:21
  22.5 0.0 collective-permute-done.2.refs_2_
  22.5 0.1 shard_map.95
  22.6 0.1 collective-permute-start.3
  22.6 0.5 %collective-permute-start.4 = (bf16[80,2048]{1,0:T(8,128)(2,1)S(1)}, bf16[80,2048]{1,0:T(8,128)(2,1)S(1)}, u32[]{:S(2)}, u32[]{:S(2)}) collective-permute-start(bf16[80,2048]{1,0:T(8,128)(2,1)S(1)} %get-tuple-element.32.refs_1_), channel_id=1, source_target_pairs={{0,16},{16,0},{1,17},{17,1},{2,18},{18,2},{3,19},{19,3},{4,20},{20... | collective-permute-start | bytes 983048 | tf_op jit(solution)/shard_map/ppermute | solution.py:21
  23.1 1.1 %collective-permute-done.3.refs_2_ = bf16[80,2048]{1,0:T(8,128)(2,1)S(1)} collective-permute-done((bf16[80,2048]{1,0:T(8,128)(2,1)S(1)}, bf16[80,2048]{1,0:T(8,128)(2,1)S(1)}, u32[]{:S(2)}, u32[]{:S(2)}) %collective-permute-start.3) | collective-permute-done | bytes 327712 | tf_op jit(solution)/shard_map/ppermute | solution.py:21
  24.3 0.5 %collective-permute-done.4.refs_3_ = bf16[80,2048]{1,0:T(8,128)(2,1)S(1)} collective-permute-done((bf16[80,2048]{1,0:T(8,128)(2,1)S(1)}, bf16[80,2048]{1,0:T(8,128)(2,1)S(1)}, u32[]{:S(2)}, u32[]{:S(2)}) %collective-permute-start.4) | collective-permute-done | bytes 327712 | tf_op jit(solution)/shard_map/ppermute | solution.py:21
  24.7 1.1 %shard_map.96 = (f32[160,2176]{1,0:T(8,128)S(1)}, f32[48,2048]{1,0:T(8,128)S(1)}, bf16[48,2048]{1,0:T(8,128)(2,1)S(1)}) custom-call(bf16[80,2048]{1,0:T(8,128)(2,1)S(1)} %get-tuple-element.31.refs_0_, bf16[80,2048]{1,0:T(8,128)(2,1)S(1)} %get-tuple-element.32.refs_1_, bf16[80,2048]{1,0:T(8,128)(2,1)S(1)} %collective-permute-done.3.refs_2_, ...), custom_call_target="tpu_custom_call" | custom-call | flops 1000000000 | bytes 4472832 | tf_op jit(solution)/shard_map/pallas_call | solution.py:37
  25.8 0.0 collective-permute-done.6.refs_6_
  25.8 0.9 %shard_map.97 = (f32[160,2176]{1,0:T(8,128)S(1)}, bf16[96,2048]{1,0:T(8,128)(2,1)S(1)}) custom-call(bf16[80,2048]{1,0:T(8,128)(2,1)S(1)} %get-tuple-element.31.refs_0_, bf16[80,2048]{1,0:T(8,128)(2,1)S(1)} %get-tuple-element.32.refs_1_, bf16[80,2048]{1,0:T(8,128)(2,1)S(1)} %collective-permute-done.3.refs_2_, ...), custom_call_target="tpu_custom_call" | custom-call | bytes 5275648 | tf_op jit(solution)/shard_map/pallas_call | solution.py:37
  26.7 1.5 %collective-permute-start.13 = (bf16[96,2048]{1,0:T(8,128)(2,1)S(1)}, bf16[96,2048]{1,0:T(8,128)(2,1)S(1)}, u32[]{:S(2)}, u32[]{:S(2)}) collective-permute-start(bf16[96,2048]{1,0:T(8,128)(2,1)S(1)} %get-tuple-element.49), channel_id=1, source_target_pairs={{0,1},{1,0},{2,3},{3,2},{16,18},{17,19},{18,16},{19,17},{4,5},{5,4... | collective-permute-start | bytes 1179656 | tf_op jit(solution)/shard_map/ppermute | solution.py:31
  28.3 0.0 collective-permute-done.7.refs_5_
  28.3 1.0 %shard_map.98 = (f32[80,2176]{1,0:T(8,128)S(1)}, bf16[40,2176]{1,0:T(8,128)(2,1)S(1)}, bf16[40,2176]{1,0:T(8,128)(2,1)S(1)}, bf16[48,2048]{1,0:T(8,128)(2,1)S(1)}) custom-call(bf16[80,2048]{1,0:T(8,128)(2,1)S(1)} %get-tuple-element.31.refs_0_, bf16[80,2048]{1,0:T(8,128)(2,1)S(1)} %get-tuple-element.32.refs_1_, ...), custom_call_target="tpu_custom_call" | custom-call | bytes 4534272 | tf_op jit(solution)/shard_map/pallas_call | solution.py:37
  29.3 0.1 collective-permute-start.8
  29.4 0.5 %collective-permute-start.11 = (bf16[40,2176]{1,0:T(8,128)(2,1)S(1)}, bf16[40,2176]{1,0:T(8,128)(2,1)S(1)}, u32[]{:S(2)}, u32[]{:S(2)}) collective-permute-start(bf16[40,2176]{1,0:T(8,128)(2,1)S(1)} %get-tuple-element.42), channel_id=1, source_target_pairs={{0,16},{16,0},{1,17},{17,1},{2,18},{18,2},{3,19},{19,3},{4,20},{20... | collective-permute-start | bytes 522248 | tf_op jit(solution)/shard_map/ppermute | solution.py:21
  29.9 0.9 %collective-permute-start.14 = (bf16[48,2048]{1,0:T(8,128)(2,1)S(1)}, bf16[48,2048]{1,0:T(8,128)(2,1)S(1)}, u32[]{:S(2)}, u32[]{:S(2)}) collective-permute-start(bf16[48,2048]{1,0:T(8,128)(2,1)S(1)} %get-tuple-element.50), channel_id=1, source_target_pairs={{0,3},{1,2},{2,1},{3,0},{16,19},{17,18},{18,17},{19,16},{4,7},{5,6... | collective-permute-start | bytes 589832 | tf_op jit(solution)/shard_map/ppermute | solution.py:31
  30.8 0.0 collective-permute-done.8.got
  30.8 0.0 copy-start
  30.8 0.1 shard_map.99
  30.9 3.1 %collective-permute-start.9 = (bf16[168,256]{1,0:T(8,128)(2,1)S(1)}, bf16[168,256]{1,0:T(8,128)(2,1)S(1)}, u32[]{:S(2)}, u32[]{:S(2)}) collective-permute-start(bf16[168,256]{1,0:T(8,128)(2,1)S(1)} %get-tuple-element.40), channel_id=1, source_target_pairs={{0,12},{4,8},{8,4},{12,0},{1,13},{5,9},{9,5},{13,1},{2,14},{6,10},... | collective-permute-start | bytes 258056 | tf_op jit(solution)/shard_map/ppermute | solution.py:21
  33.9 0.0 collective-permute-start.10
  33.9 0.0 collective-permute-done.11.got
  33.9 0.1 shard_map.100
  34.0 1.4 %collective-permute-start.12 = (bf16[168,256]{1,0:T(8,128)(2,1)S(1)}, bf16[168,256]{1,0:T(8,128)(2,1)S(1)}, u32[]{:S(2)}, u32[]{:S(2)}) collective-permute-start(bf16[168,256]{1,0:T(8,128)(2,1)S(1)} %get-tuple-element.43), channel_id=1, source_target_pairs={{0,4},{4,0},{8,12},{12,8},{1,5},{5,1},{9,13},{13,9},{2,6},{6,2},{1... | collective-permute-start | bytes 258056 | tf_op jit(solution)/shard_map/ppermute | solution.py:21
  35.5 1.1 %collective-permute-done.13.near = bf16[96,2048]{1,0:T(8,128)(2,1)S(1)} collective-permute-done((bf16[96,2048]{1,0:T(8,128)(2,1)S(1)}, bf16[96,2048]{1,0:T(8,128)(2,1)S(1)}, u32[]{:S(2)}, u32[]{:S(2)}) %collective-permute-start.13) | collective-permute-done | bytes 393248 | tf_op jit(solution)/shard_map/ppermute | solution.py:31
  36.6 2.1 %collective-permute-done.14.far = bf16[48,2048]{1,0:T(8,128)(2,1)S(1)} collective-permute-done((bf16[48,2048]{1,0:T(8,128)(2,1)S(1)}, bf16[48,2048]{1,0:T(8,128)(2,1)S(1)}, u32[]{:S(2)}, u32[]{:S(2)}) %collective-permute-start.14) | collective-permute-done | bytes 196640 | tf_op jit(solution)/shard_map/ppermute | solution.py:31
  38.7 0.1 shard_map.102.mine
  38.8 0.1 collective-permute-start.15
  38.9 0.0 collective-permute-done.9.refs_0_
  38.9 2.5 %collective-permute-done.10.refs_1_ = bf16[168,256]{1,0:T(8,128)(2,1)S(1)} collective-permute-done((bf16[168,256]{1,0:T(8,128)(2,1)S(1)}, bf16[168,256]{1,0:T(8,128)(2,1)S(1)}, u32[]{:S(2)}, u32[]{:S(2)}) %collective-permute-start.10) | collective-permute-done | bytes 86048 | tf_op jit(solution)/shard_map/ppermute | solution.py:21
  41.4 0.0 collective-permute-done.12.refs_2_
  41.4 0.0 copy-done
  41.4 1.0 %shard_map.101 = (bf16[32,2048]{1,0:T(8,128)(2,1)}, bf16[2,32]{1,0:T(2,128)(2,1)}) custom-call(bf16[168,256]{1,0:T(8,128)(2,1)S(1)} %collective-permute-done.9.refs_0_, bf16[168,256]{1,0:T(8,128)(2,1)S(1)} %collective-permute-done.10.refs_1_, bf16[168,256]{1,0:T(8,128)(2,1)S(1)} %collective-permute-done.12.refs_2_, ...), custom_call_target="tpu_custom_call" | custom-call | flops 8000000000 | bytes 475648 | tf_op jit(solution)/shard_map/pallas_call | solution.py:37
  42.4 0.0 collective-permute-done.15.theirs
  42.4 1.0 %shard_map.103 = f32[1,96,2048]{2,1,0:T(8,128)} custom-call(bf16[96,2048]{1,0:T(8,128)(2,1)S(1)} %shard_map.102.mine, bf16[96,2048]{1,0:T(8,128)(2,1)S(1)} %collective-permute-done.15.theirs), custom_call_target="tpu_custom_call" | custom-call | bytes 1572864 | tf_op jit(solution)/shard_map/pallas_call | solution.py:37
Async XLA Ops:
  2.2 10.9 %collective-permute-start.5 = (bf16[144,2048]{1,0:T(8,128)(2,1)S(1)}, bf16[144,2048]{1,0:T(8,128)(2,1)S(1)}, u32[]{:S(2)}, u32[]{:S(2)}) collective-permute-start(bf16[144,2048]{1,0:T(8,128)(2,1)S(1)} %get-tuple-element.33.refs_4_), channel_id=1, source_target_pairs={{0,1},{1,0},{2,3},{3,2},{16,18},{17,19},{18,16},{19,17},{4,5},{5,4... | collective-permute-start | bytes 1769480 | tf_op jit(solution)/shard_map/ppermute | solution.py:31
  5.2 9.9 %collective-permute-start = (bf16[40,2048]{1,0:T(8,128)(2,1)S(1)}, bf16[40,2048]{1,0:T(8,128)(2,1)S(1)}, u32[]{:S(2)}, u32[]{:S(2)}) collective-permute-start(bf16[40,2048]{1,0:T(8,128)(2,1)S(1)} %get-tuple-element.27), channel_id=1, source_target_pairs={{0,12},{4,8},{8,4},{12,0},{1,13},{5,9},{9,5},{13,1},{2,14},{6,10},... | collective-permute-start | bytes 491528 | tf_op jit(solution)/shard_map/ppermute | solution.py:21
  8.8 13.6 %collective-permute-start.1 = (bf16[40,2048]{1,0:T(8,128)(2,1)S(1)}, bf16[40,2048]{1,0:T(8,128)(2,1)S(1)}, u32[]{:S(2)}, u32[]{:S(2)}) collective-permute-start(bf16[40,2048]{1,0:T(8,128)(2,1)S(1)} %get-tuple-element.28), channel_id=1, source_target_pairs={{0,8},{4,12},{8,0},{12,4},{1,9},{5,13},{9,1},{13,5},{2,10},{6,14},... | collective-permute-start | bytes 491528 | tf_op jit(solution)/shard_map/ppermute | solution.py:21
  8.8 13.6 %collective-permute-start.2 = (bf16[40,2048]{1,0:T(8,128)(2,1)S(1)}, bf16[40,2048]{1,0:T(8,128)(2,1)S(1)}, u32[]{:S(2)}, u32[]{:S(2)}) collective-permute-start(bf16[40,2048]{1,0:T(8,128)(2,1)S(1)} %get-tuple-element.29), channel_id=1, source_target_pairs={{0,4},{4,0},{8,12},{12,8},{1,5},{5,1},{9,13},{13,9},{2,6},{6,2},{1... | collective-permute-start | bytes 491528 | tf_op jit(solution)/shard_map/ppermute | solution.py:21
  9.6 16.2 %collective-permute-start.6 = (bf16[144,2048]{1,0:T(8,128)(2,1)S(1)}, bf16[144,2048]{1,0:T(8,128)(2,1)S(1)}, u32[]{:S(2)}, u32[]{:S(2)}) collective-permute-start(bf16[144,2048]{1,0:T(8,128)(2,1)S(1)} %get-tuple-element.36), channel_id=1, source_target_pairs={{0,1},{1,0},{2,3},{3,2},{16,18},{17,19},{18,16},{19,17},{4,5},{5,4... | collective-permute-start | bytes 1769480 | tf_op jit(solution)/shard_map/ppermute | solution.py:31
  13.1 15.2 %collective-permute-start.7 = (bf16[144,2048]{1,0:T(8,128)(2,1)S(1)}, bf16[144,2048]{1,0:T(8,128)(2,1)S(1)}, u32[]{:S(2)}, u32[]{:S(2)}) collective-permute-start(bf16[144,2048]{1,0:T(8,128)(2,1)S(1)} %collective-permute-done.5.refs_5_), channel_id=1, source_target_pairs={{0,2},{1,3},{2,0},{3,1},{16,17},{17,16},{18,19},{19,18},{4,6},{5,7... | collective-permute-start | bytes 1769480 | tf_op jit(solution)/shard_map/ppermute | solution.py:31
  22.6 1.7 %collective-permute-start.3 = (bf16[80,2048]{1,0:T(8,128)(2,1)S(1)}, bf16[80,2048]{1,0:T(8,128)(2,1)S(1)}, u32[]{:S(2)}, u32[]{:S(2)}) collective-permute-start(bf16[80,2048]{1,0:T(8,128)(2,1)S(1)} %get-tuple-element.31.refs_0_), channel_id=1, source_target_pairs={{0,16},{16,0},{1,17},{17,1},{2,18},{18,2},{3,19},{19,3},{4,20},{20... | collective-permute-start | bytes 983048 | tf_op jit(solution)/shard_map/ppermute | solution.py:21
  22.6 2.1 %collective-permute-start.4 = (bf16[80,2048]{1,0:T(8,128)(2,1)S(1)}, bf16[80,2048]{1,0:T(8,128)(2,1)S(1)}, u32[]{:S(2)}, u32[]{:S(2)}) collective-permute-start(bf16[80,2048]{1,0:T(8,128)(2,1)S(1)} %get-tuple-element.32.refs_1_), channel_id=1, source_target_pairs={{0,16},{16,0},{1,17},{17,1},{2,18},{18,2},{3,19},{19,3},{4,20},{20... | collective-permute-start | bytes 983048 | tf_op jit(solution)/shard_map/ppermute | solution.py:21
  26.7 9.8 %collective-permute-start.13 = (bf16[96,2048]{1,0:T(8,128)(2,1)S(1)}, bf16[96,2048]{1,0:T(8,128)(2,1)S(1)}, u32[]{:S(2)}, u32[]{:S(2)}) collective-permute-start(bf16[96,2048]{1,0:T(8,128)(2,1)S(1)} %get-tuple-element.49), channel_id=1, source_target_pairs={{0,1},{1,0},{2,3},{3,2},{16,18},{17,19},{18,16},{19,17},{4,5},{5,4... | collective-permute-start | bytes 1179656 | tf_op jit(solution)/shard_map/ppermute | solution.py:31
  29.3 1.5 %collective-permute-start.8 = (bf16[40,2176]{1,0:T(8,128)(2,1)S(1)}, bf16[40,2176]{1,0:T(8,128)(2,1)S(1)}, u32[]{:S(2)}, u32[]{:S(2)}) collective-permute-start(bf16[40,2176]{1,0:T(8,128)(2,1)S(1)} %get-tuple-element.39), channel_id=1, source_target_pairs={{0,16},{16,0},{1,17},{17,1},{2,18},{18,2},{3,19},{19,3},{4,20},{20... | collective-permute-start | bytes 522248 | tf_op jit(solution)/shard_map/ppermute | solution.py:21
  29.4 4.6 %collective-permute-start.11 = (bf16[40,2176]{1,0:T(8,128)(2,1)S(1)}, bf16[40,2176]{1,0:T(8,128)(2,1)S(1)}, u32[]{:S(2)}, u32[]{:S(2)}) collective-permute-start(bf16[40,2176]{1,0:T(8,128)(2,1)S(1)} %get-tuple-element.42), channel_id=1, source_target_pairs={{0,16},{16,0},{1,17},{17,1},{2,18},{18,2},{3,19},{19,3},{4,20},{20... | collective-permute-start | bytes 522248 | tf_op jit(solution)/shard_map/ppermute | solution.py:21
  29.9 8.8 %collective-permute-start.14 = (bf16[48,2048]{1,0:T(8,128)(2,1)S(1)}, bf16[48,2048]{1,0:T(8,128)(2,1)S(1)}, u32[]{:S(2)}, u32[]{:S(2)}) collective-permute-start(bf16[48,2048]{1,0:T(8,128)(2,1)S(1)} %get-tuple-element.50), channel_id=1, source_target_pairs={{0,3},{1,2},{2,1},{3,0},{16,19},{17,18},{18,17},{19,16},{4,7},{5,6... | collective-permute-start | bytes 589832 | tf_op jit(solution)/shard_map/ppermute | solution.py:31
  30.8 10.6 %copy-start = (bf16[32,2]{0,1:T(2,128)(2,1)S(1)}, bf16[32,2]{0,1:T(2,128)(2,1)}, u32[]{:S(2)}) copy-start(bf16[32,2]{0,1:T(2,128)(2,1)} %param.10) | copy-start | bytes 388
  30.9 8.0 %collective-permute-start.9 = (bf16[168,256]{1,0:T(8,128)(2,1)S(1)}, bf16[168,256]{1,0:T(8,128)(2,1)S(1)}, u32[]{:S(2)}, u32[]{:S(2)}) collective-permute-start(bf16[168,256]{1,0:T(8,128)(2,1)S(1)} %get-tuple-element.40), channel_id=1, source_target_pairs={{0,12},{4,8},{8,4},{12,0},{1,13},{5,9},{9,5},{13,1},{2,14},{6,10},... | collective-permute-start | bytes 258056 | tf_op jit(solution)/shard_map/ppermute | solution.py:21
  33.9 7.4 %collective-permute-start.10 = (bf16[168,256]{1,0:T(8,128)(2,1)S(1)}, bf16[168,256]{1,0:T(8,128)(2,1)S(1)}, u32[]{:S(2)}, u32[]{:S(2)}) collective-permute-start(bf16[168,256]{1,0:T(8,128)(2,1)S(1)} %get-tuple-element.41), channel_id=1, source_target_pairs={{0,8},{4,12},{8,0},{12,4},{1,9},{5,13},{9,1},{13,5},{2,10},{6,14},... | collective-permute-start | bytes 258056 | tf_op jit(solution)/shard_map/ppermute | solution.py:21
  34.0 7.3 %collective-permute-start.12 = (bf16[168,256]{1,0:T(8,128)(2,1)S(1)}, bf16[168,256]{1,0:T(8,128)(2,1)S(1)}, u32[]{:S(2)}, u32[]{:S(2)}) collective-permute-start(bf16[168,256]{1,0:T(8,128)(2,1)S(1)} %get-tuple-element.43), channel_id=1, source_target_pairs={{0,4},{4,0},{8,12},{12,8},{1,5},{5,1},{9,13},{13,9},{2,6},{6,2},{1... | collective-permute-start | bytes 258056 | tf_op jit(solution)/shard_map/ppermute | solution.py:21
  38.8 3.6 %collective-permute-start.15 = (bf16[96,2048]{1,0:T(8,128)(2,1)S(1)}, bf16[96,2048]{1,0:T(8,128)(2,1)S(1)}, u32[]{:S(2)}, u32[]{:S(2)}) collective-permute-start(bf16[96,2048]{1,0:T(8,128)(2,1)S(1)} %shard_map.102.mine), channel_id=1, source_target_pairs={{0,16},{16,0},{1,17},{17,1},{2,18},{18,2},{3,19},{19,3},{4,20},{20... | collective-permute-start | bytes 1179656 | tf_op jit(solution)/shard_map/ppermute | solution.py:21

commit v14 on v13

--- a/solution.py
+++ b/solution.py
@@ -38,7 +38,7 @@
         body,
         out_shape=outputs,
         in_specs=kwargs.pop("in_specs", [whole] * len(inputs)),
-        out_specs=[whole] * len(outputs),
+        out_specs=kwargs.pop("out_specs", [whole] * len(outputs)),
         cost_estimate=pl.CostEstimate(flops=flops, bytes_accessed=moved, transcendentals=0),
         compiler_params=pltpu.CompilerParams(vmem_limit_bytes=VMEM_BYTES),
         **kwargs,
@@ -174,13 +174,20 @@
     out[hidden:] = near[hidden:]
 
 
-def total_kernel(mine, theirs, out):
+def finish_kernel(mine, theirs, tokens, probs, grad_out, tokens_out, probs_out, held, sems):
     hidden = mine.shape[0] // 2
     rep = lax.axis_index("rep")
+    copies = [pltpu.make_async_copy(tokens, tokens_out, sems.at[0]), pltpu.make_async_copy(probs, probs_out, sems.at[1])]
+    for copy in copies:
+        copy.start()
     for i, half in enumerate((rep, 1 - rep)):
         here, there = slice(i * hidden, (i + 1) * hidden), slice((1 - i) * hidden, (2 - i) * hidden)
         rows = pl.ds(pl.multiple_of(half * hidden, hidden), hidden)
-        out[0, rows] = mine[here].astype(f32) + theirs[there].astype(f32)
+        held[i] = mine[here].astype(f32) + theirs[there].astype(f32)
+        copies.append(pltpu.make_async_copy(held.at[i], grad_out.at[0, rows], sems.at[2 + i]))
+        copies[-1].start()
+    for copy in copies:
+        copy.wait()
 
 
 def add_kernel(start, rows, keep, got, *chunks):
@@ -304,8 +311,17 @@
 
     arrived = swap_by_core(grad_near, along), swap_by_core(grad_far, (3, 3))
     (mine,) = kernel_call(grad_kernel, [grad_own, *arrived], [shape((2 * hidden, width), bf16)])
-    (grad_total,) = kernel_call(
-        total_kernel, [mine, swap(mine, "rep", 1)], [shape((1, 2 * hidden, width), f32)]
+    results = [
+        shape((1, 2 * hidden, width), f32),
+        shape((tok_dev, width), bf16),
+        shape((top, tok_dev), bf16),
+    ]
+    grad_total, d_tokens, d_probs = kernel_call(
+        finish_kernel,
+        [mine, swap(mine, "rep", 1), d_tokens, d_probs],
+        results,
+        out_specs=[in_hbm] * 3,
+        scratch_shapes=[pltpu.VMEM((2, hidden, width), f32), pltpu.SemaphoreType.DMA((4,))],
     )
     return d_tokens, d_probs.T, grad_total
 

time: 43.5 us -> 42.8 us (0.984)
  Pallas kernels: 6.87 us -> 6.22 us
    pallas_call x10, Pallas kernels: 6.87 us -> 6.22 us  [kernel_call(): pl.pallas_call(body, out_shape=outputs, in_specs=kwargs.pop('in_specs', [...]
  transfers between devices with their start and end apart: 16 -> 16, of which waited for: 7 -> 7; matrix products, arithmetic and copies ran while one was open for 0% -> 0% of each run, Pallas kernels for 10% -> 9%
where the time goes in v14:
time: 42.8 us; the launch traced here: 42.7 us
  starting transfers between devices  17.9 us (42%)
  waiting for transfers between devices  17.8 us (42%)
  Pallas kernels  6.22 us (15%)
  between operations  0.74 us (2%)
    ppermute x11, waiting for transfers between devices, swap(): lax.ppermute(value, axis, [(i, i ^ mask) for i in range(lax.axis_size(axi...  11.4 us
    ppermute x11, starting transfers between devices, swap(): lax.ppermute(value, axis, [(i, i ^ mask) for i in range(lax.axis_size(axi...  10.1 us
    ppermute x5, starting transfers between devices, swap_by_core(): return lax.ppermute(value, ('rep', 'dp'), pairs)  7.8 us
    ppermute x5, waiting for transfers between devices, swap_by_core(): return lax.ppermute(value, ('rep', 'dp'), pairs)  6.39 us
    pallas_call x10, Pallas kernels, kernel_call(): pl.pallas_call(body, out_shape=outputs, in_specs=kwargs.pop('in_specs', [...  6.22 us
  transfers between devices with their start and end apart: 16, of which 7 were waited for; matrix products, arithmetic and copies ran while one was open for 0% of the time, Pallas kernels for 9%

profile of v14, /device:TPU:0, one launch (start us, length us, event | category | flops | bytes accessed | tf_op | source)
XLA Modules:
  0.0 42.7 jit_solution(1116240096767686005)
XLA Ops:
  0.6 1.6 %shard_map.94 = (bf16[40,2048]{1,0:T(8,128)(2,1)S(1)}, bf16[40,2048]{1,0:T(8,128)(2,1)S(1)}, bf16[40,2048]{1,0:T(8,128)(2,1)S(1)}, bf16[40,2048]{1,0:T(8,128)(2,...) custom-call(s32[2,32]{1,0:T(2,128)} %bitcast.5, bf16[2,32]{1,0:T(2,128)(2,1)} %bitcast.3, ...), custom_call_target="tpu_custom_call" | custom-call | bytes 3277440 | tf_op jit(solution)/shard_map/pallas_call | solution.py:37
  2.2 3.0 %collective-permute-start.5 = (bf16[144,2048]{1,0:T(8,128)(2,1)S(1)}, bf16[144,2048]{1,0:T(8,128)(2,1)S(1)}, u32[]{:S(2)}, u32[]{:S(2)}) collective-permute-start(bf16[144,2048]{1,0:T(8,128)(2,1)S(1)} %get-tuple-element.36.refs_4_), channel_id=1, source_target_pairs={{0,1},{1,0},{2,3},{3,2},{16,18},{17,19},{18,16},{19,17},{4,5},{5,4... | collective-permute-start | bytes 1769480 | tf_op jit(solution)/shard_map/ppermute | solution.py:31
  5.2 3.6 %collective-permute-start = (bf16[40,2048]{1,0:T(8,128)(2,1)S(1)}, bf16[40,2048]{1,0:T(8,128)(2,1)S(1)}, u32[]{:S(2)}, u32[]{:S(2)}) collective-permute-start(bf16[40,2048]{1,0:T(8,128)(2,1)S(1)} %get-tuple-element.30), channel_id=1, source_target_pairs={{0,12},{4,8},{8,4},{12,0},{1,13},{5,9},{9,5},{13,1},{2,14},{6,10},... | collective-permute-start | bytes 491528 | tf_op jit(solution)/shard_map/ppermute | solution.py:21
  8.8 0.0 collective-permute-start.1
  8.8 0.8 %collective-permute-start.2 = (bf16[40,2048]{1,0:T(8,128)(2,1)S(1)}, bf16[40,2048]{1,0:T(8,128)(2,1)S(1)}, u32[]{:S(2)}, u32[]{:S(2)}) collective-permute-start(bf16[40,2048]{1,0:T(8,128)(2,1)S(1)} %get-tuple-element.32), channel_id=1, source_target_pairs={{0,4},{4,0},{8,12},{12,8},{1,5},{5,1},{9,13},{13,9},{2,6},{6,2},{1... | collective-permute-start | bytes 491528 | tf_op jit(solution)/shard_map/ppermute | solution.py:21
  9.6 0.3 collective-permute-start.6
  9.9 3.2 %collective-permute-done.5.refs_5_ = bf16[144,2048]{1,0:T(8,128)(2,1)S(1)} collective-permute-done((bf16[144,2048]{1,0:T(8,128)(2,1)S(1)}, bf16[144,2048]{1,0:T(8,128)(2,1)S(1)}, u32[]{:S(2)}, u32[]{:S(2)}) %collective-permute-start.5) | collective-permute-done | bytes 589856 | tf_op jit(solution)/shard_map/ppermute | solution.py:31
  13.1 2.1 %collective-permute-start.8 = (bf16[144,2048]{1,0:T(8,128)(2,1)S(1)}, bf16[144,2048]{1,0:T(8,128)(2,1)S(1)}, u32[]{:S(2)}, u32[]{:S(2)}) collective-permute-start(bf16[144,2048]{1,0:T(8,128)(2,1)S(1)} %collective-permute-done.5.refs_5_), channel_id=1, source_target_pairs={{0,2},{1,3},{2,0},{3,1},{16,17},{17,16},{18,19},{19,18},{4,6},{5,7... | collective-permute-start | bytes 1769480 | tf_op jit(solution)/shard_map/ppermute | solution.py:31
  15.1 0.0 collective-permute-done.refs_0_
  15.1 7.3 %collective-permute-done.1.refs_1_ = bf16[40,2048]{1,0:T(8,128)(2,1)S(1)} collective-permute-done((bf16[40,2048]{1,0:T(8,128)(2,1)S(1)}, bf16[40,2048]{1,0:T(8,128)(2,1)S(1)}, u32[]{:S(2)}, u32[]{:S(2)}) %collective-permute-start.1) | collective-permute-done | bytes 163872 | tf_op jit(solution)/shard_map/ppermute | solution.py:21
  22.5 0.0 collective-permute-done.2.refs_2_
  22.5 0.1 shard_map.95
  22.6 0.1 collective-permute-start.3
  22.6 0.5 %collective-permute-start.4 = (bf16[80,2048]{1,0:T(8,128)(2,1)S(1)}, bf16[80,2048]{1,0:T(8,128)(2,1)S(1)}, u32[]{:S(2)}, u32[]{:S(2)}) collective-permute-start(bf16[80,2048]{1,0:T(8,128)(2,1)S(1)} %get-tuple-element.35.refs_1_), channel_id=1, source_target_pairs={{0,16},{16,0},{1,17},{17,1},{2,18},{18,2},{3,19},{19,3},{4,20},{20... | collective-permute-start | bytes 983048 | tf_op jit(solution)/shard_map/ppermute | solution.py:21
  23.1 1.1 %collective-permute-done.3.refs_2_ = bf16[80,2048]{1,0:T(8,128)(2,1)S(1)} collective-permute-done((bf16[80,2048]{1,0:T(8,128)(2,1)S(1)}, bf16[80,2048]{1,0:T(8,128)(2,1)S(1)}, u32[]{:S(2)}, u32[]{:S(2)}) %collective-permute-start.3) | collective-permute-done | bytes 327712 | tf_op jit(solution)/shard_map/ppermute | solution.py:21
  24.3 0.5 %collective-permute-done.4.refs_3_ = bf16[80,2048]{1,0:T(8,128)(2,1)S(1)} collective-permute-done((bf16[80,2048]{1,0:T(8,128)(2,1)S(1)}, bf16[80,2048]{1,0:T(8,128)(2,1)S(1)}, u32[]{:S(2)}, u32[]{:S(2)}) %collective-permute-start.4) | collective-permute-done | bytes 327712 | tf_op jit(solution)/shard_map/ppermute | solution.py:21
  24.7 1.1 %shard_map.96 = (f32[160,2176]{1,0:T(8,128)S(1)}, f32[48,2048]{1,0:T(8,128)S(1)}, bf16[48,2048]{1,0:T(8,128)(2,1)S(1)}) custom-call(bf16[80,2048]{1,0:T(8,128)(2,1)S(1)} %get-tuple-element.34.refs_0_, bf16[80,2048]{1,0:T(8,128)(2,1)S(1)} %get-tuple-element.35.refs_1_, bf16[80,2048]{1,0:T(8,128)(2,1)S(1)} %collective-permute-done.3.refs_2_, ...), custom_call_target="tpu_custom_call" | custom-call | flops 1000000000 | bytes 4472832 | tf_op jit(solution)/shard_map/pallas_call | solution.py:37
  25.8 0.0 collective-permute-done.6.refs_6_
  25.8 0.9 %shard_map.97 = (f32[160,2176]{1,0:T(8,128)S(1)}, bf16[96,2048]{1,0:T(8,128)(2,1)S(1)}) custom-call(bf16[80,2048]{1,0:T(8,128)(2,1)S(1)} %get-tuple-element.34.refs_0_, bf16[80,2048]{1,0:T(8,128)(2,1)S(1)} %get-tuple-element.35.refs_1_, bf16[80,2048]{1,0:T(8,128)(2,1)S(1)} %collective-permute-done.3.refs_2_, ...), custom_call_target="tpu_custom_call" | custom-call | bytes 5275648 | tf_op jit(solution)/shard_map/pallas_call | solution.py:37
  26.7 1.6 %collective-permute-start.7 = (bf16[96,2048]{1,0:T(8,128)(2,1)S(1)}, bf16[96,2048]{1,0:T(8,128)(2,1)S(1)}, u32[]{:S(2)}, u32[]{:S(2)}) collective-permute-start(bf16[96,2048]{1,0:T(8,128)(2,1)S(1)} %get-tuple-element.41), channel_id=1, source_target_pairs={{0,1},{1,0},{2,3},{3,2},{16,18},{17,19},{18,16},{19,17},{4,5},{5,4... | collective-permute-start | bytes 1179656 | tf_op jit(solution)/shard_map/ppermute | solution.py:31
  28.3 0.0 collective-permute-done.8.refs_5_
  28.3 1.0 %shard_map.98 = (f32[80,2176]{1,0:T(8,128)S(1)}, bf16[40,2176]{1,0:T(8,128)(2,1)S(1)}, bf16[40,2176]{1,0:T(8,128)(2,1)S(1)}, bf16[48,2048]{1,0:T(8,128)(2,1)S(1)}) custom-call(bf16[80,2048]{1,0:T(8,128)(2,1)S(1)} %get-tuple-element.34.refs_0_, bf16[80,2048]{1,0:T(8,128)(2,1)S(1)} %get-tuple-element.35.refs_1_, ...), custom_call_target="tpu_custom_call" | custom-call | bytes 4534272 | tf_op jit(solution)/shard_map/pallas_call | solution.py:37
  29.3 0.1 collective-permute-start.11
  29.4 0.5 %collective-permute-start.14 = (bf16[40,2176]{1,0:T(8,128)(2,1)S(1)}, bf16[40,2176]{1,0:T(8,128)(2,1)S(1)}, u32[]{:S(2)}, u32[]{:S(2)}) collective-permute-start(bf16[40,2176]{1,0:T(8,128)(2,1)S(1)} %get-tuple-element.48), channel_id=1, source_target_pairs={{0,16},{16,0},{1,17},{17,1},{2,18},{18,2},{3,19},{19,3},{4,20},{20... | collective-permute-start | bytes 522248 | tf_op jit(solution)/shard_map/ppermute | solution.py:21
  29.9 0.9 %collective-permute-start.9 = (bf16[48,2048]{1,0:T(8,128)(2,1)S(1)}, bf16[48,2048]{1,0:T(8,128)(2,1)S(1)}, u32[]{:S(2)}, u32[]{:S(2)}) collective-permute-start(bf16[48,2048]{1,0:T(8,128)(2,1)S(1)} %get-tuple-element.43), channel_id=1, source_target_pairs={{0,3},{1,2},{2,1},{3,0},{16,19},{17,18},{18,17},{19,16},{4,7},{5,6... | collective-permute-start | bytes 589832 | tf_op jit(solution)/shard_map/ppermute | solution.py:31
  30.8 0.0 collective-permute-done.11.got
  30.8 0.0 copy-start
  30.8 0.1 shard_map.100
  30.9 3.1 %collective-permute-start.12 = (bf16[168,256]{1,0:T(8,128)(2,1)S(1)}, bf16[168,256]{1,0:T(8,128)(2,1)S(1)}, u32[]{:S(2)}, u32[]{:S(2)}) collective-permute-start(bf16[168,256]{1,0:T(8,128)(2,1)S(1)} %get-tuple-element.46), channel_id=1, source_target_pairs={{0,12},{4,8},{8,4},{12,0},{1,13},{5,9},{9,5},{13,1},{2,14},{6,10},... | collective-permute-start | bytes 258056 | tf_op jit(solution)/shard_map/ppermute | solution.py:21
  33.9 0.0 collective-permute-start.13
  33.9 0.0 collective-permute-done.14.got
  33.9 0.1 shard_map.101
  34.0 1.4 %collective-permute-start.15 = (bf16[168,256]{1,0:T(8,128)(2,1)S(1)}, bf16[168,256]{1,0:T(8,128)(2,1)S(1)}, u32[]{:S(2)}, u32[]{:S(2)}) collective-permute-start(bf16[168,256]{1,0:T(8,128)(2,1)S(1)} %get-tuple-element.49), channel_id=1, source_target_pairs={{0,4},{4,0},{8,12},{12,8},{1,5},{5,1},{9,13},{13,9},{2,6},{6,2},{1... | collective-permute-start | bytes 258056 | tf_op jit(solution)/shard_map/ppermute | solution.py:21
  35.5 1.1 %collective-permute-done.7.near = bf16[96,2048]{1,0:T(8,128)(2,1)S(1)} collective-permute-done((bf16[96,2048]{1,0:T(8,128)(2,1)S(1)}, bf16[96,2048]{1,0:T(8,128)(2,1)S(1)}, u32[]{:S(2)}, u32[]{:S(2)}) %collective-permute-start.7) | collective-permute-done | bytes 393248 | tf_op jit(solution)/shard_map/ppermute | solution.py:31
  36.6 2.2 %collective-permute-done.9.far = bf16[48,2048]{1,0:T(8,128)(2,1)S(1)} collective-permute-done((bf16[48,2048]{1,0:T(8,128)(2,1)S(1)}, bf16[48,2048]{1,0:T(8,128)(2,1)S(1)}, u32[]{:S(2)}, u32[]{:S(2)}) %collective-permute-start.9) | collective-permute-done | bytes 196640 | tf_op jit(solution)/shard_map/ppermute | solution.py:31
  38.7 0.1 shard_map.99.mine
  38.8 0.1 collective-permute-start.10
  38.9 0.0 collective-permute-done.12.refs_0_
  38.9 2.5 %collective-permute-done.13.refs_1_ = bf16[168,256]{1,0:T(8,128)(2,1)S(1)} collective-permute-done((bf16[168,256]{1,0:T(8,128)(2,1)S(1)}, bf16[168,256]{1,0:T(8,128)(2,1)S(1)}, u32[]{:S(2)}, u32[]{:S(2)}) %collective-permute-start.13) | collective-permute-done | bytes 86048 | tf_op jit(solution)/shard_map/ppermute | solution.py:21
  41.4 0.0 collective-permute-done.15.refs_2_
  41.4 0.0 copy-done
  41.4 0.3 shard_map.102
  41.7 0.0 collective-permute-done.10.theirs
  41.7 1.0 %shard_map.103 = (f32[1,96,2048]{2,1,0:T(8,128)}, bf16[32,2048]{1,0:T(8,128)(2,1)}, bf16[2,32]{1,0:T(2,128)(2,1)}) custom-call(bf16[96,2048]{1,0:T(8,128)(2,1)S(1)} %shard_map.99.mine, bf16[96,2048]{1,0:T(8,128)(2,1)S(1)} %collective-permute-done.10.theirs, bf16[32,2048]{1,0:T(8,128)(2,1)S(1)} %get-tuple-element.52.tokens, ...), custom_call_target="tpu_custom_call" | custom-call | bytes 1835264 | tf_op jit(solution)/shard_map/pallas_call | solution.py:37
Async XLA Ops:
  2.2 10.9 %collective-permute-start.5 = (bf16[144,2048]{1,0:T(8,128)(2,1)S(1)}, bf16[144,2048]{1,0:T(8,128)(2,1)S(1)}, u32[]{:S(2)}, u32[]{:S(2)}) collective-permute-start(bf16[144,2048]{1,0:T(8,128)(2,1)S(1)} %get-tuple-element.36.refs_4_), channel_id=1, source_target_pairs={{0,1},{1,0},{2,3},{3,2},{16,18},{17,19},{18,16},{19,17},{4,5},{5,4... | collective-permute-start | bytes 1769480 | tf_op jit(solution)/shard_map/ppermute | solution.py:31
  5.2 9.9 %collective-permute-start = (bf16[40,2048]{1,0:T(8,128)(2,1)S(1)}, bf16[40,2048]{1,0:T(8,128)(2,1)S(1)}, u32[]{:S(2)}, u32[]{:S(2)}) collective-permute-start(bf16[40,2048]{1,0:T(8,128)(2,1)S(1)} %get-tuple-element.30), channel_id=1, source_target_pairs={{0,12},{4,8},{8,4},{12,0},{1,13},{5,9},{9,5},{13,1},{2,14},{6,10},... | collective-permute-start | bytes 491528 | tf_op jit(solution)/shard_map/ppermute | solution.py:21
  8.8 13.6 %collective-permute-start.1 = (bf16[40,2048]{1,0:T(8,128)(2,1)S(1)}, bf16[40,2048]{1,0:T(8,128)(2,1)S(1)}, u32[]{:S(2)}, u32[]{:S(2)}) collective-permute-start(bf16[40,2048]{1,0:T(8,128)(2,1)S(1)} %get-tuple-element.31), channel_id=1, source_target_pairs={{0,8},{4,12},{8,0},{12,4},{1,9},{5,13},{9,1},{13,5},{2,10},{6,14},... | collective-permute-start | bytes 491528 | tf_op jit(solution)/shard_map/ppermute | solution.py:21
  8.8 13.6 %collective-permute-start.2 = (bf16[40,2048]{1,0:T(8,128)(2,1)S(1)}, bf16[40,2048]{1,0:T(8,128)(2,1)S(1)}, u32[]{:S(2)}, u32[]{:S(2)}) collective-permute-start(bf16[40,2048]{1,0:T(8,128)(2,1)S(1)} %get-tuple-element.32), channel_id=1, source_target_pairs={{0,4},{4,0},{8,12},{12,8},{1,5},{5,1},{9,13},{13,9},{2,6},{6,2},{1... | collective-permute-start | bytes 491528 | tf_op jit(solution)/shard_map/ppermute | solution.py:21
  9.6 16.2 %collective-permute-start.6 = (bf16[144,2048]{1,0:T(8,128)(2,1)S(1)}, bf16[144,2048]{1,0:T(8,128)(2,1)S(1)}, u32[]{:S(2)}, u32[]{:S(2)}) collective-permute-start(bf16[144,2048]{1,0:T(8,128)(2,1)S(1)} %get-tuple-element.40), channel_id=1, source_target_pairs={{0,1},{1,0},{2,3},{3,2},{16,18},{17,19},{18,16},{19,17},{4,5},{5,4... | collective-permute-start | bytes 1769480 | tf_op jit(solution)/shard_map/ppermute | solution.py:31
  13.1 15.2 %collective-permute-start.8 = (bf16[144,2048]{1,0:T(8,128)(2,1)S(1)}, bf16[144,2048]{1,0:T(8,128)(2,1)S(1)}, u32[]{:S(2)}, u32[]{:S(2)}) collective-permute-start(bf16[144,2048]{1,0:T(8,128)(2,1)S(1)} %collective-permute-done.5.refs_5_), channel_id=1, source_target_pairs={{0,2},{1,3},{2,0},{3,1},{16,17},{17,16},{18,19},{19,18},{4,6},{5,7... | collective-permute-start | bytes 1769480 | tf_op jit(solution)/shard_map/ppermute | solution.py:31
  22.6 1.7 %collective-permute-start.3 = (bf16[80,2048]{1,0:T(8,128)(2,1)S(1)}, bf16[80,2048]{1,0:T(8,128)(2,1)S(1)}, u32[]{:S(2)}, u32[]{:S(2)}) collective-permute-start(bf16[80,2048]{1,0:T(8,128)(2,1)S(1)} %get-tuple-element.34.refs_0_), channel_id=1, source_target_pairs={{0,16},{16,0},{1,17},{17,1},{2,18},{18,2},{3,19},{19,3},{4,20},{20... | collective-permute-start | bytes 983048 | tf_op jit(solution)/shard_map/ppermute | solution.py:21
  22.6 2.1 %collective-permute-start.4 = (bf16[80,2048]{1,0:T(8,128)(2,1)S(1)}, bf16[80,2048]{1,0:T(8,128)(2,1)S(1)}, u32[]{:S(2)}, u32[]{:S(2)}) collective-permute-start(bf16[80,2048]{1,0:T(8,128)(2,1)S(1)} %get-tuple-element.35.refs_1_), channel_id=1, source_target_pairs={{0,16},{16,0},{1,17},{17,1},{2,18},{18,2},{3,19},{19,3},{4,20},{20... | collective-permute-start | bytes 983048 | tf_op jit(solution)/shard_map/ppermute | solution.py:21
  26.7 9.8 %collective-permute-start.7 = (bf16[96,2048]{1,0:T(8,128)(2,1)S(1)}, bf16[96,2048]{1,0:T(8,128)(2,1)S(1)}, u32[]{:S(2)}, u32[]{:S(2)}) collective-permute-start(bf16[96,2048]{1,0:T(8,128)(2,1)S(1)} %get-tuple-element.41), channel_id=1, source_target_pairs={{0,1},{1,0},{2,3},{3,2},{16,18},{17,19},{18,16},{19,17},{4,5},{5,4... | collective-permute-start | bytes 1179656 | tf_op jit(solution)/shard_map/ppermute | solution.py:31
  29.3 1.5 %collective-permute-start.11 = (bf16[40,2176]{1,0:T(8,128)(2,1)S(1)}, bf16[40,2176]{1,0:T(8,128)(2,1)S(1)}, u32[]{:S(2)}, u32[]{:S(2)}) collective-permute-start(bf16[40,2176]{1,0:T(8,128)(2,1)S(1)} %get-tuple-element.45), channel_id=1, source_target_pairs={{0,16},{16,0},{1,17},{17,1},{2,18},{18,2},{3,19},{19,3},{4,20},{20... | collective-permute-start | bytes 522248 | tf_op jit(solution)/shard_map/ppermute | solution.py:21
  29.4 4.6 %collective-permute-start.14 = (bf16[40,2176]{1,0:T(8,128)(2,1)S(1)}, bf16[40,2176]{1,0:T(8,128)(2,1)S(1)}, u32[]{:S(2)}, u32[]{:S(2)}) collective-permute-start(bf16[40,2176]{1,0:T(8,128)(2,1)S(1)} %get-tuple-element.48), channel_id=1, source_target_pairs={{0,16},{16,0},{1,17},{17,1},{2,18},{18,2},{3,19},{19,3},{4,20},{20... | collective-permute-start | bytes 522248 | tf_op jit(solution)/shard_map/ppermute | solution.py:21
  29.9 8.8 %collective-permute-start.9 = (bf16[48,2048]{1,0:T(8,128)(2,1)S(1)}, bf16[48,2048]{1,0:T(8,128)(2,1)S(1)}, u32[]{:S(2)}, u32[]{:S(2)}) collective-permute-start(bf16[48,2048]{1,0:T(8,128)(2,1)S(1)} %get-tuple-element.43), channel_id=1, source_target_pairs={{0,3},{1,2},{2,1},{3,0},{16,19},{17,18},{18,17},{19,16},{4,7},{5,6... | collective-permute-start | bytes 589832 | tf_op jit(solution)/shard_map/ppermute | solution.py:31
  30.8 10.6 %copy-start = (bf16[32,2]{0,1:T(2,128)(2,1)S(1)}, bf16[32,2]{0,1:T(2,128)(2,1)}, u32[]{:S(2)}) copy-start(bf16[32,2]{0,1:T(2,128)(2,1)} %param.10) | copy-start | bytes 388
  30.9 8.0 %collective-permute-start.12 = (bf16[168,256]{1,0:T(8,128)(2,1)S(1)}, bf16[168,256]{1,0:T(8,128)(2,1)S(1)}, u32[]{:S(2)}, u32[]{:S(2)}) collective-permute-start(bf16[168,256]{1,0:T(8,128)(2,1)S(1)} %get-tuple-element.46), channel_id=1, source_target_pairs={{0,12},{4,8},{8,4},{12,0},{1,13},{5,9},{9,5},{13,1},{2,14},{6,10},... | collective-permute-start | bytes 258056 | tf_op jit(solution)/shard_map/ppermute | solution.py:21
  33.9 7.4 %collective-permute-start.13 = (bf16[168,256]{1,0:T(8,128)(2,1)S(1)}, bf16[168,256]{1,0:T(8,128)(2,1)S(1)}, u32[]{:S(2)}, u32[]{:S(2)}) collective-permute-start(bf16[168,256]{1,0:T(8,128)(2,1)S(1)} %get-tuple-element.47), channel_id=1, source_target_pairs={{0,8},{4,12},{8,0},{12,4},{1,9},{5,13},{9,1},{13,5},{2,10},{6,14},... | collective-permute-start | bytes 258056 | tf_op jit(solution)/shard_map/ppermute | solution.py:21
  34.0 7.3 %collective-permute-start.15 = (bf16[168,256]{1,0:T(8,128)(2,1)S(1)}, bf16[168,256]{1,0:T(8,128)(2,1)S(1)}, u32[]{:S(2)}, u32[]{:S(2)}) collective-permute-start(bf16[168,256]{1,0:T(8,128)(2,1)S(1)} %get-tuple-element.49), channel_id=1, source_target_pairs={{0,4},{4,0},{8,12},{12,8},{1,5},{5,1},{9,13},{13,9},{2,6},{6,2},{1... | collective-permute-start | bytes 258056 | tf_op jit(solution)/shard_map/ppermute | solution.py:21
  38.8 2.9 %collective-permute-start.10 = (bf16[96,2048]{1,0:T(8,128)(2,1)S(1)}, bf16[96,2048]{1,0:T(8,128)(2,1)S(1)}, u32[]{:S(2)}, u32[]{:S(2)}) collective-permute-start(bf16[96,2048]{1,0:T(8,128)(2,1)S(1)} %shard_map.99.mine), channel_id=1, source_target_pairs={{0,16},{16,0},{1,17},{17,1},{2,18},{18,2},{3,19},{19,3},{4,20},{20... | collective-permute-start | bytes 1179656 | tf_op jit(solution)/shard_map/ppermute | solution.py:21

commit v15 on v14

--- a/solution.py
+++ b/solution.py
@@ -9,6 +9,7 @@
 
 LANES = 128
 FOLD = 256
+BLOCK = 16
 VMEM_BYTES = 32 * 1024 * 1024
 f32, bf16 = jnp.float32, jnp.bfloat16
 
@@ -49,22 +50,38 @@
     return lax.broadcasted_iota(jnp.int32, shape, dim)
 
 
+def blocks(rows):
+    return rows // BLOCK if rows % BLOCK == 0 else 1
+
+
+def block_copies(sems, source, target, start=0, offset=0, count=None):
+    count = source.shape[0] if count is None else count
+    block = count // blocks(count)
+    return [
+        pltpu.make_async_copy(
+            source.at[pl.ds(pl.multiple_of(start + i, block), block)], target.at[pl.ds(offset + i, block)], next(sems)
+        )
+        for i in range(0, count, block)
+    ]
+
+
 def dispatch_kernel(experts, cap, chunk_count, *refs):
     given, weights, refs = refs[:4], refs[4:7], refs[7:]
     chunks, (slot_out, *packed), (*held, sems) = refs[:chunk_count], refs[chunk_count:-5], refs[-5:]
     hidden = packed[0].shape[0] // 3
     rep = lax.axis_index("rep")
-    loads = [pltpu.make_async_copy(*pair, sems.at[i]) for i, pair in enumerate(zip(given, held))]
-    packs = []
-    for j, half in enumerate((rep, 1 - rep)):
-        rows = pl.ds(pl.multiple_of(half * hidden, hidden), hidden)
-        packs += [
-            pltpu.make_async_copy(weight.at[0, rows], packed[j].at[pl.ds(i * hidden, hidden)], sems.at[4 + 3 * j + i])
-            for i, weight in enumerate(weights)
-        ]
-    for copy in loads + packs:
+    free = iter([sems.at[i] for i in range(sems.shape[0])])
+    small = [pltpu.make_async_copy(*pair, next(free)) for pair in zip(given[:2], held)]
+    loads = [copy for pair in zip(given[2:], held[2:]) for copy in block_copies(free, *pair)]
+    packs = [
+        copy
+        for half, target in ((rep, packed[0]), (1 - rep, packed[1]))
+        for i, weight in enumerate(weights)
+        for copy in block_copies(free, weight.at[0], target, half * hidden, i * hidden, hidden)
+    ]
+    for copy in small + loads + packs:
         copy.start()
-    for copy in loads[:2]:
+    for copy in small:
         copy.wait()
 
     ids, route_weight, tokens, upstream = held
@@ -97,7 +114,7 @@
         scale += here_x + here_dy * route_weight[k : k + 1, :].astype(f32)
     scale = jnp.sum(scale, axis=1, keepdims=True)
     take_x, take_dy = take_x.astype(bf16), take_dy.astype(bf16)
-    for copy in loads[2:]:
+    for copy in loads:
         copy.wait()
     picked = dot(take_x, tokens[...], (1, 0)) + dot(take_dy, upstream[...], (1, 0))
     picked = picked * scale
@@ -180,11 +197,14 @@
     copies = [pltpu.make_async_copy(tokens, tokens_out, sems.at[0]), pltpu.make_async_copy(probs, probs_out, sems.at[1])]
     for copy in copies:
         copy.start()
-    for i, half in enumerate((rep, 1 - rep)):
-        here, there = slice(i * hidden, (i + 1) * hidden), slice((1 - i) * hidden, (2 - i) * hidden)
-        rows = pl.ds(pl.multiple_of(half * hidden, hidden), hidden)
-        held[i] = mine[here].astype(f32) + theirs[there].astype(f32)
-        copies.append(pltpu.make_async_copy(held.at[i], grad_out.at[0, rows], sems.at[2 + i]))
+    block = hidden // blocks(hidden)
+    for place in range(0, 2 * hidden, block):
+        across = (place + hidden) % (2 * hidden)
+        half = rep if place < hidden else 1 - rep
+        here = pl.ds(place, block)
+        held[here] = mine[here].astype(f32) + theirs[pl.ds(across, block)].astype(f32)
+        row = pl.multiple_of(half * hidden + place % hidden, block)
+        copies.append(pltpu.make_async_copy(held.at[here], grad_out.at[0, pl.ds(row, block)], sems.at[len(copies)]))
         copies[-1].start()
     for copy in copies:
         copy.wait()
@@ -249,7 +269,7 @@
         + [shape((top, tok_dev), jnp.int32)]
         + [shape((3 * hidden, width), bf16)] * 2,
         in_specs=[in_hbm] * 7,
-        scratch_shapes=[pltpu.VMEM(a.shape, a.dtype) for a in given] + [pltpu.SemaphoreType.DMA((10,))],
+        scratch_shapes=[pltpu.VMEM(a.shape, a.dtype) for a in given] + [pltpu.SemaphoreType.DMA((2 + 2 * blocks(tok_dev) + 6 * blocks(hidden),))],
     )
 
     along, across = (1, 2), (2, 1)
@@ -321,7 +341,7 @@
         [mine, swap(mine, "rep", 1), d_tokens, d_probs],
         results,
         out_specs=[in_hbm] * 3,
-        scratch_shapes=[pltpu.VMEM((2, hidden, width), f32), pltpu.SemaphoreType.DMA((4,))],
+        scratch_shapes=[pltpu.VMEM((2 * hidden, width), f32), pltpu.SemaphoreType.DMA((2 + 2 * blocks(hidden),))],
     )
     return d_tokens, d_probs.T, grad_total
 

time: 42.8 us -> 43 us (level)
  no operation moved by 1% of the time
where the time goes in v15:
time: 43 us; the launch traced here: 42.8 us
  starting transfers between devices  17.9 us (42%)
  waiting for transfers between devices  17.8 us (41%)
  Pallas kernels  6.33 us (15%)
  between operations  0.74 us (2%)
    ppermute x11, waiting for transfers between devices, swap(): lax.ppermute(value, axis, [(i, i ^ mask) for i in range(lax.axis_size(axi...  11.4 us
    ppermute x11, starting transfers between devices, swap(): lax.ppermute(value, axis, [(i, i ^ mask) for i in range(lax.axis_size(axi...  10.1 us
    ppermute x5, starting transfers between devices, swap_by_core(): return lax.ppermute(value, ('rep', 'dp'), pairs)  7.82 us
    ppermute x5, waiting for transfers between devices, swap_by_core(): return lax.ppermute(value, ('rep', 'dp'), pairs)  6.39 us
    pallas_call x10, Pallas kernels, kernel_call(): pl.pallas_call(body, out_shape=outputs, in_specs=kwargs.pop('in_specs', [...  6.33 us
  transfers between devices with their start and end apart: 16, of which 7 were waited for; matrix products, arithmetic and copies ran while one was open for 0% of the time, Pallas kernels for 9%

profile of v15, /device:TPU:0, one launch (start us, length us, event | category | flops | bytes accessed | tf_op | source)
XLA Modules:
  0.0 42.8 jit_solution(14558606827873549751)
XLA Ops:
  0.6 1.7 %shard_map.94 = (bf16[40,2048]{1,0:T(8,128)(2,1)S(1)}, bf16[40,2048]{1,0:T(8,128)(2,1)S(1)}, bf16[40,2048]{1,0:T(8,128)(2,1)S(1)}, bf16[40,2048]{1,0:T(8,128)(2,...) custom-call(s32[2,32]{1,0:T(2,128)} %bitcast.5, bf16[2,32]{1,0:T(2,128)(2,1)} %bitcast.3, ...), custom_call_target="tpu_custom_call" | custom-call | bytes 3277440 | tf_op jit(solution)/shard_map/pallas_call | solution.py:38
  2.3 3.0 %collective-permute-start.5 = (bf16[144,2048]{1,0:T(8,128)(2,1)S(1)}, bf16[144,2048]{1,0:T(8,128)(2,1)S(1)}, u32[]{:S(2)}, u32[]{:S(2)}) collective-permute-start(bf16[144,2048]{1,0:T(8,128)(2,1)S(1)} %get-tuple-element.36.refs_4_), channel_id=1, source_target_pairs={{0,1},{1,0},{2,3},{3,2},{16,18},{17,19},{18,16},{19,17},{4,5},{5,4... | collective-permute-start | bytes 1769480 | tf_op jit(solution)/shard_map/ppermute | solution.py:32
  5.3 3.6 %collective-permute-start = (bf16[40,2048]{1,0:T(8,128)(2,1)S(1)}, bf16[40,2048]{1,0:T(8,128)(2,1)S(1)}, u32[]{:S(2)}, u32[]{:S(2)}) collective-permute-start(bf16[40,2048]{1,0:T(8,128)(2,1)S(1)} %get-tuple-element.30), channel_id=1, source_target_pairs={{0,12},{4,8},{8,4},{12,0},{1,13},{5,9},{9,5},{13,1},{2,14},{6,10},... | collective-permute-start | bytes 491528 | tf_op jit(solution)/shard_map/ppermute | solution.py:22
  8.9 0.0 collective-permute-start.1
  8.9 0.8 %collective-permute-start.2 = (bf16[40,2048]{1,0:T(8,128)(2,1)S(1)}, bf16[40,2048]{1,0:T(8,128)(2,1)S(1)}, u32[]{:S(2)}, u32[]{:S(2)}) collective-permute-start(bf16[40,2048]{1,0:T(8,128)(2,1)S(1)} %get-tuple-element.32), channel_id=1, source_target_pairs={{0,4},{4,0},{8,12},{12,8},{1,5},{5,1},{9,13},{13,9},{2,6},{6,2},{1... | collective-permute-start | bytes 491528 | tf_op jit(solution)/shard_map/ppermute | solution.py:22
  9.7 0.3 collective-permute-start.6
  10.0 3.2 %collective-permute-done.5.refs_5_ = bf16[144,2048]{1,0:T(8,128)(2,1)S(1)} collective-permute-done((bf16[144,2048]{1,0:T(8,128)(2,1)S(1)}, bf16[144,2048]{1,0:T(8,128)(2,1)S(1)}, u32[]{:S(2)}, u32[]{:S(2)}) %collective-permute-start.5) | collective-permute-done | bytes 589856 | tf_op jit(solution)/shard_map/ppermute | solution.py:32
  13.2 2.1 %collective-permute-start.8 = (bf16[144,2048]{1,0:T(8,128)(2,1)S(1)}, bf16[144,2048]{1,0:T(8,128)(2,1)S(1)}, u32[]{:S(2)}, u32[]{:S(2)}) collective-permute-start(bf16[144,2048]{1,0:T(8,128)(2,1)S(1)} %collective-permute-done.5.refs_5_), channel_id=1, source_target_pairs={{0,2},{1,3},{2,0},{3,1},{16,17},{17,16},{18,19},{19,18},{4,6},{5,7... | collective-permute-start | bytes 1769480 | tf_op jit(solution)/shard_map/ppermute | solution.py:32
  15.2 0.0 collective-permute-done.refs_0_
  15.2 7.3 %collective-permute-done.1.refs_1_ = bf16[40,2048]{1,0:T(8,128)(2,1)S(1)} collective-permute-done((bf16[40,2048]{1,0:T(8,128)(2,1)S(1)}, bf16[40,2048]{1,0:T(8,128)(2,1)S(1)}, u32[]{:S(2)}, u32[]{:S(2)}) %collective-permute-start.1) | collective-permute-done | bytes 163872 | tf_op jit(solution)/shard_map/ppermute | solution.py:22
  22.6 0.0 collective-permute-done.2.refs_2_
  22.6 0.1 shard_map.95
  22.7 0.1 collective-permute-start.3
  22.8 0.5 %collective-permute-start.4 = (bf16[80,2048]{1,0:T(8,128)(2,1)S(1)}, bf16[80,2048]{1,0:T(8,128)(2,1)S(1)}, u32[]{:S(2)}, u32[]{:S(2)}) collective-permute-start(bf16[80,2048]{1,0:T(8,128)(2,1)S(1)} %get-tuple-element.35.refs_1_), channel_id=1, source_target_pairs={{0,16},{16,0},{1,17},{17,1},{2,18},{18,2},{3,19},{19,3},{4,20},{20... | collective-permute-start | bytes 983048 | tf_op jit(solution)/shard_map/ppermute | solution.py:22
  23.3 1.1 %collective-permute-done.3.refs_2_ = bf16[80,2048]{1,0:T(8,128)(2,1)S(1)} collective-permute-done((bf16[80,2048]{1,0:T(8,128)(2,1)S(1)}, bf16[80,2048]{1,0:T(8,128)(2,1)S(1)}, u32[]{:S(2)}, u32[]{:S(2)}) %collective-permute-start.3) | collective-permute-done | bytes 327712 | tf_op jit(solution)/shard_map/ppermute | solution.py:22
  24.4 0.5 %collective-permute-done.4.refs_3_ = bf16[80,2048]{1,0:T(8,128)(2,1)S(1)} collective-permute-done((bf16[80,2048]{1,0:T(8,128)(2,1)S(1)}, bf16[80,2048]{1,0:T(8,128)(2,1)S(1)}, u32[]{:S(2)}, u32[]{:S(2)}) %collective-permute-start.4) | collective-permute-done | bytes 327712 | tf_op jit(solution)/shard_map/ppermute | solution.py:22
  24.8 1.1 %shard_map.96 = (f32[160,2176]{1,0:T(8,128)S(1)}, f32[48,2048]{1,0:T(8,128)S(1)}, bf16[48,2048]{1,0:T(8,128)(2,1)S(1)}) custom-call(bf16[80,2048]{1,0:T(8,128)(2,1)S(1)} %get-tuple-element.34.refs_0_, bf16[80,2048]{1,0:T(8,128)(2,1)S(1)} %get-tuple-element.35.refs_1_, bf16[80,2048]{1,0:T(8,128)(2,1)S(1)} %collective-permute-done.3.refs_2_, ...), custom_call_target="tpu_custom_call" | custom-call | flops 1000000000 | bytes 4472832 | tf_op jit(solution)/shard_map/pallas_call | solution.py:38
  25.9 0.0 collective-permute-done.6.refs_6_
  25.9 0.9 %shard_map.97 = (f32[160,2176]{1,0:T(8,128)S(1)}, bf16[96,2048]{1,0:T(8,128)(2,1)S(1)}) custom-call(bf16[80,2048]{1,0:T(8,128)(2,1)S(1)} %get-tuple-element.34.refs_0_, bf16[80,2048]{1,0:T(8,128)(2,1)S(1)} %get-tuple-element.35.refs_1_, bf16[80,2048]{1,0:T(8,128)(2,1)S(1)} %collective-permute-done.3.refs_2_, ...), custom_call_target="tpu_custom_call" | custom-call | bytes 5275648 | tf_op jit(solution)/shard_map/pallas_call | solution.py:38
  26.8 1.6 %collective-permute-start.7 = (bf16[96,2048]{1,0:T(8,128)(2,1)S(1)}, bf16[96,2048]{1,0:T(8,128)(2,1)S(1)}, u32[]{:S(2)}, u32[]{:S(2)}) collective-permute-start(bf16[96,2048]{1,0:T(8,128)(2,1)S(1)} %get-tuple-element.41), channel_id=1, source_target_pairs={{0,1},{1,0},{2,3},{3,2},{16,18},{17,19},{18,16},{19,17},{4,5},{5,4... | collective-permute-start | bytes 1179656 | tf_op jit(solution)/shard_map/ppermute | solution.py:32
  28.4 0.0 collective-permute-done.8.refs_5_
  28.4 1.0 %shard_map.98 = (f32[80,2176]{1,0:T(8,128)S(1)}, bf16[40,2176]{1,0:T(8,128)(2,1)S(1)}, bf16[40,2176]{1,0:T(8,128)(2,1)S(1)}, bf16[48,2048]{1,0:T(8,128)(2,1)S(1)}) custom-call(bf16[80,2048]{1,0:T(8,128)(2,1)S(1)} %get-tuple-element.34.refs_0_, bf16[80,2048]{1,0:T(8,128)(2,1)S(1)} %get-tuple-element.35.refs_1_, ...), custom_call_target="tpu_custom_call" | custom-call | bytes 4534272 | tf_op jit(solution)/shard_map/pallas_call | solution.py:38
  29.4 0.1 collective-permute-start.11
  29.5 0.5 %collective-permute-start.14 = (bf16[40,2176]{1,0:T(8,128)(2,1)S(1)}, bf16[40,2176]{1,0:T(8,128)(2,1)S(1)}, u32[]{:S(2)}, u32[]{:S(2)}) collective-permute-start(bf16[40,2176]{1,0:T(8,128)(2,1)S(1)} %get-tuple-element.48), channel_id=1, source_target_pairs={{0,16},{16,0},{1,17},{17,1},{2,18},{18,2},{3,19},{19,3},{4,20},{20... | collective-permute-start | bytes 522248 | tf_op jit(solution)/shard_map/ppermute | solution.py:22
  30.0 0.9 %collective-permute-start.9 = (bf16[48,2048]{1,0:T(8,128)(2,1)S(1)}, bf16[48,2048]{1,0:T(8,128)(2,1)S(1)}, u32[]{:S(2)}, u32[]{:S(2)}) collective-permute-start(bf16[48,2048]{1,0:T(8,128)(2,1)S(1)} %get-tuple-element.43), channel_id=1, source_target_pairs={{0,3},{1,2},{2,1},{3,0},{16,19},{17,18},{18,17},{19,16},{4,7},{5,6... | collective-permute-start | bytes 589832 | tf_op jit(solution)/shard_map/ppermute | solution.py:32
  30.9 0.0 collective-permute-done.11.got
  30.9 0.0 copy-start
  30.9 0.1 shard_map.100
  31.0 3.1 %collective-permute-start.12 = (bf16[168,256]{1,0:T(8,128)(2,1)S(1)}, bf16[168,256]{1,0:T(8,128)(2,1)S(1)}, u32[]{:S(2)}, u32[]{:S(2)}) collective-permute-start(bf16[168,256]{1,0:T(8,128)(2,1)S(1)} %get-tuple-element.46), channel_id=1, source_target_pairs={{0,12},{4,8},{8,4},{12,0},{1,13},{5,9},{9,5},{13,1},{2,14},{6,10},... | collective-permute-start | bytes 258056 | tf_op jit(solution)/shard_map/ppermute | solution.py:22
  34.0 0.0 collective-permute-start.13
  34.1 0.0 collective-permute-done.14.got
  34.1 0.1 shard_map.101
  34.1 1.5 %collective-permute-start.15 = (bf16[168,256]{1,0:T(8,128)(2,1)S(1)}, bf16[168,256]{1,0:T(8,128)(2,1)S(1)}, u32[]{:S(2)}, u32[]{:S(2)}) collective-permute-start(bf16[168,256]{1,0:T(8,128)(2,1)S(1)} %get-tuple-element.49), channel_id=1, source_target_pairs={{0,4},{4,0},{8,12},{12,8},{1,5},{5,1},{9,13},{13,9},{2,6},{6,2},{1... | collective-permute-start | bytes 258056 | tf_op jit(solution)/shard_map/ppermute | solution.py:22
  35.6 1.1 %collective-permute-done.7.near = bf16[96,2048]{1,0:T(8,128)(2,1)S(1)} collective-permute-done((bf16[96,2048]{1,0:T(8,128)(2,1)S(1)}, bf16[96,2048]{1,0:T(8,128)(2,1)S(1)}, u32[]{:S(2)}, u32[]{:S(2)}) %collective-permute-start.7) | collective-permute-done | bytes 393248 | tf_op jit(solution)/shard_map/ppermute | solution.py:32
  36.7 2.2 %collective-permute-done.9.far = bf16[48,2048]{1,0:T(8,128)(2,1)S(1)} collective-permute-done((bf16[48,2048]{1,0:T(8,128)(2,1)S(1)}, bf16[48,2048]{1,0:T(8,128)(2,1)S(1)}, u32[]{:S(2)}, u32[]{:S(2)}) %collective-permute-start.9) | collective-permute-done | bytes 196640 | tf_op jit(solution)/shard_map/ppermute | solution.py:32
  38.8 0.1 shard_map.99.mine
  38.9 0.1 collective-permute-start.10
  39.0 0.0 collective-permute-done.12.refs_0_
  39.0 2.5 %collective-permute-done.13.refs_1_ = bf16[168,256]{1,0:T(8,128)(2,1)S(1)} collective-permute-done((bf16[168,256]{1,0:T(8,128)(2,1)S(1)}, bf16[168,256]{1,0:T(8,128)(2,1)S(1)}, u32[]{:S(2)}, u32[]{:S(2)}) %collective-permute-start.13) | collective-permute-done | bytes 86048 | tf_op jit(solution)/shard_map/ppermute | solution.py:22
  41.5 0.0 collective-permute-done.15.refs_2_
  41.5 0.0 copy-done
  41.5 0.3 shard_map.102
  41.8 0.0 collective-permute-done.10.theirs
  41.8 1.0 %shard_map.103 = (f32[1,96,2048]{2,1,0:T(8,128)}, bf16[32,2048]{1,0:T(8,128)(2,1)}, bf16[2,32]{1,0:T(2,128)(2,1)}) custom-call(bf16[96,2048]{1,0:T(8,128)(2,1)S(1)} %shard_map.99.mine, bf16[96,2048]{1,0:T(8,128)(2,1)S(1)} %collective-permute-done.10.theirs, bf16[32,2048]{1,0:T(8,128)(2,1)S(1)} %get-tuple-element.52.tokens, ...), custom_call_target="tpu_custom_call" | custom-call | bytes 1835264 | tf_op jit(solution)/shard_map/pallas_call | solution.py:38
Async XLA Ops:
  2.3 10.9 %collective-permute-start.5 = (bf16[144,2048]{1,0:T(8,128)(2,1)S(1)}, bf16[144,2048]{1,0:T(8,128)(2,1)S(1)}, u32[]{:S(2)}, u32[]{:S(2)}) collective-permute-start(bf16[144,2048]{1,0:T(8,128)(2,1)S(1)} %get-tuple-element.36.refs_4_), channel_id=1, source_target_pairs={{0,1},{1,0},{2,3},{3,2},{16,18},{17,19},{18,16},{19,17},{4,5},{5,4... | collective-permute-start | bytes 1769480 | tf_op jit(solution)/shard_map/ppermute | solution.py:32
  5.3 9.9 %collective-permute-start = (bf16[40,2048]{1,0:T(8,128)(2,1)S(1)}, bf16[40,2048]{1,0:T(8,128)(2,1)S(1)}, u32[]{:S(2)}, u32[]{:S(2)}) collective-permute-start(bf16[40,2048]{1,0:T(8,128)(2,1)S(1)} %get-tuple-element.30), channel_id=1, source_target_pairs={{0,12},{4,8},{8,4},{12,0},{1,13},{5,9},{9,5},{13,1},{2,14},{6,10},... | collective-permute-start | bytes 491528 | tf_op jit(solution)/shard_map/ppermute | solution.py:22
  8.9 13.6 %collective-permute-start.1 = (bf16[40,2048]{1,0:T(8,128)(2,1)S(1)}, bf16[40,2048]{1,0:T(8,128)(2,1)S(1)}, u32[]{:S(2)}, u32[]{:S(2)}) collective-permute-start(bf16[40,2048]{1,0:T(8,128)(2,1)S(1)} %get-tuple-element.31), channel_id=1, source_target_pairs={{0,8},{4,12},{8,0},{12,4},{1,9},{5,13},{9,1},{13,5},{2,10},{6,14},... | collective-permute-start | bytes 491528 | tf_op jit(solution)/shard_map/ppermute | solution.py:22
  8.9 13.6 %collective-permute-start.2 = (bf16[40,2048]{1,0:T(8,128)(2,1)S(1)}, bf16[40,2048]{1,0:T(8,128)(2,1)S(1)}, u32[]{:S(2)}, u32[]{:S(2)}) collective-permute-start(bf16[40,2048]{1,0:T(8,128)(2,1)S(1)} %get-tuple-element.32), channel_id=1, source_target_pairs={{0,4},{4,0},{8,12},{12,8},{1,5},{5,1},{9,13},{13,9},{2,6},{6,2},{1... | collective-permute-start | bytes 491528 | tf_op jit(solution)/shard_map/ppermute | solution.py:22
  9.7 16.2 %collective-permute-start.6 = (bf16[144,2048]{1,0:T(8,128)(2,1)S(1)}, bf16[144,2048]{1,0:T(8,128)(2,1)S(1)}, u32[]{:S(2)}, u32[]{:S(2)}) collective-permute-start(bf16[144,2048]{1,0:T(8,128)(2,1)S(1)} %get-tuple-element.40), channel_id=1, source_target_pairs={{0,1},{1,0},{2,3},{3,2},{16,18},{17,19},{18,16},{19,17},{4,5},{5,4... | collective-permute-start | bytes 1769480 | tf_op jit(solution)/shard_map/ppermute | solution.py:32
  13.2 15.2 %collective-permute-start.8 = (bf16[144,2048]{1,0:T(8,128)(2,1)S(1)}, bf16[144,2048]{1,0:T(8,128)(2,1)S(1)}, u32[]{:S(2)}, u32[]{:S(2)}) collective-permute-start(bf16[144,2048]{1,0:T(8,128)(2,1)S(1)} %collective-permute-done.5.refs_5_), channel_id=1, source_target_pairs={{0,2},{1,3},{2,0},{3,1},{16,17},{17,16},{18,19},{19,18},{4,6},{5,7... | collective-permute-start | bytes 1769480 | tf_op jit(solution)/shard_map/ppermute | solution.py:32
  22.7 1.7 %collective-permute-start.3 = (bf16[80,2048]{1,0:T(8,128)(2,1)S(1)}, bf16[80,2048]{1,0:T(8,128)(2,1)S(1)}, u32[]{:S(2)}, u32[]{:S(2)}) collective-permute-start(bf16[80,2048]{1,0:T(8,128)(2,1)S(1)} %get-tuple-element.34.refs_0_), channel_id=1, source_target_pairs={{0,16},{16,0},{1,17},{17,1},{2,18},{18,2},{3,19},{19,3},{4,20},{20... | collective-permute-start | bytes 983048 | tf_op jit(solution)/shard_map/ppermute | solution.py:22
  22.8 2.1 %collective-permute-start.4 = (bf16[80,2048]{1,0:T(8,128)(2,1)S(1)}, bf16[80,2048]{1,0:T(8,128)(2,1)S(1)}, u32[]{:S(2)}, u32[]{:S(2)}) collective-permute-start(bf16[80,2048]{1,0:T(8,128)(2,1)S(1)} %get-tuple-element.35.refs_1_), channel_id=1, source_target_pairs={{0,16},{16,0},{1,17},{17,1},{2,18},{18,2},{3,19},{19,3},{4,20},{20... | collective-permute-start | bytes 983048 | tf_op jit(solution)/shard_map/ppermute | solution.py:22
  26.8 9.8 %collective-permute-start.7 = (bf16[96,2048]{1,0:T(8,128)(2,1)S(1)}, bf16[96,2048]{1,0:T(8,128)(2,1)S(1)}, u32[]{:S(2)}, u32[]{:S(2)}) collective-permute-start(bf16[96,2048]{1,0:T(8,128)(2,1)S(1)} %get-tuple-element.41), channel_id=1, source_target_pairs={{0,1},{1,0},{2,3},{3,2},{16,18},{17,19},{18,16},{19,17},{4,5},{5,4... | collective-permute-start | bytes 1179656 | tf_op jit(solution)/shard_map/ppermute | solution.py:32
  29.4 1.5 %collective-permute-start.11 = (bf16[40,2176]{1,0:T(8,128)(2,1)S(1)}, bf16[40,2176]{1,0:T(8,128)(2,1)S(1)}, u32[]{:S(2)}, u32[]{:S(2)}) collective-permute-start(bf16[40,2176]{1,0:T(8,128)(2,1)S(1)} %get-tuple-element.45), channel_id=1, source_target_pairs={{0,16},{16,0},{1,17},{17,1},{2,18},{18,2},{3,19},{19,3},{4,20},{20... | collective-permute-start | bytes 522248 | tf_op jit(solution)/shard_map/ppermute | solution.py:22
  29.5 4.6 %collective-permute-start.14 = (bf16[40,2176]{1,0:T(8,128)(2,1)S(1)}, bf16[40,2176]{1,0:T(8,128)(2,1)S(1)}, u32[]{:S(2)}, u32[]{:S(2)}) collective-permute-start(bf16[40,2176]{1,0:T(8,128)(2,1)S(1)} %get-tuple-element.48), channel_id=1, source_target_pairs={{0,16},{16,0},{1,17},{17,1},{2,18},{18,2},{3,19},{19,3},{4,20},{20... | collective-permute-start | bytes 522248 | tf_op jit(solution)/shard_map/ppermute | solution.py:22
  30.0 8.8 %collective-permute-start.9 = (bf16[48,2048]{1,0:T(8,128)(2,1)S(1)}, bf16[48,2048]{1,0:T(8,128)(2,1)S(1)}, u32[]{:S(2)}, u32[]{:S(2)}) collective-permute-start(bf16[48,2048]{1,0:T(8,128)(2,1)S(1)} %get-tuple-element.43), channel_id=1, source_target_pairs={{0,3},{1,2},{2,1},{3,0},{16,19},{17,18},{18,17},{19,16},{4,7},{5,6... | collective-permute-start | bytes 589832 | tf_op jit(solution)/shard_map/ppermute | solution.py:32
  30.9 10.6 %copy-start = (bf16[32,2]{0,1:T(2,128)(2,1)S(1)}, bf16[32,2]{0,1:T(2,128)(2,1)}, u32[]{:S(2)}) copy-start(bf16[32,2]{0,1:T(2,128)(2,1)} %param.10) | copy-start | bytes 388
  31.0 8.0 %collective-permute-start.12 = (bf16[168,256]{1,0:T(8,128)(2,1)S(1)}, bf16[168,256]{1,0:T(8,128)(2,1)S(1)}, u32[]{:S(2)}, u32[]{:S(2)}) collective-permute-start(bf16[168,256]{1,0:T(8,128)(2,1)S(1)} %get-tuple-element.46), channel_id=1, source_target_pairs={{0,12},{4,8},{8,4},{12,0},{1,13},{5,9},{9,5},{13,1},{2,14},{6,10},... | collective-permute-start | bytes 258056 | tf_op jit(solution)/shard_map/ppermute | solution.py:22
  34.0 7.4 %collective-permute-start.13 = (bf16[168,256]{1,0:T(8,128)(2,1)S(1)}, bf16[168,256]{1,0:T(8,128)(2,1)S(1)}, u32[]{:S(2)}, u32[]{:S(2)}) collective-permute-start(bf16[168,256]{1,0:T(8,128)(2,1)S(1)} %get-tuple-element.47), channel_id=1, source_target_pairs={{0,8},{4,12},{8,0},{12,4},{1,9},{5,13},{9,1},{13,5},{2,10},{6,14},... | collective-permute-start | bytes 258056 | tf_op jit(solution)/shard_map/ppermute | solution.py:22
  34.1 7.3 %collective-permute-start.15 = (bf16[168,256]{1,0:T(8,128)(2,1)S(1)}, bf16[168,256]{1,0:T(8,128)(2,1)S(1)}, u32[]{:S(2)}, u32[]{:S(2)}) collective-permute-start(bf16[168,256]{1,0:T(8,128)(2,1)S(1)} %get-tuple-element.49), channel_id=1, source_target_pairs={{0,4},{4,0},{8,12},{12,8},{1,5},{5,1},{9,13},{13,9},{2,6},{6,2},{1... | collective-permute-start | bytes 258056 | tf_op jit(solution)/shard_map/ppermute | solution.py:22
  38.9 2.9 %collective-permute-start.10 = (bf16[96,2048]{1,0:T(8,128)(2,1)S(1)}, bf16[96,2048]{1,0:T(8,128)(2,1)S(1)}, u32[]{:S(2)}, u32[]{:S(2)}) collective-permute-start(bf16[96,2048]{1,0:T(8,128)(2,1)S(1)} %shard_map.99.mine), channel_id=1, source_target_pairs={{0,16},{16,0},{1,17},{17,1},{2,18},{18,2},{3,19},{19,3},{4,20},{20... | collective-permute-start | bytes 1179656 | tf_op jit(solution)/shard_map/ppermute | solution.py:22

commit v16 on v14

--- a/solution.py
+++ b/solution.py
@@ -120,7 +120,7 @@
     prob = jnp.sum(act * d_act, axis=1, keepdims=True)
     d_gate = d_act * up_pre * sig * (1.0 + gate_pre * (1.0 - sig))
     d_pre = jnp.concatenate([d_gate, d_act * silu], axis=1).astype(bf16)
-    return dot(d_pre, mixers, (1, 0)), prob, dot(act.astype(bf16), d_rows, (0, 0))
+    return d_pre, mixers, prob, dot(act.astype(bf16), d_rows, (0, 0))
 
 
 def gather_kernel(*refs):
@@ -137,29 +137,31 @@
 
 def early_kernel(*refs):
     *pieces, dx_out, grad_own, grad_near = refs[4:]
-    dx, prob, grad = expert_math(*both_cores(*refs[:4]), pieces)
-    width, hidden = dx.shape[1], grad_own.shape[0]
-    dx_out[:, :width] = dx
+    d_pre, mixers, prob, grad = expert_math(*both_cores(*refs[:4]), pieces)
+    width, hidden = mixers.shape[1], grad_own.shape[0]
+    dx_out[:, :width] = dot(d_pre, mixers, (1, 0))
     dx_out[:, width:] = jnp.broadcast_to(prob, (prob.shape[0], LANES))
     grad_own[...] = grad[:hidden]
     grad_near[...] = grad[hidden:].astype(bf16)
 
 
 def middle_kernel(*refs):
-    dx_ref, grad_ref, piece, dx_out, grad_out = refs[4:]
-    dx, prob, grad = expert_math(*both_cores(*refs[:4]), [piece])
-    width, hidden = dx.shape[1], grad.shape[0]
-    dx_out[:, :width] = dx_ref[:, :width] + dx
-    dx_out[:, width:] = dx_ref[:, width:] + prob
+    grad_ref, piece, pre_out, prob_out, grad_out = refs[4:]
+    pre_out[...], _, prob, grad = expert_math(*both_cores(*refs[:4]), [piece])
+    hidden = grad.shape[0]
+    prob_out[...] = jnp.broadcast_to(prob, prob_out.shape)
     grad_out[:hidden] = grad_ref[...]
     grad_out[hidden:] = grad.astype(bf16)
 
 
 def late_kernel(*refs):
-    dx_ref, far, keep, *gives, grad_far = refs[4:]
-    dx, prob, grad = expert_math(*both_cores(*refs[:4]), [far])
+    dx_ref, pre_ref, prob_ref, near, far, keep, *gives, grad_far = refs[4:]
+    d_pre, mixers, prob, grad = expert_math(*both_cores(*refs[:4]), [far])
+    mixers = jnp.concatenate([near[: mixers.shape[0]], mixers])
+    dx = dot(jnp.concatenate([pre_ref[...], d_pre], axis=1), mixers, (1, 0))
+    prob = prob_ref[...] + prob
     width, slots = dx.shape[1], keep.shape[0]
-    for side, value in ((slice(0, width), dx), (slice(width, None), jnp.broadcast_to(prob, (prob.shape[0], LANES)))):
+    for side, value in ((slice(0, width), dx), (slice(width, None), prob)):
         total = value + dx_ref[:, side]
         keep[:, side] = total[:slots]
         for i, give in enumerate(reversed(gives)):
@@ -272,16 +274,20 @@
         [shape((2 * slots, wide), f32), shape((hidden, width), f32), shape((hidden, width), bf16)],
         flops=10**9,
     )
-    dx, grad_near = kernel_call(
+    d_pre, prob, grad_near = kernel_call(
         middle_kernel,
-        [*own, *other, dx, grad_near, near[1]],
-        [shape((2 * slots, wide), f32), shape((2 * hidden, width), bf16)],
+        [*own, *other, grad_near, near[1]],
+        [
+            shape((2 * slots, 2 * hidden), bf16),
+            shape((2 * slots, LANES), f32),
+            shape((2 * hidden, width), bf16),
+        ],
         flops=0,
     )
     parts = 2 if chunk_count % 2 == 0 else 1
     keep, *gives, grad_far = kernel_call(
         late_kernel,
-        [*own, *other, dx, far],
+        [*own, *other, dx, d_pre, prob, near[1], far],
         [shape((slots, wide), f32)]
         + [shape((slots // parts, wide), bf16)] * parts
         + [shape((hidden, width), bf16)],

time: 42.8 us -> 42.8 us (level)
  no operation moved by 1% of the time
where the time goes in v16:
time: 42.8 us; the launch traced here: 42.6 us
  starting transfers between devices  17.9 us (42%)
  waiting for transfers between devices  17.7 us (41%)
  Pallas kernels  6.24 us (15%)
  between operations  0.74 us (2%)
    ppermute x11, waiting for transfers between devices, swap(): lax.ppermute(value, axis, [(i, i ^ mask) for i in range(lax.axis_size(axi...  11.4 us
    ppermute x11, starting transfers between devices, swap(): lax.ppermute(value, axis, [(i, i ^ mask) for i in range(lax.axis_size(axi...  10.1 us
    ppermute x5, starting transfers between devices, swap_by_core(): return lax.ppermute(value, ('rep', 'dp'), pairs)  7.8 us
    ppermute x5, waiting for transfers between devices, swap_by_core(): return lax.ppermute(value, ('rep', 'dp'), pairs)  6.36 us
    pallas_call x10, Pallas kernels, kernel_call(): pl.pallas_call(body, out_shape=outputs, in_specs=kwargs.pop('in_specs', [...  6.24 us
  transfers between devices with their start and end apart: 16, of which 7 were waited for; matrix products, arithmetic and copies ran while one was open for 0% of the time, Pallas kernels for 9%

profile of v16, /device:TPU:0, one launch (start us, length us, event | category | flops | bytes accessed | tf_op | source)
XLA Modules:
  0.0 42.6 jit_solution(2874148992812956126)
XLA Ops:
  0.6 1.6 %shard_map.94 = (bf16[40,2048]{1,0:T(8,128)(2,1)S(1)}, bf16[40,2048]{1,0:T(8,128)(2,1)S(1)}, bf16[40,2048]{1,0:T(8,128)(2,1)S(1)}, bf16[40,2048]{1,0:T(8,128)(2,...) custom-call(s32[2,32]{1,0:T(2,128)} %bitcast.5, bf16[2,32]{1,0:T(2,128)(2,1)} %bitcast.3, ...), custom_call_target="tpu_custom_call" | custom-call | bytes 3277440 | tf_op jit(solution)/shard_map/pallas_call | solution.py:37
  2.2 3.0 %collective-permute-start.5 = (bf16[144,2048]{1,0:T(8,128)(2,1)S(1)}, bf16[144,2048]{1,0:T(8,128)(2,1)S(1)}, u32[]{:S(2)}, u32[]{:S(2)}) collective-permute-start(bf16[144,2048]{1,0:T(8,128)(2,1)S(1)} %get-tuple-element.37.refs_4_), channel_id=1, source_target_pairs={{0,1},{1,0},{2,3},{3,2},{16,18},{17,19},{18,16},{19,17},{4,5},{5,4... | collective-permute-start | bytes 1769480 | tf_op jit(solution)/shard_map/ppermute | solution.py:31
  5.2 3.6 %collective-permute-start = (bf16[40,2048]{1,0:T(8,128)(2,1)S(1)}, bf16[40,2048]{1,0:T(8,128)(2,1)S(1)}, u32[]{:S(2)}, u32[]{:S(2)}) collective-permute-start(bf16[40,2048]{1,0:T(8,128)(2,1)S(1)} %get-tuple-element.31), channel_id=1, source_target_pairs={{0,12},{4,8},{8,4},{12,0},{1,13},{5,9},{9,5},{13,1},{2,14},{6,10},... | collective-permute-start | bytes 491528 | tf_op jit(solution)/shard_map/ppermute | solution.py:21
  8.8 0.0 collective-permute-start.1
  8.8 0.8 %collective-permute-start.2 = (bf16[40,2048]{1,0:T(8,128)(2,1)S(1)}, bf16[40,2048]{1,0:T(8,128)(2,1)S(1)}, u32[]{:S(2)}, u32[]{:S(2)}) collective-permute-start(bf16[40,2048]{1,0:T(8,128)(2,1)S(1)} %get-tuple-element.33), channel_id=1, source_target_pairs={{0,4},{4,0},{8,12},{12,8},{1,5},{5,1},{9,13},{13,9},{2,6},{6,2},{1... | collective-permute-start | bytes 491528 | tf_op jit(solution)/shard_map/ppermute | solution.py:21
  9.6 0.3 collective-permute-start.6
  9.9 3.2 %collective-permute-done.5.refs_5_ = bf16[144,2048]{1,0:T(8,128)(2,1)S(1)} collective-permute-done((bf16[144,2048]{1,0:T(8,128)(2,1)S(1)}, bf16[144,2048]{1,0:T(8,128)(2,1)S(1)}, u32[]{:S(2)}, u32[]{:S(2)}) %collective-permute-start.5) | collective-permute-done | bytes 589856 | tf_op jit(solution)/shard_map/ppermute | solution.py:31
  13.1 2.1 %collective-permute-start.8 = (bf16[144,2048]{1,0:T(8,128)(2,1)S(1)}, bf16[144,2048]{1,0:T(8,128)(2,1)S(1)}, u32[]{:S(2)}, u32[]{:S(2)}) collective-permute-start(bf16[144,2048]{1,0:T(8,128)(2,1)S(1)} %collective-permute-done.5.refs_5_), channel_id=1, source_target_pairs={{0,2},{1,3},{2,0},{3,1},{16,17},{17,16},{18,19},{19,18},{4,6},{5,7... | collective-permute-start | bytes 1769480 | tf_op jit(solution)/shard_map/ppermute | solution.py:31
  15.1 0.0 collective-permute-done.refs_0_
  15.1 7.3 %collective-permute-done.1.refs_1_ = bf16[40,2048]{1,0:T(8,128)(2,1)S(1)} collective-permute-done((bf16[40,2048]{1,0:T(8,128)(2,1)S(1)}, bf16[40,2048]{1,0:T(8,128)(2,1)S(1)}, u32[]{:S(2)}, u32[]{:S(2)}) %collective-permute-start.1) | collective-permute-done | bytes 163872 | tf_op jit(solution)/shard_map/ppermute | solution.py:21
  22.5 0.0 collective-permute-done.2.refs_2_
  22.5 0.1 shard_map.95
  22.6 0.1 collective-permute-start.3
  22.6 0.5 %collective-permute-start.4 = (bf16[80,2048]{1,0:T(8,128)(2,1)S(1)}, bf16[80,2048]{1,0:T(8,128)(2,1)S(1)}, u32[]{:S(2)}, u32[]{:S(2)}) collective-permute-start(bf16[80,2048]{1,0:T(8,128)(2,1)S(1)} %get-tuple-element.36.refs_1_), channel_id=1, source_target_pairs={{0,16},{16,0},{1,17},{17,1},{2,18},{18,2},{3,19},{19,3},{4,20},{20... | collective-permute-start | bytes 983048 | tf_op jit(solution)/shard_map/ppermute | solution.py:21
  23.1 1.1 %collective-permute-done.3.refs_2_ = bf16[80,2048]{1,0:T(8,128)(2,1)S(1)} collective-permute-done((bf16[80,2048]{1,0:T(8,128)(2,1)S(1)}, bf16[80,2048]{1,0:T(8,128)(2,1)S(1)}, u32[]{:S(2)}, u32[]{:S(2)}) %collective-permute-start.3) | collective-permute-done | bytes 327712 | tf_op jit(solution)/shard_map/ppermute | solution.py:21
  24.3 0.5 %collective-permute-done.4.refs_3_ = bf16[80,2048]{1,0:T(8,128)(2,1)S(1)} collective-permute-done((bf16[80,2048]{1,0:T(8,128)(2,1)S(1)}, bf16[80,2048]{1,0:T(8,128)(2,1)S(1)}, u32[]{:S(2)}, u32[]{:S(2)}) %collective-permute-start.4) | collective-permute-done | bytes 327712 | tf_op jit(solution)/shard_map/ppermute | solution.py:21
  24.7 1.2 %shard_map.96 = (f32[160,2176]{1,0:T(8,128)S(1)}, f32[48,2048]{1,0:T(8,128)S(1)}, bf16[48,2048]{1,0:T(8,128)(2,1)S(1)}) custom-call(bf16[80,2048]{1,0:T(8,128)(2,1)S(1)} %get-tuple-element.35.refs_0_, bf16[80,2048]{1,0:T(8,128)(2,1)S(1)} %get-tuple-element.36.refs_1_, bf16[80,2048]{1,0:T(8,128)(2,1)S(1)} %collective-permute-done.3.refs_2_, ...), custom_call_target="tpu_custom_call" | custom-call | flops 1000000000 | bytes 4472832 | tf_op jit(solution)/shard_map/pallas_call | solution.py:37
  25.9 0.0 collective-permute-done.6.refs_5_.refs_7_
  25.9 0.8 %shard_map.97 = (bf16[160,96]{1,0:T(8,128)(2,1)S(1)}, f32[160,128]{1,0:T(8,128)S(1)}, bf16[96,2048]{1,0:T(8,128)(2,1)S(1)}) custom-call(bf16[80,2048]{1,0:T(8,128)(2,1)S(1)} %get-tuple-element.35.refs_0_, bf16[80,2048]{1,0:T(8,128)(2,1)S(1)} %get-tuple-element.36.refs_1_, bf16[80,2048]{1,0:T(8,128)(2,1)S(1)} %collective-permute-done.3.refs_2_, ...), custom_call_target="tpu_custom_call" | custom-call | bytes 2603008 | tf_op jit(solution)/shard_map/pallas_call | solution.py:37
  26.7 1.6 %collective-permute-start.7 = (bf16[96,2048]{1,0:T(8,128)(2,1)S(1)}, bf16[96,2048]{1,0:T(8,128)(2,1)S(1)}, u32[]{:S(2)}, u32[]{:S(2)}) collective-permute-start(bf16[96,2048]{1,0:T(8,128)(2,1)S(1)} %get-tuple-element.41), channel_id=1, source_target_pairs={{0,1},{1,0},{2,3},{3,2},{16,18},{17,19},{18,16},{19,17},{4,5},{5,4... | collective-permute-start | bytes 1179656 | tf_op jit(solution)/shard_map/ppermute | solution.py:31
  28.3 0.0 collective-permute-done.8.refs_8_
  28.3 1.1 %shard_map.98 = (f32[80,2176]{1,0:T(8,128)S(1)}, bf16[40,2176]{1,0:T(8,128)(2,1)S(1)}, bf16[40,2176]{1,0:T(8,128)(2,1)S(1)}, bf16[48,2048]{1,0:T(8,128)(2,1)S(1)}) custom-call(bf16[80,2048]{1,0:T(8,128)(2,1)S(1)} %get-tuple-element.35.refs_0_, bf16[80,2048]{1,0:T(8,128)(2,1)S(1)} %get-tuple-element.36.refs_1_, ...), custom_call_target="tpu_custom_call" | custom-call | bytes 5236736 | tf_op jit(solution)/shard_map/pallas_call | solution.py:37
  29.3 0.1 collective-permute-start.11
  29.4 0.5 %collective-permute-start.14 = (bf16[40,2176]{1,0:T(8,128)(2,1)S(1)}, bf16[40,2176]{1,0:T(8,128)(2,1)S(1)}, u32[]{:S(2)}, u32[]{:S(2)}) collective-permute-start(bf16[40,2176]{1,0:T(8,128)(2,1)S(1)} %get-tuple-element.50), channel_id=1, source_target_pairs={{0,16},{16,0},{1,17},{17,1},{2,18},{18,2},{3,19},{19,3},{4,20},{20... | collective-permute-start | bytes 522248 | tf_op jit(solution)/shard_map/ppermute | solution.py:21
  29.9 0.9 %collective-permute-start.9 = (bf16[48,2048]{1,0:T(8,128)(2,1)S(1)}, bf16[48,2048]{1,0:T(8,128)(2,1)S(1)}, u32[]{:S(2)}, u32[]{:S(2)}) collective-permute-start(bf16[48,2048]{1,0:T(8,128)(2,1)S(1)} %get-tuple-element.45), channel_id=1, source_target_pairs={{0,3},{1,2},{2,1},{3,0},{16,19},{17,18},{18,17},{19,16},{4,7},{5,6... | collective-permute-start | bytes 589832 | tf_op jit(solution)/shard_map/ppermute | solution.py:31
  30.8 0.0 collective-permute-done.11.got
  30.8 0.0 copy-start
  30.8 0.1 shard_map.100
  30.9 3.0 %collective-permute-start.12 = (bf16[168,256]{1,0:T(8,128)(2,1)S(1)}, bf16[168,256]{1,0:T(8,128)(2,1)S(1)}, u32[]{:S(2)}, u32[]{:S(2)}) collective-permute-start(bf16[168,256]{1,0:T(8,128)(2,1)S(1)} %get-tuple-element.48), channel_id=1, source_target_pairs={{0,12},{4,8},{8,4},{12,0},{1,13},{5,9},{9,5},{13,1},{2,14},{6,10},... | collective-permute-start | bytes 258056 | tf_op jit(solution)/shard_map/ppermute | solution.py:21
  33.9 0.0 collective-permute-start.13
  33.9 0.0 collective-permute-done.14.got
  33.9 0.1 shard_map.101
  34.0 1.5 %collective-permute-start.15 = (bf16[168,256]{1,0:T(8,128)(2,1)S(1)}, bf16[168,256]{1,0:T(8,128)(2,1)S(1)}, u32[]{:S(2)}, u32[]{:S(2)}) collective-permute-start(bf16[168,256]{1,0:T(8,128)(2,1)S(1)} %get-tuple-element.51), channel_id=1, source_target_pairs={{0,4},{4,0},{8,12},{12,8},{1,5},{5,1},{9,13},{13,9},{2,6},{6,2},{1... | collective-permute-start | bytes 258056 | tf_op jit(solution)/shard_map/ppermute | solution.py:21
  35.5 1.0 %collective-permute-done.7.near = bf16[96,2048]{1,0:T(8,128)(2,1)S(1)} collective-permute-done((bf16[96,2048]{1,0:T(8,128)(2,1)S(1)}, bf16[96,2048]{1,0:T(8,128)(2,1)S(1)}, u32[]{:S(2)}, u32[]{:S(2)}) %collective-permute-start.7) | collective-permute-done | bytes 393248 | tf_op jit(solution)/shard_map/ppermute | solution.py:31
  36.5 2.2 %collective-permute-done.9.far = bf16[48,2048]{1,0:T(8,128)(2,1)S(1)} collective-permute-done((bf16[48,2048]{1,0:T(8,128)(2,1)S(1)}, bf16[48,2048]{1,0:T(8,128)(2,1)S(1)}, u32[]{:S(2)}, u32[]{:S(2)}) %collective-permute-start.9) | collective-permute-done | bytes 196640 | tf_op jit(solution)/shard_map/ppermute | solution.py:31
  38.7 0.1 shard_map.99.mine
  38.8 0.1 collective-permute-start.10
  38.9 0.0 collective-permute-done.12.refs_0_
  38.9 2.4 %collective-permute-done.13.refs_1_ = bf16[168,256]{1,0:T(8,128)(2,1)S(1)} collective-permute-done((bf16[168,256]{1,0:T(8,128)(2,1)S(1)}, bf16[168,256]{1,0:T(8,128)(2,1)S(1)}, u32[]{:S(2)}, u32[]{:S(2)}) %collective-permute-start.13) | collective-permute-done | bytes 86048 | tf_op jit(solution)/shard_map/ppermute | solution.py:21
  41.3 0.0 collective-permute-done.15.refs_2_
  41.3 0.0 copy-done
  41.3 0.3 shard_map.102
  41.6 0.0 collective-permute-done.10.theirs
  41.7 1.0 %shard_map.103 = (f32[1,96,2048]{2,1,0:T(8,128)}, bf16[32,2048]{1,0:T(8,128)(2,1)}, bf16[2,32]{1,0:T(2,128)(2,1)}) custom-call(bf16[96,2048]{1,0:T(8,128)(2,1)S(1)} %shard_map.99.mine, bf16[96,2048]{1,0:T(8,128)(2,1)S(1)} %collective-permute-done.10.theirs, bf16[32,2048]{1,0:T(8,128)(2,1)S(1)} %get-tuple-element.54.tokens, ...), custom_call_target="tpu_custom_call" | custom-call | bytes 1835264 | tf_op jit(solution)/shard_map/pallas_call | solution.py:37
Async XLA Ops:
  2.2 10.9 %collective-permute-start.5 = (bf16[144,2048]{1,0:T(8,128)(2,1)S(1)}, bf16[144,2048]{1,0:T(8,128)(2,1)S(1)}, u32[]{:S(2)}, u32[]{:S(2)}) collective-permute-start(bf16[144,2048]{1,0:T(8,128)(2,1)S(1)} %get-tuple-element.37.refs_4_), channel_id=1, source_target_pairs={{0,1},{1,0},{2,3},{3,2},{16,18},{17,19},{18,16},{19,17},{4,5},{5,4... | collective-permute-start | bytes 1769480 | tf_op jit(solution)/shard_map/ppermute | solution.py:31
  5.2 9.9 %collective-permute-start = (bf16[40,2048]{1,0:T(8,128)(2,1)S(1)}, bf16[40,2048]{1,0:T(8,128)(2,1)S(1)}, u32[]{:S(2)}, u32[]{:S(2)}) collective-permute-start(bf16[40,2048]{1,0:T(8,128)(2,1)S(1)} %get-tuple-element.31), channel_id=1, source_target_pairs={{0,12},{4,8},{8,4},{12,0},{1,13},{5,9},{9,5},{13,1},{2,14},{6,10},... | collective-permute-start | bytes 491528 | tf_op jit(solution)/shard_map/ppermute | solution.py:21
  8.8 13.6 %collective-permute-start.1 = (bf16[40,2048]{1,0:T(8,128)(2,1)S(1)}, bf16[40,2048]{1,0:T(8,128)(2,1)S(1)}, u32[]{:S(2)}, u32[]{:S(2)}) collective-permute-start(bf16[40,2048]{1,0:T(8,128)(2,1)S(1)} %get-tuple-element.32), channel_id=1, source_target_pairs={{0,8},{4,12},{8,0},{12,4},{1,9},{5,13},{9,1},{13,5},{2,10},{6,14},... | collective-permute-start | bytes 491528 | tf_op jit(solution)/shard_map/ppermute | solution.py:21
  8.8 13.6 %collective-permute-start.2 = (bf16[40,2048]{1,0:T(8,128)(2,1)S(1)}, bf16[40,2048]{1,0:T(8,128)(2,1)S(1)}, u32[]{:S(2)}, u32[]{:S(2)}) collective-permute-start(bf16[40,2048]{1,0:T(8,128)(2,1)S(1)} %get-tuple-element.33), channel_id=1, source_target_pairs={{0,4},{4,0},{8,12},{12,8},{1,5},{5,1},{9,13},{13,9},{2,6},{6,2},{1... | collective-permute-start | bytes 491528 | tf_op jit(solution)/shard_map/ppermute | solution.py:21
  9.6 16.3 %collective-permute-start.6 = (bf16[144,2048]{1,0:T(8,128)(2,1)S(1)}, bf16[144,2048]{1,0:T(8,128)(2,1)S(1)}, u32[]{:S(2)}, u32[]{:S(2)}) collective-permute-start(bf16[144,2048]{1,0:T(8,128)(2,1)S(1)} %get-tuple-element.40), channel_id=1, source_target_pairs={{0,1},{1,0},{2,3},{3,2},{16,18},{17,19},{18,16},{19,17},{4,5},{5,4... | collective-permute-start | bytes 1769480 | tf_op jit(solution)/shard_map/ppermute | solution.py:31
  13.1 15.2 %collective-permute-start.8 = (bf16[144,2048]{1,0:T(8,128)(2,1)S(1)}, bf16[144,2048]{1,0:T(8,128)(2,1)S(1)}, u32[]{:S(2)}, u32[]{:S(2)}) collective-permute-start(bf16[144,2048]{1,0:T(8,128)(2,1)S(1)} %collective-permute-done.5.refs_5_), channel_id=1, source_target_pairs={{0,2},{1,3},{2,0},{3,1},{16,17},{17,16},{18,19},{19,18},{4,6},{5,7... | collective-permute-start | bytes 1769480 | tf_op jit(solution)/shard_map/ppermute | solution.py:31
  22.6 1.7 %collective-permute-start.3 = (bf16[80,2048]{1,0:T(8,128)(2,1)S(1)}, bf16[80,2048]{1,0:T(8,128)(2,1)S(1)}, u32[]{:S(2)}, u32[]{:S(2)}) collective-permute-start(bf16[80,2048]{1,0:T(8,128)(2,1)S(1)} %get-tuple-element.35.refs_0_), channel_id=1, source_target_pairs={{0,16},{16,0},{1,17},{17,1},{2,18},{18,2},{3,19},{19,3},{4,20},{20... | collective-permute-start | bytes 983048 | tf_op jit(solution)/shard_map/ppermute | solution.py:21
  22.6 2.1 %collective-permute-start.4 = (bf16[80,2048]{1,0:T(8,128)(2,1)S(1)}, bf16[80,2048]{1,0:T(8,128)(2,1)S(1)}, u32[]{:S(2)}, u32[]{:S(2)}) collective-permute-start(bf16[80,2048]{1,0:T(8,128)(2,1)S(1)} %get-tuple-element.36.refs_1_), channel_id=1, source_target_pairs={{0,16},{16,0},{1,17},{17,1},{2,18},{18,2},{3,19},{19,3},{4,20},{20... | collective-permute-start | bytes 983048 | tf_op jit(solution)/shard_map/ppermute | solution.py:21
  26.7 9.8 %collective-permute-start.7 = (bf16[96,2048]{1,0:T(8,128)(2,1)S(1)}, bf16[96,2048]{1,0:T(8,128)(2,1)S(1)}, u32[]{:S(2)}, u32[]{:S(2)}) collective-permute-start(bf16[96,2048]{1,0:T(8,128)(2,1)S(1)} %get-tuple-element.41), channel_id=1, source_target_pairs={{0,1},{1,0},{2,3},{3,2},{16,18},{17,19},{18,16},{19,17},{4,5},{5,4... | collective-permute-start | bytes 1179656 | tf_op jit(solution)/shard_map/ppermute | solution.py:31
  29.3 1.5 %collective-permute-start.11 = (bf16[40,2176]{1,0:T(8,128)(2,1)S(1)}, bf16[40,2176]{1,0:T(8,128)(2,1)S(1)}, u32[]{:S(2)}, u32[]{:S(2)}) collective-permute-start(bf16[40,2176]{1,0:T(8,128)(2,1)S(1)} %get-tuple-element.47), channel_id=1, source_target_pairs={{0,16},{16,0},{1,17},{17,1},{2,18},{18,2},{3,19},{19,3},{4,20},{20... | collective-permute-start | bytes 522248 | tf_op jit(solution)/shard_map/ppermute | solution.py:21
  29.4 4.5 %collective-permute-start.14 = (bf16[40,2176]{1,0:T(8,128)(2,1)S(1)}, bf16[40,2176]{1,0:T(8,128)(2,1)S(1)}, u32[]{:S(2)}, u32[]{:S(2)}) collective-permute-start(bf16[40,2176]{1,0:T(8,128)(2,1)S(1)} %get-tuple-element.50), channel_id=1, source_target_pairs={{0,16},{16,0},{1,17},{17,1},{2,18},{18,2},{3,19},{19,3},{4,20},{20... | collective-permute-start | bytes 522248 | tf_op jit(solution)/shard_map/ppermute | solution.py:21
  29.9 8.8 %collective-permute-start.9 = (bf16[48,2048]{1,0:T(8,128)(2,1)S(1)}, bf16[48,2048]{1,0:T(8,128)(2,1)S(1)}, u32[]{:S(2)}, u32[]{:S(2)}) collective-permute-start(bf16[48,2048]{1,0:T(8,128)(2,1)S(1)} %get-tuple-element.45), channel_id=1, source_target_pairs={{0,3},{1,2},{2,1},{3,0},{16,19},{17,18},{18,17},{19,16},{4,7},{5,6... | collective-permute-start | bytes 589832 | tf_op jit(solution)/shard_map/ppermute | solution.py:31
  30.8 10.5 %copy-start = (bf16[32,2]{0,1:T(2,128)(2,1)S(1)}, bf16[32,2]{0,1:T(2,128)(2,1)}, u32[]{:S(2)}) copy-start(bf16[32,2]{0,1:T(2,128)(2,1)} %param.10) | copy-start | bytes 388
  30.9 8.0 %collective-permute-start.12 = (bf16[168,256]{1,0:T(8,128)(2,1)S(1)}, bf16[168,256]{1,0:T(8,128)(2,1)S(1)}, u32[]{:S(2)}, u32[]{:S(2)}) collective-permute-start(bf16[168,256]{1,0:T(8,128)(2,1)S(1)} %get-tuple-element.48), channel_id=1, source_target_pairs={{0,12},{4,8},{8,4},{12,0},{1,13},{5,9},{9,5},{13,1},{2,14},{6,10},... | collective-permute-start | bytes 258056 | tf_op jit(solution)/shard_map/ppermute | solution.py:21
  33.9 7.4 %collective-permute-start.13 = (bf16[168,256]{1,0:T(8,128)(2,1)S(1)}, bf16[168,256]{1,0:T(8,128)(2,1)S(1)}, u32[]{:S(2)}, u32[]{:S(2)}) collective-permute-start(bf16[168,256]{1,0:T(8,128)(2,1)S(1)} %get-tuple-element.49), channel_id=1, source_target_pairs={{0,8},{4,12},{8,0},{12,4},{1,9},{5,13},{9,1},{13,5},{2,10},{6,14},... | collective-permute-start | bytes 258056 | tf_op jit(solution)/shard_map/ppermute | solution.py:21
  34.0 7.3 %collective-permute-start.15 = (bf16[168,256]{1,0:T(8,128)(2,1)S(1)}, bf16[168,256]{1,0:T(8,128)(2,1)S(1)}, u32[]{:S(2)}, u32[]{:S(2)}) collective-permute-start(bf16[168,256]{1,0:T(8,128)(2,1)S(1)} %get-tuple-element.51), channel_id=1, source_target_pairs={{0,4},{4,0},{8,12},{12,8},{1,5},{5,1},{9,13},{13,9},{2,6},{6,2},{1... | collective-permute-start | bytes 258056 | tf_op jit(solution)/shard_map/ppermute | solution.py:21
  38.8 2.9 %collective-permute-start.10 = (bf16[96,2048]{1,0:T(8,128)(2,1)S(1)}, bf16[96,2048]{1,0:T(8,128)(2,1)S(1)}, u32[]{:S(2)}, u32[]{:S(2)}) collective-permute-start(bf16[96,2048]{1,0:T(8,128)(2,1)S(1)} %shard_map.99.mine), channel_id=1, source_target_pairs={{0,16},{16,0},{1,17},{17,1},{2,18},{18,2},{3,19},{19,3},{4,20},{20... | collective-permute-start | bytes 1179656 | tf_op jit(solution)/shard_map/ppermute | solution.py:21

commit v17 on v16

--- a/solution.py
+++ b/solution.py
@@ -51,7 +51,7 @@
 
 def dispatch_kernel(experts, cap, chunk_count, *refs):
     given, weights, refs = refs[:4], refs[4:7], refs[7:]
-    chunks, (slot_out, *packed), (*held, sems) = refs[:chunk_count], refs[chunk_count:-5], refs[-5:]
+    chunks, (slot_out, weight_out, *packed), (*held, sems) = refs[:chunk_count], refs[chunk_count:-5], refs[-5:]
     hidden = packed[0].shape[0] // 3
     rep = lax.axis_index("rep")
     loads = [pltpu.make_async_copy(*pair, sems.at[i]) for i, pair in enumerate(zip(given, held))]
@@ -69,6 +69,7 @@
 
     ids, route_weight, tokens, upstream = held
     top, tok_dev = ids.shape
+    weight_out[...] = route_weight[...].astype(f32)
     rows = experts * cap // chunk_count
     me = lax.axis_index("ep")
     expert_of_row = iota((experts, tok_dev), 0)
@@ -176,22 +177,6 @@
     out[hidden:] = near[hidden:]
 
 
-def finish_kernel(mine, theirs, tokens, probs, grad_out, tokens_out, probs_out, held, sems):
-    hidden = mine.shape[0] // 2
-    rep = lax.axis_index("rep")
-    copies = [pltpu.make_async_copy(tokens, tokens_out, sems.at[0]), pltpu.make_async_copy(probs, probs_out, sems.at[1])]
-    for copy in copies:
-        copy.start()
-    for i, half in enumerate((rep, 1 - rep)):
-        here, there = slice(i * hidden, (i + 1) * hidden), slice((1 - i) * hidden, (2 - i) * hidden)
-        rows = pl.ds(pl.multiple_of(half * hidden, hidden), hidden)
-        held[i] = mine[here].astype(f32) + theirs[there].astype(f32)
-        copies.append(pltpu.make_async_copy(held.at[i], grad_out.at[0, rows], sems.at[2 + i]))
-        copies[-1].start()
-    for copy in copies:
-        copy.wait()
-
-
 def add_kernel(start, rows, keep, got, *chunks):
     total = keep[start : start + got.shape[0]] + got[...].astype(f32)
     width = total.shape[1] - LANES
@@ -205,13 +190,12 @@
         chunk[...] = value.astype(bf16)
 
 
-def combine_kernel(chunk_count, rows, *refs):
-    chunks, (slot, route_weight, tokens_out, probs_out) = refs[:chunk_count], refs[chunk_count:]
+def combine(chunks, rows, slot, route_weight, tokens_out, probs_out):
     tok_dev, width = tokens_out.shape
     top = slot.shape[0]
     total = 0.0
     probs = [0.0] * top
-    for c, place in enumerate(reversed(range(chunk_count))):
+    for c, place in enumerate(reversed(range(len(chunks)))):
         slot_of_row = iota((rows, tok_dev), 0) + place * rows
         hits = [(slot_of_row == slot[k : k + 1, :]).astype(f32) for k in range(top)]
         value = chunks[c][...].astype(f32)
@@ -228,7 +212,31 @@
             probs[k] = probs[k] + jnp.sum(hits[k] * prob, axis=0, keepdims=True)
     tokens_out[...] = total.astype(bf16)
     for k in range(top):
-        probs_out[k : k + 1, :] = (probs[k] / route_weight[k : k + 1, :].astype(f32)).astype(bf16)
+        probs_out[k : k + 1, :] = (probs[k] / route_weight[k : k + 1, :]).astype(bf16)
+
+
+def pass_kernel(*refs):
+    pass
+
+
+def finish_kernel(chunk_count, rows_of_chunk, *refs):
+    chunks, (slot, route_weight, mine, theirs, *refs) = refs[:chunk_count], refs[chunk_count:]
+    grad_out, tokens_out, probs_out, held, tokens, probs, sems = refs
+    hidden = mine.shape[0] // 2
+    rep = lax.axis_index("rep")
+    copies = []
+    for i, half in enumerate((rep, 1 - rep)):
+        here, there = slice(i * hidden, (i + 1) * hidden), slice((1 - i) * hidden, (2 - i) * hidden)
+        rows = pl.ds(pl.multiple_of(half * hidden, hidden), hidden)
+        held[i] = mine[here].astype(f32) + theirs[there].astype(f32)
+        copies.append(pltpu.make_async_copy(held.at[i], grad_out.at[0, rows], sems.at[i]))
+        copies[-1].start()
+    combine(chunks, rows_of_chunk, slot, route_weight, tokens, probs)
+    for i, pair in enumerate(((tokens, tokens_out), (probs, probs_out))):
+        copies.append(pltpu.make_async_copy(*pair, sems.at[2 + i]))
+        copies[-1].start()
+    for copy in copies:
+        copy.wait()
 
 
 def local(tokens, upstream, expert_ids, route_weight, gate_weight, up_weight, down_weight):
@@ -244,11 +252,11 @@
     in_hbm = pl.BlockSpec(memory_space=pltpu.HBM)
 
     given = [expert_ids.T, route_weight.T, tokens, upstream]
-    *chunks, slot, first, second = kernel_call(
+    *chunks, slot, weight, first, second = kernel_call(
         functools.partial(dispatch_kernel, experts, cap, chunk_count),
         [pltpu.with_memory_space_constraint(a, pltpu.HBM) for a in [*given, gate_weight, up_weight, down_weight]],
         [shape((2 * rows, width), bf16)] * chunk_count
-        + [shape((top, tok_dev), jnp.int32)]
+        + [shape((top, tok_dev), jnp.int32), shape((top, tok_dev), f32)]
         + [shape((3 * hidden, width), bf16)] * 2,
         in_specs=[in_hbm] * 7,
         scratch_shapes=[pltpu.VMEM(a.shape, a.dtype) for a in given] + [pltpu.SemaphoreType.DMA((10,))],
@@ -308,13 +316,13 @@
         moved = back[0].reshape(experts, cap, wide)
         moved = lax.all_to_all(moved, "ep", split_axis=0, concat_axis=0, tiled=True)
         back = [moved.reshape(rows, wide)]
-    d_tokens, d_probs = kernel_call(
-        functools.partial(combine_kernel, chunk_count, rows),
-        back[::-1] + [slot, route_weight.T],
-        [shape((tok_dev, width), bf16), shape((top, tok_dev), bf16)],
+    back = kernel_call(
+        pass_kernel,
+        back[::-1],
+        [shape(b.shape, b.dtype) for b in back],
         flops=8 * 10**9,
-    )
-
+        input_output_aliases={i: i for i in range(len(back))},
+    )
     arrived = swap_by_core(grad_near, along), swap_by_core(grad_far, (3, 3))
     (mine,) = kernel_call(grad_kernel, [grad_own, *arrived], [shape((2 * hidden, width), bf16)])
     results = [
@@ -323,11 +331,15 @@
         shape((top, tok_dev), bf16),
     ]
     grad_total, d_tokens, d_probs = kernel_call(
-        finish_kernel,
-        [mine, swap(mine, "rep", 1), d_tokens, d_probs],
+        functools.partial(finish_kernel, chunk_count, rows),
+        [*back, slot, weight, mine, swap(mine, "rep", 1)],
         results,
         out_specs=[in_hbm] * 3,
-        scratch_shapes=[pltpu.VMEM((2, hidden, width), f32), pltpu.SemaphoreType.DMA((4,))],
+        scratch_shapes=[
+            pltpu.VMEM((2, hidden, width), f32),
+            *(pltpu.VMEM(result.shape, result.dtype) for result in results[1:]),
+            pltpu.SemaphoreType.DMA((4,)),
+        ],
     )
     return d_tokens, d_probs.T, grad_total
 

time: 42.8 us -> 42.7 us (level)
  transfers between devices with their start and end apart: 16 -> 16, of which waited for: 7 -> 7; matrix products, arithmetic and copies ran while one was open for 0% -> 0% of each run, Pallas kernels for 9% -> 8%
where the time goes in v17:
time: 42.7 us; the launch traced here: 42.6 us
  starting transfers between devices  17.9 us (42%)
  waiting for transfers between devices  17.7 us (41%)
  Pallas kernels  6.22 us (15%)
  between operations  0.73 us (2%)
    ppermute x11, waiting for transfers between devices, swap(): lax.ppermute(value, axis, [(i, i ^ mask) for i in range(lax.axis_size(axi...  11.3 us
    ppermute x11, starting transfers between devices, swap(): lax.ppermute(value, axis, [(i, i ^ mask) for i in range(lax.axis_size(axi...  10.1 us
    ppermute x5, starting transfers between devices, swap_by_core(): return lax.ppermute(value, ('rep', 'dp'), pairs)  7.81 us
    ppermute x5, waiting for transfers between devices, swap_by_core(): return lax.ppermute(value, ('rep', 'dp'), pairs)  6.36 us
    pallas_call x10, Pallas kernels, kernel_call(): pl.pallas_call(body, out_shape=outputs, in_specs=kwargs.pop('in_specs', [...  6.22 us
  transfers between devices with their start and end apart: 16, of which 7 were waited for; matrix products, arithmetic and copies ran while one was open for 0% of the time, Pallas kernels for 8%

profile of v17, /device:TPU:0, one launch (start us, length us, event | category | flops | bytes accessed | tf_op | source)
XLA Modules:
  0.0 42.6 jit_solution(7594905582237733534)
XLA Ops:
  0.6 1.6 %shard_map.94 = (bf16[40,2048]{1,0:T(8,128)(2,1)S(1)}, bf16[40,2048]{1,0:T(8,128)(2,1)S(1)}, bf16[40,2048]{1,0:T(8,128)(2,1)S(1)}, bf16[40,2048]{1,0:T(8,128)(2,...) custom-call(s32[2,32]{1,0:T(2,128)} %bitcast.3, ...), custom_call_target="tpu_custom_call" | custom-call | bytes 3277696 | tf_op jit(solution)/shard_map/pallas_call | solution.py:37
  2.2 3.0 %collective-permute-start.5 = (bf16[144,2048]{1,0:T(8,128)(2,1)S(1)}, bf16[144,2048]{1,0:T(8,128)(2,1)S(1)}, u32[]{:S(2)}, u32[]{:S(2)}) collective-permute-start(bf16[144,2048]{1,0:T(8,128)(2,1)S(1)} %get-tuple-element.40.refs_4_), channel_id=1, source_target_pairs={{0,1},{1,0},{2,3},{3,2},{16,18},{17,19},{18,16},{19,17},{4,5},{5,4... | collective-permute-start | bytes 1769480 | tf_op jit(solution)/shard_map/ppermute | solution.py:31
  5.2 3.6 %collective-permute-start = (bf16[40,2048]{1,0:T(8,128)(2,1)S(1)}, bf16[40,2048]{1,0:T(8,128)(2,1)S(1)}, u32[]{:S(2)}, u32[]{:S(2)}) collective-permute-start(bf16[40,2048]{1,0:T(8,128)(2,1)S(1)} %get-tuple-element.34), channel_id=1, source_target_pairs={{0,12},{4,8},{8,4},{12,0},{1,13},{5,9},{9,5},{13,1},{2,14},{6,10},... | collective-permute-start | bytes 491528 | tf_op jit(solution)/shard_map/ppermute | solution.py:21
  8.8 0.0 collective-permute-start.1
  8.8 0.8 %collective-permute-start.2 = (bf16[40,2048]{1,0:T(8,128)(2,1)S(1)}, bf16[40,2048]{1,0:T(8,128)(2,1)S(1)}, u32[]{:S(2)}, u32[]{:S(2)}) collective-permute-start(bf16[40,2048]{1,0:T(8,128)(2,1)S(1)} %get-tuple-element.36), channel_id=1, source_target_pairs={{0,4},{4,0},{8,12},{12,8},{1,5},{5,1},{9,13},{13,9},{2,6},{6,2},{1... | collective-permute-start | bytes 491528 | tf_op jit(solution)/shard_map/ppermute | solution.py:21
  9.6 0.3 collective-permute-start.6
  9.9 3.2 %collective-permute-done.5.refs_5_ = bf16[144,2048]{1,0:T(8,128)(2,1)S(1)} collective-permute-done((bf16[144,2048]{1,0:T(8,128)(2,1)S(1)}, bf16[144,2048]{1,0:T(8,128)(2,1)S(1)}, u32[]{:S(2)}, u32[]{:S(2)}) %collective-permute-start.5) | collective-permute-done | bytes 589856 | tf_op jit(solution)/shard_map/ppermute | solution.py:31
  13.1 2.1 %collective-permute-start.7 = (bf16[144,2048]{1,0:T(8,128)(2,1)S(1)}, bf16[144,2048]{1,0:T(8,128)(2,1)S(1)}, u32[]{:S(2)}, u32[]{:S(2)}) collective-permute-start(bf16[144,2048]{1,0:T(8,128)(2,1)S(1)} %collective-permute-done.5.refs_5_), channel_id=1, source_target_pairs={{0,2},{1,3},{2,0},{3,1},{16,17},{17,16},{18,19},{19,18},{4,6},{5,7... | collective-permute-start | bytes 1769480 | tf_op jit(solution)/shard_map/ppermute | solution.py:31
  15.1 0.0 collective-permute-done.refs_0_
  15.1 7.3 %collective-permute-done.1.refs_1_ = bf16[40,2048]{1,0:T(8,128)(2,1)S(1)} collective-permute-done((bf16[40,2048]{1,0:T(8,128)(2,1)S(1)}, bf16[40,2048]{1,0:T(8,128)(2,1)S(1)}, u32[]{:S(2)}, u32[]{:S(2)}) %collective-permute-start.1) | collective-permute-done | bytes 163872 | tf_op jit(solution)/shard_map/ppermute | solution.py:21
  22.5 0.0 collective-permute-done.2.refs_2_
  22.5 0.1 shard_map.95
  22.6 0.1 collective-permute-start.3
  22.6 0.5 %collective-permute-start.4 = (bf16[80,2048]{1,0:T(8,128)(2,1)S(1)}, bf16[80,2048]{1,0:T(8,128)(2,1)S(1)}, u32[]{:S(2)}, u32[]{:S(2)}) collective-permute-start(bf16[80,2048]{1,0:T(8,128)(2,1)S(1)} %get-tuple-element.39.refs_1_), channel_id=1, source_target_pairs={{0,16},{16,0},{1,17},{17,1},{2,18},{18,2},{3,19},{19,3},{4,20},{20... | collective-permute-start | bytes 983048 | tf_op jit(solution)/shard_map/ppermute | solution.py:21
  23.1 1.1 %collective-permute-done.3.refs_2_ = bf16[80,2048]{1,0:T(8,128)(2,1)S(1)} collective-permute-done((bf16[80,2048]{1,0:T(8,128)(2,1)S(1)}, bf16[80,2048]{1,0:T(8,128)(2,1)S(1)}, u32[]{:S(2)}, u32[]{:S(2)}) %collective-permute-start.3) | collective-permute-done | bytes 327712 | tf_op jit(solution)/shard_map/ppermute | solution.py:21
  24.3 0.5 %collective-permute-done.4.refs_3_ = bf16[80,2048]{1,0:T(8,128)(2,1)S(1)} collective-permute-done((bf16[80,2048]{1,0:T(8,128)(2,1)S(1)}, bf16[80,2048]{1,0:T(8,128)(2,1)S(1)}, u32[]{:S(2)}, u32[]{:S(2)}) %collective-permute-start.4) | collective-permute-done | bytes 327712 | tf_op jit(solution)/shard_map/ppermute | solution.py:21
  24.7 1.2 %shard_map.96 = (f32[160,2176]{1,0:T(8,128)S(1)}, f32[48,2048]{1,0:T(8,128)S(1)}, bf16[48,2048]{1,0:T(8,128)(2,1)S(1)}) custom-call(bf16[80,2048]{1,0:T(8,128)(2,1)S(1)} %get-tuple-element.38.refs_0_, bf16[80,2048]{1,0:T(8,128)(2,1)S(1)} %get-tuple-element.39.refs_1_, bf16[80,2048]{1,0:T(8,128)(2,1)S(1)} %collective-permute-done.3.refs_2_, ...), custom_call_target="tpu_custom_call" | custom-call | flops 1000000000 | bytes 4472832 | tf_op jit(solution)/shard_map/pallas_call | solution.py:37
  25.9 0.0 collective-permute-done.6.refs_5_.refs_7_
  25.9 0.8 %shard_map.97 = (bf16[160,96]{1,0:T(8,128)(2,1)S(1)}, f32[160,128]{1,0:T(8,128)S(1)}, bf16[96,2048]{1,0:T(8,128)(2,1)S(1)}) custom-call(bf16[80,2048]{1,0:T(8,128)(2,1)S(1)} %get-tuple-element.38.refs_0_, bf16[80,2048]{1,0:T(8,128)(2,1)S(1)} %get-tuple-element.39.refs_1_, bf16[80,2048]{1,0:T(8,128)(2,1)S(1)} %collective-permute-done.3.refs_2_, ...), custom_call_target="tpu_custom_call" | custom-call | bytes 2603008 | tf_op jit(solution)/shard_map/pallas_call | solution.py:37
  26.7 1.6 %collective-permute-start.13 = (bf16[96,2048]{1,0:T(8,128)(2,1)S(1)}, bf16[96,2048]{1,0:T(8,128)(2,1)S(1)}, u32[]{:S(2)}, u32[]{:S(2)}) collective-permute-start(bf16[96,2048]{1,0:T(8,128)(2,1)S(1)} %get-tuple-element.60), channel_id=1, source_target_pairs={{0,1},{1,0},{2,3},{3,2},{16,18},{17,19},{18,16},{19,17},{4,5},{5,4... | collective-permute-start | bytes 1179656 | tf_op jit(solution)/shard_map/ppermute | solution.py:31
  28.3 0.0 collective-permute-done.7.refs_8_
  28.3 1.0 %shard_map.98 = (f32[80,2176]{1,0:T(8,128)S(1)}, bf16[40,2176]{1,0:T(8,128)(2,1)S(1)}, bf16[40,2176]{1,0:T(8,128)(2,1)S(1)}, bf16[48,2048]{1,0:T(8,128)(2,1)S(1)}) custom-call(bf16[80,2048]{1,0:T(8,128)(2,1)S(1)} %get-tuple-element.38.refs_0_, bf16[80,2048]{1,0:T(8,128)(2,1)S(1)} %get-tuple-element.39.refs_1_, ...), custom_call_target="tpu_custom_call" | custom-call | bytes 5236736 | tf_op jit(solution)/shard_map/pallas_call | solution.py:37
  29.3 0.1 collective-permute-start.8
  29.4 0.5 %collective-permute-start.11 = (bf16[40,2176]{1,0:T(8,128)(2,1)S(1)}, bf16[40,2176]{1,0:T(8,128)(2,1)S(1)}, u32[]{:S(2)}, u32[]{:S(2)}) collective-permute-start(bf16[40,2176]{1,0:T(8,128)(2,1)S(1)} %get-tuple-element.50), channel_id=1, source_target_pairs={{0,16},{16,0},{1,17},{17,1},{2,18},{18,2},{3,19},{19,3},{4,20},{20... | collective-permute-start | bytes 522248 | tf_op jit(solution)/shard_map/ppermute | solution.py:21
  29.9 0.9 %collective-permute-start.14 = (bf16[48,2048]{1,0:T(8,128)(2,1)S(1)}, bf16[48,2048]{1,0:T(8,128)(2,1)S(1)}, u32[]{:S(2)}, u32[]{:S(2)}) collective-permute-start(bf16[48,2048]{1,0:T(8,128)(2,1)S(1)} %get-tuple-element.61), channel_id=1, source_target_pairs={{0,3},{1,2},{2,1},{3,0},{16,19},{17,18},{18,17},{19,16},{4,7},{5,6... | collective-permute-start | bytes 589832 | tf_op jit(solution)/shard_map/ppermute | solution.py:31
  30.8 0.0 collective-permute-done.8.got
  30.8 0.1 shard_map.99
  30.9 3.0 %collective-permute-start.9 = (bf16[168,256]{1,0:T(8,128)(2,1)S(1)}, bf16[168,256]{1,0:T(8,128)(2,1)S(1)}, u32[]{:S(2)}, u32[]{:S(2)}) collective-permute-start(bf16[168,256]{1,0:T(8,128)(2,1)S(1)} %get-tuple-element.48), channel_id=1, source_target_pairs={{0,12},{4,8},{8,4},{12,0},{1,13},{5,9},{9,5},{13,1},{2,14},{6,10},... | collective-permute-start | bytes 258056 | tf_op jit(solution)/shard_map/ppermute | solution.py:21
  33.9 0.0 collective-permute-start.10
  33.9 0.0 collective-permute-done.11.got
  33.9 0.1 shard_map.100
  34.0 1.5 %collective-permute-start.12 = (bf16[168,256]{1,0:T(8,128)(2,1)S(1)}, bf16[168,256]{1,0:T(8,128)(2,1)S(1)}, u32[]{:S(2)}, u32[]{:S(2)}) collective-permute-start(bf16[168,256]{1,0:T(8,128)(2,1)S(1)} %get-tuple-element.51), channel_id=1, source_target_pairs={{0,4},{4,0},{8,12},{12,8},{1,5},{5,1},{9,13},{13,9},{2,6},{6,2},{1... | collective-permute-start | bytes 258056 | tf_op jit(solution)/shard_map/ppermute | solution.py:21
  35.5 1.0 %collective-permute-done.13.near = bf16[96,2048]{1,0:T(8,128)(2,1)S(1)} collective-permute-done((bf16[96,2048]{1,0:T(8,128)(2,1)S(1)}, bf16[96,2048]{1,0:T(8,128)(2,1)S(1)}, u32[]{:S(2)}, u32[]{:S(2)}) %collective-permute-start.13) | collective-permute-done | bytes 393248 | tf_op jit(solution)/shard_map/ppermute | solution.py:31
  36.5 2.2 %collective-permute-done.14.far = bf16[48,2048]{1,0:T(8,128)(2,1)S(1)} collective-permute-done((bf16[48,2048]{1,0:T(8,128)(2,1)S(1)}, bf16[48,2048]{1,0:T(8,128)(2,1)S(1)}, u32[]{:S(2)}, u32[]{:S(2)}) %collective-permute-start.14) | collective-permute-done | bytes 196640 | tf_op jit(solution)/shard_map/ppermute | solution.py:31
  38.7 0.1 shard_map.102.refs_6_
  38.8 0.1 collective-permute-start.15
  38.9 0.0 collective-permute-done.9.refs_0_
  38.9 2.4 %collective-permute-done.10.refs_1_ = bf16[168,256]{1,0:T(8,128)(2,1)S(1)} collective-permute-done((bf16[168,256]{1,0:T(8,128)(2,1)S(1)}, bf16[168,256]{1,0:T(8,128)(2,1)S(1)}, u32[]{:S(2)}, u32[]{:S(2)}) %collective-permute-start.10) | collective-permute-done | bytes 86048 | tf_op jit(solution)/shard_map/ppermute | solution.py:21
  41.3 0.0 collective-permute-done.12.refs_2_
  41.3 0.0 collective-permute-done.15.refs_7_
  41.3 1.3 %shard_map.103 = (f32[1,96,2048]{2,1,0:T(8,128)}, bf16[32,2048]{1,0:T(8,128)(2,1)}, bf16[2,32]{1,0:T(2,128)(2,1)}) custom-call(bf16[168,256]{1,0:T(8,128)(2,1)S(1)} %get-tuple-element.53.refs_0_, bf16[168,256]{1,0:T(8,128)(2,1)S(1)} %get-tuple-element.54.refs_1_, bf16[168,256]{1,0:T(8,128)(2,1)S(1)} %get-tuple-element.55.refs_2_, ...), custom_call_target="tpu_custom_call" | custom-call | bytes 2048640 | tf_op jit(solution)/shard_map/pallas_call | solution.py:37
  (1 shorter events, 0.0 us)
Async XLA Ops:
  2.2 10.9 %collective-permute-start.5 = (bf16[144,2048]{1,0:T(8,128)(2,1)S(1)}, bf16[144,2048]{1,0:T(8,128)(2,1)S(1)}, u32[]{:S(2)}, u32[]{:S(2)}) collective-permute-start(bf16[144,2048]{1,0:T(8,128)(2,1)S(1)} %get-tuple-element.40.refs_4_), channel_id=1, source_target_pairs={{0,1},{1,0},{2,3},{3,2},{16,18},{17,19},{18,16},{19,17},{4,5},{5,4... | collective-permute-start | bytes 1769480 | tf_op jit(solution)/shard_map/ppermute | solution.py:31
  5.2 9.9 %collective-permute-start = (bf16[40,2048]{1,0:T(8,128)(2,1)S(1)}, bf16[40,2048]{1,0:T(8,128)(2,1)S(1)}, u32[]{:S(2)}, u32[]{:S(2)}) collective-permute-start(bf16[40,2048]{1,0:T(8,128)(2,1)S(1)} %get-tuple-element.34), channel_id=1, source_target_pairs={{0,12},{4,8},{8,4},{12,0},{1,13},{5,9},{9,5},{13,1},{2,14},{6,10},... | collective-permute-start | bytes 491528 | tf_op jit(solution)/shard_map/ppermute | solution.py:21
  8.8 13.6 %collective-permute-start.1 = (bf16[40,2048]{1,0:T(8,128)(2,1)S(1)}, bf16[40,2048]{1,0:T(8,128)(2,1)S(1)}, u32[]{:S(2)}, u32[]{:S(2)}) collective-permute-start(bf16[40,2048]{1,0:T(8,128)(2,1)S(1)} %get-tuple-element.35), channel_id=1, source_target_pairs={{0,8},{4,12},{8,0},{12,4},{1,9},{5,13},{9,1},{13,5},{2,10},{6,14},... | collective-permute-start | bytes 491528 | tf_op jit(solution)/shard_map/ppermute | solution.py:21
  8.8 13.6 %collective-permute-start.2 = (bf16[40,2048]{1,0:T(8,128)(2,1)S(1)}, bf16[40,2048]{1,0:T(8,128)(2,1)S(1)}, u32[]{:S(2)}, u32[]{:S(2)}) collective-permute-start(bf16[40,2048]{1,0:T(8,128)(2,1)S(1)} %get-tuple-element.36), channel_id=1, source_target_pairs={{0,4},{4,0},{8,12},{12,8},{1,5},{5,1},{9,13},{13,9},{2,6},{6,2},{1... | collective-permute-start | bytes 491528 | tf_op jit(solution)/shard_map/ppermute | solution.py:21
  9.6 16.3 %collective-permute-start.6 = (bf16[144,2048]{1,0:T(8,128)(2,1)S(1)}, bf16[144,2048]{1,0:T(8,128)(2,1)S(1)}, u32[]{:S(2)}, u32[]{:S(2)}) collective-permute-start(bf16[144,2048]{1,0:T(8,128)(2,1)S(1)} %get-tuple-element.43), channel_id=1, source_target_pairs={{0,1},{1,0},{2,3},{3,2},{16,18},{17,19},{18,16},{19,17},{4,5},{5,4... | collective-permute-start | bytes 1769480 | tf_op jit(solution)/shard_map/ppermute | solution.py:31
  13.1 15.2 %collective-permute-start.7 = (bf16[144,2048]{1,0:T(8,128)(2,1)S(1)}, bf16[144,2048]{1,0:T(8,128)(2,1)S(1)}, u32[]{:S(2)}, u32[]{:S(2)}) collective-permute-start(bf16[144,2048]{1,0:T(8,128)(2,1)S(1)} %collective-permute-done.5.refs_5_), channel_id=1, source_target_pairs={{0,2},{1,3},{2,0},{3,1},{16,17},{17,16},{18,19},{19,18},{4,6},{5,7... | collective-permute-start | bytes 1769480 | tf_op jit(solution)/shard_map/ppermute | solution.py:31
  22.6 1.7 %collective-permute-start.3 = (bf16[80,2048]{1,0:T(8,128)(2,1)S(1)}, bf16[80,2048]{1,0:T(8,128)(2,1)S(1)}, u32[]{:S(2)}, u32[]{:S(2)}) collective-permute-start(bf16[80,2048]{1,0:T(8,128)(2,1)S(1)} %get-tuple-element.38.refs_0_), channel_id=1, source_target_pairs={{0,16},{16,0},{1,17},{17,1},{2,18},{18,2},{3,19},{19,3},{4,20},{20... | collective-permute-start | bytes 983048 | tf_op jit(solution)/shard_map/ppermute | solution.py:21
  22.6 2.1 %collective-permute-start.4 = (bf16[80,2048]{1,0:T(8,128)(2,1)S(1)}, bf16[80,2048]{1,0:T(8,128)(2,1)S(1)}, u32[]{:S(2)}, u32[]{:S(2)}) collective-permute-start(bf16[80,2048]{1,0:T(8,128)(2,1)S(1)} %get-tuple-element.39.refs_1_), channel_id=1, source_target_pairs={{0,16},{16,0},{1,17},{17,1},{2,18},{18,2},{3,19},{19,3},{4,20},{20... | collective-permute-start | bytes 983048 | tf_op jit(solution)/shard_map/ppermute | solution.py:21
  26.7 9.8 %collective-permute-start.13 = (bf16[96,2048]{1,0:T(8,128)(2,1)S(1)}, bf16[96,2048]{1,0:T(8,128)(2,1)S(1)}, u32[]{:S(2)}, u32[]{:S(2)}) collective-permute-start(bf16[96,2048]{1,0:T(8,128)(2,1)S(1)} %get-tuple-element.60), channel_id=1, source_target_pairs={{0,1},{1,0},{2,3},{3,2},{16,18},{17,19},{18,16},{19,17},{4,5},{5,4... | collective-permute-start | bytes 1179656 | tf_op jit(solution)/shard_map/ppermute | solution.py:31
  29.3 1.5 %collective-permute-start.8 = (bf16[40,2176]{1,0:T(8,128)(2,1)S(1)}, bf16[40,2176]{1,0:T(8,128)(2,1)S(1)}, u32[]{:S(2)}, u32[]{:S(2)}) collective-permute-start(bf16[40,2176]{1,0:T(8,128)(2,1)S(1)} %get-tuple-element.47), channel_id=1, source_target_pairs={{0,16},{16,0},{1,17},{17,1},{2,18},{18,2},{3,19},{19,3},{4,20},{20... | collective-permute-start | bytes 522248 | tf_op jit(solution)/shard_map/ppermute | solution.py:21
  29.4 4.5 %collective-permute-start.11 = (bf16[40,2176]{1,0:T(8,128)(2,1)S(1)}, bf16[40,2176]{1,0:T(8,128)(2,1)S(1)}, u32[]{:S(2)}, u32[]{:S(2)}) collective-permute-start(bf16[40,2176]{1,0:T(8,128)(2,1)S(1)} %get-tuple-element.50), channel_id=1, source_target_pairs={{0,16},{16,0},{1,17},{17,1},{2,18},{18,2},{3,19},{19,3},{4,20},{20... | collective-permute-start | bytes 522248 | tf_op jit(solution)/shard_map/ppermute | solution.py:21
  29.9 8.8 %collective-permute-start.14 = (bf16[48,2048]{1,0:T(8,128)(2,1)S(1)}, bf16[48,2048]{1,0:T(8,128)(2,1)S(1)}, u32[]{:S(2)}, u32[]{:S(2)}) collective-permute-start(bf16[48,2048]{1,0:T(8,128)(2,1)S(1)} %get-tuple-element.61), channel_id=1, source_target_pairs={{0,3},{1,2},{2,1},{3,0},{16,19},{17,18},{18,17},{19,16},{4,7},{5,6... | collective-permute-start | bytes 589832 | tf_op jit(solution)/shard_map/ppermute | solution.py:31
  30.9 8.0 %collective-permute-start.9 = (bf16[168,256]{1,0:T(8,128)(2,1)S(1)}, bf16[168,256]{1,0:T(8,128)(2,1)S(1)}, u32[]{:S(2)}, u32[]{:S(2)}) collective-permute-start(bf16[168,256]{1,0:T(8,128)(2,1)S(1)} %get-tuple-element.48), channel_id=1, source_target_pairs={{0,12},{4,8},{8,4},{12,0},{1,13},{5,9},{9,5},{13,1},{2,14},{6,10},... | collective-permute-start | bytes 258056 | tf_op jit(solution)/shard_map/ppermute | solution.py:21
  33.9 7.4 %collective-permute-start.10 = (bf16[168,256]{1,0:T(8,128)(2,1)S(1)}, bf16[168,256]{1,0:T(8,128)(2,1)S(1)}, u32[]{:S(2)}, u32[]{:S(2)}) collective-permute-start(bf16[168,256]{1,0:T(8,128)(2,1)S(1)} %get-tuple-element.49), channel_id=1, source_target_pairs={{0,8},{4,12},{8,0},{12,4},{1,9},{5,13},{9,1},{13,5},{2,10},{6,14},... | collective-permute-start | bytes 258056 | tf_op jit(solution)/shard_map/ppermute | solution.py:21
  34.0 7.3 %collective-permute-start.12 = (bf16[168,256]{1,0:T(8,128)(2,1)S(1)}, bf16[168,256]{1,0:T(8,128)(2,1)S(1)}, u32[]{:S(2)}, u32[]{:S(2)}) collective-permute-start(bf16[168,256]{1,0:T(8,128)(2,1)S(1)} %get-tuple-element.51), channel_id=1, source_target_pairs={{0,4},{4,0},{8,12},{12,8},{1,5},{5,1},{9,13},{13,9},{2,6},{6,2},{1... | collective-permute-start | bytes 258056 | tf_op jit(solution)/shard_map/ppermute | solution.py:21
  38.8 2.5 %collective-permute-start.15 = (bf16[96,2048]{1,0:T(8,128)(2,1)S(1)}, bf16[96,2048]{1,0:T(8,128)(2,1)S(1)}, u32[]{:S(2)}, u32[]{:S(2)}) collective-permute-start(bf16[96,2048]{1,0:T(8,128)(2,1)S(1)} %shard_map.102.refs_6_), channel_id=1, source_target_pairs={{0,16},{16,0},{1,17},{17,1},{2,18},{18,2},{3,19},{19,3},{4,20},{20... | collective-permute-start | bytes 1179656 | tf_op jit(solution)/shard_map/ppermute | solution.py:21

commit v18 on v17

--- a/solution.py
+++ b/solution.py
@@ -51,9 +51,11 @@
 
 def dispatch_kernel(experts, cap, chunk_count, *refs):
     given, weights, refs = refs[:4], refs[4:7], refs[7:]
-    chunks, (slot_out, weight_out, *packed), (*held, sems) = refs[:chunk_count], refs[chunk_count:-5], refs[-5:]
+    chunks, (slot_out, weight_out, *packed), (ids, route_weight, both, sems) = refs[:chunk_count], refs[chunk_count:-4], refs[-4:]
     hidden = packed[0].shape[0] // 3
     rep = lax.axis_index("rep")
+    top, tok_dev = ids.shape
+    held = (ids, route_weight, both.at[pl.ds(0, tok_dev)], both.at[pl.ds(tok_dev, tok_dev)])
     loads = [pltpu.make_async_copy(*pair, sems.at[i]) for i, pair in enumerate(zip(given, held))]
     packs = []
     for j, half in enumerate((rep, 1 - rep)):
@@ -67,8 +69,6 @@
     for copy in loads[:2]:
         copy.wait()
 
-    ids, route_weight, tokens, upstream = held
-    top, tok_dev = ids.shape
     weight_out[...] = route_weight[...].astype(f32)
     rows = experts * cap // chunk_count
     me = lax.axis_index("ep")
@@ -76,9 +76,8 @@
     named = [(expert_of_row == ids[k : k + 1, :]).astype(f32) for k in range(top)]
     earlier = (iota((tok_dev, tok_dev), 0) < iota((tok_dev, tok_dev), 1)).astype(bf16)
     before = dot(sum(named).astype(bf16), earlier, (1, 0))
-    row = iota((2 * experts * cap, tok_dev), 0)
-    take_x = jnp.zeros(row.shape, f32)
-    take_dy = jnp.zeros(row.shape, f32)
+    row = iota((2 * experts * cap, 2 * tok_dev), 0)
+    take = jnp.zeros(row.shape, f32)
     scale = jnp.zeros(row.shape, f32)
     for k in range(top):
         rank = jnp.sum(before * named[k], axis=0, keepdims=True).astype(jnp.int32)
@@ -91,17 +90,15 @@
             slot = expert * cap + rank
             x_row = slot
         slot_out[k : k + 1, :] = slot
-        here_x = (row == x_row).astype(f32)
-        here_dy = (row == x_row + rows).astype(f32)
-        take_x += here_x
-        take_dy += here_dy
-        scale += here_x + here_dy * route_weight[k : k + 1, :].astype(f32)
+        weight = route_weight[k : k + 1, :].astype(f32)
+        here = (row == jnp.concatenate([x_row, x_row + rows], axis=1)).astype(f32)
+        take += here
+        scale += here * jnp.concatenate([jnp.ones_like(weight), weight], axis=1)
     scale = jnp.sum(scale, axis=1, keepdims=True)
-    take_x, take_dy = take_x.astype(bf16), take_dy.astype(bf16)
+    take = take.astype(bf16)
     for copy in loads[2:]:
         copy.wait()
-    picked = dot(take_x, tokens[...], (1, 0)) + dot(take_dy, upstream[...], (1, 0))
-    picked = picked * scale
+    picked = dot(take, both[...], (1, 0)) * scale
     for c in range(chunk_count):
         chunks[c][...] = picked[2 * rows * c : 2 * rows * (c + 1)].astype(bf16)
     for copy in packs:
@@ -259,7 +256,11 @@
         + [shape((top, tok_dev), jnp.int32), shape((top, tok_dev), f32)]
         + [shape((3 * hidden, width), bf16)] * 2,
         in_specs=[in_hbm] * 7,
-        scratch_shapes=[pltpu.VMEM(a.shape, a.dtype) for a in given] + [pltpu.SemaphoreType.DMA((10,))],
+        scratch_shapes=[
+            *(pltpu.VMEM(a.shape, a.dtype) for a in given[:2]),
+            pltpu.VMEM((2 * tok_dev, width), bf16),
+            pltpu.SemaphoreType.DMA((10,)),
+        ],
     )
 
     along, across = (1, 2), (2, 1)

time: 42.7 us -> 42.7 us (level)
  no operation moved by 1% of the time
where the time goes in v18:
time: 42.7 us; the launch traced here: 42.5 us
  starting transfers between devices  17.9 us (42%)
  waiting for transfers between devices  17.7 us (41%)
  Pallas kernels  6.17 us (14%)
  between operations  0.73 us (2%)
    ppermute x11, waiting for transfers between devices, swap(): lax.ppermute(value, axis, [(i, i ^ mask) for i in range(lax.axis_size(axi...  11.3 us
    ppermute x11, starting transfers between devices, swap(): lax.ppermute(value, axis, [(i, i ^ mask) for i in range(lax.axis_size(axi...  10.1 us
    ppermute x5, starting transfers between devices, swap_by_core(): return lax.ppermute(value, ('rep', 'dp'), pairs)  7.82 us
    ppermute x5, waiting for transfers between devices, swap_by_core(): return lax.ppermute(value, ('rep', 'dp'), pairs)  6.37 us
    pallas_call x10, Pallas kernels, kernel_call(): pl.pallas_call(body, out_shape=outputs, in_specs=kwargs.pop('in_specs', [...  6.17 us
  transfers between devices with their start and end apart: 16, of which 7 were waited for; matrix products, arithmetic and copies ran while one was open for 0% of the time, Pallas kernels for 8%

profile of v18, /device:TPU:0, one launch (start us, length us, event | category | flops | bytes accessed | tf_op | source)
XLA Modules:
  0.0 42.5 jit_solution(8212445249587873697)
XLA Ops:
  0.6 1.5 %shard_map.94 = (bf16[40,2048]{1,0:T(8,128)(2,1)S(1)}, bf16[40,2048]{1,0:T(8,128)(2,1)S(1)}, bf16[40,2048]{1,0:T(8,128)(2,1)S(1)}, bf16[40,2048]{1,0:T(8,128)(2,...) custom-call(s32[2,32]{1,0:T(2,128)} %bitcast.3, ...), custom_call_target="tpu_custom_call" | custom-call | bytes 3277696 | tf_op jit(solution)/shard_map/pallas_call | solution.py:37
  2.2 3.0 %collective-permute-start.5 = (bf16[144,2048]{1,0:T(8,128)(2,1)S(1)}, bf16[144,2048]{1,0:T(8,128)(2,1)S(1)}, u32[]{:S(2)}, u32[]{:S(2)}) collective-permute-start(bf16[144,2048]{1,0:T(8,128)(2,1)S(1)} %get-tuple-element.40.refs_4_), channel_id=1, source_target_pairs={{0,1},{1,0},{2,3},{3,2},{16,18},{17,19},{18,16},{19,17},{4,5},{5,4... | collective-permute-start | bytes 1769480 | tf_op jit(solution)/shard_map/ppermute | solution.py:31
  5.2 3.6 %collective-permute-start = (bf16[40,2048]{1,0:T(8,128)(2,1)S(1)}, bf16[40,2048]{1,0:T(8,128)(2,1)S(1)}, u32[]{:S(2)}, u32[]{:S(2)}) collective-permute-start(bf16[40,2048]{1,0:T(8,128)(2,1)S(1)} %get-tuple-element.34), channel_id=1, source_target_pairs={{0,12},{4,8},{8,4},{12,0},{1,13},{5,9},{9,5},{13,1},{2,14},{6,10},... | collective-permute-start | bytes 491528 | tf_op jit(solution)/shard_map/ppermute | solution.py:21
  8.8 0.0 collective-permute-start.1
  8.8 0.8 %collective-permute-start.2 = (bf16[40,2048]{1,0:T(8,128)(2,1)S(1)}, bf16[40,2048]{1,0:T(8,128)(2,1)S(1)}, u32[]{:S(2)}, u32[]{:S(2)}) collective-permute-start(bf16[40,2048]{1,0:T(8,128)(2,1)S(1)} %get-tuple-element.36), channel_id=1, source_target_pairs={{0,4},{4,0},{8,12},{12,8},{1,5},{5,1},{9,13},{13,9},{2,6},{6,2},{1... | collective-permute-start | bytes 491528 | tf_op jit(solution)/shard_map/ppermute | solution.py:21
  9.6 0.3 collective-permute-start.6
  9.9 3.2 %collective-permute-done.5.refs_5_ = bf16[144,2048]{1,0:T(8,128)(2,1)S(1)} collective-permute-done((bf16[144,2048]{1,0:T(8,128)(2,1)S(1)}, bf16[144,2048]{1,0:T(8,128)(2,1)S(1)}, u32[]{:S(2)}, u32[]{:S(2)}) %collective-permute-start.5) | collective-permute-done | bytes 589856 | tf_op jit(solution)/shard_map/ppermute | solution.py:31
  13.1 2.0 %collective-permute-start.7 = (bf16[144,2048]{1,0:T(8,128)(2,1)S(1)}, bf16[144,2048]{1,0:T(8,128)(2,1)S(1)}, u32[]{:S(2)}, u32[]{:S(2)}) collective-permute-start(bf16[144,2048]{1,0:T(8,128)(2,1)S(1)} %collective-permute-done.5.refs_5_), channel_id=1, source_target_pairs={{0,2},{1,3},{2,0},{3,1},{16,17},{17,16},{18,19},{19,18},{4,6},{5,7... | collective-permute-start | bytes 1769480 | tf_op jit(solution)/shard_map/ppermute | solution.py:31
  15.1 0.0 collective-permute-done.refs_0_
  15.1 7.3 %collective-permute-done.1.refs_1_ = bf16[40,2048]{1,0:T(8,128)(2,1)S(1)} collective-permute-done((bf16[40,2048]{1,0:T(8,128)(2,1)S(1)}, bf16[40,2048]{1,0:T(8,128)(2,1)S(1)}, u32[]{:S(2)}, u32[]{:S(2)}) %collective-permute-start.1) | collective-permute-done | bytes 163872 | tf_op jit(solution)/shard_map/ppermute | solution.py:21
  22.4 0.0 collective-permute-done.2.refs_2_
  22.4 0.1 shard_map.95
  22.5 0.1 collective-permute-start.3
  22.6 0.5 %collective-permute-start.4 = (bf16[80,2048]{1,0:T(8,128)(2,1)S(1)}, bf16[80,2048]{1,0:T(8,128)(2,1)S(1)}, u32[]{:S(2)}, u32[]{:S(2)}) collective-permute-start(bf16[80,2048]{1,0:T(8,128)(2,1)S(1)} %get-tuple-element.39.refs_1_), channel_id=1, source_target_pairs={{0,16},{16,0},{1,17},{17,1},{2,18},{18,2},{3,19},{19,3},{4,20},{20... | collective-permute-start | bytes 983048 | tf_op jit(solution)/shard_map/ppermute | solution.py:21
  23.1 1.1 %collective-permute-done.3.refs_2_ = bf16[80,2048]{1,0:T(8,128)(2,1)S(1)} collective-permute-done((bf16[80,2048]{1,0:T(8,128)(2,1)S(1)}, bf16[80,2048]{1,0:T(8,128)(2,1)S(1)}, u32[]{:S(2)}, u32[]{:S(2)}) %collective-permute-start.3) | collective-permute-done | bytes 327712 | tf_op jit(solution)/shard_map/ppermute | solution.py:21
  24.2 0.5 %collective-permute-done.4.refs_3_ = bf16[80,2048]{1,0:T(8,128)(2,1)S(1)} collective-permute-done((bf16[80,2048]{1,0:T(8,128)(2,1)S(1)}, bf16[80,2048]{1,0:T(8,128)(2,1)S(1)}, u32[]{:S(2)}, u32[]{:S(2)}) %collective-permute-start.4) | collective-permute-done | bytes 327712 | tf_op jit(solution)/shard_map/ppermute | solution.py:21
  24.7 1.2 %shard_map.96 = (f32[160,2176]{1,0:T(8,128)S(1)}, f32[48,2048]{1,0:T(8,128)S(1)}, bf16[48,2048]{1,0:T(8,128)(2,1)S(1)}) custom-call(bf16[80,2048]{1,0:T(8,128)(2,1)S(1)} %get-tuple-element.38.refs_0_, bf16[80,2048]{1,0:T(8,128)(2,1)S(1)} %get-tuple-element.39.refs_1_, bf16[80,2048]{1,0:T(8,128)(2,1)S(1)} %collective-permute-done.3.refs_2_, ...), custom_call_target="tpu_custom_call" | custom-call | flops 1000000000 | bytes 4472832 | tf_op jit(solution)/shard_map/pallas_call | solution.py:37
  25.9 0.0 collective-permute-done.6.refs_5_.refs_7_
  25.9 0.8 %shard_map.97 = (bf16[160,96]{1,0:T(8,128)(2,1)S(1)}, f32[160,128]{1,0:T(8,128)S(1)}, bf16[96,2048]{1,0:T(8,128)(2,1)S(1)}) custom-call(bf16[80,2048]{1,0:T(8,128)(2,1)S(1)} %get-tuple-element.38.refs_0_, bf16[80,2048]{1,0:T(8,128)(2,1)S(1)} %get-tuple-element.39.refs_1_, bf16[80,2048]{1,0:T(8,128)(2,1)S(1)} %collective-permute-done.3.refs_2_, ...), custom_call_target="tpu_custom_call" | custom-call | bytes 2603008 | tf_op jit(solution)/shard_map/pallas_call | solution.py:37
  26.7 1.5 %collective-permute-start.13 = (bf16[96,2048]{1,0:T(8,128)(2,1)S(1)}, bf16[96,2048]{1,0:T(8,128)(2,1)S(1)}, u32[]{:S(2)}, u32[]{:S(2)}) collective-permute-start(bf16[96,2048]{1,0:T(8,128)(2,1)S(1)} %get-tuple-element.60), channel_id=1, source_target_pairs={{0,1},{1,0},{2,3},{3,2},{16,18},{17,19},{18,16},{19,17},{4,5},{5,4... | collective-permute-start | bytes 1179656 | tf_op jit(solution)/shard_map/ppermute | solution.py:31
  28.2 0.0 collective-permute-done.7.refs_8_
  28.2 1.0 %shard_map.98 = (f32[80,2176]{1,0:T(8,128)S(1)}, bf16[40,2176]{1,0:T(8,128)(2,1)S(1)}, bf16[40,2176]{1,0:T(8,128)(2,1)S(1)}, bf16[48,2048]{1,0:T(8,128)(2,1)S(1)}) custom-call(bf16[80,2048]{1,0:T(8,128)(2,1)S(1)} %get-tuple-element.38.refs_0_, bf16[80,2048]{1,0:T(8,128)(2,1)S(1)} %get-tuple-element.39.refs_1_, ...), custom_call_target="tpu_custom_call" | custom-call | bytes 5236736 | tf_op jit(solution)/shard_map/pallas_call | solution.py:37
  29.3 0.1 collective-permute-start.8
  29.4 0.5 %collective-permute-start.11 = (bf16[40,2176]{1,0:T(8,128)(2,1)S(1)}, bf16[40,2176]{1,0:T(8,128)(2,1)S(1)}, u32[]{:S(2)}, u32[]{:S(2)}) collective-permute-start(bf16[40,2176]{1,0:T(8,128)(2,1)S(1)} %get-tuple-element.50), channel_id=1, source_target_pairs={{0,16},{16,0},{1,17},{17,1},{2,18},{18,2},{3,19},{19,3},{4,20},{20... | collective-permute-start | bytes 522248 | tf_op jit(solution)/shard_map/ppermute | solution.py:21
  29.9 0.9 %collective-permute-start.14 = (bf16[48,2048]{1,0:T(8,128)(2,1)S(1)}, bf16[48,2048]{1,0:T(8,128)(2,1)S(1)}, u32[]{:S(2)}, u32[]{:S(2)}) collective-permute-start(bf16[48,2048]{1,0:T(8,128)(2,1)S(1)} %get-tuple-element.61), channel_id=1, source_target_pairs={{0,3},{1,2},{2,1},{3,0},{16,19},{17,18},{18,17},{19,16},{4,7},{5,6... | collective-permute-start | bytes 589832 | tf_op jit(solution)/shard_map/ppermute | solution.py:31
  30.8 0.0 collective-permute-done.8.got
  30.8 0.1 shard_map.99
  30.9 3.0 %collective-permute-start.9 = (bf16[168,256]{1,0:T(8,128)(2,1)S(1)}, bf16[168,256]{1,0:T(8,128)(2,1)S(1)}, u32[]{:S(2)}, u32[]{:S(2)}) collective-permute-start(bf16[168,256]{1,0:T(8,128)(2,1)S(1)} %get-tuple-element.48), channel_id=1, source_target_pairs={{0,12},{4,8},{8,4},{12,0},{1,13},{5,9},{9,5},{13,1},{2,14},{6,10},... | collective-permute-start | bytes 258056 | tf_op jit(solution)/shard_map/ppermute | solution.py:21
  33.9 0.0 collective-permute-start.10
  33.9 0.0 collective-permute-done.11.got
  33.9 0.1 shard_map.100
  34.0 1.5 %collective-permute-start.12 = (bf16[168,256]{1,0:T(8,128)(2,1)S(1)}, bf16[168,256]{1,0:T(8,128)(2,1)S(1)}, u32[]{:S(2)}, u32[]{:S(2)}) collective-permute-start(bf16[168,256]{1,0:T(8,128)(2,1)S(1)} %get-tuple-element.51), channel_id=1, source_target_pairs={{0,4},{4,0},{8,12},{12,8},{1,5},{5,1},{9,13},{13,9},{2,6},{6,2},{1... | collective-permute-start | bytes 258056 | tf_op jit(solution)/shard_map/ppermute | solution.py:21
  35.5 1.0 %collective-permute-done.13.near = bf16[96,2048]{1,0:T(8,128)(2,1)S(1)} collective-permute-done((bf16[96,2048]{1,0:T(8,128)(2,1)S(1)}, bf16[96,2048]{1,0:T(8,128)(2,1)S(1)}, u32[]{:S(2)}, u32[]{:S(2)}) %collective-permute-start.13) | collective-permute-done | bytes 393248 | tf_op jit(solution)/shard_map/ppermute | solution.py:31
  36.5 2.2 %collective-permute-done.14.far = bf16[48,2048]{1,0:T(8,128)(2,1)S(1)} collective-permute-done((bf16[48,2048]{1,0:T(8,128)(2,1)S(1)}, bf16[48,2048]{1,0:T(8,128)(2,1)S(1)}, u32[]{:S(2)}, u32[]{:S(2)}) %collective-permute-start.14) | collective-permute-done | bytes 196640 | tf_op jit(solution)/shard_map/ppermute | solution.py:31
  38.7 0.1 shard_map.102.refs_6_
  38.8 0.1 collective-permute-start.15
  38.9 0.0 collective-permute-done.9.refs_0_
  38.9 2.4 %collective-permute-done.10.refs_1_ = bf16[168,256]{1,0:T(8,128)(2,1)S(1)} collective-permute-done((bf16[168,256]{1,0:T(8,128)(2,1)S(1)}, bf16[168,256]{1,0:T(8,128)(2,1)S(1)}, u32[]{:S(2)}, u32[]{:S(2)}) %collective-permute-start.10) | collective-permute-done | bytes 86048 | tf_op jit(solution)/shard_map/ppermute | solution.py:21
  41.3 0.0 collective-permute-done.12.refs_2_
  41.3 0.0 collective-permute-done.15.refs_7_
  41.3 1.2 %shard_map.103 = (f32[1,96,2048]{2,1,0:T(8,128)}, bf16[32,2048]{1,0:T(8,128)(2,1)}, bf16[2,32]{1,0:T(2,128)(2,1)}) custom-call(bf16[168,256]{1,0:T(8,128)(2,1)S(1)} %get-tuple-element.53.refs_0_, bf16[168,256]{1,0:T(8,128)(2,1)S(1)} %get-tuple-element.54.refs_1_, bf16[168,256]{1,0:T(8,128)(2,1)S(1)} %get-tuple-element.55.refs_2_, ...), custom_call_target="tpu_custom_call" | custom-call | bytes 2048640 | tf_op jit(solution)/shard_map/pallas_call | solution.py:37
  (1 shorter events, 0.0 us)
Async XLA Ops:
  2.2 10.9 %collective-permute-start.5 = (bf16[144,2048]{1,0:T(8,128)(2,1)S(1)}, bf16[144,2048]{1,0:T(8,128)(2,1)S(1)}, u32[]{:S(2)}, u32[]{:S(2)}) collective-permute-start(bf16[144,2048]{1,0:T(8,128)(2,1)S(1)} %get-tuple-element.40.refs_4_), channel_id=1, source_target_pairs={{0,1},{1,0},{2,3},{3,2},{16,18},{17,19},{18,16},{19,17},{4,5},{5,4... | collective-permute-start | bytes 1769480 | tf_op jit(solution)/shard_map/ppermute | solution.py:31
  5.2 9.9 %collective-permute-start = (bf16[40,2048]{1,0:T(8,128)(2,1)S(1)}, bf16[40,2048]{1,0:T(8,128)(2,1)S(1)}, u32[]{:S(2)}, u32[]{:S(2)}) collective-permute-start(bf16[40,2048]{1,0:T(8,128)(2,1)S(1)} %get-tuple-element.34), channel_id=1, source_target_pairs={{0,12},{4,8},{8,4},{12,0},{1,13},{5,9},{9,5},{13,1},{2,14},{6,10},... | collective-permute-start | bytes 491528 | tf_op jit(solution)/shard_map/ppermute | solution.py:21
  8.8 13.6 %collective-permute-start.1 = (bf16[40,2048]{1,0:T(8,128)(2,1)S(1)}, bf16[40,2048]{1,0:T(8,128)(2,1)S(1)}, u32[]{:S(2)}, u32[]{:S(2)}) collective-permute-start(bf16[40,2048]{1,0:T(8,128)(2,1)S(1)} %get-tuple-element.35), channel_id=1, source_target_pairs={{0,8},{4,12},{8,0},{12,4},{1,9},{5,13},{9,1},{13,5},{2,10},{6,14},... | collective-permute-start | bytes 491528 | tf_op jit(solution)/shard_map/ppermute | solution.py:21
  8.8 13.6 %collective-permute-start.2 = (bf16[40,2048]{1,0:T(8,128)(2,1)S(1)}, bf16[40,2048]{1,0:T(8,128)(2,1)S(1)}, u32[]{:S(2)}, u32[]{:S(2)}) collective-permute-start(bf16[40,2048]{1,0:T(8,128)(2,1)S(1)} %get-tuple-element.36), channel_id=1, source_target_pairs={{0,4},{4,0},{8,12},{12,8},{1,5},{5,1},{9,13},{13,9},{2,6},{6,2},{1... | collective-permute-start | bytes 491528 | tf_op jit(solution)/shard_map/ppermute | solution.py:21
  9.6 16.3 %collective-permute-start.6 = (bf16[144,2048]{1,0:T(8,128)(2,1)S(1)}, bf16[144,2048]{1,0:T(8,128)(2,1)S(1)}, u32[]{:S(2)}, u32[]{:S(2)}) collective-permute-start(bf16[144,2048]{1,0:T(8,128)(2,1)S(1)} %get-tuple-element.43), channel_id=1, source_target_pairs={{0,1},{1,0},{2,3},{3,2},{16,18},{17,19},{18,16},{19,17},{4,5},{5,4... | collective-permute-start | bytes 1769480 | tf_op jit(solution)/shard_map/ppermute | solution.py:31
  13.1 15.2 %collective-permute-start.7 = (bf16[144,2048]{1,0:T(8,128)(2,1)S(1)}, bf16[144,2048]{1,0:T(8,128)(2,1)S(1)}, u32[]{:S(2)}, u32[]{:S(2)}) collective-permute-start(bf16[144,2048]{1,0:T(8,128)(2,1)S(1)} %collective-permute-done.5.refs_5_), channel_id=1, source_target_pairs={{0,2},{1,3},{2,0},{3,1},{16,17},{17,16},{18,19},{19,18},{4,6},{5,7... | collective-permute-start | bytes 1769480 | tf_op jit(solution)/shard_map/ppermute | solution.py:31
  22.5 1.7 %collective-permute-start.3 = (bf16[80,2048]{1,0:T(8,128)(2,1)S(1)}, bf16[80,2048]{1,0:T(8,128)(2,1)S(1)}, u32[]{:S(2)}, u32[]{:S(2)}) collective-permute-start(bf16[80,2048]{1,0:T(8,128)(2,1)S(1)} %get-tuple-element.38.refs_0_), channel_id=1, source_target_pairs={{0,16},{16,0},{1,17},{17,1},{2,18},{18,2},{3,19},{19,3},{4,20},{20... | collective-permute-start | bytes 983048 | tf_op jit(solution)/shard_map/ppermute | solution.py:21
  22.6 2.1 %collective-permute-start.4 = (bf16[80,2048]{1,0:T(8,128)(2,1)S(1)}, bf16[80,2048]{1,0:T(8,128)(2,1)S(1)}, u32[]{:S(2)}, u32[]{:S(2)}) collective-permute-start(bf16[80,2048]{1,0:T(8,128)(2,1)S(1)} %get-tuple-element.39.refs_1_), channel_id=1, source_target_pairs={{0,16},{16,0},{1,17},{17,1},{2,18},{18,2},{3,19},{19,3},{4,20},{20... | collective-permute-start | bytes 983048 | tf_op jit(solution)/shard_map/ppermute | solution.py:21
  26.7 9.8 %collective-permute-start.13 = (bf16[96,2048]{1,0:T(8,128)(2,1)S(1)}, bf16[96,2048]{1,0:T(8,128)(2,1)S(1)}, u32[]{:S(2)}, u32[]{:S(2)}) collective-permute-start(bf16[96,2048]{1,0:T(8,128)(2,1)S(1)} %get-tuple-element.60), channel_id=1, source_target_pairs={{0,1},{1,0},{2,3},{3,2},{16,18},{17,19},{18,16},{19,17},{4,5},{5,4... | collective-permute-start | bytes 1179656 | tf_op jit(solution)/shard_map/ppermute | solution.py:31
  29.3 1.5 %collective-permute-start.8 = (bf16[40,2176]{1,0:T(8,128)(2,1)S(1)}, bf16[40,2176]{1,0:T(8,128)(2,1)S(1)}, u32[]{:S(2)}, u32[]{:S(2)}) collective-permute-start(bf16[40,2176]{1,0:T(8,128)(2,1)S(1)} %get-tuple-element.47), channel_id=1, source_target_pairs={{0,16},{16,0},{1,17},{17,1},{2,18},{18,2},{3,19},{19,3},{4,20},{20... | collective-permute-start | bytes 522248 | tf_op jit(solution)/shard_map/ppermute | solution.py:21
  29.4 4.5 %collective-permute-start.11 = (bf16[40,2176]{1,0:T(8,128)(2,1)S(1)}, bf16[40,2176]{1,0:T(8,128)(2,1)S(1)}, u32[]{:S(2)}, u32[]{:S(2)}) collective-permute-start(bf16[40,2176]{1,0:T(8,128)(2,1)S(1)} %get-tuple-element.50), channel_id=1, source_target_pairs={{0,16},{16,0},{1,17},{17,1},{2,18},{18,2},{3,19},{19,3},{4,20},{20... | collective-permute-start | bytes 522248 | tf_op jit(solution)/shard_map/ppermute | solution.py:21
  29.9 8.8 %collective-permute-start.14 = (bf16[48,2048]{1,0:T(8,128)(2,1)S(1)}, bf16[48,2048]{1,0:T(8,128)(2,1)S(1)}, u32[]{:S(2)}, u32[]{:S(2)}) collective-permute-start(bf16[48,2048]{1,0:T(8,128)(2,1)S(1)} %get-tuple-element.61), channel_id=1, source_target_pairs={{0,3},{1,2},{2,1},{3,0},{16,19},{17,18},{18,17},{19,16},{4,7},{5,6... | collective-permute-start | bytes 589832 | tf_op jit(solution)/shard_map/ppermute | solution.py:31
  30.9 8.0 %collective-permute-start.9 = (bf16[168,256]{1,0:T(8,128)(2,1)S(1)}, bf16[168,256]{1,0:T(8,128)(2,1)S(1)}, u32[]{:S(2)}, u32[]{:S(2)}) collective-permute-start(bf16[168,256]{1,0:T(8,128)(2,1)S(1)} %get-tuple-element.48), channel_id=1, source_target_pairs={{0,12},{4,8},{8,4},{12,0},{1,13},{5,9},{9,5},{13,1},{2,14},{6,10},... | collective-permute-start | bytes 258056 | tf_op jit(solution)/shard_map/ppermute | solution.py:21
  33.9 7.4 %collective-permute-start.10 = (bf16[168,256]{1,0:T(8,128)(2,1)S(1)}, bf16[168,256]{1,0:T(8,128)(2,1)S(1)}, u32[]{:S(2)}, u32[]{:S(2)}) collective-permute-start(bf16[168,256]{1,0:T(8,128)(2,1)S(1)} %get-tuple-element.49), channel_id=1, source_target_pairs={{0,8},{4,12},{8,0},{12,4},{1,9},{5,13},{9,1},{13,5},{2,10},{6,14},... | collective-permute-start | bytes 258056 | tf_op jit(solution)/shard_map/ppermute | solution.py:21
  34.0 7.3 %collective-permute-start.12 = (bf16[168,256]{1,0:T(8,128)(2,1)S(1)}, bf16[168,256]{1,0:T(8,128)(2,1)S(1)}, u32[]{:S(2)}, u32[]{:S(2)}) collective-permute-start(bf16[168,256]{1,0:T(8,128)(2,1)S(1)} %get-tuple-element.51), channel_id=1, source_target_pairs={{0,4},{4,0},{8,12},{12,8},{1,5},{5,1},{9,13},{13,9},{2,6},{6,2},{1... | collective-permute-start | bytes 258056 | tf_op jit(solution)/shard_map/ppermute | solution.py:21
  38.8 2.5 %collective-permute-start.15 = (bf16[96,2048]{1,0:T(8,128)(2,1)S(1)}, bf16[96,2048]{1,0:T(8,128)(2,1)S(1)}, u32[]{:S(2)}, u32[]{:S(2)}) collective-permute-start(bf16[96,2048]{1,0:T(8,128)(2,1)S(1)} %shard_map.102.refs_6_), channel_id=1, source_target_pairs={{0,16},{16,0},{1,17},{17,1},{2,18},{18,2},{3,19},{19,3},{4,20},{20... | collective-permute-start | bytes 1179656 | tf_op jit(solution)/shard_map/ppermute | solution.py:21

commit v19 on v16

--- a/solution.py
+++ b/solution.py
@@ -51,9 +51,11 @@
 
 def dispatch_kernel(experts, cap, chunk_count, *refs):
     given, weights, refs = refs[:4], refs[4:7], refs[7:]
-    chunks, (slot_out, *packed), (*held, sems) = refs[:chunk_count], refs[chunk_count:-5], refs[-5:]
+    chunks, (slot_out, *packed), (ids, route_weight, both, sems) = refs[:chunk_count], refs[chunk_count:-4], refs[-4:]
     hidden = packed[0].shape[0] // 3
     rep = lax.axis_index("rep")
+    top, tok_dev = ids.shape
+    held = (ids, route_weight, both.at[pl.ds(0, tok_dev)], both.at[pl.ds(tok_dev, tok_dev)])
     loads = [pltpu.make_async_copy(*pair, sems.at[i]) for i, pair in enumerate(zip(given, held))]
     packs = []
     for j, half in enumerate((rep, 1 - rep)):
@@ -67,17 +69,14 @@
     for copy in loads[:2]:
         copy.wait()
 
-    ids, route_weight, tokens, upstream = held
-    top, tok_dev = ids.shape
     rows = experts * cap // chunk_count
     me = lax.axis_index("ep")
     expert_of_row = iota((experts, tok_dev), 0)
     named = [(expert_of_row == ids[k : k + 1, :]).astype(f32) for k in range(top)]
     earlier = (iota((tok_dev, tok_dev), 0) < iota((tok_dev, tok_dev), 1)).astype(bf16)
     before = dot(sum(named).astype(bf16), earlier, (1, 0))
-    row = iota((2 * experts * cap, tok_dev), 0)
-    take_x = jnp.zeros(row.shape, f32)
-    take_dy = jnp.zeros(row.shape, f32)
+    row = iota((2 * experts * cap, 2 * tok_dev), 0)
+    take = jnp.zeros(row.shape, f32)
     scale = jnp.zeros(row.shape, f32)
     for k in range(top):
         rank = jnp.sum(before * named[k], axis=0, keepdims=True).astype(jnp.int32)
@@ -90,17 +89,15 @@
             slot = expert * cap + rank
             x_row = slot
         slot_out[k : k + 1, :] = slot
-        here_x = (row == x_row).astype(f32)
-        here_dy = (row == x_row + rows).astype(f32)
-        take_x += here_x
-        take_dy += here_dy
-        scale += here_x + here_dy * route_weight[k : k + 1, :].astype(f32)
+        weight = route_weight[k : k + 1, :].astype(f32)
+        here = (row == jnp.concatenate([x_row, x_row + rows], axis=1)).astype(f32)
+        take += here
+        scale += here * jnp.concatenate([jnp.ones_like(weight), weight], axis=1)
     scale = jnp.sum(scale, axis=1, keepdims=True)
-    take_x, take_dy = take_x.astype(bf16), take_dy.astype(bf16)
+    take = take.astype(bf16)
     for copy in loads[2:]:
         copy.wait()
-    picked = dot(take_x, tokens[...], (1, 0)) + dot(take_dy, upstream[...], (1, 0))
-    picked = picked * scale
+    picked = dot(take, both[...], (1, 0)) * scale
     for c in range(chunk_count):
         chunks[c][...] = picked[2 * rows * c : 2 * rows * (c + 1)].astype(bf16)
     for copy in packs:
@@ -251,7 +248,11 @@
         + [shape((top, tok_dev), jnp.int32)]
         + [shape((3 * hidden, width), bf16)] * 2,
         in_specs=[in_hbm] * 7,
-        scratch_shapes=[pltpu.VMEM(a.shape, a.dtype) for a in given] + [pltpu.SemaphoreType.DMA((10,))],
+        scratch_shapes=[
+            *(pltpu.VMEM(a.shape, a.dtype) for a in given[:2]),
+            pltpu.VMEM((2 * tok_dev, width), bf16),
+            pltpu.SemaphoreType.DMA((10,)),
+        ],
     )
 
     along, across = (1, 2), (2, 1)

time: 42.8 us -> 42.7 us (level)
  no operation moved by 1% of the time
where the time goes in v19:
time: 42.7 us; the launch traced here: 42.6 us
  starting transfers between devices  17.9 us (42%)
  waiting for transfers between devices  17.7 us (41%)
  Pallas kernels  6.19 us (14%)
  between operations  0.74 us (2%)
    ppermute x11, waiting for transfers between devices, swap(): lax.ppermute(value, axis, [(i, i ^ mask) for i in range(lax.axis_size(axi...  11.4 us
    ppermute x11, starting transfers between devices, swap(): lax.ppermute(value, axis, [(i, i ^ mask) for i in range(lax.axis_size(axi...  10.1 us
    ppermute x5, starting transfers between devices, swap_by_core(): return lax.ppermute(value, ('rep', 'dp'), pairs)  7.83 us
    ppermute x5, waiting for transfers between devices, swap_by_core(): return lax.ppermute(value, ('rep', 'dp'), pairs)  6.35 us
    pallas_call x10, Pallas kernels, kernel_call(): pl.pallas_call(body, out_shape=outputs, in_specs=kwargs.pop('in_specs', [...  6.19 us
  transfers between devices with their start and end apart: 16, of which 7 were waited for; matrix products, arithmetic and copies ran while one was open for 0% of the time, Pallas kernels for 9%

profile of v19, /device:TPU:0, one launch (start us, length us, event | category | flops | bytes accessed | tf_op | source)
XLA Modules:
  0.0 42.6 jit_solution(11085972838726143483)
XLA Ops:
  0.6 1.5 %shard_map.94 = (bf16[40,2048]{1,0:T(8,128)(2,1)S(1)}, bf16[40,2048]{1,0:T(8,128)(2,1)S(1)}, bf16[40,2048]{1,0:T(8,128)(2,1)S(1)}, bf16[40,2048]{1,0:T(8,128)(2,...) custom-call(s32[2,32]{1,0:T(2,128)} %bitcast.5, bf16[2,32]{1,0:T(2,128)(2,1)} %bitcast.3, ...), custom_call_target="tpu_custom_call" | custom-call | bytes 3277440 | tf_op jit(solution)/shard_map/pallas_call | solution.py:37
  2.2 3.0 %collective-permute-start.5 = (bf16[144,2048]{1,0:T(8,128)(2,1)S(1)}, bf16[144,2048]{1,0:T(8,128)(2,1)S(1)}, u32[]{:S(2)}, u32[]{:S(2)}) collective-permute-start(bf16[144,2048]{1,0:T(8,128)(2,1)S(1)} %get-tuple-element.37.refs_4_), channel_id=1, source_target_pairs={{0,1},{1,0},{2,3},{3,2},{16,18},{17,19},{18,16},{19,17},{4,5},{5,4... | collective-permute-start | bytes 1769480 | tf_op jit(solution)/shard_map/ppermute | solution.py:31
  5.2 3.6 %collective-permute-start = (bf16[40,2048]{1,0:T(8,128)(2,1)S(1)}, bf16[40,2048]{1,0:T(8,128)(2,1)S(1)}, u32[]{:S(2)}, u32[]{:S(2)}) collective-permute-start(bf16[40,2048]{1,0:T(8,128)(2,1)S(1)} %get-tuple-element.31), channel_id=1, source_target_pairs={{0,12},{4,8},{8,4},{12,0},{1,13},{5,9},{9,5},{13,1},{2,14},{6,10},... | collective-permute-start | bytes 491528 | tf_op jit(solution)/shard_map/ppermute | solution.py:21
  8.8 0.0 collective-permute-start.1
  8.8 0.8 %collective-permute-start.2 = (bf16[40,2048]{1,0:T(8,128)(2,1)S(1)}, bf16[40,2048]{1,0:T(8,128)(2,1)S(1)}, u32[]{:S(2)}, u32[]{:S(2)}) collective-permute-start(bf16[40,2048]{1,0:T(8,128)(2,1)S(1)} %get-tuple-element.33), channel_id=1, source_target_pairs={{0,4},{4,0},{8,12},{12,8},{1,5},{5,1},{9,13},{13,9},{2,6},{6,2},{1... | collective-permute-start | bytes 491528 | tf_op jit(solution)/shard_map/ppermute | solution.py:21
  9.6 0.3 collective-permute-start.6
  9.9 3.2 %collective-permute-done.5.refs_5_ = bf16[144,2048]{1,0:T(8,128)(2,1)S(1)} collective-permute-done((bf16[144,2048]{1,0:T(8,128)(2,1)S(1)}, bf16[144,2048]{1,0:T(8,128)(2,1)S(1)}, u32[]{:S(2)}, u32[]{:S(2)}) %collective-permute-start.5) | collective-permute-done | bytes 589856 | tf_op jit(solution)/shard_map/ppermute | solution.py:31
  13.1 2.0 %collective-permute-start.8 = (bf16[144,2048]{1,0:T(8,128)(2,1)S(1)}, bf16[144,2048]{1,0:T(8,128)(2,1)S(1)}, u32[]{:S(2)}, u32[]{:S(2)}) collective-permute-start(bf16[144,2048]{1,0:T(8,128)(2,1)S(1)} %collective-permute-done.5.refs_5_), channel_id=1, source_target_pairs={{0,2},{1,3},{2,0},{3,1},{16,17},{17,16},{18,19},{19,18},{4,6},{5,7... | collective-permute-start | bytes 1769480 | tf_op jit(solution)/shard_map/ppermute | solution.py:31
  15.1 0.0 collective-permute-done.refs_0_
  15.1 7.3 %collective-permute-done.1.refs_1_ = bf16[40,2048]{1,0:T(8,128)(2,1)S(1)} collective-permute-done((bf16[40,2048]{1,0:T(8,128)(2,1)S(1)}, bf16[40,2048]{1,0:T(8,128)(2,1)S(1)}, u32[]{:S(2)}, u32[]{:S(2)}) %collective-permute-start.1) | collective-permute-done | bytes 163872 | tf_op jit(solution)/shard_map/ppermute | solution.py:21
  22.4 0.0 collective-permute-done.2.refs_2_
  22.4 0.1 shard_map.95
  22.5 0.1 collective-permute-start.3
  22.6 0.5 %collective-permute-start.4 = (bf16[80,2048]{1,0:T(8,128)(2,1)S(1)}, bf16[80,2048]{1,0:T(8,128)(2,1)S(1)}, u32[]{:S(2)}, u32[]{:S(2)}) collective-permute-start(bf16[80,2048]{1,0:T(8,128)(2,1)S(1)} %get-tuple-element.36.refs_1_), channel_id=1, source_target_pairs={{0,16},{16,0},{1,17},{17,1},{2,18},{18,2},{3,19},{19,3},{4,20},{20... | collective-permute-start | bytes 983048 | tf_op jit(solution)/shard_map/ppermute | solution.py:21
  23.1 1.1 %collective-permute-done.3.refs_2_ = bf16[80,2048]{1,0:T(8,128)(2,1)S(1)} collective-permute-done((bf16[80,2048]{1,0:T(8,128)(2,1)S(1)}, bf16[80,2048]{1,0:T(8,128)(2,1)S(1)}, u32[]{:S(2)}, u32[]{:S(2)}) %collective-permute-start.3) | collective-permute-done | bytes 327712 | tf_op jit(solution)/shard_map/ppermute | solution.py:21
  24.2 0.5 %collective-permute-done.4.refs_3_ = bf16[80,2048]{1,0:T(8,128)(2,1)S(1)} collective-permute-done((bf16[80,2048]{1,0:T(8,128)(2,1)S(1)}, bf16[80,2048]{1,0:T(8,128)(2,1)S(1)}, u32[]{:S(2)}, u32[]{:S(2)}) %collective-permute-start.4) | collective-permute-done | bytes 327712 | tf_op jit(solution)/shard_map/ppermute | solution.py:21
  24.7 1.1 %shard_map.96 = (f32[160,2176]{1,0:T(8,128)S(1)}, f32[48,2048]{1,0:T(8,128)S(1)}, bf16[48,2048]{1,0:T(8,128)(2,1)S(1)}) custom-call(bf16[80,2048]{1,0:T(8,128)(2,1)S(1)} %get-tuple-element.35.refs_0_, bf16[80,2048]{1,0:T(8,128)(2,1)S(1)} %get-tuple-element.36.refs_1_, bf16[80,2048]{1,0:T(8,128)(2,1)S(1)} %collective-permute-done.3.refs_2_, ...), custom_call_target="tpu_custom_call" | custom-call | flops 1000000000 | bytes 4472832 | tf_op jit(solution)/shard_map/pallas_call | solution.py:37
  25.8 0.0 collective-permute-done.6.refs_5_.refs_7_
  25.9 0.8 %shard_map.97 = (bf16[160,96]{1,0:T(8,128)(2,1)S(1)}, f32[160,128]{1,0:T(8,128)S(1)}, bf16[96,2048]{1,0:T(8,128)(2,1)S(1)}) custom-call(bf16[80,2048]{1,0:T(8,128)(2,1)S(1)} %get-tuple-element.35.refs_0_, bf16[80,2048]{1,0:T(8,128)(2,1)S(1)} %get-tuple-element.36.refs_1_, bf16[80,2048]{1,0:T(8,128)(2,1)S(1)} %collective-permute-done.3.refs_2_, ...), custom_call_target="tpu_custom_call" | custom-call | bytes 2603008 | tf_op jit(solution)/shard_map/pallas_call | solution.py:37
  26.7 1.6 %collective-permute-start.7 = (bf16[96,2048]{1,0:T(8,128)(2,1)S(1)}, bf16[96,2048]{1,0:T(8,128)(2,1)S(1)}, u32[]{:S(2)}, u32[]{:S(2)}) collective-permute-start(bf16[96,2048]{1,0:T(8,128)(2,1)S(1)} %get-tuple-element.41), channel_id=1, source_target_pairs={{0,1},{1,0},{2,3},{3,2},{16,18},{17,19},{18,16},{19,17},{4,5},{5,4... | collective-permute-start | bytes 1179656 | tf_op jit(solution)/shard_map/ppermute | solution.py:31
  28.3 0.0 collective-permute-done.8.refs_8_
  28.3 1.0 %shard_map.98 = (f32[80,2176]{1,0:T(8,128)S(1)}, bf16[40,2176]{1,0:T(8,128)(2,1)S(1)}, bf16[40,2176]{1,0:T(8,128)(2,1)S(1)}, bf16[48,2048]{1,0:T(8,128)(2,1)S(1)}) custom-call(bf16[80,2048]{1,0:T(8,128)(2,1)S(1)} %get-tuple-element.35.refs_0_, bf16[80,2048]{1,0:T(8,128)(2,1)S(1)} %get-tuple-element.36.refs_1_, ...), custom_call_target="tpu_custom_call" | custom-call | bytes 5236736 | tf_op jit(solution)/shard_map/pallas_call | solution.py:37
  29.3 0.1 collective-permute-start.11
  29.4 0.5 %collective-permute-start.14 = (bf16[40,2176]{1,0:T(8,128)(2,1)S(1)}, bf16[40,2176]{1,0:T(8,128)(2,1)S(1)}, u32[]{:S(2)}, u32[]{:S(2)}) collective-permute-start(bf16[40,2176]{1,0:T(8,128)(2,1)S(1)} %get-tuple-element.50), channel_id=1, source_target_pairs={{0,16},{16,0},{1,17},{17,1},{2,18},{18,2},{3,19},{19,3},{4,20},{20... | collective-permute-start | bytes 522248 | tf_op jit(solution)/shard_map/ppermute | solution.py:21
  29.9 0.9 %collective-permute-start.9 = (bf16[48,2048]{1,0:T(8,128)(2,1)S(1)}, bf16[48,2048]{1,0:T(8,128)(2,1)S(1)}, u32[]{:S(2)}, u32[]{:S(2)}) collective-permute-start(bf16[48,2048]{1,0:T(8,128)(2,1)S(1)} %get-tuple-element.45), channel_id=1, source_target_pairs={{0,3},{1,2},{2,1},{3,0},{16,19},{17,18},{18,17},{19,16},{4,7},{5,6... | collective-permute-start | bytes 589832 | tf_op jit(solution)/shard_map/ppermute | solution.py:31
  30.8 0.0 collective-permute-done.11.got
  30.8 0.0 copy-start
  30.8 0.1 shard_map.100
  30.9 3.0 %collective-permute-start.12 = (bf16[168,256]{1,0:T(8,128)(2,1)S(1)}, bf16[168,256]{1,0:T(8,128)(2,1)S(1)}, u32[]{:S(2)}, u32[]{:S(2)}) collective-permute-start(bf16[168,256]{1,0:T(8,128)(2,1)S(1)} %get-tuple-element.48), channel_id=1, source_target_pairs={{0,12},{4,8},{8,4},{12,0},{1,13},{5,9},{9,5},{13,1},{2,14},{6,10},... | collective-permute-start | bytes 258056 | tf_op jit(solution)/shard_map/ppermute | solution.py:21
  33.9 0.0 collective-permute-start.13
  33.9 0.0 collective-permute-done.14.got
  33.9 0.1 shard_map.101
  34.0 1.5 %collective-permute-start.15 = (bf16[168,256]{1,0:T(8,128)(2,1)S(1)}, bf16[168,256]{1,0:T(8,128)(2,1)S(1)}, u32[]{:S(2)}, u32[]{:S(2)}) collective-permute-start(bf16[168,256]{1,0:T(8,128)(2,1)S(1)} %get-tuple-element.51), channel_id=1, source_target_pairs={{0,4},{4,0},{8,12},{12,8},{1,5},{5,1},{9,13},{13,9},{2,6},{6,2},{1... | collective-permute-start | bytes 258056 | tf_op jit(solution)/shard_map/ppermute | solution.py:21
  35.5 1.0 %collective-permute-done.7.near = bf16[96,2048]{1,0:T(8,128)(2,1)S(1)} collective-permute-done((bf16[96,2048]{1,0:T(8,128)(2,1)S(1)}, bf16[96,2048]{1,0:T(8,128)(2,1)S(1)}, u32[]{:S(2)}, u32[]{:S(2)}) %collective-permute-start.7) | collective-permute-done | bytes 393248 | tf_op jit(solution)/shard_map/ppermute | solution.py:31
  36.5 2.2 %collective-permute-done.9.far = bf16[48,2048]{1,0:T(8,128)(2,1)S(1)} collective-permute-done((bf16[48,2048]{1,0:T(8,128)(2,1)S(1)}, bf16[48,2048]{1,0:T(8,128)(2,1)S(1)}, u32[]{:S(2)}, u32[]{:S(2)}) %collective-permute-start.9) | collective-permute-done | bytes 196640 | tf_op jit(solution)/shard_map/ppermute | solution.py:31
  38.7 0.1 shard_map.99.mine
  38.8 0.1 collective-permute-start.10
  38.8 0.0 collective-permute-done.12.refs_0_
  38.8 2.4 %collective-permute-done.13.refs_1_ = bf16[168,256]{1,0:T(8,128)(2,1)S(1)} collective-permute-done((bf16[168,256]{1,0:T(8,128)(2,1)S(1)}, bf16[168,256]{1,0:T(8,128)(2,1)S(1)}, u32[]{:S(2)}, u32[]{:S(2)}) %collective-permute-start.13) | collective-permute-done | bytes 86048 | tf_op jit(solution)/shard_map/ppermute | solution.py:21
  41.3 0.0 collective-permute-done.15.refs_2_
  41.3 0.0 copy-done
  41.3 0.3 shard_map.102
  41.6 0.0 collective-permute-done.10.theirs
  41.6 1.0 %shard_map.103 = (f32[1,96,2048]{2,1,0:T(8,128)}, bf16[32,2048]{1,0:T(8,128)(2,1)}, bf16[2,32]{1,0:T(2,128)(2,1)}) custom-call(bf16[96,2048]{1,0:T(8,128)(2,1)S(1)} %shard_map.99.mine, bf16[96,2048]{1,0:T(8,128)(2,1)S(1)} %collective-permute-done.10.theirs, bf16[32,2048]{1,0:T(8,128)(2,1)S(1)} %get-tuple-element.54.tokens, ...), custom_call_target="tpu_custom_call" | custom-call | bytes 1835264 | tf_op jit(solution)/shard_map/pallas_call | solution.py:37
Async XLA Ops:
  2.2 10.9 %collective-permute-start.5 = (bf16[144,2048]{1,0:T(8,128)(2,1)S(1)}, bf16[144,2048]{1,0:T(8,128)(2,1)S(1)}, u32[]{:S(2)}, u32[]{:S(2)}) collective-permute-start(bf16[144,2048]{1,0:T(8,128)(2,1)S(1)} %get-tuple-element.37.refs_4_), channel_id=1, source_target_pairs={{0,1},{1,0},{2,3},{3,2},{16,18},{17,19},{18,16},{19,17},{4,5},{5,4... | collective-permute-start | bytes 1769480 | tf_op jit(solution)/shard_map/ppermute | solution.py:31
  5.2 9.9 %collective-permute-start = (bf16[40,2048]{1,0:T(8,128)(2,1)S(1)}, bf16[40,2048]{1,0:T(8,128)(2,1)S(1)}, u32[]{:S(2)}, u32[]{:S(2)}) collective-permute-start(bf16[40,2048]{1,0:T(8,128)(2,1)S(1)} %get-tuple-element.31), channel_id=1, source_target_pairs={{0,12},{4,8},{8,4},{12,0},{1,13},{5,9},{9,5},{13,1},{2,14},{6,10},... | collective-permute-start | bytes 491528 | tf_op jit(solution)/shard_map/ppermute | solution.py:21
  8.8 13.6 %collective-permute-start.1 = (bf16[40,2048]{1,0:T(8,128)(2,1)S(1)}, bf16[40,2048]{1,0:T(8,128)(2,1)S(1)}, u32[]{:S(2)}, u32[]{:S(2)}) collective-permute-start(bf16[40,2048]{1,0:T(8,128)(2,1)S(1)} %get-tuple-element.32), channel_id=1, source_target_pairs={{0,8},{4,12},{8,0},{12,4},{1,9},{5,13},{9,1},{13,5},{2,10},{6,14},... | collective-permute-start | bytes 491528 | tf_op jit(solution)/shard_map/ppermute | solution.py:21
  8.8 13.6 %collective-permute-start.2 = (bf16[40,2048]{1,0:T(8,128)(2,1)S(1)}, bf16[40,2048]{1,0:T(8,128)(2,1)S(1)}, u32[]{:S(2)}, u32[]{:S(2)}) collective-permute-start(bf16[40,2048]{1,0:T(8,128)(2,1)S(1)} %get-tuple-element.33), channel_id=1, source_target_pairs={{0,4},{4,0},{8,12},{12,8},{1,5},{5,1},{9,13},{13,9},{2,6},{6,2},{1... | collective-permute-start | bytes 491528 | tf_op jit(solution)/shard_map/ppermute | solution.py:21
  9.6 16.3 %collective-permute-start.6 = (bf16[144,2048]{1,0:T(8,128)(2,1)S(1)}, bf16[144,2048]{1,0:T(8,128)(2,1)S(1)}, u32[]{:S(2)}, u32[]{:S(2)}) collective-permute-start(bf16[144,2048]{1,0:T(8,128)(2,1)S(1)} %get-tuple-element.40), channel_id=1, source_target_pairs={{0,1},{1,0},{2,3},{3,2},{16,18},{17,19},{18,16},{19,17},{4,5},{5,4... | collective-permute-start | bytes 1769480 | tf_op jit(solution)/shard_map/ppermute | solution.py:31
  13.1 15.2 %collective-permute-start.8 = (bf16[144,2048]{1,0:T(8,128)(2,1)S(1)}, bf16[144,2048]{1,0:T(8,128)(2,1)S(1)}, u32[]{:S(2)}, u32[]{:S(2)}) collective-permute-start(bf16[144,2048]{1,0:T(8,128)(2,1)S(1)} %collective-permute-done.5.refs_5_), channel_id=1, source_target_pairs={{0,2},{1,3},{2,0},{3,1},{16,17},{17,16},{18,19},{19,18},{4,6},{5,7... | collective-permute-start | bytes 1769480 | tf_op jit(solution)/shard_map/ppermute | solution.py:31
  22.5 1.7 %collective-permute-start.3 = (bf16[80,2048]{1,0:T(8,128)(2,1)S(1)}, bf16[80,2048]{1,0:T(8,128)(2,1)S(1)}, u32[]{:S(2)}, u32[]{:S(2)}) collective-permute-start(bf16[80,2048]{1,0:T(8,128)(2,1)S(1)} %get-tuple-element.35.refs_0_), channel_id=1, source_target_pairs={{0,16},{16,0},{1,17},{17,1},{2,18},{18,2},{3,19},{19,3},{4,20},{20... | collective-permute-start | bytes 983048 | tf_op jit(solution)/shard_map/ppermute | solution.py:21
  22.6 2.1 %collective-permute-start.4 = (bf16[80,2048]{1,0:T(8,128)(2,1)S(1)}, bf16[80,2048]{1,0:T(8,128)(2,1)S(1)}, u32[]{:S(2)}, u32[]{:S(2)}) collective-permute-start(bf16[80,2048]{1,0:T(8,128)(2,1)S(1)} %get-tuple-element.36.refs_1_), channel_id=1, source_target_pairs={{0,16},{16,0},{1,17},{17,1},{2,18},{18,2},{3,19},{19,3},{4,20},{20... | collective-permute-start | bytes 983048 | tf_op jit(solution)/shard_map/ppermute | solution.py:21
  26.7 9.8 %collective-permute-start.7 = (bf16[96,2048]{1,0:T(8,128)(2,1)S(1)}, bf16[96,2048]{1,0:T(8,128)(2,1)S(1)}, u32[]{:S(2)}, u32[]{:S(2)}) collective-permute-start(bf16[96,2048]{1,0:T(8,128)(2,1)S(1)} %get-tuple-element.41), channel_id=1, source_target_pairs={{0,1},{1,0},{2,3},{3,2},{16,18},{17,19},{18,16},{19,17},{4,5},{5,4... | collective-permute-start | bytes 1179656 | tf_op jit(solution)/shard_map/ppermute | solution.py:31
  29.3 1.5 %collective-permute-start.11 = (bf16[40,2176]{1,0:T(8,128)(2,1)S(1)}, bf16[40,2176]{1,0:T(8,128)(2,1)S(1)}, u32[]{:S(2)}, u32[]{:S(2)}) collective-permute-start(bf16[40,2176]{1,0:T(8,128)(2,1)S(1)} %get-tuple-element.47), channel_id=1, source_target_pairs={{0,16},{16,0},{1,17},{17,1},{2,18},{18,2},{3,19},{19,3},{4,20},{20... | collective-permute-start | bytes 522248 | tf_op jit(solution)/shard_map/ppermute | solution.py:21
  29.4 4.5 %collective-permute-start.14 = (bf16[40,2176]{1,0:T(8,128)(2,1)S(1)}, bf16[40,2176]{1,0:T(8,128)(2,1)S(1)}, u32[]{:S(2)}, u32[]{:S(2)}) collective-permute-start(bf16[40,2176]{1,0:T(8,128)(2,1)S(1)} %get-tuple-element.50), channel_id=1, source_target_pairs={{0,16},{16,0},{1,17},{17,1},{2,18},{18,2},{3,19},{19,3},{4,20},{20... | collective-permute-start | bytes 522248 | tf_op jit(solution)/shard_map/ppermute | solution.py:21
  29.9 8.8 %collective-permute-start.9 = (bf16[48,2048]{1,0:T(8,128)(2,1)S(1)}, bf16[48,2048]{1,0:T(8,128)(2,1)S(1)}, u32[]{:S(2)}, u32[]{:S(2)}) collective-permute-start(bf16[48,2048]{1,0:T(8,128)(2,1)S(1)} %get-tuple-element.45), channel_id=1, source_target_pairs={{0,3},{1,2},{2,1},{3,0},{16,19},{17,18},{18,17},{19,16},{4,7},{5,6... | collective-permute-start | bytes 589832 | tf_op jit(solution)/shard_map/ppermute | solution.py:31
  30.8 10.5 %copy-start = (bf16[32,2]{0,1:T(2,128)(2,1)S(1)}, bf16[32,2]{0,1:T(2,128)(2,1)}, u32[]{:S(2)}) copy-start(bf16[32,2]{0,1:T(2,128)(2,1)} %param.10) | copy-start | bytes 388
  30.9 8.0 %collective-permute-start.12 = (bf16[168,256]{1,0:T(8,128)(2,1)S(1)}, bf16[168,256]{1,0:T(8,128)(2,1)S(1)}, u32[]{:S(2)}, u32[]{:S(2)}) collective-permute-start(bf16[168,256]{1,0:T(8,128)(2,1)S(1)} %get-tuple-element.48), channel_id=1, source_target_pairs={{0,12},{4,8},{8,4},{12,0},{1,13},{5,9},{9,5},{13,1},{2,14},{6,10},... | collective-permute-start | bytes 258056 | tf_op jit(solution)/shard_map/ppermute | solution.py:21
  33.9 7.4 %collective-permute-start.13 = (bf16[168,256]{1,0:T(8,128)(2,1)S(1)}, bf16[168,256]{1,0:T(8,128)(2,1)S(1)}, u32[]{:S(2)}, u32[]{:S(2)}) collective-permute-start(bf16[168,256]{1,0:T(8,128)(2,1)S(1)} %get-tuple-element.49), channel_id=1, source_target_pairs={{0,8},{4,12},{8,0},{12,4},{1,9},{5,13},{9,1},{13,5},{2,10},{6,14},... | collective-permute-start | bytes 258056 | tf_op jit(solution)/shard_map/ppermute | solution.py:21
  34.0 7.3 %collective-permute-start.15 = (bf16[168,256]{1,0:T(8,128)(2,1)S(1)}, bf16[168,256]{1,0:T(8,128)(2,1)S(1)}, u32[]{:S(2)}, u32[]{:S(2)}) collective-permute-start(bf16[168,256]{1,0:T(8,128)(2,1)S(1)} %get-tuple-element.51), channel_id=1, source_target_pairs={{0,4},{4,0},{8,12},{12,8},{1,5},{5,1},{9,13},{13,9},{2,6},{6,2},{1... | collective-permute-start | bytes 258056 | tf_op jit(solution)/shard_map/ppermute | solution.py:21
  38.8 2.9 %collective-permute-start.10 = (bf16[96,2048]{1,0:T(8,128)(2,1)S(1)}, bf16[96,2048]{1,0:T(8,128)(2,1)S(1)}, u32[]{:S(2)}, u32[]{:S(2)}) collective-permute-start(bf16[96,2048]{1,0:T(8,128)(2,1)S(1)} %shard_map.99.mine), channel_id=1, source_target_pairs={{0,16},{16,0},{1,17},{17,1},{2,18},{18,2},{3,19},{19,3},{4,20},{20... | collective-permute-start | bytes 1179656 | tf_op jit(solution)/shard_map/ppermute | solution.py:21

commit v20 on v19

--- a/solution.py
+++ b/solution.py
@@ -8,7 +8,7 @@
 from jax.sharding import PartitionSpec as P
 
 LANES = 128
-FOLD = 256
+FOLD = 128
 VMEM_BYTES = 32 * 1024 * 1024
 f32, bf16 = jnp.float32, jnp.bfloat16
 

time: 42.7 us -> 42.6 us (level)
  no operation moved by 1% of the time
where the time goes in v20:
time: 42.6 us; the launch traced here: 42.4 us
  starting transfers between devices  17.9 us (42%)
  waiting for transfers between devices  17.6 us (41%)
  Pallas kernels  6.19 us (15%)
  between operations  0.74 us (2%)
    ppermute x11, waiting for transfers between devices, swap(): lax.ppermute(value, axis, [(i, i ^ mask) for i in range(lax.axis_size(axi...  11.2 us
    ppermute x11, starting transfers between devices, swap(): lax.ppermute(value, axis, [(i, i ^ mask) for i in range(lax.axis_size(axi...  10.1 us
    ppermute x5, starting transfers between devices, swap_by_core(): return lax.ppermute(value, ('rep', 'dp'), pairs)  7.83 us
    ppermute x5, waiting for transfers between devices, swap_by_core(): return lax.ppermute(value, ('rep', 'dp'), pairs)  6.35 us
    pallas_call x10, Pallas kernels, kernel_call(): pl.pallas_call(body, out_shape=outputs, in_specs=kwargs.pop('in_specs', [...  6.19 us
  transfers between devices with their start and end apart: 16, of which 7 were waited for; matrix products, arithmetic and copies ran while one was open for 0% of the time, Pallas kernels for 9%

profile of v20, /device:TPU:0, one launch (start us, length us, event | category | flops | bytes accessed | tf_op | source)
XLA Modules:
  0.0 42.4 jit_solution(14165454213800885576)
XLA Ops:
  0.6 1.5 %shard_map.94 = (bf16[40,2048]{1,0:T(8,128)(2,1)S(1)}, bf16[40,2048]{1,0:T(8,128)(2,1)S(1)}, bf16[40,2048]{1,0:T(8,128)(2,1)S(1)}, bf16[40,2048]{1,0:T(8,128)(2,...) custom-call(s32[2,32]{1,0:T(2,128)} %bitcast.5, bf16[2,32]{1,0:T(2,128)(2,1)} %bitcast.3, ...), custom_call_target="tpu_custom_call" | custom-call | bytes 3277440 | tf_op jit(solution)/shard_map/pallas_call | solution.py:37
  2.2 3.0 %collective-permute-start.5 = (bf16[144,2048]{1,0:T(8,128)(2,1)S(1)}, bf16[144,2048]{1,0:T(8,128)(2,1)S(1)}, u32[]{:S(2)}, u32[]{:S(2)}) collective-permute-start(bf16[144,2048]{1,0:T(8,128)(2,1)S(1)} %get-tuple-element.37.refs_4_), channel_id=1, source_target_pairs={{0,1},{1,0},{2,3},{3,2},{16,18},{17,19},{18,16},{19,17},{4,5},{5,4... | collective-permute-start | bytes 1769480 | tf_op jit(solution)/shard_map/ppermute | solution.py:31
  5.2 3.6 %collective-permute-start = (bf16[40,2048]{1,0:T(8,128)(2,1)S(1)}, bf16[40,2048]{1,0:T(8,128)(2,1)S(1)}, u32[]{:S(2)}, u32[]{:S(2)}) collective-permute-start(bf16[40,2048]{1,0:T(8,128)(2,1)S(1)} %get-tuple-element.31), channel_id=1, source_target_pairs={{0,12},{4,8},{8,4},{12,0},{1,13},{5,9},{9,5},{13,1},{2,14},{6,10},... | collective-permute-start | bytes 491528 | tf_op jit(solution)/shard_map/ppermute | solution.py:21
  8.8 0.0 collective-permute-start.1
  8.8 0.8 %collective-permute-start.2 = (bf16[40,2048]{1,0:T(8,128)(2,1)S(1)}, bf16[40,2048]{1,0:T(8,128)(2,1)S(1)}, u32[]{:S(2)}, u32[]{:S(2)}) collective-permute-start(bf16[40,2048]{1,0:T(8,128)(2,1)S(1)} %get-tuple-element.33), channel_id=1, source_target_pairs={{0,4},{4,0},{8,12},{12,8},{1,5},{5,1},{9,13},{13,9},{2,6},{6,2},{1... | collective-permute-start | bytes 491528 | tf_op jit(solution)/shard_map/ppermute | solution.py:21
  9.6 0.3 collective-permute-start.6
  9.9 3.2 %collective-permute-done.5.refs_5_ = bf16[144,2048]{1,0:T(8,128)(2,1)S(1)} collective-permute-done((bf16[144,2048]{1,0:T(8,128)(2,1)S(1)}, bf16[144,2048]{1,0:T(8,128)(2,1)S(1)}, u32[]{:S(2)}, u32[]{:S(2)}) %collective-permute-start.5) | collective-permute-done | bytes 589856 | tf_op jit(solution)/shard_map/ppermute | solution.py:31
  13.1 2.0 %collective-permute-start.8 = (bf16[144,2048]{1,0:T(8,128)(2,1)S(1)}, bf16[144,2048]{1,0:T(8,128)(2,1)S(1)}, u32[]{:S(2)}, u32[]{:S(2)}) collective-permute-start(bf16[144,2048]{1,0:T(8,128)(2,1)S(1)} %collective-permute-done.5.refs_5_), channel_id=1, source_target_pairs={{0,2},{1,3},{2,0},{3,1},{16,17},{17,16},{18,19},{19,18},{4,6},{5,7... | collective-permute-start | bytes 1769480 | tf_op jit(solution)/shard_map/ppermute | solution.py:31
  15.1 0.0 collective-permute-done.refs_0_
  15.1 7.3 %collective-permute-done.1.refs_1_ = bf16[40,2048]{1,0:T(8,128)(2,1)S(1)} collective-permute-done((bf16[40,2048]{1,0:T(8,128)(2,1)S(1)}, bf16[40,2048]{1,0:T(8,128)(2,1)S(1)}, u32[]{:S(2)}, u32[]{:S(2)}) %collective-permute-start.1) | collective-permute-done | bytes 163872 | tf_op jit(solution)/shard_map/ppermute | solution.py:21
  22.4 0.0 collective-permute-done.2.refs_2_
  22.4 0.1 shard_map.95
  22.5 0.1 collective-permute-start.3
  22.6 0.5 %collective-permute-start.4 = (bf16[80,2048]{1,0:T(8,128)(2,1)S(1)}, bf16[80,2048]{1,0:T(8,128)(2,1)S(1)}, u32[]{:S(2)}, u32[]{:S(2)}) collective-permute-start(bf16[80,2048]{1,0:T(8,128)(2,1)S(1)} %get-tuple-element.36.refs_1_), channel_id=1, source_target_pairs={{0,16},{16,0},{1,17},{17,1},{2,18},{18,2},{3,19},{19,3},{4,20},{20... | collective-permute-start | bytes 983048 | tf_op jit(solution)/shard_map/ppermute | solution.py:21
  23.1 1.1 %collective-permute-done.3.refs_2_ = bf16[80,2048]{1,0:T(8,128)(2,1)S(1)} collective-permute-done((bf16[80,2048]{1,0:T(8,128)(2,1)S(1)}, bf16[80,2048]{1,0:T(8,128)(2,1)S(1)}, u32[]{:S(2)}, u32[]{:S(2)}) %collective-permute-start.3) | collective-permute-done | bytes 327712 | tf_op jit(solution)/shard_map/ppermute | solution.py:21
  24.2 0.5 %collective-permute-done.4.refs_3_ = bf16[80,2048]{1,0:T(8,128)(2,1)S(1)} collective-permute-done((bf16[80,2048]{1,0:T(8,128)(2,1)S(1)}, bf16[80,2048]{1,0:T(8,128)(2,1)S(1)}, u32[]{:S(2)}, u32[]{:S(2)}) %collective-permute-start.4) | collective-permute-done | bytes 327712 | tf_op jit(solution)/shard_map/ppermute | solution.py:21
  24.7 1.1 %shard_map.96 = (f32[160,2176]{1,0:T(8,128)S(1)}, f32[48,2048]{1,0:T(8,128)S(1)}, bf16[48,2048]{1,0:T(8,128)(2,1)S(1)}) custom-call(bf16[80,2048]{1,0:T(8,128)(2,1)S(1)} %get-tuple-element.35.refs_0_, bf16[80,2048]{1,0:T(8,128)(2,1)S(1)} %get-tuple-element.36.refs_1_, bf16[80,2048]{1,0:T(8,128)(2,1)S(1)} %collective-permute-done.3.refs_2_, ...), custom_call_target="tpu_custom_call" | custom-call | flops 1000000000 | bytes 4472832 | tf_op jit(solution)/shard_map/pallas_call | solution.py:37
  25.8 0.0 collective-permute-done.6.refs_5_.refs_7_
  25.9 0.8 %shard_map.97 = (bf16[160,96]{1,0:T(8,128)(2,1)S(1)}, f32[160,128]{1,0:T(8,128)S(1)}, bf16[96,2048]{1,0:T(8,128)(2,1)S(1)}) custom-call(bf16[80,2048]{1,0:T(8,128)(2,1)S(1)} %get-tuple-element.35.refs_0_, bf16[80,2048]{1,0:T(8,128)(2,1)S(1)} %get-tuple-element.36.refs_1_, bf16[80,2048]{1,0:T(8,128)(2,1)S(1)} %collective-permute-done.3.refs_2_, ...), custom_call_target="tpu_custom_call" | custom-call | bytes 2603008 | tf_op jit(solution)/shard_map/pallas_call | solution.py:37
  26.7 1.6 %collective-permute-start.7 = (bf16[96,2048]{1,0:T(8,128)(2,1)S(1)}, bf16[96,2048]{1,0:T(8,128)(2,1)S(1)}, u32[]{:S(2)}, u32[]{:S(2)}) collective-permute-start(bf16[96,2048]{1,0:T(8,128)(2,1)S(1)} %get-tuple-element.41), channel_id=1, source_target_pairs={{0,1},{1,0},{2,3},{3,2},{16,18},{17,19},{18,16},{19,17},{4,5},{5,4... | collective-permute-start | bytes 1179656 | tf_op jit(solution)/shard_map/ppermute | solution.py:31
  28.3 0.0 collective-permute-done.8.refs_8_
  28.3 1.0 %shard_map.98 = (f32[80,2176]{1,0:T(8,128)S(1)}, bf16[40,2176]{1,0:T(8,128)(2,1)S(1)}, bf16[40,2176]{1,0:T(8,128)(2,1)S(1)}, bf16[48,2048]{1,0:T(8,128)(2,1)S(1)}) custom-call(bf16[80,2048]{1,0:T(8,128)(2,1)S(1)} %get-tuple-element.35.refs_0_, bf16[80,2048]{1,0:T(8,128)(2,1)S(1)} %get-tuple-element.36.refs_1_, ...), custom_call_target="tpu_custom_call" | custom-call | bytes 5236736 | tf_op jit(solution)/shard_map/pallas_call | solution.py:37
  29.3 0.1 collective-permute-start.11
  29.4 0.5 %collective-permute-start.14 = (bf16[40,2176]{1,0:T(8,128)(2,1)S(1)}, bf16[40,2176]{1,0:T(8,128)(2,1)S(1)}, u32[]{:S(2)}, u32[]{:S(2)}) collective-permute-start(bf16[40,2176]{1,0:T(8,128)(2,1)S(1)} %get-tuple-element.50), channel_id=1, source_target_pairs={{0,16},{16,0},{1,17},{17,1},{2,18},{18,2},{3,19},{19,3},{4,20},{20... | collective-permute-start | bytes 522248 | tf_op jit(solution)/shard_map/ppermute | solution.py:21
  29.9 0.9 %collective-permute-start.9 = (bf16[48,2048]{1,0:T(8,128)(2,1)S(1)}, bf16[48,2048]{1,0:T(8,128)(2,1)S(1)}, u32[]{:S(2)}, u32[]{:S(2)}) collective-permute-start(bf16[48,2048]{1,0:T(8,128)(2,1)S(1)} %get-tuple-element.45), channel_id=1, source_target_pairs={{0,3},{1,2},{2,1},{3,0},{16,19},{17,18},{18,17},{19,16},{4,7},{5,6... | collective-permute-start | bytes 589832 | tf_op jit(solution)/shard_map/ppermute | solution.py:31
  30.8 0.0 collective-permute-done.11.got
  30.8 0.0 copy-start
  30.8 0.1 shard_map.100
  30.9 3.0 %collective-permute-start.12 = (bf16[328,128]{1,0:T(8,128)(2,1)S(1)}, bf16[328,128]{1,0:T(8,128)(2,1)S(1)}, u32[]{:S(2)}, u32[]{:S(2)}) collective-permute-start(bf16[328,128]{1,0:T(8,128)(2,1)S(1)} %get-tuple-element.48), channel_id=1, source_target_pairs={{0,12},{4,8},{8,4},{12,0},{1,13},{5,9},{9,5},{13,1},{2,14},{6,10},... | collective-permute-start | bytes 251912 | tf_op jit(solution)/shard_map/ppermute | solution.py:21
  33.9 0.0 collective-permute-start.13
  33.9 0.0 collective-permute-done.14.got
  33.9 0.1 shard_map.101
  34.0 1.5 %collective-permute-start.15 = (bf16[328,128]{1,0:T(8,128)(2,1)S(1)}, bf16[328,128]{1,0:T(8,128)(2,1)S(1)}, u32[]{:S(2)}, u32[]{:S(2)}) collective-permute-start(bf16[328,128]{1,0:T(8,128)(2,1)S(1)} %get-tuple-element.51), channel_id=1, source_target_pairs={{0,4},{4,0},{8,12},{12,8},{1,5},{5,1},{9,13},{13,9},{2,6},{6,2},{1... | collective-permute-start | bytes 251912 | tf_op jit(solution)/shard_map/ppermute | solution.py:21
  35.5 1.0 %collective-permute-done.7.near = bf16[96,2048]{1,0:T(8,128)(2,1)S(1)} collective-permute-done((bf16[96,2048]{1,0:T(8,128)(2,1)S(1)}, bf16[96,2048]{1,0:T(8,128)(2,1)S(1)}, u32[]{:S(2)}, u32[]{:S(2)}) %collective-permute-start.7) | collective-permute-done | bytes 393248 | tf_op jit(solution)/shard_map/ppermute | solution.py:31
  36.5 2.2 %collective-permute-done.9.far = bf16[48,2048]{1,0:T(8,128)(2,1)S(1)} collective-permute-done((bf16[48,2048]{1,0:T(8,128)(2,1)S(1)}, bf16[48,2048]{1,0:T(8,128)(2,1)S(1)}, u32[]{:S(2)}, u32[]{:S(2)}) %collective-permute-start.9) | collective-permute-done | bytes 196640 | tf_op jit(solution)/shard_map/ppermute | solution.py:31
  38.7 0.1 shard_map.99.mine
  38.8 0.1 collective-permute-start.10
  38.8 0.0 collective-permute-done.12.refs_0_
  38.8 2.3 %collective-permute-done.13.refs_1_ = bf16[328,128]{1,0:T(8,128)(2,1)S(1)} collective-permute-done((bf16[328,128]{1,0:T(8,128)(2,1)S(1)}, bf16[328,128]{1,0:T(8,128)(2,1)S(1)}, u32[]{:S(2)}, u32[]{:S(2)}) %collective-permute-start.13) | collective-permute-done | bytes 84000 | tf_op jit(solution)/shard_map/ppermute | solution.py:21
  41.1 0.0 collective-permute-done.15.refs_2_
  41.1 0.0 copy-done
  41.1 0.3 shard_map.102
  41.5 0.0 collective-permute-done.10.theirs
  41.5 1.0 %shard_map.103 = (f32[1,96,2048]{2,1,0:T(8,128)}, bf16[32,2048]{1,0:T(8,128)(2,1)}, bf16[2,32]{1,0:T(2,128)(2,1)}) custom-call(bf16[96,2048]{1,0:T(8,128)(2,1)S(1)} %shard_map.99.mine, bf16[96,2048]{1,0:T(8,128)(2,1)S(1)} %collective-permute-done.10.theirs, bf16[32,2048]{1,0:T(8,128)(2,1)S(1)} %get-tuple-element.54.tokens, ...), custom_call_target="tpu_custom_call" | custom-call | bytes 1835264 | tf_op jit(solution)/shard_map/pallas_call | solution.py:37
Async XLA Ops:
  2.2 10.9 %collective-permute-start.5 = (bf16[144,2048]{1,0:T(8,128)(2,1)S(1)}, bf16[144,2048]{1,0:T(8,128)(2,1)S(1)}, u32[]{:S(2)}, u32[]{:S(2)}) collective-permute-start(bf16[144,2048]{1,0:T(8,128)(2,1)S(1)} %get-tuple-element.37.refs_4_), channel_id=1, source_target_pairs={{0,1},{1,0},{2,3},{3,2},{16,18},{17,19},{18,16},{19,17},{4,5},{5,4... | collective-permute-start | bytes 1769480 | tf_op jit(solution)/shard_map/ppermute | solution.py:31
  5.2 9.9 %collective-permute-start = (bf16[40,2048]{1,0:T(8,128)(2,1)S(1)}, bf16[40,2048]{1,0:T(8,128)(2,1)S(1)}, u32[]{:S(2)}, u32[]{:S(2)}) collective-permute-start(bf16[40,2048]{1,0:T(8,128)(2,1)S(1)} %get-tuple-element.31), channel_id=1, source_target_pairs={{0,12},{4,8},{8,4},{12,0},{1,13},{5,9},{9,5},{13,1},{2,14},{6,10},... | collective-permute-start | bytes 491528 | tf_op jit(solution)/shard_map/ppermute | solution.py:21
  8.8 13.6 %collective-permute-start.1 = (bf16[40,2048]{1,0:T(8,128)(2,1)S(1)}, bf16[40,2048]{1,0:T(8,128)(2,1)S(1)}, u32[]{:S(2)}, u32[]{:S(2)}) collective-permute-start(bf16[40,2048]{1,0:T(8,128)(2,1)S(1)} %get-tuple-element.32), channel_id=1, source_target_pairs={{0,8},{4,12},{8,0},{12,4},{1,9},{5,13},{9,1},{13,5},{2,10},{6,14},... | collective-permute-start | bytes 491528 | tf_op jit(solution)/shard_map/ppermute | solution.py:21
  8.8 13.6 %collective-permute-start.2 = (bf16[40,2048]{1,0:T(8,128)(2,1)S(1)}, bf16[40,2048]{1,0:T(8,128)(2,1)S(1)}, u32[]{:S(2)}, u32[]{:S(2)}) collective-permute-start(bf16[40,2048]{1,0:T(8,128)(2,1)S(1)} %get-tuple-element.33), channel_id=1, source_target_pairs={{0,4},{4,0},{8,12},{12,8},{1,5},{5,1},{9,13},{13,9},{2,6},{6,2},{1... | collective-permute-start | bytes 491528 | tf_op jit(solution)/shard_map/ppermute | solution.py:21
  9.6 16.3 %collective-permute-start.6 = (bf16[144,2048]{1,0:T(8,128)(2,1)S(1)}, bf16[144,2048]{1,0:T(8,128)(2,1)S(1)}, u32[]{:S(2)}, u32[]{:S(2)}) collective-permute-start(bf16[144,2048]{1,0:T(8,128)(2,1)S(1)} %get-tuple-element.40), channel_id=1, source_target_pairs={{0,1},{1,0},{2,3},{3,2},{16,18},{17,19},{18,16},{19,17},{4,5},{5,4... | collective-permute-start | bytes 1769480 | tf_op jit(solution)/shard_map/ppermute | solution.py:31
  13.1 15.2 %collective-permute-start.8 = (bf16[144,2048]{1,0:T(8,128)(2,1)S(1)}, bf16[144,2048]{1,0:T(8,128)(2,1)S(1)}, u32[]{:S(2)}, u32[]{:S(2)}) collective-permute-start(bf16[144,2048]{1,0:T(8,128)(2,1)S(1)} %collective-permute-done.5.refs_5_), channel_id=1, source_target_pairs={{0,2},{1,3},{2,0},{3,1},{16,17},{17,16},{18,19},{19,18},{4,6},{5,7... | collective-permute-start | bytes 1769480 | tf_op jit(solution)/shard_map/ppermute | solution.py:31
  22.5 1.7 %collective-permute-start.3 = (bf16[80,2048]{1,0:T(8,128)(2,1)S(1)}, bf16[80,2048]{1,0:T(8,128)(2,1)S(1)}, u32[]{:S(2)}, u32[]{:S(2)}) collective-permute-start(bf16[80,2048]{1,0:T(8,128)(2,1)S(1)} %get-tuple-element.35.refs_0_), channel_id=1, source_target_pairs={{0,16},{16,0},{1,17},{17,1},{2,18},{18,2},{3,19},{19,3},{4,20},{20... | collective-permute-start | bytes 983048 | tf_op jit(solution)/shard_map/ppermute | solution.py:21
  22.6 2.1 %collective-permute-start.4 = (bf16[80,2048]{1,0:T(8,128)(2,1)S(1)}, bf16[80,2048]{1,0:T(8,128)(2,1)S(1)}, u32[]{:S(2)}, u32[]{:S(2)}) collective-permute-start(bf16[80,2048]{1,0:T(8,128)(2,1)S(1)} %get-tuple-element.36.refs_1_), channel_id=1, source_target_pairs={{0,16},{16,0},{1,17},{17,1},{2,18},{18,2},{3,19},{19,3},{4,20},{20... | collective-permute-start | bytes 983048 | tf_op jit(solution)/shard_map/ppermute | solution.py:21
  26.7 9.8 %collective-permute-start.7 = (bf16[96,2048]{1,0:T(8,128)(2,1)S(1)}, bf16[96,2048]{1,0:T(8,128)(2,1)S(1)}, u32[]{:S(2)}, u32[]{:S(2)}) collective-permute-start(bf16[96,2048]{1,0:T(8,128)(2,1)S(1)} %get-tuple-element.41), channel_id=1, source_target_pairs={{0,1},{1,0},{2,3},{3,2},{16,18},{17,19},{18,16},{19,17},{4,5},{5,4... | collective-permute-start | bytes 1179656 | tf_op jit(solution)/shard_map/ppermute | solution.py:31
  29.3 1.5 %collective-permute-start.11 = (bf16[40,2176]{1,0:T(8,128)(2,1)S(1)}, bf16[40,2176]{1,0:T(8,128)(2,1)S(1)}, u32[]{:S(2)}, u32[]{:S(2)}) collective-permute-start(bf16[40,2176]{1,0:T(8,128)(2,1)S(1)} %get-tuple-element.47), channel_id=1, source_target_pairs={{0,16},{16,0},{1,17},{17,1},{2,18},{18,2},{3,19},{19,3},{4,20},{20... | collective-permute-start | bytes 522248 | tf_op jit(solution)/shard_map/ppermute | solution.py:21
  29.4 4.5 %collective-permute-start.14 = (bf16[40,2176]{1,0:T(8,128)(2,1)S(1)}, bf16[40,2176]{1,0:T(8,128)(2,1)S(1)}, u32[]{:S(2)}, u32[]{:S(2)}) collective-permute-start(bf16[40,2176]{1,0:T(8,128)(2,1)S(1)} %get-tuple-element.50), channel_id=1, source_target_pairs={{0,16},{16,0},{1,17},{17,1},{2,18},{18,2},{3,19},{19,3},{4,20},{20... | collective-permute-start | bytes 522248 | tf_op jit(solution)/shard_map/ppermute | solution.py:21
  29.9 8.8 %collective-permute-start.9 = (bf16[48,2048]{1,0:T(8,128)(2,1)S(1)}, bf16[48,2048]{1,0:T(8,128)(2,1)S(1)}, u32[]{:S(2)}, u32[]{:S(2)}) collective-permute-start(bf16[48,2048]{1,0:T(8,128)(2,1)S(1)} %get-tuple-element.45), channel_id=1, source_target_pairs={{0,3},{1,2},{2,1},{3,0},{16,19},{17,18},{18,17},{19,16},{4,7},{5,6... | collective-permute-start | bytes 589832 | tf_op jit(solution)/shard_map/ppermute | solution.py:31
  30.8 10.3 %copy-start = (bf16[32,2]{0,1:T(2,128)(2,1)S(1)}, bf16[32,2]{0,1:T(2,128)(2,1)}, u32[]{:S(2)}) copy-start(bf16[32,2]{0,1:T(2,128)(2,1)} %param.10) | copy-start | bytes 388
  30.9 8.0 %collective-permute-start.12 = (bf16[328,128]{1,0:T(8,128)(2,1)S(1)}, bf16[328,128]{1,0:T(8,128)(2,1)S(1)}, u32[]{:S(2)}, u32[]{:S(2)}) collective-permute-start(bf16[328,128]{1,0:T(8,128)(2,1)S(1)} %get-tuple-element.48), channel_id=1, source_target_pairs={{0,12},{4,8},{8,4},{12,0},{1,13},{5,9},{9,5},{13,1},{2,14},{6,10},... | collective-permute-start | bytes 251912 | tf_op jit(solution)/shard_map/ppermute | solution.py:21
  33.9 7.3 %collective-permute-start.13 = (bf16[328,128]{1,0:T(8,128)(2,1)S(1)}, bf16[328,128]{1,0:T(8,128)(2,1)S(1)}, u32[]{:S(2)}, u32[]{:S(2)}) collective-permute-start(bf16[328,128]{1,0:T(8,128)(2,1)S(1)} %get-tuple-element.49), channel_id=1, source_target_pairs={{0,8},{4,12},{8,0},{12,4},{1,9},{5,13},{9,1},{13,5},{2,10},{6,14},... | collective-permute-start | bytes 251912 | tf_op jit(solution)/shard_map/ppermute | solution.py:21
  34.0 7.2 %collective-permute-start.15 = (bf16[328,128]{1,0:T(8,128)(2,1)S(1)}, bf16[328,128]{1,0:T(8,128)(2,1)S(1)}, u32[]{:S(2)}, u32[]{:S(2)}) collective-permute-start(bf16[328,128]{1,0:T(8,128)(2,1)S(1)} %get-tuple-element.51), channel_id=1, source_target_pairs={{0,4},{4,0},{8,12},{12,8},{1,5},{5,1},{9,13},{13,9},{2,6},{6,2},{1... | collective-permute-start | bytes 251912 | tf_op jit(solution)/shard_map/ppermute | solution.py:21
  38.8 2.7 %collective-permute-start.10 = (bf16[96,2048]{1,0:T(8,128)(2,1)S(1)}, bf16[96,2048]{1,0:T(8,128)(2,1)S(1)}, u32[]{:S(2)}, u32[]{:S(2)}) collective-permute-start(bf16[96,2048]{1,0:T(8,128)(2,1)S(1)} %shard_map.99.mine), channel_id=1, source_target_pairs={{0,16},{16,0},{1,17},{17,1},{2,18},{18,2},{3,19},{19,3},{4,20},{20... | collective-permute-start | bytes 1179656 | tf_op jit(solution)/shard_map/ppermute | solution.py:21

commit v21 on v20

--- a/solution.py
+++ b/solution.py
@@ -49,21 +49,31 @@
     return lax.broadcasted_iota(jnp.int32, shape, dim)
 
 
+def pack_copies(weights, packed, half, sems, start):
+    hidden = packed.shape[0] // 3
+    rows = pl.ds(pl.multiple_of(half * hidden, hidden), hidden)
+    return [
+        pltpu.make_async_copy(weight.at[0, rows], packed.at[pl.ds(i * hidden, hidden)], sems.at[start + i])
+        for i, weight in enumerate(weights)
+    ]
+
+
+def pack_kernel(gate, up, down, packed, sems):
+    copies = pack_copies((gate, up, down), packed, 1 - lax.axis_index("rep"), sems, 0)
+    for copy in copies:
+        copy.start()
+    for copy in copies:
+        copy.wait()
+
+
 def dispatch_kernel(experts, cap, chunk_count, *refs):
     given, weights, refs = refs[:4], refs[4:7], refs[7:]
-    chunks, (slot_out, *packed), (ids, route_weight, both, sems) = refs[:chunk_count], refs[chunk_count:-4], refs[-4:]
-    hidden = packed[0].shape[0] // 3
+    chunks, (slot_out, packed), (ids, route_weight, both, sems) = refs[:chunk_count], refs[chunk_count:-4], refs[-4:]
     rep = lax.axis_index("rep")
     top, tok_dev = ids.shape
     held = (ids, route_weight, both.at[pl.ds(0, tok_dev)], both.at[pl.ds(tok_dev, tok_dev)])
     loads = [pltpu.make_async_copy(*pair, sems.at[i]) for i, pair in enumerate(zip(given, held))]
-    packs = []
-    for j, half in enumerate((rep, 1 - rep)):
-        rows = pl.ds(pl.multiple_of(half * hidden, hidden), hidden)
-        packs += [
-            pltpu.make_async_copy(weight.at[0, rows], packed[j].at[pl.ds(i * hidden, hidden)], sems.at[4 + 3 * j + i])
-            for i, weight in enumerate(weights)
-        ]
+    packs = pack_copies(weights, packed, rep, sems, 4)
     for copy in loads + packs:
         copy.start()
     for copy in loads[:2]:
@@ -241,18 +251,27 @@
     in_hbm = pl.BlockSpec(memory_space=pltpu.HBM)
 
     given = [expert_ids.T, route_weight.T, tokens, upstream]
-    *chunks, slot, first, second = kernel_call(
+    *chunks, slot, first = kernel_call(
         functools.partial(dispatch_kernel, experts, cap, chunk_count),
         [pltpu.with_memory_space_constraint(a, pltpu.HBM) for a in [*given, gate_weight, up_weight, down_weight]],
         [shape((2 * rows, width), bf16)] * chunk_count
         + [shape((top, tok_dev), jnp.int32)]
-        + [shape((3 * hidden, width), bf16)] * 2,
+        + [shape((3 * hidden, width), bf16)],
         in_specs=[in_hbm] * 7,
         scratch_shapes=[
             *(pltpu.VMEM(a.shape, a.dtype) for a in given[:2]),
             pltpu.VMEM((2 * tok_dev, width), bf16),
-            pltpu.SemaphoreType.DMA((10,)),
+            pltpu.SemaphoreType.DMA((7,)),
         ],
+    )
+
+    weights, _ = lax.optimization_barrier(((gate_weight, up_weight, down_weight), slot))
+    (second,) = kernel_call(
+        pack_kernel,
+        [pltpu.with_memory_space_constraint(a, pltpu.HBM) for a in weights],
+        [shape((3 * hidden, width), bf16)],
+        in_specs=[in_hbm] * 3,
+        scratch_shapes=[pltpu.SemaphoreType.DMA((3,))],
     )
 
     along, across = (1, 2), (2, 1)

time: 42.6 us -> 43.3 us (1.016)
  Pallas kernels: 6.19 us -> 7.17 us
  waiting for transfers between devices: 17.6 us -> 16.9 us
  starting transfers between devices: 17.9 us -> 18.4 us
    pallas_call x10 -> x11, Pallas kernels: 6.19 us -> 7.17 us  [kernel_call(): pl.pallas_call(body, out_shape=outputs, in_specs=kwargs.pop('in_specs', [...]
    ppermute x11, waiting for transfers between devices: 11.2 us -> 10.7 us  [swap(): lax.ppermute(value, axis, [(i, i ^ mask) for i in range(lax.axis_size(axi...]
  transfers between devices with their start and end apart: 16 -> 16, of which waited for: 7 -> 8; matrix products, arithmetic and copies ran while one was open for 0% -> 0% of each run, Pallas kernels for 9% -> 11%
where the time goes in v21:
time: 43.3 us; the launch traced here: 43.2 us
  starting transfers between devices  18.4 us (42%)
  waiting for transfers between devices  16.9 us (39%)
  Pallas kernels  7.17 us (17%)
  between operations  0.74 us (2%)
    ppermute x11, waiting for transfers between devices, swap(): lax.ppermute(value, axis, [(i, i ^ mask) for i in range(lax.axis_size(axi...  10.7 us
    ppermute x11, starting transfers between devices, swap(): lax.ppermute(value, axis, [(i, i ^ mask) for i in range(lax.axis_size(axi...  10.1 us
    ppermute x5, starting transfers between devices, swap_by_core(): return lax.ppermute(value, ('rep', 'dp'), pairs)  8.25 us
    pallas_call x11, Pallas kernels, kernel_call(): pl.pallas_call(body, out_shape=outputs, in_specs=kwargs.pop('in_specs', [...  7.17 us
    ppermute x5, waiting for transfers between devices, swap_by_core(): return lax.ppermute(value, ('rep', 'dp'), pairs)  6.17 us
  transfers between devices with their start and end apart: 16, of which 8 were waited for; matrix products, arithmetic and copies ran while one was open for 0% of the time, Pallas kernels for 11%

profile of v21, /device:TPU:0, one launch (start us, length us, event | category | flops | bytes accessed | tf_op | source)
XLA Modules:
  0.0 43.2 jit_solution(15747083153484110168)
XLA Ops:
  0.6 1.4 %shard_map.94 = (bf16[40,2048]{1,0:T(8,128)(2,1)S(1)}, bf16[40,2048]{1,0:T(8,128)(2,1)S(1)}, bf16[40,2048]{1,0:T(8,128)(2,1)S(1)}, bf16[40,2048]{1,0:T(8,128)(2,...) custom-call(s32[2,32]{1,0:T(2,128)} %bitcast.5, bf16[2,32]{1,0:T(2,128)(2,1)} %bitcast.3, ...), custom_call_target="tpu_custom_call" | custom-call | bytes 2687616 | tf_op jit(solution)/shard_map/pallas_call | solution.py:37
  2.0 3.0 %collective-permute-start.5 = (bf16[144,2048]{1,0:T(8,128)(2,1)S(1)}, bf16[144,2048]{1,0:T(8,128)(2,1)S(1)}, u32[]{:S(2)}, u32[]{:S(2)}) collective-permute-start(bf16[144,2048]{1,0:T(8,128)(2,1)S(1)} %get-tuple-element.39.refs_4_), channel_id=1, source_target_pairs={{0,1},{1,0},{2,3},{3,2},{16,18},{17,19},{18,16},{19,17},{4,5},{5,4... | collective-permute-start | bytes 1769480 | tf_op jit(solution)/shard_map/ppermute | solution.py:31
  5.0 3.6 %collective-permute-start = (bf16[40,2048]{1,0:T(8,128)(2,1)S(1)}, bf16[40,2048]{1,0:T(8,128)(2,1)S(1)}, u32[]{:S(2)}, u32[]{:S(2)}) collective-permute-start(bf16[40,2048]{1,0:T(8,128)(2,1)S(1)} %get-tuple-element.33), channel_id=1, source_target_pairs={{0,12},{4,8},{8,4},{12,0},{1,13},{5,9},{9,5},{13,1},{2,14},{6,10},... | collective-permute-start | bytes 491528 | tf_op jit(solution)/shard_map/ppermute | solution.py:21
  8.6 0.0 collective-permute-start.1
  8.6 0.8 %collective-permute-start.2 = (bf16[40,2048]{1,0:T(8,128)(2,1)S(1)}, bf16[40,2048]{1,0:T(8,128)(2,1)S(1)}, u32[]{:S(2)}, u32[]{:S(2)}) collective-permute-start(bf16[40,2048]{1,0:T(8,128)(2,1)S(1)} %get-tuple-element.35), channel_id=1, source_target_pairs={{0,4},{4,0},{8,12},{12,8},{1,5},{5,1},{9,13},{13,9},{2,6},{6,2},{1... | collective-permute-start | bytes 491528 | tf_op jit(solution)/shard_map/ppermute | solution.py:21
  9.4 1.1 %shard_map.97 = bf16[144,2048]{1,0:T(8,128)(2,1)S(1)} custom-call(bf16[1,96,2048]{2,1,0:T(8,128)(2,1)} %gate, bf16[1,96,2048]{2,1,0:T(8,128)(2,1)} %up, bf16[1,96,2048]{2,1,0:T(8,128)(2,1)} %down), custom_call_target="tpu_custom_call" | custom-call | bytes 1769472 | tf_op jit(solution)/shard_map/pallas_call | solution.py:37
  10.6 0.4 collective-permute-start.6
  10.9 1.9 %collective-permute-done.5.refs_5_ = bf16[144,2048]{1,0:T(8,128)(2,1)S(1)} collective-permute-done((bf16[144,2048]{1,0:T(8,128)(2,1)S(1)}, bf16[144,2048]{1,0:T(8,128)(2,1)S(1)}, u32[]{:S(2)}, u32[]{:S(2)}) %collective-permute-start.5) | collective-permute-done | bytes 589856 | tf_op jit(solution)/shard_map/ppermute | solution.py:31
  12.9 2.0 %collective-permute-start.8 = (bf16[144,2048]{1,0:T(8,128)(2,1)S(1)}, bf16[144,2048]{1,0:T(8,128)(2,1)S(1)}, u32[]{:S(2)}, u32[]{:S(2)}) collective-permute-start(bf16[144,2048]{1,0:T(8,128)(2,1)S(1)} %collective-permute-done.5.refs_5_), channel_id=1, source_target_pairs={{0,2},{1,3},{2,0},{3,1},{16,17},{17,16},{18,19},{19,18},{4,6},{5,7... | collective-permute-start | bytes 1769480 | tf_op jit(solution)/shard_map/ppermute | solution.py:31
  14.9 0.0 collective-permute-done.refs_0_
  14.9 7.3 %collective-permute-done.1.refs_1_ = bf16[40,2048]{1,0:T(8,128)(2,1)S(1)} collective-permute-done((bf16[40,2048]{1,0:T(8,128)(2,1)S(1)}, bf16[40,2048]{1,0:T(8,128)(2,1)S(1)}, u32[]{:S(2)}, u32[]{:S(2)}) %collective-permute-start.1) | collective-permute-done | bytes 163872 | tf_op jit(solution)/shard_map/ppermute | solution.py:21
  22.3 0.0 collective-permute-done.2.refs_2_
  22.3 0.1 shard_map.95
  22.4 0.1 collective-permute-start.3
  22.4 0.5 %collective-permute-start.4 = (bf16[80,2048]{1,0:T(8,128)(2,1)S(1)}, bf16[80,2048]{1,0:T(8,128)(2,1)S(1)}, u32[]{:S(2)}, u32[]{:S(2)}) collective-permute-start(bf16[80,2048]{1,0:T(8,128)(2,1)S(1)} %get-tuple-element.38.refs_1_), channel_id=1, source_target_pairs={{0,16},{16,0},{1,17},{17,1},{2,18},{18,2},{3,19},{19,3},{4,20},{20... | collective-permute-start | bytes 983048 | tf_op jit(solution)/shard_map/ppermute | solution.py:21
  22.9 1.1 %collective-permute-done.3.refs_2_ = bf16[80,2048]{1,0:T(8,128)(2,1)S(1)} collective-permute-done((bf16[80,2048]{1,0:T(8,128)(2,1)S(1)}, bf16[80,2048]{1,0:T(8,128)(2,1)S(1)}, u32[]{:S(2)}, u32[]{:S(2)}) %collective-permute-start.3) | collective-permute-done | bytes 327712 | tf_op jit(solution)/shard_map/ppermute | solution.py:21
  24.1 0.5 %collective-permute-done.4.refs_3_ = bf16[80,2048]{1,0:T(8,128)(2,1)S(1)} collective-permute-done((bf16[80,2048]{1,0:T(8,128)(2,1)S(1)}, bf16[80,2048]{1,0:T(8,128)(2,1)S(1)}, u32[]{:S(2)}, u32[]{:S(2)}) %collective-permute-start.4) | collective-permute-done | bytes 327712 | tf_op jit(solution)/shard_map/ppermute | solution.py:21
  24.5 1.2 %shard_map.96 = (f32[160,2176]{1,0:T(8,128)S(1)}, f32[48,2048]{1,0:T(8,128)S(1)}, bf16[48,2048]{1,0:T(8,128)(2,1)S(1)}) custom-call(bf16[80,2048]{1,0:T(8,128)(2,1)S(1)} %get-tuple-element.37.refs_0_, bf16[80,2048]{1,0:T(8,128)(2,1)S(1)} %get-tuple-element.38.refs_1_, bf16[80,2048]{1,0:T(8,128)(2,1)S(1)} %collective-permute-done.3.refs_2_, ...), custom_call_target="tpu_custom_call" | custom-call | flops 1000000000 | bytes 4472832 | tf_op jit(solution)/shard_map/pallas_call | solution.py:37
  25.7 0.6 %collective-permute-done.6.refs_5_.refs_7_ = bf16[144,2048]{1,0:T(8,128)(2,1)S(1)} collective-permute-done((bf16[144,2048]{1,0:T(8,128)(2,1)S(1)}, bf16[144,2048]{1,0:T(8,128)(2,1)S(1)}, u32[]{:S(2)}, u32[]{:S(2)}) %collective-permute-start.6) | collective-permute-done | bytes 589856 | tf_op jit(solution)/shard_map/ppermute | solution.py:31
  26.3 0.8 %shard_map.98 = (bf16[160,96]{1,0:T(8,128)(2,1)S(1)}, f32[160,128]{1,0:T(8,128)S(1)}, bf16[96,2048]{1,0:T(8,128)(2,1)S(1)}) custom-call(bf16[80,2048]{1,0:T(8,128)(2,1)S(1)} %get-tuple-element.37.refs_0_, bf16[80,2048]{1,0:T(8,128)(2,1)S(1)} %get-tuple-element.38.refs_1_, bf16[80,2048]{1,0:T(8,128)(2,1)S(1)} %collective-permute-done.3.refs_2_, ...), custom_call_target="tpu_custom_call" | custom-call | bytes 2603008 | tf_op jit(solution)/shard_map/pallas_call | solution.py:37
  27.1 0.9 %collective-permute-start.7 = (bf16[96,2048]{1,0:T(8,128)(2,1)S(1)}, bf16[96,2048]{1,0:T(8,128)(2,1)S(1)}, u32[]{:S(2)}, u32[]{:S(2)}) collective-permute-start(bf16[96,2048]{1,0:T(8,128)(2,1)S(1)} %get-tuple-element.46), channel_id=1, source_target_pairs={{0,1},{1,0},{2,3},{3,2},{16,18},{17,19},{18,16},{19,17},{4,5},{5,4... | collective-permute-start | bytes 1179656 | tf_op jit(solution)/shard_map/ppermute | solution.py:31
  28.1 0.0 collective-permute-done.8.refs_8_
  28.1 1.1 %shard_map.99 = (f32[80,2176]{1,0:T(8,128)S(1)}, bf16[40,2176]{1,0:T(8,128)(2,1)S(1)}, bf16[40,2176]{1,0:T(8,128)(2,1)S(1)}, bf16[48,2048]{1,0:T(8,128)(2,1)S(1)}) custom-call(bf16[80,2048]{1,0:T(8,128)(2,1)S(1)} %get-tuple-element.37.refs_0_, bf16[80,2048]{1,0:T(8,128)(2,1)S(1)} %get-tuple-element.38.refs_1_, ...), custom_call_target="tpu_custom_call" | custom-call | bytes 5236736 | tf_op jit(solution)/shard_map/pallas_call | solution.py:37
  29.1 0.1 collective-permute-start.11
  29.2 0.5 %collective-permute-start.14 = (bf16[40,2176]{1,0:T(8,128)(2,1)S(1)}, bf16[40,2176]{1,0:T(8,128)(2,1)S(1)}, u32[]{:S(2)}, u32[]{:S(2)}) collective-permute-start(bf16[40,2176]{1,0:T(8,128)(2,1)S(1)} %get-tuple-element.55), channel_id=1, source_target_pairs={{0,16},{16,0},{1,17},{17,1},{2,18},{18,2},{3,19},{19,3},{4,20},{20... | collective-permute-start | bytes 522248 | tf_op jit(solution)/shard_map/ppermute | solution.py:21
  29.7 1.9 %collective-permute-start.9 = (bf16[48,2048]{1,0:T(8,128)(2,1)S(1)}, bf16[48,2048]{1,0:T(8,128)(2,1)S(1)}, u32[]{:S(2)}, u32[]{:S(2)}) collective-permute-start(bf16[48,2048]{1,0:T(8,128)(2,1)S(1)} %get-tuple-element.50), channel_id=1, source_target_pairs={{0,3},{1,2},{2,1},{3,0},{16,19},{17,18},{18,17},{19,16},{4,7},{5,6... | collective-permute-start | bytes 589832 | tf_op jit(solution)/shard_map/ppermute | solution.py:31
  31.6 0.0 collective-permute-done.11.got
  31.6 0.0 copy-start
  31.6 0.1 shard_map.101
  31.7 3.6 %collective-permute-start.12 = (bf16[328,128]{1,0:T(8,128)(2,1)S(1)}, bf16[328,128]{1,0:T(8,128)(2,1)S(1)}, u32[]{:S(2)}, u32[]{:S(2)}) collective-permute-start(bf16[328,128]{1,0:T(8,128)(2,1)S(1)} %get-tuple-element.53), channel_id=1, source_target_pairs={{0,12},{4,8},{8,4},{12,0},{1,13},{5,9},{9,5},{13,1},{2,14},{6,10},... | collective-permute-start | bytes 251912 | tf_op jit(solution)/shard_map/ppermute | solution.py:21
  35.3 0.0 collective-permute-start.13
  35.3 0.0 collective-permute-done.14.got
  35.3 0.1 shard_map.102
  35.4 0.9 %collective-permute-start.15 = (bf16[328,128]{1,0:T(8,128)(2,1)S(1)}, bf16[328,128]{1,0:T(8,128)(2,1)S(1)}, u32[]{:S(2)}, u32[]{:S(2)}) collective-permute-start(bf16[328,128]{1,0:T(8,128)(2,1)S(1)} %get-tuple-element.56), channel_id=1, source_target_pairs={{0,4},{4,0},{8,12},{12,8},{1,5},{5,1},{9,13},{13,9},{2,6},{6,2},{1... | collective-permute-start | bytes 251912 | tf_op jit(solution)/shard_map/ppermute | solution.py:21
  36.3 0.8 %collective-permute-done.7.near = bf16[96,2048]{1,0:T(8,128)(2,1)S(1)} collective-permute-done((bf16[96,2048]{1,0:T(8,128)(2,1)S(1)}, bf16[96,2048]{1,0:T(8,128)(2,1)S(1)}, u32[]{:S(2)}, u32[]{:S(2)}) %collective-permute-start.7) | collective-permute-done | bytes 393248 | tf_op jit(solution)/shard_map/ppermute | solution.py:31
  37.1 2.8 %collective-permute-done.9.far = bf16[48,2048]{1,0:T(8,128)(2,1)S(1)} collective-permute-done((bf16[48,2048]{1,0:T(8,128)(2,1)S(1)}, bf16[48,2048]{1,0:T(8,128)(2,1)S(1)}, u32[]{:S(2)}, u32[]{:S(2)}) %collective-permute-start.9) | collective-permute-done | bytes 196640 | tf_op jit(solution)/shard_map/ppermute | solution.py:31
  39.9 0.1 shard_map.100.mine
  40.0 0.1 collective-permute-start.10
  40.0 0.0 collective-permute-done.12.refs_0_
  40.1 1.8 %collective-permute-done.13.refs_1_ = bf16[328,128]{1,0:T(8,128)(2,1)S(1)} collective-permute-done((bf16[328,128]{1,0:T(8,128)(2,1)S(1)}, bf16[328,128]{1,0:T(8,128)(2,1)S(1)}, u32[]{:S(2)}, u32[]{:S(2)}) %collective-permute-start.13) | collective-permute-done | bytes 84000 | tf_op jit(solution)/shard_map/ppermute | solution.py:21
  41.9 0.0 collective-permute-done.15.refs_2_
  41.9 0.0 copy-done
  41.9 0.3 shard_map.103
  42.2 0.0 collective-permute-done.10.theirs
  42.2 1.0 %shard_map.104 = (f32[1,96,2048]{2,1,0:T(8,128)}, bf16[32,2048]{1,0:T(8,128)(2,1)}, bf16[2,32]{1,0:T(2,128)(2,1)}) custom-call(bf16[96,2048]{1,0:T(8,128)(2,1)S(1)} %shard_map.100.mine, bf16[96,2048]{1,0:T(8,128)(2,1)S(1)} %collective-permute-done.10.theirs, bf16[32,2048]{1,0:T(8,128)(2,1)S(1)} %get-tuple-element.58.tokens, ...), custom_call_target="tpu_custom_call" | custom-call | bytes 1835264 | tf_op jit(solution)/shard_map/pallas_call | solution.py:37
Async XLA Ops:
  2.0 10.9 %collective-permute-start.5 = (bf16[144,2048]{1,0:T(8,128)(2,1)S(1)}, bf16[144,2048]{1,0:T(8,128)(2,1)S(1)}, u32[]{:S(2)}, u32[]{:S(2)}) collective-permute-start(bf16[144,2048]{1,0:T(8,128)(2,1)S(1)} %get-tuple-element.39.refs_4_), channel_id=1, source_target_pairs={{0,1},{1,0},{2,3},{3,2},{16,18},{17,19},{18,16},{19,17},{4,5},{5,4... | collective-permute-start | bytes 1769480 | tf_op jit(solution)/shard_map/ppermute | solution.py:31
  5.0 9.9 %collective-permute-start = (bf16[40,2048]{1,0:T(8,128)(2,1)S(1)}, bf16[40,2048]{1,0:T(8,128)(2,1)S(1)}, u32[]{:S(2)}, u32[]{:S(2)}) collective-permute-start(bf16[40,2048]{1,0:T(8,128)(2,1)S(1)} %get-tuple-element.33), channel_id=1, source_target_pairs={{0,12},{4,8},{8,4},{12,0},{1,13},{5,9},{9,5},{13,1},{2,14},{6,10},... | collective-permute-start | bytes 491528 | tf_op jit(solution)/shard_map/ppermute | solution.py:21
  8.6 13.6 %collective-permute-start.1 = (bf16[40,2048]{1,0:T(8,128)(2,1)S(1)}, bf16[40,2048]{1,0:T(8,128)(2,1)S(1)}, u32[]{:S(2)}, u32[]{:S(2)}) collective-permute-start(bf16[40,2048]{1,0:T(8,128)(2,1)S(1)} %get-tuple-element.34), channel_id=1, source_target_pairs={{0,8},{4,12},{8,0},{12,4},{1,9},{5,13},{9,1},{13,5},{2,10},{6,14},... | collective-permute-start | bytes 491528 | tf_op jit(solution)/shard_map/ppermute | solution.py:21
  8.6 13.6 %collective-permute-start.2 = (bf16[40,2048]{1,0:T(8,128)(2,1)S(1)}, bf16[40,2048]{1,0:T(8,128)(2,1)S(1)}, u32[]{:S(2)}, u32[]{:S(2)}) collective-permute-start(bf16[40,2048]{1,0:T(8,128)(2,1)S(1)} %get-tuple-element.35), channel_id=1, source_target_pairs={{0,4},{4,0},{8,12},{12,8},{1,5},{5,1},{9,13},{13,9},{2,6},{6,2},{1... | collective-permute-start | bytes 491528 | tf_op jit(solution)/shard_map/ppermute | solution.py:21
  10.6 15.7 %collective-permute-start.6 = (bf16[144,2048]{1,0:T(8,128)(2,1)S(1)}, bf16[144,2048]{1,0:T(8,128)(2,1)S(1)}, u32[]{:S(2)}, u32[]{:S(2)}) collective-permute-start(bf16[144,2048]{1,0:T(8,128)(2,1)S(1)} %shard_map.97), channel_id=1, source_target_pairs={{0,1},{1,0},{2,3},{3,2},{16,18},{17,19},{18,16},{19,17},{4,5},{5,4... | collective-permute-start | bytes 1769480 | tf_op jit(solution)/shard_map/ppermute | solution.py:31
  12.9 15.2 %collective-permute-start.8 = (bf16[144,2048]{1,0:T(8,128)(2,1)S(1)}, bf16[144,2048]{1,0:T(8,128)(2,1)S(1)}, u32[]{:S(2)}, u32[]{:S(2)}) collective-permute-start(bf16[144,2048]{1,0:T(8,128)(2,1)S(1)} %collective-permute-done.5.refs_5_), channel_id=1, source_target_pairs={{0,2},{1,3},{2,0},{3,1},{16,17},{17,16},{18,19},{19,18},{4,6},{5,7... | collective-permute-start | bytes 1769480 | tf_op jit(solution)/shard_map/ppermute | solution.py:31
  22.4 1.7 %collective-permute-start.3 = (bf16[80,2048]{1,0:T(8,128)(2,1)S(1)}, bf16[80,2048]{1,0:T(8,128)(2,1)S(1)}, u32[]{:S(2)}, u32[]{:S(2)}) collective-permute-start(bf16[80,2048]{1,0:T(8,128)(2,1)S(1)} %get-tuple-element.37.refs_0_), channel_id=1, source_target_pairs={{0,16},{16,0},{1,17},{17,1},{2,18},{18,2},{3,19},{19,3},{4,20},{20... | collective-permute-start | bytes 983048 | tf_op jit(solution)/shard_map/ppermute | solution.py:21
  22.4 2.1 %collective-permute-start.4 = (bf16[80,2048]{1,0:T(8,128)(2,1)S(1)}, bf16[80,2048]{1,0:T(8,128)(2,1)S(1)}, u32[]{:S(2)}, u32[]{:S(2)}) collective-permute-start(bf16[80,2048]{1,0:T(8,128)(2,1)S(1)} %get-tuple-element.38.refs_1_), channel_id=1, source_target_pairs={{0,16},{16,0},{1,17},{17,1},{2,18},{18,2},{3,19},{19,3},{4,20},{20... | collective-permute-start | bytes 983048 | tf_op jit(solution)/shard_map/ppermute | solution.py:21
  27.1 9.9 %collective-permute-start.7 = (bf16[96,2048]{1,0:T(8,128)(2,1)S(1)}, bf16[96,2048]{1,0:T(8,128)(2,1)S(1)}, u32[]{:S(2)}, u32[]{:S(2)}) collective-permute-start(bf16[96,2048]{1,0:T(8,128)(2,1)S(1)} %get-tuple-element.46), channel_id=1, source_target_pairs={{0,1},{1,0},{2,3},{3,2},{16,18},{17,19},{18,16},{19,17},{4,5},{5,4... | collective-permute-start | bytes 1179656 | tf_op jit(solution)/shard_map/ppermute | solution.py:31
  29.1 2.4 %collective-permute-start.11 = (bf16[40,2176]{1,0:T(8,128)(2,1)S(1)}, bf16[40,2176]{1,0:T(8,128)(2,1)S(1)}, u32[]{:S(2)}, u32[]{:S(2)}) collective-permute-start(bf16[40,2176]{1,0:T(8,128)(2,1)S(1)} %get-tuple-element.52), channel_id=1, source_target_pairs={{0,16},{16,0},{1,17},{17,1},{2,18},{18,2},{3,19},{19,3},{4,20},{20... | collective-permute-start | bytes 522248 | tf_op jit(solution)/shard_map/ppermute | solution.py:21
  29.2 6.1 %collective-permute-start.14 = (bf16[40,2176]{1,0:T(8,128)(2,1)S(1)}, bf16[40,2176]{1,0:T(8,128)(2,1)S(1)}, u32[]{:S(2)}, u32[]{:S(2)}) collective-permute-start(bf16[40,2176]{1,0:T(8,128)(2,1)S(1)} %get-tuple-element.55), channel_id=1, source_target_pairs={{0,16},{16,0},{1,17},{17,1},{2,18},{18,2},{3,19},{19,3},{4,20},{20... | collective-permute-start | bytes 522248 | tf_op jit(solution)/shard_map/ppermute | solution.py:21
  29.7 10.2 %collective-permute-start.9 = (bf16[48,2048]{1,0:T(8,128)(2,1)S(1)}, bf16[48,2048]{1,0:T(8,128)(2,1)S(1)}, u32[]{:S(2)}, u32[]{:S(2)}) collective-permute-start(bf16[48,2048]{1,0:T(8,128)(2,1)S(1)} %get-tuple-element.50), channel_id=1, source_target_pairs={{0,3},{1,2},{2,1},{3,0},{16,19},{17,18},{18,17},{19,16},{4,7},{5,6... | collective-permute-start | bytes 589832 | tf_op jit(solution)/shard_map/ppermute | solution.py:31
  31.6 10.3 %copy-start = (bf16[32,2]{0,1:T(2,128)(2,1)S(1)}, bf16[32,2]{0,1:T(2,128)(2,1)}, u32[]{:S(2)}) copy-start(bf16[32,2]{0,1:T(2,128)(2,1)} %param.10) | copy-start | bytes 388
  31.7 8.4 %collective-permute-start.12 = (bf16[328,128]{1,0:T(8,128)(2,1)S(1)}, bf16[328,128]{1,0:T(8,128)(2,1)S(1)}, u32[]{:S(2)}, u32[]{:S(2)}) collective-permute-start(bf16[328,128]{1,0:T(8,128)(2,1)S(1)} %get-tuple-element.53), channel_id=1, source_target_pairs={{0,12},{4,8},{8,4},{12,0},{1,13},{5,9},{9,5},{13,1},{2,14},{6,10},... | collective-permute-start | bytes 251912 | tf_op jit(solution)/shard_map/ppermute | solution.py:21
  35.3 6.6 %collective-permute-start.13 = (bf16[328,128]{1,0:T(8,128)(2,1)S(1)}, bf16[328,128]{1,0:T(8,128)(2,1)S(1)}, u32[]{:S(2)}, u32[]{:S(2)}) collective-permute-start(bf16[328,128]{1,0:T(8,128)(2,1)S(1)} %get-tuple-element.54), channel_id=1, source_target_pairs={{0,8},{4,12},{8,0},{12,4},{1,9},{5,13},{9,1},{13,5},{2,10},{6,14},... | collective-permute-start | bytes 251912 | tf_op jit(solution)/shard_map/ppermute | solution.py:21
  35.4 6.5 %collective-permute-start.15 = (bf16[328,128]{1,0:T(8,128)(2,1)S(1)}, bf16[328,128]{1,0:T(8,128)(2,1)S(1)}, u32[]{:S(2)}, u32[]{:S(2)}) collective-permute-start(bf16[328,128]{1,0:T(8,128)(2,1)S(1)} %get-tuple-element.56), channel_id=1, source_target_pairs={{0,4},{4,0},{8,12},{12,8},{1,5},{5,1},{9,13},{13,9},{2,6},{6,2},{1... | collective-permute-start | bytes 251912 | tf_op jit(solution)/shard_map/ppermute | solution.py:21
  40.0 2.3 %collective-permute-start.10 = (bf16[96,2048]{1,0:T(8,128)(2,1)S(1)}, bf16[96,2048]{1,0:T(8,128)(2,1)S(1)}, u32[]{:S(2)}, u32[]{:S(2)}) collective-permute-start(bf16[96,2048]{1,0:T(8,128)(2,1)S(1)} %shard_map.100.mine), channel_id=1, source_target_pairs={{0,16},{16,0},{1,17},{17,1},{2,18},{18,2},{3,19},{19,3},{4,20},{20... | collective-permute-start | bytes 1179656 | tf_op jit(solution)/shard_map/ppermute | solution.py:21

commit v22 on v20

--- a/solution.py
+++ b/solution.py
@@ -120,10 +120,10 @@
     return d_pre, mixers, prob, dot(act.astype(bf16), d_rows, (0, 0))
 
 
-def gather_kernel(*refs):
+def gather_kernel(order, *refs):
     *chunks, x_out, d_out = refs
     rows = chunks[0].shape[0] // 2
-    values = [c[...].astype(f32) for c in reversed(chunks)]
+    values = [chunks[order.index(c)][...].astype(f32) for c in range(len(order))]
     x_out[...] = jnp.concatenate([v[:rows] for v in values]).astype(bf16)
     d_out[...] = jnp.concatenate([v[rows:] for v in values]).astype(bf16)
 
@@ -265,7 +265,9 @@
         moved = chunks[0].reshape(2, experts, cap, width)
         moved = lax.all_to_all(moved, "ep", split_axis=1, concat_axis=1, tiled=True)
         chunks = [moved.reshape(2 * rows, width)]
-    own = kernel_call(gather_kernel, chunks[::-1], [shape((slots, width), bf16)] * 2, flops=2 * 10**9)
+    order = [*range(chunk_count)][::-1]
+    order = [*order[1:2], *order[:1], *order[2:]]
+    own = kernel_call(functools.partial(gather_kernel, order), [chunks[c] for c in order], [shape((slots, width), bf16)] * 2, flops=2 * 10**9)
     other = [swap(part, "rep", 1) for part in own]
 
     wide = width + LANES

time: 42.6 us -> 43.1 us (1.012)
  starting transfers between devices: 17.9 us -> 19.4 us
  waiting for transfers between devices: 17.6 us -> 16.7 us
    ppermute x5, starting transfers between devices: 7.83 us -> 9.48 us  [swap_by_core(): return lax.ppermute(value, ('rep', 'dp'), pairs)]
    ppermute x11, waiting for transfers between devices: 11.2 us -> 9.77 us  [swap(): lax.ppermute(value, axis, [(i, i ^ mask) for i in range(lax.axis_size(axi...]
    ppermute x5, waiting for transfers between devices: 6.35 us -> 6.92 us  [swap_by_core(): return lax.ppermute(value, ('rep', 'dp'), pairs)]
  transfers between devices with their start and end apart: 16 -> 16, of which waited for: 7 -> 8; matrix products, arithmetic and copies ran while one was open for 0% -> 0% of each run, Pallas kernels for 9% -> 9%
where the time goes in v22:
time: 43.1 us; the launch traced here: 43 us
  starting transfers between devices  19.4 us (45%)
  waiting for transfers between devices  16.7 us (39%)
  Pallas kernels  6.2 us (14%)
  between operations  0.73 us (2%)
    ppermute x11, starting transfers between devices, swap(): lax.ppermute(value, axis, [(i, i ^ mask) for i in range(lax.axis_size(axi...  9.89 us
    ppermute x11, waiting for transfers between devices, swap(): lax.ppermute(value, axis, [(i, i ^ mask) for i in range(lax.axis_size(axi...  9.77 us
    ppermute x5, starting transfers between devices, swap_by_core(): return lax.ppermute(value, ('rep', 'dp'), pairs)  9.48 us
    ppermute x5, waiting for transfers between devices, swap_by_core(): return lax.ppermute(value, ('rep', 'dp'), pairs)  6.92 us
    pallas_call x10, Pallas kernels, kernel_call(): pl.pallas_call(body, out_shape=outputs, in_specs=kwargs.pop('in_specs', [...  6.2 us
  transfers between devices with their start and end apart: 16, of which 8 were waited for; matrix products, arithmetic and copies ran while one was open for 0% of the time, Pallas kernels for 9%

profile of v22, /device:TPU:0, one launch (start us, length us, event | category | flops | bytes accessed | tf_op | source)
XLA Modules:
  0.0 43.0 jit_solution(9139120954387618072)
XLA Ops:
  0.6 1.5 %shard_map.94 = (bf16[40,2048]{1,0:T(8,128)(2,1)S(1)}, bf16[40,2048]{1,0:T(8,128)(2,1)S(1)}, bf16[40,2048]{1,0:T(8,128)(2,1)S(1)}, bf16[40,2048]{1,0:T(8,128)(2,...) custom-call(s32[2,32]{1,0:T(2,128)} %bitcast.5, bf16[2,32]{1,0:T(2,128)(2,1)} %bitcast.3, ...), custom_call_target="tpu_custom_call" | custom-call | bytes 3277440 | tf_op jit(solution)/shard_map/pallas_call | solution.py:37
  2.2 3.0 %collective-permute-start.5 = (bf16[144,2048]{1,0:T(8,128)(2,1)S(1)}, bf16[144,2048]{1,0:T(8,128)(2,1)S(1)}, u32[]{:S(2)}, u32[]{:S(2)}) collective-permute-start(bf16[144,2048]{1,0:T(8,128)(2,1)S(1)} %get-tuple-element.37.refs_4_), channel_id=1, source_target_pairs={{0,1},{1,0},{2,3},{3,2},{16,18},{17,19},{18,16},{19,17},{4,5},{5,4... | collective-permute-start | bytes 1769480 | tf_op jit(solution)/shard_map/ppermute | solution.py:31
  5.2 2.6 %collective-permute-start = (bf16[40,2048]{1,0:T(8,128)(2,1)S(1)}, bf16[40,2048]{1,0:T(8,128)(2,1)S(1)}, u32[]{:S(2)}, u32[]{:S(2)}) collective-permute-start(bf16[40,2048]{1,0:T(8,128)(2,1)S(1)} %get-tuple-element.31), channel_id=1, source_target_pairs={{0,8},{4,12},{8,0},{12,4},{1,9},{5,13},{9,1},{13,5},{2,10},{6,14},... | collective-permute-start | bytes 491528 | tf_op jit(solution)/shard_map/ppermute | solution.py:21
  7.8 1.3 %collective-permute-start.1 = (bf16[40,2048]{1,0:T(8,128)(2,1)S(1)}, bf16[40,2048]{1,0:T(8,128)(2,1)S(1)}, u32[]{:S(2)}, u32[]{:S(2)}) collective-permute-start(bf16[40,2048]{1,0:T(8,128)(2,1)S(1)} %get-tuple-element.32), channel_id=1, source_target_pairs={{0,12},{4,8},{8,4},{12,0},{1,13},{5,9},{9,5},{13,1},{2,14},{6,10},... | collective-permute-start | bytes 491528 | tf_op jit(solution)/shard_map/ppermute | solution.py:21
  9.1 0.2 collective-permute-start.2
  9.4 0.5 %collective-permute-start.6 = (bf16[144,2048]{1,0:T(8,128)(2,1)S(1)}, bf16[144,2048]{1,0:T(8,128)(2,1)S(1)}, u32[]{:S(2)}, u32[]{:S(2)}) collective-permute-start(bf16[144,2048]{1,0:T(8,128)(2,1)S(1)} %get-tuple-element.40), channel_id=1, source_target_pairs={{0,1},{1,0},{2,3},{3,2},{16,18},{17,19},{18,16},{19,17},{4,5},{5,4... | collective-permute-start | bytes 1769480 | tf_op jit(solution)/shard_map/ppermute | solution.py:31
  9.9 3.2 %collective-permute-done.5.refs_5_ = bf16[144,2048]{1,0:T(8,128)(2,1)S(1)} collective-permute-done((bf16[144,2048]{1,0:T(8,128)(2,1)S(1)}, bf16[144,2048]{1,0:T(8,128)(2,1)S(1)}, u32[]{:S(2)}, u32[]{:S(2)}) %collective-permute-start.5) | collective-permute-done | bytes 589856 | tf_op jit(solution)/shard_map/ppermute | solution.py:31
  13.1 2.0 %collective-permute-start.8 = (bf16[144,2048]{1,0:T(8,128)(2,1)S(1)}, bf16[144,2048]{1,0:T(8,128)(2,1)S(1)}, u32[]{:S(2)}, u32[]{:S(2)}) collective-permute-start(bf16[144,2048]{1,0:T(8,128)(2,1)S(1)} %collective-permute-done.5.refs_5_), channel_id=1, source_target_pairs={{0,2},{1,3},{2,0},{3,1},{16,17},{17,16},{18,19},{19,18},{4,6},{5,7... | collective-permute-start | bytes 1769480 | tf_op jit(solution)/shard_map/ppermute | solution.py:31
  15.1 4.9 %collective-permute-done.refs_0_ = bf16[40,2048]{1,0:T(8,128)(2,1)S(1)} collective-permute-done((bf16[40,2048]{1,0:T(8,128)(2,1)S(1)}, bf16[40,2048]{1,0:T(8,128)(2,1)S(1)}, u32[]{:S(2)}, u32[]{:S(2)}) %collective-permute-start) | collective-permute-done | bytes 163872 | tf_op jit(solution)/shard_map/ppermute | solution.py:21
  20.0 0.0 collective-permute-done.1.refs_1_
  20.0 0.2 collective-permute-done.2.refs_2_
  20.2 0.1 shard_map.95
  20.3 0.1 collective-permute-start.3
  20.4 0.5 %collective-permute-start.4 = (bf16[80,2048]{1,0:T(8,128)(2,1)S(1)}, bf16[80,2048]{1,0:T(8,128)(2,1)S(1)}, u32[]{:S(2)}, u32[]{:S(2)}) collective-permute-start(bf16[80,2048]{1,0:T(8,128)(2,1)S(1)} %get-tuple-element.36.refs_1_), channel_id=1, source_target_pairs={{0,16},{16,0},{1,17},{17,1},{2,18},{18,2},{3,19},{19,3},{4,20},{20... | collective-permute-start | bytes 983048 | tf_op jit(solution)/shard_map/ppermute | solution.py:21
  20.8 1.1 %collective-permute-done.3.refs_2_ = bf16[80,2048]{1,0:T(8,128)(2,1)S(1)} collective-permute-done((bf16[80,2048]{1,0:T(8,128)(2,1)S(1)}, bf16[80,2048]{1,0:T(8,128)(2,1)S(1)}, u32[]{:S(2)}, u32[]{:S(2)}) %collective-permute-start.3) | collective-permute-done | bytes 327712 | tf_op jit(solution)/shard_map/ppermute | solution.py:21
  22.0 0.5 %collective-permute-done.4.refs_3_ = bf16[80,2048]{1,0:T(8,128)(2,1)S(1)} collective-permute-done((bf16[80,2048]{1,0:T(8,128)(2,1)S(1)}, bf16[80,2048]{1,0:T(8,128)(2,1)S(1)}, u32[]{:S(2)}, u32[]{:S(2)}) %collective-permute-start.4) | collective-permute-done | bytes 327712 | tf_op jit(solution)/shard_map/ppermute | solution.py:21
  22.4 1.2 %shard_map.96 = (f32[160,2176]{1,0:T(8,128)S(1)}, f32[48,2048]{1,0:T(8,128)S(1)}, bf16[48,2048]{1,0:T(8,128)(2,1)S(1)}) custom-call(bf16[80,2048]{1,0:T(8,128)(2,1)S(1)} %get-tuple-element.35.refs_0_, bf16[80,2048]{1,0:T(8,128)(2,1)S(1)} %get-tuple-element.36.refs_1_, bf16[80,2048]{1,0:T(8,128)(2,1)S(1)} %collective-permute-done.3.refs_2_, ...), custom_call_target="tpu_custom_call" | custom-call | flops 1000000000 | bytes 4472832 | tf_op jit(solution)/shard_map/pallas_call | solution.py:37
  23.6 0.1 collective-permute-done.6.refs_5_.refs_7_
  23.7 0.8 %shard_map.97 = (bf16[160,96]{1,0:T(8,128)(2,1)S(1)}, f32[160,128]{1,0:T(8,128)S(1)}, bf16[96,2048]{1,0:T(8,128)(2,1)S(1)}) custom-call(bf16[80,2048]{1,0:T(8,128)(2,1)S(1)} %get-tuple-element.35.refs_0_, bf16[80,2048]{1,0:T(8,128)(2,1)S(1)} %get-tuple-element.36.refs_1_, bf16[80,2048]{1,0:T(8,128)(2,1)S(1)} %collective-permute-done.3.refs_2_, ...), custom_call_target="tpu_custom_call" | custom-call | bytes 2603008 | tf_op jit(solution)/shard_map/pallas_call | solution.py:37
  24.6 2.4 %collective-permute-start.7 = (bf16[96,2048]{1,0:T(8,128)(2,1)S(1)}, bf16[96,2048]{1,0:T(8,128)(2,1)S(1)}, u32[]{:S(2)}, u32[]{:S(2)}) collective-permute-start(bf16[96,2048]{1,0:T(8,128)(2,1)S(1)} %get-tuple-element.41), channel_id=1, source_target_pairs={{0,1},{1,0},{2,3},{3,2},{16,18},{17,19},{18,16},{19,17},{4,5},{5,4... | collective-permute-start | bytes 1179656 | tf_op jit(solution)/shard_map/ppermute | solution.py:31
  27.0 0.0 collective-permute-done.8.refs_8_
  27.0 1.0 %shard_map.98 = (f32[80,2176]{1,0:T(8,128)S(1)}, bf16[40,2176]{1,0:T(8,128)(2,1)S(1)}, bf16[40,2176]{1,0:T(8,128)(2,1)S(1)}, bf16[48,2048]{1,0:T(8,128)(2,1)S(1)}) custom-call(bf16[80,2048]{1,0:T(8,128)(2,1)S(1)} %get-tuple-element.35.refs_0_, bf16[80,2048]{1,0:T(8,128)(2,1)S(1)} %get-tuple-element.36.refs_1_, ...), custom_call_target="tpu_custom_call" | custom-call | bytes 5236736 | tf_op jit(solution)/shard_map/pallas_call | solution.py:37
  28.0 0.1 collective-permute-start.11
  28.1 0.5 %collective-permute-start.14 = (bf16[40,2176]{1,0:T(8,128)(2,1)S(1)}, bf16[40,2176]{1,0:T(8,128)(2,1)S(1)}, u32[]{:S(2)}, u32[]{:S(2)}) collective-permute-start(bf16[40,2176]{1,0:T(8,128)(2,1)S(1)} %get-tuple-element.50), channel_id=1, source_target_pairs={{0,16},{16,0},{1,17},{17,1},{2,18},{18,2},{3,19},{19,3},{4,20},{20... | collective-permute-start | bytes 522248 | tf_op jit(solution)/shard_map/ppermute | solution.py:21
  28.6 1.5 %collective-permute-start.9 = (bf16[48,2048]{1,0:T(8,128)(2,1)S(1)}, bf16[48,2048]{1,0:T(8,128)(2,1)S(1)}, u32[]{:S(2)}, u32[]{:S(2)}) collective-permute-start(bf16[48,2048]{1,0:T(8,128)(2,1)S(1)} %get-tuple-element.45), channel_id=1, source_target_pairs={{0,3},{1,2},{2,1},{3,0},{16,19},{17,18},{18,17},{19,16},{4,7},{5,6... | collective-permute-start | bytes 589832 | tf_op jit(solution)/shard_map/ppermute | solution.py:31
  30.1 0.0 collective-permute-done.11.got
  30.1 0.0 copy-start
  30.1 0.1 shard_map.100
  30.2 3.7 %collective-permute-start.12 = (bf16[328,128]{1,0:T(8,128)(2,1)S(1)}, bf16[328,128]{1,0:T(8,128)(2,1)S(1)}, u32[]{:S(2)}, u32[]{:S(2)}) collective-permute-start(bf16[328,128]{1,0:T(8,128)(2,1)S(1)} %get-tuple-element.48), channel_id=1, source_target_pairs={{0,12},{4,8},{8,4},{12,0},{1,13},{5,9},{9,5},{13,1},{2,14},{6,10},... | collective-permute-start | bytes 251912 | tf_op jit(solution)/shard_map/ppermute | solution.py:21
  33.9 0.0 collective-permute-start.13
  33.9 0.0 collective-permute-done.14.got
  33.9 0.1 shard_map.101
  34.0 0.8 %collective-permute-start.15 = (bf16[328,128]{1,0:T(8,128)(2,1)S(1)}, bf16[328,128]{1,0:T(8,128)(2,1)S(1)}, u32[]{:S(2)}, u32[]{:S(2)}) collective-permute-start(bf16[328,128]{1,0:T(8,128)(2,1)S(1)} %get-tuple-element.51), channel_id=1, source_target_pairs={{0,4},{4,0},{8,12},{12,8},{1,5},{5,1},{9,13},{13,9},{2,6},{6,2},{1... | collective-permute-start | bytes 251912 | tf_op jit(solution)/shard_map/ppermute | solution.py:21
  34.8 0.0 collective-permute-done.7.near
  34.8 3.6 %collective-permute-done.9.far = bf16[48,2048]{1,0:T(8,128)(2,1)S(1)} collective-permute-done((bf16[48,2048]{1,0:T(8,128)(2,1)S(1)}, bf16[48,2048]{1,0:T(8,128)(2,1)S(1)}, u32[]{:S(2)}, u32[]{:S(2)}) %collective-permute-start.9) | collective-permute-done | bytes 196640 | tf_op jit(solution)/shard_map/ppermute | solution.py:31
  38.4 0.1 shard_map.99.mine
  38.5 0.1 collective-permute-start.10
  38.6 0.0 collective-permute-done.12.refs_0_
  38.6 3.1 %collective-permute-done.13.refs_1_ = bf16[328,128]{1,0:T(8,128)(2,1)S(1)} collective-permute-done((bf16[328,128]{1,0:T(8,128)(2,1)S(1)}, bf16[328,128]{1,0:T(8,128)(2,1)S(1)}, u32[]{:S(2)}, u32[]{:S(2)}) %collective-permute-start.13) | collective-permute-done | bytes 84000 | tf_op jit(solution)/shard_map/ppermute | solution.py:21
  41.7 0.0 collective-permute-done.15.refs_2_
  41.7 0.0 copy-done
  41.7 0.3 shard_map.102
  42.0 0.0 collective-permute-done.10.theirs
  42.0 1.0 %shard_map.103 = (f32[1,96,2048]{2,1,0:T(8,128)}, bf16[32,2048]{1,0:T(8,128)(2,1)}, bf16[2,32]{1,0:T(2,128)(2,1)}) custom-call(bf16[96,2048]{1,0:T(8,128)(2,1)S(1)} %shard_map.99.mine, bf16[96,2048]{1,0:T(8,128)(2,1)S(1)} %collective-permute-done.10.theirs, bf16[32,2048]{1,0:T(8,128)(2,1)S(1)} %get-tuple-element.54.tokens, ...), custom_call_target="tpu_custom_call" | custom-call | bytes 1835264 | tf_op jit(solution)/shard_map/pallas_call | solution.py:37
Async XLA Ops:
  2.2 10.9 %collective-permute-start.5 = (bf16[144,2048]{1,0:T(8,128)(2,1)S(1)}, bf16[144,2048]{1,0:T(8,128)(2,1)S(1)}, u32[]{:S(2)}, u32[]{:S(2)}) collective-permute-start(bf16[144,2048]{1,0:T(8,128)(2,1)S(1)} %get-tuple-element.37.refs_4_), channel_id=1, source_target_pairs={{0,1},{1,0},{2,3},{3,2},{16,18},{17,19},{18,16},{19,17},{4,5},{5,4... | collective-permute-start | bytes 1769480 | tf_op jit(solution)/shard_map/ppermute | solution.py:31
  5.2 14.8 %collective-permute-start = (bf16[40,2048]{1,0:T(8,128)(2,1)S(1)}, bf16[40,2048]{1,0:T(8,128)(2,1)S(1)}, u32[]{:S(2)}, u32[]{:S(2)}) collective-permute-start(bf16[40,2048]{1,0:T(8,128)(2,1)S(1)} %get-tuple-element.31), channel_id=1, source_target_pairs={{0,8},{4,12},{8,0},{12,4},{1,9},{5,13},{9,1},{13,5},{2,10},{6,14},... | collective-permute-start | bytes 491528 | tf_op jit(solution)/shard_map/ppermute | solution.py:21
  7.8 12.2 %collective-permute-start.1 = (bf16[40,2048]{1,0:T(8,128)(2,1)S(1)}, bf16[40,2048]{1,0:T(8,128)(2,1)S(1)}, u32[]{:S(2)}, u32[]{:S(2)}) collective-permute-start(bf16[40,2048]{1,0:T(8,128)(2,1)S(1)} %get-tuple-element.32), channel_id=1, source_target_pairs={{0,12},{4,8},{8,4},{12,0},{1,13},{5,9},{9,5},{13,1},{2,14},{6,10},... | collective-permute-start | bytes 491528 | tf_op jit(solution)/shard_map/ppermute | solution.py:21
  9.1 11.0 %collective-permute-start.2 = (bf16[40,2048]{1,0:T(8,128)(2,1)S(1)}, bf16[40,2048]{1,0:T(8,128)(2,1)S(1)}, u32[]{:S(2)}, u32[]{:S(2)}) collective-permute-start(bf16[40,2048]{1,0:T(8,128)(2,1)S(1)} %get-tuple-element.33), channel_id=1, source_target_pairs={{0,4},{4,0},{8,12},{12,8},{1,5},{5,1},{9,13},{13,9},{2,6},{6,2},{1... | collective-permute-start | bytes 491528 | tf_op jit(solution)/shard_map/ppermute | solution.py:21
  9.4 14.4 %collective-permute-start.6 = (bf16[144,2048]{1,0:T(8,128)(2,1)S(1)}, bf16[144,2048]{1,0:T(8,128)(2,1)S(1)}, u32[]{:S(2)}, u32[]{:S(2)}) collective-permute-start(bf16[144,2048]{1,0:T(8,128)(2,1)S(1)} %get-tuple-element.40), channel_id=1, source_target_pairs={{0,1},{1,0},{2,3},{3,2},{16,18},{17,19},{18,16},{19,17},{4,5},{5,4... | collective-permute-start | bytes 1769480 | tf_op jit(solution)/shard_map/ppermute | solution.py:31
  13.1 13.9 %collective-permute-start.8 = (bf16[144,2048]{1,0:T(8,128)(2,1)S(1)}, bf16[144,2048]{1,0:T(8,128)(2,1)S(1)}, u32[]{:S(2)}, u32[]{:S(2)}) collective-permute-start(bf16[144,2048]{1,0:T(8,128)(2,1)S(1)} %collective-permute-done.5.refs_5_), channel_id=1, source_target_pairs={{0,2},{1,3},{2,0},{3,1},{16,17},{17,16},{18,19},{19,18},{4,6},{5,7... | collective-permute-start | bytes 1769480 | tf_op jit(solution)/shard_map/ppermute | solution.py:31
  20.3 1.7 %collective-permute-start.3 = (bf16[80,2048]{1,0:T(8,128)(2,1)S(1)}, bf16[80,2048]{1,0:T(8,128)(2,1)S(1)}, u32[]{:S(2)}, u32[]{:S(2)}) collective-permute-start(bf16[80,2048]{1,0:T(8,128)(2,1)S(1)} %get-tuple-element.35.refs_0_), channel_id=1, source_target_pairs={{0,16},{16,0},{1,17},{17,1},{2,18},{18,2},{3,19},{19,3},{4,20},{20... | collective-permute-start | bytes 983048 | tf_op jit(solution)/shard_map/ppermute | solution.py:21
  20.4 2.1 %collective-permute-start.4 = (bf16[80,2048]{1,0:T(8,128)(2,1)S(1)}, bf16[80,2048]{1,0:T(8,128)(2,1)S(1)}, u32[]{:S(2)}, u32[]{:S(2)}) collective-permute-start(bf16[80,2048]{1,0:T(8,128)(2,1)S(1)} %get-tuple-element.36.refs_1_), channel_id=1, source_target_pairs={{0,16},{16,0},{1,17},{17,1},{2,18},{18,2},{3,19},{19,3},{4,20},{20... | collective-permute-start | bytes 983048 | tf_op jit(solution)/shard_map/ppermute | solution.py:21
  24.6 10.2 %collective-permute-start.7 = (bf16[96,2048]{1,0:T(8,128)(2,1)S(1)}, bf16[96,2048]{1,0:T(8,128)(2,1)S(1)}, u32[]{:S(2)}, u32[]{:S(2)}) collective-permute-start(bf16[96,2048]{1,0:T(8,128)(2,1)S(1)} %get-tuple-element.41), channel_id=1, source_target_pairs={{0,1},{1,0},{2,3},{3,2},{16,18},{17,19},{18,16},{19,17},{4,5},{5,4... | collective-permute-start | bytes 1179656 | tf_op jit(solution)/shard_map/ppermute | solution.py:31
  28.0 2.1 %collective-permute-start.11 = (bf16[40,2176]{1,0:T(8,128)(2,1)S(1)}, bf16[40,2176]{1,0:T(8,128)(2,1)S(1)}, u32[]{:S(2)}, u32[]{:S(2)}) collective-permute-start(bf16[40,2176]{1,0:T(8,128)(2,1)S(1)} %get-tuple-element.47), channel_id=1, source_target_pairs={{0,16},{16,0},{1,17},{17,1},{2,18},{18,2},{3,19},{19,3},{4,20},{20... | collective-permute-start | bytes 522248 | tf_op jit(solution)/shard_map/ppermute | solution.py:21
  28.1 5.8 %collective-permute-start.14 = (bf16[40,2176]{1,0:T(8,128)(2,1)S(1)}, bf16[40,2176]{1,0:T(8,128)(2,1)S(1)}, u32[]{:S(2)}, u32[]{:S(2)}) collective-permute-start(bf16[40,2176]{1,0:T(8,128)(2,1)S(1)} %get-tuple-element.50), channel_id=1, source_target_pairs={{0,16},{16,0},{1,17},{17,1},{2,18},{18,2},{3,19},{19,3},{4,20},{20... | collective-permute-start | bytes 522248 | tf_op jit(solution)/shard_map/ppermute | solution.py:21
  28.6 9.8 %collective-permute-start.9 = (bf16[48,2048]{1,0:T(8,128)(2,1)S(1)}, bf16[48,2048]{1,0:T(8,128)(2,1)S(1)}, u32[]{:S(2)}, u32[]{:S(2)}) collective-permute-start(bf16[48,2048]{1,0:T(8,128)(2,1)S(1)} %get-tuple-element.45), channel_id=1, source_target_pairs={{0,3},{1,2},{2,1},{3,0},{16,19},{17,18},{18,17},{19,16},{4,7},{5,6... | collective-permute-start | bytes 589832 | tf_op jit(solution)/shard_map/ppermute | solution.py:31
  30.1 11.6 %copy-start = (bf16[32,2]{0,1:T(2,128)(2,1)S(1)}, bf16[32,2]{0,1:T(2,128)(2,1)}, u32[]{:S(2)}) copy-start(bf16[32,2]{0,1:T(2,128)(2,1)} %param.10) | copy-start | bytes 388
  30.2 8.4 %collective-permute-start.12 = (bf16[328,128]{1,0:T(8,128)(2,1)S(1)}, bf16[328,128]{1,0:T(8,128)(2,1)S(1)}, u32[]{:S(2)}, u32[]{:S(2)}) collective-permute-start(bf16[328,128]{1,0:T(8,128)(2,1)S(1)} %get-tuple-element.48), channel_id=1, source_target_pairs={{0,12},{4,8},{8,4},{12,0},{1,13},{5,9},{9,5},{13,1},{2,14},{6,10},... | collective-permute-start | bytes 251912 | tf_op jit(solution)/shard_map/ppermute | solution.py:21
  33.9 7.8 %collective-permute-start.13 = (bf16[328,128]{1,0:T(8,128)(2,1)S(1)}, bf16[328,128]{1,0:T(8,128)(2,1)S(1)}, u32[]{:S(2)}, u32[]{:S(2)}) collective-permute-start(bf16[328,128]{1,0:T(8,128)(2,1)S(1)} %get-tuple-element.49), channel_id=1, source_target_pairs={{0,8},{4,12},{8,0},{12,4},{1,9},{5,13},{9,1},{13,5},{2,10},{6,14},... | collective-permute-start | bytes 251912 | tf_op jit(solution)/shard_map/ppermute | solution.py:21
  34.0 7.7 %collective-permute-start.15 = (bf16[328,128]{1,0:T(8,128)(2,1)S(1)}, bf16[328,128]{1,0:T(8,128)(2,1)S(1)}, u32[]{:S(2)}, u32[]{:S(2)}) collective-permute-start(bf16[328,128]{1,0:T(8,128)(2,1)S(1)} %get-tuple-element.51), channel_id=1, source_target_pairs={{0,4},{4,0},{8,12},{12,8},{1,5},{5,1},{9,13},{13,9},{2,6},{6,2},{1... | collective-permute-start | bytes 251912 | tf_op jit(solution)/shard_map/ppermute | solution.py:21
  38.5 3.5 %collective-permute-start.10 = (bf16[96,2048]{1,0:T(8,128)(2,1)S(1)}, bf16[96,2048]{1,0:T(8,128)(2,1)S(1)}, u32[]{:S(2)}, u32[]{:S(2)}) collective-permute-start(bf16[96,2048]{1,0:T(8,128)(2,1)S(1)} %shard_map.99.mine), channel_id=1, source_target_pairs={{0,16},{16,0},{1,17},{17,1},{2,18},{18,2},{3,19},{19,3},{4,20},{20... | collective-permute-start | bytes 1179656 | tf_op jit(solution)/shard_map/ppermute | solution.py:21
